TPU v7x, 256 devices: a whole 4x4x8 slice. The times are simulated.
256 devices in a mesh: dp: 16 (over x_lo, y, core), blk: 16 (over x_hi, z).
Axes of the slice: x: 4 (x_hi: 2, x_lo: 2; x = x_hi * 2 + x_lo), y: 4, z: 8, core: 2. Of those that a mesh axis runs over, the one named last changes fastest.
Arguments:
- activations: bfloat16 [4096, 14336], P('dp'), may hold values from -6 to 6
- out_grads: bfloat16 [4096, 4096], P('dp'), may hold values from -0.75 to 0.75
- basis_in: bfloat16 [14336, 8192], P('dp', 'blk'), may hold values from -0.046875 to 0.046875
- basis_out: bfloat16 [4096, 4096], P(None, 'blk'), may hold values from -0.09375 to 0.09375
Outputs:
- correction: float32 [4096, 8192], P('dp', 'blk')
All inputs are finite; a program needn't handle non-finite values.
Results may differ from a plain program's by a relative error of at most 0.0017.
Values may be sent and summed in bfloat16 or wider, within the bound.
No kernel may reach another device: no remote copies, remote signals or barrier semaphores. Data moves between devices by JAX's collectives and lax.ppermute only.
A program may use at most 128 MiB of HBM per device.

v0:
```python
import jax
import jax.numpy as jnp
from jax import lax
from jax.sharding import PartitionSpec as P

TOK = 128
EXAMPLES = 2


def on_device(activations, out_grads, basis_in, basis_out):
    panel = basis_in.shape[1]
    groups = lax.axis_size("dp")
    scale = 1.0 / float(EXAMPLES * groups)
    columns = activations
    proj_in = jnp.dot(
        columns,
        lax.all_gather(basis_in, "dp", axis=0, tiled=True),
        preferred_element_type=jnp.float32,
    ).astype(jnp.bfloat16)
    out_panel = jnp.dot(out_grads, basis_out, preferred_element_type=jnp.float32).astype(
        jnp.bfloat16
    )
    proj_out = lax.all_gather(out_panel, "blk", axis=1, tiled=True)
    owned = proj_out.shape[1] // groups
    columns = proj_out

    def add_example(example, total):
        out_rows = lax.dynamic_slice_in_dim(columns, example * TOK, TOK, 0)
        in_rows = lax.dynamic_slice_in_dim(proj_in, example * TOK, TOK, 0)
        rotated = lax.dot_general(
            out_rows, in_rows, (((0,), (0,)), ((), ())), preferred_element_type=jnp.float32
        )
        return total + rotated * rotated

    summed = lax.psum_scatter(
        lax.fori_loop(
            0, EXAMPLES, add_example, jnp.zeros((lax.axis_size("dp") * owned, panel), jnp.float32)
        ),
        "dp",
        scatter_dimension=0,
        tiled=True,
    )
    return summed * jnp.float32(scale)


def solution(mesh):
    return jax.shard_map(
        on_device,
        mesh=mesh,
        in_specs=(P("dp", None), P("dp", None), P("dp", "blk"), P(None, "blk")),
        out_specs=P("dp", "blk"),
        check_vma=False,
    )
```

profile of v0, /device:TPU:1, one launch (start us, length us, event | category | flops | bytes accessed | tf_op | source)
XLA Modules:
  0.0 278.5 jit_solution(5109260517131308646)
XLA Ops:
  6.5 0.0 copy-start
  6.5 0.0 all-gather.5.cloned.1.call-start
  6.5 0.7 all-gather.5.cloned.1.call-update
  7.3 0.0 all-gather.3.cloned.1.call-start
  7.3 0.8 copy-done
  8.1 3.0 %convolution_convert_fusion.1 = bf16[256,256]{1,0:T(8,128)(2,1)} fusion(bf16[256,4096]{1,0:T(8,128)(2,1)S(1)} %copy-done, bf16[4096,256]{1,0:T(8,128)(2,1)} %param.9), kind=kOutput, calls=%fused_computation.5 | convolution fusion | flops 536936448 | bytes 4325376 | tf_op jit(solution)/shard_map/dot_general | solution.py:20
  11.1 0.0 all-gather.3.cloned.1.call-update
  11.1 0.0 reduce-scatter.2.cloned.1.call-start
  11.2 86.6 %all-gather.5.cloned.1.call-done = bf16[14336,512]{1,0:T(8,128)(2,1)} async-done(((bf16[896,512]{1,0:T(8,128)(2,1)}), bf16[14336,512]{1,0:T(8,128)(2,1)}) %all-gather.5.cloned.1.call-update) | async-done | bytes 14680080 | tf_op jit(solution)/shard_map/all_gather | solution.py:17
  97.7 11.2 %convolution_convert_fusion = bf16[256,512]{1,0:T(8,128)(2,1)S(1)} fusion(bf16[256,14336]{1,0:T(8,128)(2,1)} %param.6, bf16[14336,512]{1,0:T(8,128)(2,1)} %all-gather.5.cloned.1.call-done), kind=kOutput, calls=%fused_computation.4 | convolution fusion | flops 3758227456 | bytes 22282240 | tf_op jit(solution)/shard_map/dot_general | solution.py:15
  108.9 73.8 %all-gather.3.cloned.1.call-done = bf16[256,4096]{1,0:T(8,128)(2,1)} async-done(((bf16[256,256]{1,0:T(8,128)(2,1)}), bf16[256,4096]{1,0:T(8,128)(2,1)}) %all-gather.3.cloned.1.call-update) | async-done | bytes 2097168 | tf_op jit(solution)/shard_map/all_gather | solution.py:23
  182.7 14.1 %while.14 = (s32[]{:T(128)}, f32[4096,512]{1,0:T(8,128)}, bf16[256,4096]{1,0:T(8,128)(2,1)}, bf16[256,512]{1,0:T(8,128)(2,1)S(1)}, s32[]{:T(128)}, /*index=5*/s32[]{:T(128)}, s32[]{:T(128)}, s32[]{:T(128)}) while((s32[]{:T(128)}, f32[4096,512]{1,0:T(8,128)}, bf16[256,4096]{1,0:T(8,128)(2,1)}, bf16[256,512]{1,0:T(8,128)(2,1)S(1)}, ...), condition=%wide.region_1.0_spmd.clone, body=%wide.region_0.0_spmd.clone.sunk | while | flops 543162368 | bytes 17958548 | solution.py:36
  182.7 5.8 %select_add_fusion.2 = f32[4096,512]{1,0:T(8,128)} fusion(f32[4096,512]{1,0:T(8,128)} %get-tuple-element.142, pred[]{:T(512)S(6)} %compare.3, bf16[256,4096]{1,0:T(8,128)(2,1)} %get-tuple-element.151, s32[]{:T(128)S(6)} %select_n.10, bf16[256,512]{1,0:T(8,128)(2,1)S(1)} %get-tuple-element.152), kind=kOutput, calls=%fused_computation.clone.1 | convolution fusion | flops 543162368 | bytes 17958400 | tf_op jit(solution)/shard_map/while/body/eval_jaxpr/dot_general | solution.py:30
  188.5 8.3 %select_add_fusion.2 = f32[4096,512]{1,0:T(8,128)} fusion(f32[4096,512]{1,0:T(8,128)} %get-tuple-element.142, pred[]{:T(512)S(6)} %compare.3, bf16[256,4096]{1,0:T(8,128)(2,1)} %get-tuple-element.151, s32[]{:T(128)S(6)} %select_n.10, bf16[256,512]{1,0:T(8,128)(2,1)S(1)} %get-tuple-element.152), kind=kOutput, calls=%fused_computation.clone.1 | convolution fusion | flops 543162368 | bytes 17958400 | tf_op jit(solution)/shard_map/while/body/eval_jaxpr/dot_general | solution.py:30
  196.8 0.0 reduce-scatter.2.cloned.1.call-update
  196.8 73.3 %reduce-scatter.2.cloned.1.call-done = f32[256,512]{1,0:T(8,128)} async-done(((f32[4096,512]{1,0:T(8,128)}), f32[256,512]{1,0:T(8,128)}) %reduce-scatter.2.cloned.1.call-update) | async-done | bytes 524304 | tf_op jit(solution)/shard_map/reduce_scatter | solution.py:35
  270.1 1.9 broadcast_multiply_fusion
  (1 shorter events, 0.0 us)
Async XLA Ops:
  6.5 1.6 copy-start
  6.5 91.2 %all-gather.5.cloned.1.call-start = ((), (), s32[]{:S(2)}) async-start(), calls=%async_computation.2 | async-start | bytes 15597568 | tf_op jit(solution)/shard_map/all_gather | solution.py:17
  7.3 175.5 %all-gather.3.cloned.1.call-start = ((), (), s32[]{:S(2)}) async-start(), calls=%async_computation.1 | async-start | bytes 2228224 | tf_op jit(solution)/shard_map/all_gather | solution.py:23
  11.1 259.0 %reduce-scatter.2.cloned.1.call-start = ((), (), s32[]{:S(2)}) async-start(), calls=%async_computation.3 | async-start | bytes 8912896 | tf_op jit(solution)/shard_map/reduce_scatter | solution.py:35
Sparse Core Ops, SparseCore 0:
  9.2 88.4 all-gather.4
  100.2 82.4 all-gather.2
  196.9 73.0 reduce-scatter.1
where the time goes:
time: 281 us; the launch traced here: 278 us
  waiting for transfers between devices  234 us (83%)
  matrix products  28.2 us (10%)
  between operations  13.1 us (5%)
    all_gather x1, waiting for transfers between devices, on_device(): lax.all_gather(basis_in, 'dp', axis=0, tiled=True)  86.6 us
    all_gather x1, waiting for transfers between devices, on_device(): proj_out = lax.all_gather(out_panel, 'blk', axis=1, tiled=True)  73.8 us
    reduce_scatter x1, waiting for transfers between devices, on_device(): lax.psum_scatter(lax.fori_loop(0, EXAMPLES, add_example, jnp.zeros((lax.a...  73.3 us
    dot_general x2, matrix products, add_example(): lax.dot_general(out_rows, in_rows, (((0,), (0,)), ((), ())), preferred_el...  14.1 us
    dot_general x1, matrix products, on_device(): jnp.dot(columns, lax.all_gather(basis_in, 'dp', axis=0, tiled=True), pref...  11.2 us
  transfers between devices with their start and end apart: 3, of which 3 were waited for; matrix products, arithmetic and copies ran while one was open for 5% of the time, Pallas kernels for 0%

commit v1 on v0

v1 whole, which is shorter than its diff:
```python
import jax
import jax.numpy as jnp
from jax import lax
from jax.experimental import pallas as pl
from jax.experimental.pallas import tpu as pltpu
from jax.sharding import PartitionSpec as P

TOK = 128
EXAMPLES = 2
NX, NY, NC = 2, 4, 2
NH, NZ = 2, 8
SHORT = 384
CHUNKS = ((0, 256), (256, 256))
OWN, LEFT, RIGHT, ACROSS, FAR = (0, 0), (0, 3), (0, 1), (1, 0), (0, 2)
X_LEFT, X_RIGHT, X_FAR = (1, 3), (1, 1), (1, 2)
ORDER = (OWN, LEFT, RIGHT, ACROSS, FAR, X_LEFT, X_RIGHT, X_FAR)


def dp_index(x, y, c):
    return (x * NY + y) * NC + c


def shift(value, dx=0, dy=0, dc=0):
    pairs = [
        (dp_index(x, y, c), dp_index((x + dx) % NX, (y + dy) % NY, (c + dc) % NC))
        for x in range(NX)
        for y in range(NY)
        for c in range(NC)
    ]
    return lax.ppermute(value, "dp", pairs)


def dot(a, b):
    return jnp.dot(a, b, preferred_element_type=jnp.float32)


def squares_kernel(where_ref, out_ref_rows, *refs):
    in_rows, total_ref = refs[:-1], refs[-1]
    half = total_ref.shape[0] // 2
    for part in range(2):
        rows = pl.ds(part * half, half)
        total = None
        for k, block in enumerate(in_rows):
            at = where_ref[k]
            for example in range(EXAMPLES):
                tokens = pl.ds(example * TOK, TOK)
                rotated = dot(out_ref_rows[at, rows, tokens], block[tokens, :])
                squared = rotated * rotated
                total = squared if total is None else total + squared
        total_ref[rows, :] = total


def sums_of_squares(where, out_rows, in_rows):
    rows, width = out_rows.shape[1], in_rows[0].shape[1]
    vmem = pl.BlockSpec(memory_space=pltpu.VMEM)
    return pl.pallas_call(
        squares_kernel,
        out_shape=jax.ShapeDtypeStruct((rows, width), jnp.float32),
        in_specs=[pl.BlockSpec(memory_space=pltpu.SMEM)] + [vmem] * (1 + len(in_rows)),
        out_specs=vmem,
        compiler_params=pltpu.CompilerParams(vmem_limit_bytes=32 * 1024 * 1024),
        cost_estimate=pl.CostEstimate(
            flops=2 * rows * width * len(in_rows) * EXAMPLES * TOK,
            bytes_accessed=out_rows.size * 2 + rows * width * 4,
            transcendentals=0,
        ),
    )(where, out_rows, *in_rows)


def on_device(activations, out_grads, basis_in, basis_out):
    d, b = lax.axis_index("dp"), lax.axis_index("blk")
    core, y, x = d % NC, (d // NC) % NY, d // (NC * NY)
    scale = 1.0 / float(EXAMPLES * NX * NY * NC)
    depth = basis_in.shape[0]
    place = [((x + dx) % NX) * NY + (y + dy) % NY for dx, dy in ORDER]

    block = dot(out_grads, basis_out).astype(jnp.bfloat16).T
    pairs = []
    for sx in range(NX):
        for sy in range(NY):
            for sc in range(NC):
                for tx in range(NX):
                    for ty in range(NY):
                        for tc in range(NC):
                            source = dp_index(sx, sy, sc) * NH * NZ + dp_index(tx, ty, tc)
                            target = dp_index(tx, ty, sc) * NH * NZ + tc * NZ + sx * NY + sy
                            pairs.append((source, target))
    block = lax.ppermute(block, ("dp", "blk"), pairs)
    other = lax.ppermute(
        block, "blk", [(h * NZ + z, (1 - h) * NZ + z) for h in range(NH) for z in range(NZ)]
    )
    mine = (b // NZ) == core
    block = jnp.concatenate([jnp.where(mine, block, other), jnp.where(mine, other, block)], 0)
    out_rows = lax.all_gather(
        block,
        "blk",
        axis=0,
        axis_index_groups=[[h * NZ + z for z in range(NZ)] for h in range(NH)],
    )
    where = jnp.stack(place).astype(jnp.int32)

    def columns(parity):
        return jnp.stack(
            [
                lax.dynamic_slice_in_dim(activations, (p * NC + parity) * depth, depth, 1)
                for p in place
            ]
        )

    rows = jnp.concatenate([columns(core), shift(columns(1 - core), dc=1)], 1)
    a = dict(zip(ORDER, [rows[k] for k in range(len(ORDER))]))
    tokens = activations.shape[0]

    results = []
    for start, width in CHUNKS:
        own = lax.slice_in_dim(basis_in, start, start + width, axis=1)
        left, right, across = shift(own, dy=1), shift(own, dy=3), shift(own, dx=1)
        total = dot(a[OWN], own) + dot(a[LEFT], left) + dot(a[RIGHT], right)
        total = total + dot(a[ACROSS], across)
        up = shift(jnp.concatenate([across[:SHORT], left[:SHORT]], 0), dy=1)
        down = shift(jnp.concatenate([across[:SHORT], right[SHORT:]], 0), dy=3)
        over = shift(jnp.concatenate([left[SHORT:], right[SHORT:]], 0), dx=1)
        long = depth - SHORT
        far = jnp.concatenate([up[SHORT:], down[SHORT:]], 0)
        x_left = jnp.concatenate([up[:SHORT], over[:long]], 0)
        x_right = jnp.concatenate([down[:SHORT], over[long:]], 0)
        total = total + dot(a[FAR], far) + dot(a[X_LEFT], x_left) + dot(a[X_RIGHT], x_right)
        x_far = jnp.concatenate(
            [shift(x_left[:SHORT], dy=1), shift(x_right[SHORT:], dy=3)], 0
        )
        total = total + dot(a[X_FAR], x_far)
        proj_in = (total[:tokens] + shift(total[tokens:], dc=1)).astype(jnp.bfloat16)

        p_left, p_right, p_far = shift(proj_in, dy=1), shift(proj_in, dy=3), shift(proj_in, dy=2)
        p_across = shift(proj_in, dx=1)
        px_left, px_right = shift(p_across, dy=1), shift(p_across, dy=3)
        px_far = shift(p_far, dx=1)
        sums = sums_of_squares(
            where,
            out_rows,
            (proj_in, p_left, p_right, p_across, p_far, px_left, px_right, px_far),
        )
        half = sums.shape[0] // 2
        results.append((sums[:half] + shift(sums[half:], dc=1)) * jnp.float32(scale))
    return jnp.concatenate(results, 1)


def solution(mesh):
    return jax.shard_map(
        on_device,
        mesh=mesh,
        in_specs=(P("dp", None), P("dp", None), P("dp", "blk"), P(None, "blk")),
        out_specs=P("dp", "blk"),
        check_vma=False,
    )
```

time: 281 us -> 171 us (0.61)
  waiting for transfers between devices: 234 us -> 42.4 us
  starting transfers between devices: 0.08 us -> 59.3 us
  local copies, waits for them, and re-layouts: 0.82 us -> 28.5 us
  matrix products: 28.2 us -> 15.5 us
  other arithmetic: 1.88 us -> 6.36 us
  Pallas kernels: 0 us -> 3.93 us
    all_gather x2 -> x1, waiting for transfers between devices: 160 us -> 0.01 us  [on_device(): lax.all_gather(block, 'blk', axis=0, axis_index_groups=[[h * NZ + z for z...]
    reduce_scatter x1 -> x0, waiting for transfers between devices: 73.3 us -> none  [on_device(): lax.psum_scatter(lax.fori_loop(0, EXAMPLES, add_example, jnp.zeros((lax.a...]
    ppermute x0 -> x37, starting transfers between devices: none -> 59.3 us  [the longest x35 41.3 us: shift(): return lax.ppermute(value, 'dp', pairs)]
    ppermute x0 -> x37, waiting for transfers between devices: none -> 42.4 us  [the longest x35 42.4 us: shift(): return lax.ppermute(value, 'dp', pairs)]
    unnamed x2 -> x20, local copies, waits for them, and re-layouts: 0.82 us -> 18.4 us
    dot_general x4 -> x17, matrix products: 28.2 us -> 15.5 us  [dot(): return jnp.dot(a, b, preferred_element_type=jnp.float32)]
    slice x0 -> x25, local copies, waits for them, and re-layouts: none -> 6.05 us  [the longest x4 2.83 us: on_device(): up = shift(jnp.concatenate([across[:SHORT], left[:SHORT]], 0), dy=1)]
    concatenate x0 -> x9, other arithmetic: none -> 5.23 us  [the longest x1 3.45 us: on_device(): rows = jnp.concatenate([columns(core), shift(columns(1 - core), dc=1)], 1)]
  transfers between devices with their start and end apart: 3 -> 38, of which waited for: 3 -> 13; matrix products, arithmetic and copies ran while one was open for 5% -> 16% of each run, Pallas kernels for 0% -> 2%
where the time goes in v1:
time: 171 us; the launch traced here: 170 us
  starting transfers between devices  59.3 us (35%)
  waiting for transfers between devices  42.4 us (25%)
  local copies, waits for them, and re-layouts  28.5 us (17%)
  matrix products  15.5 us (9%)
  between operations  14 us (8%)
  other arithmetic  6.36 us (4%)
  Pallas kernels  3.93 us (2%)
    ppermute x35, waiting for transfers between devices, shift(): return lax.ppermute(value, 'dp', pairs)  42.4 us
    ppermute x35, starting transfers between devices, shift(): return lax.ppermute(value, 'dp', pairs)  41.3 us
    unnamed x20, local copies, waits for them, and re-layouts  18.4 us
    ppermute x1, starting transfers between devices, on_device(): lax.ppermute(block, 'blk', [(h * NZ + z, (1 - h) * NZ + z) for h in range...  16.7 us
    dot_general x17, matrix products, dot(): return jnp.dot(a, b, preferred_element_type=jnp.float32)  15.5 us
    another operation x2, local copies, waits for them, and re-layouts, columns(): jnp.stack([lax.dynamic_slice_in_dim(activations, (p * NC + parity) * dept...  4.02 us
    pallas_call x2, Pallas kernels, sums_of_squares(): pl.pallas_call(squares_kernel, out_shape=jax.ShapeDtypeStruct((rows, widt...  3.93 us
    concatenate x1, other arithmetic, on_device(): rows = jnp.concatenate([columns(core), shift(columns(1 - core), dc=1)], 1)  3.45 us
  transfers between devices with their start and end apart: 38, of which 13 were waited for; matrix products, arithmetic and copies ran while one was open for 16% of the time, Pallas kernels for 2%

profile of v1, /device:TPU:1, one launch (start us, length us, event | category | flops | bytes accessed | tf_op | source)
XLA Modules:
  0.0 170.0 jit_solution(15185858817934012662)
XLA Ops:
  6.5 2.0 %bitcast_dynamic-update-slice_fusion.15 = bf16[8,256,896]{2,1,0:T(8,128)(2,1)} fusion(bf16[256,14336]{1,0:T(8,128)(2,1)} %param.4, s32[]{:T(128)S(6)} %select_n.139), kind=kLoop, calls=%fused_computation.110 | loop fusion | bytes 917508
  8.6 1.9 %bitcast_dynamic-update-slice_fusion.14 = bf16[8,256,896]{2,1,0:T(8,128)(2,1)} fusion(bf16[8,256,896]{2,1,0:T(8,128)(2,1)} %bitcast_dynamic-update-slice_fusion.15, bf16[256,14336]{1,0:T(8,128)(2,1)} %param.4, s32[]{:T(128)S(6)} %select_n.140), kind=kLoop, calls=%fused_computation.109 | loop fusion | bytes 917508
  10.5 2.2 %bitcast_dynamic-update-slice_fusion.13 = (bf16[8,256,896]{2,1,0:T(8,128)(2,1)}, bf16[8,256,896]{2,1,0:T(8,128)(2,1)}) fusion(bf16[8,256,896]{2,1,0:T(8,128)(2,1)} %bitcast_dynamic-update-slice_fusion.14, bf16[256,14336]{1,0:T(8,128)(2,1)} %param.4, s32[]{:T(128)S(6)} %select_n.141, s32[]{:T(128)S(6)} %select_n.147), kind=kLoop, calls=%fused_computation.108 | loop fusion | bytes 1835016
  12.7 2.2 %bitcast_dynamic-update-slice_fusion.12 = (bf16[8,256,896]{2,1,0:T(8,128)(2,1)}, bf16[8,256,896]{2,1,0:T(8,128)(2,1)}) fusion(bf16[8,256,896]{2,1,0:T(8,128)(2,1)} %get-tuple-element.22, bf16[256,14336]{1,0:T(8,128)(2,1)} %param.4, s32[]{:T(128)S(6)} %select_n.142, bf16[8,256,896]{2,1,0:T(8,128)(2,1)} %get-tuple-element.23, s32[]{:T(128)S(6)} %select_n.148), kind=kLoop, calls=%fused_computation.107 | loop fusion | bytes 1835016
  14.8 2.2 %bitcast_dynamic-update-slice_fusion.11 = (bf16[8,256,896]{2,1,0:T(8,128)(2,1)}, bf16[8,256,896]{2,1,0:T(8,128)(2,1)}) fusion(bf16[8,256,896]{2,1,0:T(8,128)(2,1)} %get-tuple-element.20, bf16[256,14336]{1,0:T(8,128)(2,1)} %param.4, s32[]{:T(128)S(6)} %select_n.143, bf16[8,256,896]{2,1,0:T(8,128)(2,1)} %get-tuple-element.21, s32[]{:T(128)S(6)} %select_n.149), kind=kLoop, calls=%fused_computation.106 | loop fusion | bytes 1835016
  17.0 2.3 %bitcast_dynamic-update-slice_fusion.10 = (bf16[8,256,896]{2,1,0:T(8,128)(2,1)}, bf16[8,256,896]{2,1,0:T(8,128)(2,1)}) fusion(bf16[8,256,896]{2,1,0:T(8,128)(2,1)} %get-tuple-element.18, bf16[256,14336]{1,0:T(8,128)(2,1)} %param.4, s32[]{:T(128)S(6)} %select_n.144, bf16[8,256,896]{2,1,0:T(8,128)(2,1)} %get-tuple-element.19, s32[]{:T(128)S(6)} %select_n.150), kind=kLoop, calls=%fused_computation.105 | loop fusion | bytes 1835016
  19.3 2.2 %bitcast_dynamic-update-slice_fusion.9 = (bf16[8,256,896]{2,1,0:T(8,128)(2,1)}, bf16[8,256,896]{2,1,0:T(8,128)(2,1)}) fusion(bf16[8,256,896]{2,1,0:T(8,128)(2,1)} %get-tuple-element.16, bf16[256,14336]{1,0:T(8,128)(2,1)} %param.4, s32[]{:T(128)S(6)} %select_n.145, bf16[8,256,896]{2,1,0:T(8,128)(2,1)} %get-tuple-element.17, s32[]{:T(128)S(6)} %select_n.151), kind=kLoop, calls=%fused_computation.104 | loop fusion | bytes 1835016
  21.5 2.2 %bitcast_dynamic-update-slice_fusion.8 = (bf16[8,256,896]{2,1,0:T(8,128)(2,1)}, bf16[8,256,896]{2,1,0:T(8,128)(2,1)}) fusion(bf16[8,256,896]{2,1,0:T(8,128)(2,1)} %get-tuple-element.14, bf16[256,14336]{1,0:T(8,128)(2,1)} %param.4, s32[]{:T(128)S(6)} %select_n.146, bf16[8,256,896]{2,1,0:T(8,128)(2,1)} %get-tuple-element.15, s32[]{:T(128)S(6)} %select_n.152), kind=kLoop, calls=%fused_computation.103 | loop fusion | bytes 1835016 | tf_op jit(solution)/shard_map/stack | solution.py:103
  23.7 1.8 %bitcast_dynamic-update-slice_fusion.1 = bf16[8,256,896]{2,1,0:T(8,128)(2,1)} fusion(bf16[8,256,896]{2,1,0:T(8,128)(2,1)} %get-tuple-element.13, bf16[256,14336]{1,0:T(8,128)(2,1)} %param.4, s32[]{:T(128)S(6)} %select_n.153), kind=kLoop, calls=%fused_computation.96 | loop fusion | bytes 917508
  25.5 1.9 %bitcast_dynamic-update-slice_fusion = bf16[8,256,896]{2,1,0:T(8,128)(2,1)} fusion(bf16[8,256,896]{2,1,0:T(8,128)(2,1)} %bitcast_dynamic-update-slice_fusion.1, bf16[256,14336]{1,0:T(8,128)(2,1)} %param.4, s32[]{:T(128)S(6)} %select_n.154), kind=kLoop, calls=%fused_computation.95 | loop fusion | bytes 917508 | tf_op jit(solution)/shard_map/stack | solution.py:103
  27.3 3.2 %collective-permute-start.2 = (bf16[8,256,896]{2,1,0:T(8,128)(2,1)}, bf16[8,256,896]{2,1,0:T(8,128)(2,1)}, u32[]{:S(2)}, u32[]{:S(2)}) collective-permute-start(bf16[8,256,896]{2,1,0:T(8,128)(2,1)} %bitcast_dynamic-update-slice_fusion), channel_id=1, source_target_pairs={{0,16},{16,0},{32,48},{48,32},{64,80},{80,64},{96,112},{112,96},{1... | collective-permute-start | bytes 11010056 | tf_op jit(solution)/shard_map/ppermute | solution.py:30
  31.6 2.3 %convolution_convert_fusion = bf16[256,256]{1,0:T(8,128)(2,1)S(1)} fusion(bf16[4096,256]{1,0:T(8,128)(2,1)S(1)} %copy-done, bf16[256,4096]{1,0:T(8,128)(2,1)} %param.5), kind=kOutput, calls=%fused_computation.28 | convolution fusion | flops 536936448 | bytes 4325376 | tf_op jit(solution)/shard_map/dot_general | solution.py:34
  35.3 16.7 %collective-permute-start.1 = (bf16[256,256]{1,0:T(8,128)(2,1)}, bf16[256,256]{1,0:T(8,128)(2,1)}, u32[]{:S(2)}, u32[]{:S(2)}) collective-permute-start(bf16[256,256]{1,0:T(8,128)(2,1)} %collective-permute-done), channel_id=1, source_target_pairs={{0,8},{1,9},{2,10},{3,11},{4,12},{5,13},{6,14},{7,15},{8,0},{9,1},... | collective-permute-start | bytes 393224 | tf_op jit(solution)/shard_map/ppermute | solution.py:89
  52.0 7.4 %collective-permute-start.4 = (bf16[896,256]{1,0:T(8,128)(2,1)}, bf16[896,256]{1,0:T(8,128)(2,1)}, u32[]{:S(2)}, u32[]{:S(2)}) collective-permute-start(bf16[896,256]{1,0:T(8,128)(2,1)} %get-tuple-element.24), channel_id=1, source_target_pairs={{0,96},{16,112},{32,0},{48,16},{64,32},{80,48},{96,64},{112,80},{1... | collective-permute-start | bytes 1376264 | tf_op jit(solution)/shard_map/ppermute | solution.py:30
  62.2 7.5 %collective-permute-done.3 = bf16[896,256]{1,0:T(8,128)(2,1)S(1)} collective-permute-done((bf16[896,256]{1,0:T(8,128)(2,1)}, bf16[896,256]{1,0:T(8,128)(2,1)S(1)}, u32[]{:S(2)}, u32[]{:S(2)}) %collective-permute-start.3) | collective-permute-done | bytes 458784 | tf_op jit(solution)/shard_map/ppermute | solution.py:30
  72.3 7.4 %collective-permute-done.20 = bf16[896,256]{1,0:T(8,128)(2,1)} collective-permute-done((bf16[896,256]{1,0:T(8,128)(2,1)}, bf16[896,256]{1,0:T(8,128)(2,1)}, u32[]{:S(2)}, u32[]{:S(2)}) %collective-permute-start.20) | collective-permute-done | bytes 458784 | tf_op jit(solution)/shard_map/ppermute | solution.py:30
  82.9 2.7 %collective-permute-start.7 = (bf16[896,256]{1,0:T(8,128)(2,1)S(1)}, bf16[896,256]{1,0:T(8,128)(2,1)S(1)}, u32[]{:S(2)}, u32[]{:S(2)}) collective-permute-start(bf16[896,256]{1,0:T(8,128)(2,1)S(1)} %pad_maximum_fusion.4), channel_id=1, source_target_pairs={{0,96},{16,112},{32,0},{48,16},{64,32},{80,48},{96,64},{112,80},{1... | collective-permute-start | bytes 1376264 | tf_op jit(solution)/shard_map/ppermute | solution.py:30
  85.8 2.3 %collective-permute-done.6 = bf16[768,256]{1,0:T(8,128)(2,1)S(1)} collective-permute-done((bf16[768,256]{1,0:T(8,128)(2,1)S(1)}, bf16[768,256]{1,0:T(8,128)(2,1)S(1)}, u32[]{:S(2)}, u32[]{:S(2)}) %collective-permute-start.6) | collective-permute-done | bytes 393248 | tf_op jit(solution)/shard_map/ppermute | solution.py:30
  89.3 7.2 %collective-permute-done.23 = bf16[768,256]{1,0:T(8,128)(2,1)S(1)} collective-permute-done((bf16[768,256]{1,0:T(8,128)(2,1)S(1)}, bf16[768,256]{1,0:T(8,128)(2,1)S(1)}, u32[]{:S(2)}, u32[]{:S(2)}) %collective-permute-start.23) | collective-permute-done | bytes 393248 | tf_op jit(solution)/shard_map/ppermute | solution.py:30
  96.8 5.7 %collective-permute-done.24 = bf16[896,256]{1,0:T(8,128)(2,1)S(1)} collective-permute-done((bf16[896,256]{1,0:T(8,128)(2,1)S(1)}, bf16[896,256]{1,0:T(8,128)(2,1)S(1)}, u32[]{:S(2)}, u32[]{:S(2)}) %collective-permute-start.24) | collective-permute-done | bytes 458784 | tf_op jit(solution)/shard_map/ppermute | solution.py:30
  102.6 3.6 %collective-permute-start.10 = (bf16[512,256]{1,0:T(8,128)(2,1)S(1)}, bf16[512,256]{1,0:T(8,128)(2,1)S(1)}, u32[]{:S(2)}, u32[]{:S(2)}) collective-permute-start(bf16[512,256]{1,0:T(8,128)(2,1)S(1)} %get-tuple-element.27), channel_id=1, source_target_pairs={{0,96},{16,112},{32,0},{48,16},{64,32},{80,48},{96,64},{112,80},{1... | collective-permute-start | bytes 786440 | tf_op jit(solution)/shard_map/ppermute | solution.py:30
  106.2 2.3 %collective-permute-done.25 = bf16[1024,256]{1,0:T(8,128)(2,1)S(1)} collective-permute-done((bf16[1024,256]{1,0:T(8,128)(2,1)S(1)}, bf16[1024,256]{1,0:T(8,128)(2,1)S(1)}, u32[]{:S(2)}, u32[]{:S(2)}) %collective-permute-start.25) | collective-permute-done | bytes 524320 | tf_op jit(solution)/shard_map/ppermute | solution.py:30
  109.7 3.5 %fusion.14 = (bf16[1,512,896]{2,1,0:T(8,128)(2,1)S(1)}, bf16[1,512,896]{2,1,0:T(8,128)(2,1)S(1)}, bf16[1,512,896]{2,1,0:T(8,128)(2,1)S(1)}, bf16[1,512,896]{2,1,...) fusion(bf16[8,256,896]{2,1,0:T(8,128)(2,1)S(1)} %copy-done.2, ...), kind=kLoop, calls=%fused_computation.31 | loop fusion | flops 12845056 | bytes 13762560 | tf_op jit(solution)/shard_map/concatenate | solution.py:110
  120.0 2.8 %collective-permute-start.11 = (f32[256,256]{1,0:T(8,128)S(1)}, f32[256,256]{1,0:T(8,128)S(1)}, u32[]{:S(2)}, u32[]{:S(2)}) collective-permute-start(f32[256,256]{1,0:T(8,128)S(1)} %slice.181), channel_id=1, source_target_pairs={{0,16},{16,0},{32,48},{48,32},{64,80},{80,64},{96,112},{112,96},{1... | collective-permute-start | bytes 786440 | tf_op jit(solution)/shard_map/ppermute | solution.py:30
  131.3 2.3 %collective-permute-start.13 = (bf16[256,256]{1,0:T(8,128)(2,1)S(1)}, bf16[256,256]{1,0:T(8,128)(2,1)S(1)}, u32[]{:S(2)}, u32[]{:S(2)}) collective-permute-start(bf16[256,256]{1,0:T(8,128)(2,1)S(1)} %fusion.75.refs_0_), channel_id=1, source_target_pairs={{0,96},{16,112},{32,0},{48,16},{64,32},{80,48},{96,64},{112,80},{1... | collective-permute-start | bytes 393224 | tf_op jit(solution)/shard_map/ppermute | solution.py:30
  134.5 2.5 %collective-permute-start.17 = (bf16[256,256]{1,0:T(8,128)(2,1)S(1)}, bf16[256,256]{1,0:T(8,128)(2,1)S(1)}, u32[]{:S(2)}, u32[]{:S(2)}) collective-permute-start(bf16[256,256]{1,0:T(8,128)(2,1)S(1)} %collective-permute-done.14.refs_3_), channel_id=1, source_target_pairs={{0,96},{16,112},{32,0},{48,16},{64,32},{80,48},{96,64},{112,80},{1... | collective-permute-start | bytes 393224 | tf_op jit(solution)/shard_map/ppermute | solution.py:30
  138.3 1.8 %collective-permute-done.12.refs_1_ = bf16[256,256]{1,0:T(8,128)(2,1)S(1)} collective-permute-done((bf16[256,256]{1,0:T(8,128)(2,1)S(1)}, bf16[256,256]{1,0:T(8,128)(2,1)S(1)}, u32[]{:S(2)}, u32[]{:S(2)}) %collective-permute-start.12) | collective-permute-done | bytes 131104 | tf_op jit(solution)/shard_map/ppermute | solution.py:30
  140.7 2.2 %collective-permute-done.16.refs_5_ = bf16[256,256]{1,0:T(8,128)(2,1)S(1)} collective-permute-done((bf16[256,256]{1,0:T(8,128)(2,1)S(1)}, bf16[256,256]{1,0:T(8,128)(2,1)S(1)}, u32[]{:S(2)}, u32[]{:S(2)}) %collective-permute-start.16) | collective-permute-done | bytes 131104 | tf_op jit(solution)/shard_map/ppermute | solution.py:30
  144.6 2.2 %shard_map.46 = f32[512,256]{1,0:T(8,128)S(1)} custom-call(s32[8]{0:T(128)S(1)} %stack.89.where_ref, bf16[8,512,256]{2,1,0:T(8,128)(2,1)S(1)} %bitcast.88, bf16[256,256]{1,0:T(8,128)(2,1)S(1)} %fusion.75.refs_0_, bf16[256,256]{1,0:T(8,128)(2,1)S(1)} %collective-permute-done.12.refs_1_, bf16[256,256]{1,0:T(8,128)(2,1)S(1)} %collective-permute-done.13.refs_2_, ...), custom_call_target="tpu_custom_call" | custom-call | flops 536870912 | bytes 2621440 | tf_op jit(solution)/shard_map/pallas_call | solution.py:56
  146.8 3.2 %collective-permute-start.19 = (f32[256,256]{1,0:T(8,128)S(1)}, f32[256,256]{1,0:T(8,128)S(1)}, u32[]{:S(2)}, u32[]{:S(2)}) collective-permute-start(f32[256,256]{1,0:T(8,128)S(1)} %slice.183), channel_id=1, source_target_pairs={{0,16},{16,0},{32,48},{48,32},{64,80},{80,64},{96,112},{112,96},{1... | collective-permute-start | bytes 786440 | tf_op jit(solution)/shard_map/ppermute | solution.py:30
  151.4 1.9 %collective-permute-start.34 = (bf16[256,256]{1,0:T(8,128)(2,1)S(1)}, bf16[256,256]{1,0:T(8,128)(2,1)S(1)}, u32[]{:S(2)}, u32[]{:S(2)}) collective-permute-start(bf16[256,256]{1,0:T(8,128)(2,1)S(1)} %collective-permute-done.31.refs_3_), channel_id=1, source_target_pairs={{0,96},{16,112},{32,0},{48,16},{64,32},{80,48},{96,64},{112,80},{1... | collective-permute-start | bytes 393224 | tf_op jit(solution)/shard_map/ppermute | solution.py:30
  157.8 1.8 %shard_map.47 = f32[512,256]{1,0:T(8,128)S(1)} custom-call(s32[8]{0:T(128)S(1)} %stack.89.where_ref, bf16[8,512,256]{2,1,0:T(8,128)(2,1)S(1)} %bitcast.89, bf16[256,256]{1,0:T(8,128)(2,1)S(1)} %fusion.73.refs_0_, bf16[256,256]{1,0:T(8,128)(2,1)S(1)} %collective-permute-done.29.refs_1_, bf16[256,256]{1,0:T(8,128)(2,1)S(1)} %collective-permute-done.30.refs_2_, ...), custom_call_target="tpu_custom_call" | custom-call | flops 536870912 | bytes 2621440 | tf_op jit(solution)/shard_map/pallas_call | solution.py:56
  (126 shorter events, 42.8 us)
Async XLA Ops:
  6.5 136.4 %all-gather.3.cloned.1.call-start = ((), (), s32[]{:S(2)}) async-start(), calls=%async_computation | async-start | bytes 2359296 | tf_op jit(solution)/shard_map/all_gather | solution.py:94
  27.3 82.4 %collective-permute-start.2 = (bf16[8,256,896]{2,1,0:T(8,128)(2,1)}, bf16[8,256,896]{2,1,0:T(8,128)(2,1)}, u32[]{:S(2)}, u32[]{:S(2)}) collective-permute-start(bf16[8,256,896]{2,1,0:T(8,128)(2,1)} %bitcast_dynamic-update-slice_fusion), channel_id=1, source_target_pairs={{0,16},{16,0},{32,48},{48,32},{64,80},{80,64},{96,112},{112,96},{1... | collective-permute-start | bytes 11010056 | tf_op jit(solution)/shard_map/ppermute | solution.py:30
  31.6 27.8 %collective-permute-start.5 = (bf16[896,256]{1,0:T(8,128)(2,1)}, bf16[896,256]{1,0:T(8,128)(2,1)}, u32[]{:S(2)}, u32[]{:S(2)}) collective-permute-start(bf16[896,256]{1,0:T(8,128)(2,1)} %get-tuple-element.24), channel_id=1, source_target_pairs={{0,128},{16,144},{32,160},{48,176},{64,192},{80,208},{96,224},{112... | collective-permute-start | bytes 1376264 | tf_op jit(solution)/shard_map/ppermute | solution.py:30
  35.3 24.2 %collective-permute-start.1 = (bf16[256,256]{1,0:T(8,128)(2,1)}, bf16[256,256]{1,0:T(8,128)(2,1)}, u32[]{:S(2)}, u32[]{:S(2)}) collective-permute-start(bf16[256,256]{1,0:T(8,128)(2,1)} %collective-permute-done), channel_id=1, source_target_pairs={{0,8},{1,9},{2,10},{3,11},{4,12},{5,13},{6,14},{7,15},{8,0},{9,1},... | collective-permute-start | bytes 393224 | tf_op jit(solution)/shard_map/ppermute | solution.py:89
  52.0 17.7 %collective-permute-start.3 = (bf16[896,256]{1,0:T(8,128)(2,1)}, bf16[896,256]{1,0:T(8,128)(2,1)S(1)}, u32[]{:S(2)}, u32[]{:S(2)}) collective-permute-start(bf16[896,256]{1,0:T(8,128)(2,1)} %get-tuple-element.24), channel_id=1, source_target_pairs={{0,32},{16,48},{32,64},{48,80},{64,96},{80,112},{96,0},{112,16},{1... | collective-permute-start | bytes 1376264 | tf_op jit(solution)/shard_map/ppermute | solution.py:30
  52.0 28.8 %collective-permute-start.4 = (bf16[896,256]{1,0:T(8,128)(2,1)}, bf16[896,256]{1,0:T(8,128)(2,1)}, u32[]{:S(2)}, u32[]{:S(2)}) collective-permute-start(bf16[896,256]{1,0:T(8,128)(2,1)} %get-tuple-element.24), channel_id=1, source_target_pairs={{0,96},{16,112},{32,0},{48,16},{64,32},{80,48},{96,64},{112,80},{1... | collective-permute-start | bytes 1376264 | tf_op jit(solution)/shard_map/ppermute | solution.py:30
  59.4 11.6 %collective-permute-start.22 = (bf16[896,256]{1,0:T(8,128)(2,1)}, bf16[896,256]{1,0:T(8,128)(2,1)}, u32[]{:S(2)}, u32[]{:S(2)}) collective-permute-start(bf16[896,256]{1,0:T(8,128)(2,1)} %get-tuple-element.25), channel_id=1, source_target_pairs={{0,128},{16,144},{32,160},{48,176},{64,192},{80,208},{96,224},{112... | collective-permute-start | bytes 1376264 | tf_op jit(solution)/shard_map/ppermute | solution.py:30
  59.4 20.2 %collective-permute-start.20 = (bf16[896,256]{1,0:T(8,128)(2,1)}, bf16[896,256]{1,0:T(8,128)(2,1)}, u32[]{:S(2)}, u32[]{:S(2)}) collective-permute-start(bf16[896,256]{1,0:T(8,128)(2,1)} %get-tuple-element.25), channel_id=1, source_target_pairs={{0,32},{16,48},{32,64},{48,80},{64,96},{80,112},{96,0},{112,16},{1... | collective-permute-start | bytes 1376264 | tf_op jit(solution)/shard_map/ppermute | solution.py:30
  69.7 13.2 %collective-permute-start.21 = (bf16[896,256]{1,0:T(8,128)(2,1)}, bf16[896,256]{1,0:T(8,128)(2,1)S(1)}, u32[]{:S(2)}, u32[]{:S(2)}) collective-permute-start(bf16[896,256]{1,0:T(8,128)(2,1)} %get-tuple-element.25), channel_id=1, source_target_pairs={{0,96},{16,112},{32,0},{48,16},{64,32},{80,48},{96,64},{112,80},{1... | collective-permute-start | bytes 1376264 | tf_op jit(solution)/shard_map/ppermute | solution.py:30
  71.1 17.0 %collective-permute-start.6 = (bf16[768,256]{1,0:T(8,128)(2,1)S(1)}, bf16[768,256]{1,0:T(8,128)(2,1)S(1)}, u32[]{:S(2)}, u32[]{:S(2)}) collective-permute-start(bf16[768,256]{1,0:T(8,128)(2,1)S(1)} %pad_maximum_fusion.6), channel_id=1, source_target_pairs={{0,32},{16,48},{32,64},{48,80},{64,96},{80,112},{96,0},{112,16},{1... | collective-permute-start | bytes 1179656 | tf_op jit(solution)/shard_map/ppermute | solution.py:30
  80.7 15.8 %collective-permute-start.23 = (bf16[768,256]{1,0:T(8,128)(2,1)S(1)}, bf16[768,256]{1,0:T(8,128)(2,1)S(1)}, u32[]{:S(2)}, u32[]{:S(2)}) collective-permute-start(bf16[768,256]{1,0:T(8,128)(2,1)S(1)} %pad_maximum_fusion.7), channel_id=1, source_target_pairs={{0,32},{16,48},{32,64},{48,80},{64,96},{80,112},{96,0},{112,16},{1... | collective-permute-start | bytes 1179656 | tf_op jit(solution)/shard_map/ppermute | solution.py:30
  81.8 20.7 %collective-permute-start.8 = (bf16[1024,256]{1,0:T(8,128)(2,1)S(1)}, bf16[1024,256]{1,0:T(8,128)(2,1)S(1)}, u32[]{:S(2)}, u32[]{:S(2)}) collective-permute-start(bf16[1024,256]{1,0:T(8,128)(2,1)S(1)} %pad_maximum_fusion.1), channel_id=1, source_target_pairs={{0,128},{16,144},{32,160},{48,176},{64,192},{80,208},{96,224},{112... | collective-permute-start | bytes 1572872 | tf_op jit(solution)/shard_map/ppermute | solution.py:30
  82.9 13.6 %collective-permute-start.7 = (bf16[896,256]{1,0:T(8,128)(2,1)S(1)}, bf16[896,256]{1,0:T(8,128)(2,1)S(1)}, u32[]{:S(2)}, u32[]{:S(2)}) collective-permute-start(bf16[896,256]{1,0:T(8,128)(2,1)S(1)} %pad_maximum_fusion.4), channel_id=1, source_target_pairs={{0,96},{16,112},{32,0},{48,16},{64,32},{80,48},{96,64},{112,80},{1... | collective-permute-start | bytes 1376264 | tf_op jit(solution)/shard_map/ppermute | solution.py:30
  88.1 14.4 %collective-permute-start.24 = (bf16[896,256]{1,0:T(8,128)(2,1)S(1)}, bf16[896,256]{1,0:T(8,128)(2,1)S(1)}, u32[]{:S(2)}, u32[]{:S(2)}) collective-permute-start(bf16[896,256]{1,0:T(8,128)(2,1)S(1)} %pad_maximum_fusion.5), channel_id=1, source_target_pairs={{0,96},{16,112},{32,0},{48,16},{64,32},{80,48},{96,64},{112,80},{1... | collective-permute-start | bytes 1376264 | tf_op jit(solution)/shard_map/ppermute | solution.py:30
  96.4 12.0 %collective-permute-start.25 = (bf16[1024,256]{1,0:T(8,128)(2,1)S(1)}, bf16[1024,256]{1,0:T(8,128)(2,1)S(1)}, u32[]{:S(2)}, u32[]{:S(2)}) collective-permute-start(bf16[1024,256]{1,0:T(8,128)(2,1)S(1)} %pad_maximum_fusion.2), channel_id=1, source_target_pairs={{0,128},{16,144},{32,160},{48,176},{64,192},{80,208},{96,224},{112... | collective-permute-start | bytes 1572872 | tf_op jit(solution)/shard_map/ppermute | solution.py:30
  96.5 21.0 %collective-permute-start.9 = (bf16[384,256]{1,0:T(8,128)(2,1)S(1)}, bf16[384,256]{1,0:T(8,128)(2,1)S(1)}, u32[]{:S(2)}, u32[]{:S(2)}) collective-permute-start(bf16[384,256]{1,0:T(8,128)(2,1)S(1)} %get-tuple-element.31), channel_id=1, source_target_pairs={{0,32},{16,48},{32,64},{48,80},{64,96},{80,112},{96,0},{112,16},{1... | collective-permute-start | bytes 589832 | tf_op jit(solution)/shard_map/ppermute | solution.py:30
  102.5 21.6 %collective-permute-start.26 = (bf16[384,256]{1,0:T(8,128)(2,1)S(1)}, bf16[384,256]{1,0:T(8,128)(2,1)S(1)}, u32[]{:S(2)}, u32[]{:S(2)}) collective-permute-start(bf16[384,256]{1,0:T(8,128)(2,1)S(1)} %get-tuple-element.33), channel_id=1, source_target_pairs={{0,32},{16,48},{32,64},{48,80},{64,96},{80,112},{96,0},{112,16},{1... | collective-permute-start | bytes 589832 | tf_op jit(solution)/shard_map/ppermute | solution.py:30
  102.6 15.0 %collective-permute-start.10 = (bf16[512,256]{1,0:T(8,128)(2,1)S(1)}, bf16[512,256]{1,0:T(8,128)(2,1)S(1)}, u32[]{:S(2)}, u32[]{:S(2)}) collective-permute-start(bf16[512,256]{1,0:T(8,128)(2,1)S(1)} %get-tuple-element.27), channel_id=1, source_target_pairs={{0,96},{16,112},{32,0},{48,16},{64,32},{80,48},{96,64},{112,80},{1... | collective-permute-start | bytes 786440 | tf_op jit(solution)/shard_map/ppermute | solution.py:30
  108.5 15.6 %collective-permute-start.27 = (bf16[512,256]{1,0:T(8,128)(2,1)S(1)}, bf16[512,256]{1,0:T(8,128)(2,1)S(1)}, u32[]{:S(2)}, u32[]{:S(2)}) collective-permute-start(bf16[512,256]{1,0:T(8,128)(2,1)S(1)} %get-tuple-element.29), channel_id=1, source_target_pairs={{0,96},{16,112},{32,0},{48,16},{64,32},{80,48},{96,64},{112,80},{1... | collective-permute-start | bytes 786440 | tf_op jit(solution)/shard_map/ppermute | solution.py:30
  120.0 9.6 %collective-permute-start.11 = (f32[256,256]{1,0:T(8,128)S(1)}, f32[256,256]{1,0:T(8,128)S(1)}, u32[]{:S(2)}, u32[]{:S(2)}) collective-permute-start(f32[256,256]{1,0:T(8,128)S(1)} %slice.181), channel_id=1, source_target_pairs={{0,16},{16,0},{32,48},{48,32},{64,80},{80,64},{96,112},{112,96},{1... | collective-permute-start | bytes 786440 | tf_op jit(solution)/shard_map/ppermute | solution.py:30
  131.0 6.0 %collective-permute-start.15 = (bf16[256,256]{1,0:T(8,128)(2,1)S(1)}, bf16[256,256]{1,0:T(8,128)(2,1)S(1)}, u32[]{:S(2)}, u32[]{:S(2)}) collective-permute-start(bf16[256,256]{1,0:T(8,128)(2,1)S(1)} %fusion.75.refs_0_), channel_id=1, source_target_pairs={{0,64},{16,80},{32,96},{48,112},{64,0},{80,16},{96,32},{112,48},{1... | collective-permute-start | bytes 393224 | tf_op jit(solution)/shard_map/ppermute | solution.py:30
  131.0 9.1 %collective-permute-start.12 = (bf16[256,256]{1,0:T(8,128)(2,1)S(1)}, bf16[256,256]{1,0:T(8,128)(2,1)S(1)}, u32[]{:S(2)}, u32[]{:S(2)}) collective-permute-start(bf16[256,256]{1,0:T(8,128)(2,1)S(1)} %fusion.75.refs_0_), channel_id=1, source_target_pairs={{0,32},{16,48},{32,64},{48,80},{64,96},{80,112},{96,0},{112,16},{1... | collective-permute-start | bytes 393224 | tf_op jit(solution)/shard_map/ppermute | solution.py:30
  131.3 9.4 %collective-permute-start.13 = (bf16[256,256]{1,0:T(8,128)(2,1)S(1)}, bf16[256,256]{1,0:T(8,128)(2,1)S(1)}, u32[]{:S(2)}, u32[]{:S(2)}) collective-permute-start(bf16[256,256]{1,0:T(8,128)(2,1)S(1)} %fusion.75.refs_0_), channel_id=1, source_target_pairs={{0,96},{16,112},{32,0},{48,16},{64,32},{80,48},{96,64},{112,80},{1... | collective-permute-start | bytes 393224 | tf_op jit(solution)/shard_map/ppermute | solution.py:30
  134.3 8.6 %collective-permute-start.16 = (bf16[256,256]{1,0:T(8,128)(2,1)S(1)}, bf16[256,256]{1,0:T(8,128)(2,1)S(1)}, u32[]{:S(2)}, u32[]{:S(2)}) collective-permute-start(bf16[256,256]{1,0:T(8,128)(2,1)S(1)} %collective-permute-done.14.refs_3_), channel_id=1, source_target_pairs={{0,32},{16,48},{32,64},{48,80},{64,96},{80,112},{96,0},{112,16},{1... | collective-permute-start | bytes 393224 | tf_op jit(solution)/shard_map/ppermute | solution.py:30
  134.5 8.4 %collective-permute-start.17 = (bf16[256,256]{1,0:T(8,128)(2,1)S(1)}, bf16[256,256]{1,0:T(8,128)(2,1)S(1)}, u32[]{:S(2)}, u32[]{:S(2)}) collective-permute-start(bf16[256,256]{1,0:T(8,128)(2,1)S(1)} %collective-permute-done.14.refs_3_), channel_id=1, source_target_pairs={{0,96},{16,112},{32,0},{48,16},{64,32},{80,48},{96,64},{112,80},{1... | collective-permute-start | bytes 393224 | tf_op jit(solution)/shard_map/ppermute | solution.py:30
  137.0 6.0 %collective-permute-start.18 = (bf16[256,256]{1,0:T(8,128)(2,1)S(1)}, bf16[256,256]{1,0:T(8,128)(2,1)}, u32[]{:S(2)}, u32[]{:S(2)}) collective-permute-start(bf16[256,256]{1,0:T(8,128)(2,1)S(1)} %collective-permute-done.15.refs_4_), channel_id=1, source_target_pairs={{0,128},{16,144},{32,160},{48,176},{64,192},{80,208},{96,224},{112... | collective-permute-start | bytes 393224 | tf_op jit(solution)/shard_map/ppermute | solution.py:30
  140.1 10.6 %collective-permute-start.31 = (bf16[256,256]{1,0:T(8,128)(2,1)S(1)}, bf16[256,256]{1,0:T(8,128)(2,1)S(1)}, u32[]{:S(2)}, u32[]{:S(2)}) collective-permute-start(bf16[256,256]{1,0:T(8,128)(2,1)S(1)} %fusion.73.refs_0_), channel_id=1, source_target_pairs={{0,128},{16,144},{32,160},{48,176},{64,192},{80,208},{96,224},{112... | collective-permute-start | bytes 393224 | tf_op jit(solution)/shard_map/ppermute | solution.py:30
  140.7 10.8 %collective-permute-start.32 = (bf16[256,256]{1,0:T(8,128)(2,1)S(1)}, bf16[256,256]{1,0:T(8,128)(2,1)S(1)}, u32[]{:S(2)}, u32[]{:S(2)}) collective-permute-start(bf16[256,256]{1,0:T(8,128)(2,1)S(1)} %fusion.73.refs_0_), channel_id=1, source_target_pairs={{0,64},{16,80},{32,96},{48,112},{64,0},{80,16},{96,32},{112,48},{1... | collective-permute-start | bytes 393224 | tf_op jit(solution)/shard_map/ppermute | solution.py:30
  142.9 10.4 %collective-permute-start.29 = (bf16[256,256]{1,0:T(8,128)(2,1)S(1)}, bf16[256,256]{1,0:T(8,128)(2,1)S(1)}, u32[]{:S(2)}, u32[]{:S(2)}) collective-permute-start(bf16[256,256]{1,0:T(8,128)(2,1)S(1)} %fusion.73.refs_0_), channel_id=1, source_target_pairs={{0,32},{16,48},{32,64},{48,80},{64,96},{80,112},{96,0},{112,16},{1... | collective-permute-start | bytes 393224 | tf_op jit(solution)/shard_map/ppermute | solution.py:30
  146.8 14.4 %collective-permute-start.19 = (f32[256,256]{1,0:T(8,128)S(1)}, f32[256,256]{1,0:T(8,128)S(1)}, u32[]{:S(2)}, u32[]{:S(2)}) collective-permute-start(f32[256,256]{1,0:T(8,128)S(1)} %slice.183), channel_id=1, source_target_pairs={{0,16},{16,0},{32,48},{48,32},{64,80},{80,64},{96,112},{112,96},{1... | collective-permute-start | bytes 786440 | tf_op jit(solution)/shard_map/ppermute | solution.py:30
  150.6 5.9 %collective-permute-start.33 = (bf16[256,256]{1,0:T(8,128)(2,1)S(1)}, bf16[256,256]{1,0:T(8,128)(2,1)S(1)}, u32[]{:S(2)}, u32[]{:S(2)}) collective-permute-start(bf16[256,256]{1,0:T(8,128)(2,1)S(1)} %collective-permute-done.31.refs_3_), channel_id=1, source_target_pairs={{0,32},{16,48},{32,64},{48,80},{64,96},{80,112},{96,0},{112,16},{1... | collective-permute-start | bytes 393224 | tf_op jit(solution)/shard_map/ppermute | solution.py:30
  151.4 6.4 %collective-permute-start.34 = (bf16[256,256]{1,0:T(8,128)(2,1)S(1)}, bf16[256,256]{1,0:T(8,128)(2,1)S(1)}, u32[]{:S(2)}, u32[]{:S(2)}) collective-permute-start(bf16[256,256]{1,0:T(8,128)(2,1)S(1)} %collective-permute-done.31.refs_3_), channel_id=1, source_target_pairs={{0,96},{16,112},{32,0},{48,16},{64,32},{80,48},{96,64},{112,80},{1... | collective-permute-start | bytes 393224 | tf_op jit(solution)/shard_map/ppermute | solution.py:30
  (16 other events, 130.6 us)
Sparse Core Ops, SparseCore 0:
  61.4 42.3 all-gather.2

commit v2 on v0

v2 whole, which is shorter than its diff:
```python
import jax
import jax.numpy as jnp
from jax import lax
from jax.experimental import pallas as pl
from jax.experimental.pallas import tpu as pltpu
from jax.sharding import PartitionSpec as P

TOK = 128
EXAMPLES = 2
NX, NY, NC = 2, 4, 2
NH, NZ = 2, 8
SHORT = 384
SPLIT = 3
CHUNKS = ((0, 512),)
FACTOR = 32.0
VMEM = 18 * 1024 * 1024
BLOCKS = ((0, 0), (0, 1), (3, 0), (3, 1), (1, 0), (1, 1), (2, 0), (2, 1))
ORDER = ((0, 0), (0, 3), (0, 1), (1, 0), (0, 2), (1, 3), (1, 1), (1, 2))


def index(x, y, z, c):
    return ((x % NX * NY + y) * NC + c) * NH * NZ + x // NX * NZ + z


def shift(value, dx=0, dy=0, dz=0, dc=0):
    size = NX * NH
    pairs = [
        (index(x, y, z, c), index((x + dx) % size, (y + dy) % NY, (z + dz) % NZ, (c + dc) % NC))
        for x in range(size)
        for y in range(NY)
        for z in range(NZ)
        for c in range(NC)
    ]
    return lax.ppermute(value, ("dp", "blk"), pairs)


def swap(value, dy=0):
    pairs = [
        (index(x, y, z, c), index(x ^ 1, (y + dy) % NY, z, c))
        for x in range(NX * NH)
        for y in range(NY)
        for z in range(NZ)
        for c in range(NC)
    ]
    return lax.ppermute(value, ("dp", "blk"), pairs)


def dot(a, b):
    return jnp.dot(a, b, preferred_element_type=jnp.float32)


def space(kind):
    return pl.BlockSpec(memory_space=kind)


def pieces_kernel(columns_ref, source, *refs):
    outs, semaphore = refs[:-1], refs[-1]
    copies = []
    for part, count in ((0, SPLIT), (SPLIT, len(BLOCKS) - 2 * SPLIT)):
        for example in range(EXAMPLES):
            out = outs[(2 if part else 0) + example]
            for i in range(count):
                column = pl.multiple_of(columns_ref[part + i], 128)
                copies.append(
                    pltpu.make_async_copy(
                        source.at[pl.ds(example * TOK, TOK), pl.ds(column, out.shape[2])],
                        out.at[i],
                        semaphore.at[len(copies)],
                    )
                )
    for copy in copies:
        copy.start()
    for copy in copies:
        copy.wait()


def pieces(columns, activations, depth):
    rest = len(BLOCKS) - 2 * SPLIT
    kinds = [SPLIT, SPLIT, rest, rest]
    return pl.pallas_call(
        pieces_kernel,
        out_shape=[jax.ShapeDtypeStruct((n, TOK, depth), activations.dtype) for n in kinds],
        in_specs=[space(pltpu.SMEM), space(pl.ANY)],
        out_specs=[space(pl.ANY)] * 4,
        scratch_shapes=[pltpu.SemaphoreType.DMA((sum(kinds),))],
        cost_estimate=pl.CostEstimate(flops=0, bytes_accessed=2**23, transcendentals=0),
    )(columns, activations)


def times_basis(block, panels, blocks, columns):
    total = None
    for k in range(len(BLOCKS)):
        a = block(k)
        if k < len(BLOCKS) - 2:
            term = dot(a, panels[k][:, columns])
        else:
            short, long = panels[2 * k - 6], panels[2 * k - 5]
            term = dot(a[:, :SHORT], short[:, columns]) + dot(a[:, SHORT:], long[:, columns])
        total = term if total is None else total + term
    return total


TILE = 256


def theirs_kernel(start, parity_ref, *refs):
    near, rest, panels, out = refs[:4], refs[4:6], refs[6:-1], refs[-1]

    def work(low, high):
        def block(k):
            pair, at = (low, k) if k < SPLIT else (high, k - SPLIT) if k < 2 * SPLIT else (rest, k - 2 * SPLIT)
            return jnp.concatenate([pair[0][at], pair[1][at]], 0)

        @pl.loop(0, out.shape[1] // TILE)
        def _(n):
            offset = pl.multiple_of(n * TILE, TILE)
            out[:, pl.ds(offset, TILE)] = times_basis(
                block, panels, BLOCKS, pl.ds(pl.multiple_of(start + offset, TILE), TILE)
            )

    @pl.when(parity_ref[0] == 0)
    def _():
        work(near[:2], near[2:])

    @pl.when(parity_ref[0] != 0)
    def _():
        work(near[2:], near[:2])


def theirs(parity, near, rest, panels, start, width):
    tokens = EXAMPLES * TOK
    return pl.pallas_call(
        lambda *refs: theirs_kernel(start, *refs),
        out_shape=jax.ShapeDtypeStruct((tokens, width), jnp.float32),
        in_specs=[space(pltpu.SMEM)] + [space(pltpu.VMEM)] * (6 + len(panels)),
        out_specs=space(pltpu.VMEM),
        compiler_params=pltpu.CompilerParams(vmem_limit_bytes=VMEM),
        cost_estimate=pl.CostEstimate(
            flops=2 * tokens * width * 7168, bytes_accessed=2**22, transcendentals=0
        ),
    )(parity, *near, *rest, *panels)


def ours_kernel(start, columns_ref, source, *refs):
    panels, out, rows, semaphore = refs[:-3], refs[-3], refs[-2], refs[-1]
    copies = [
        pltpu.make_async_copy(
            source.at[:, pl.ds(pl.multiple_of(columns_ref[k], 128), rows.shape[2])],
            rows.at[k],
            semaphore.at[k],
        )
        for k in range(len(BLOCKS))
    ]
    for copy in copies:
        copy.start()
    for copy in copies:
        copy.wait()

    @pl.loop(0, out.shape[1] // TILE)
    def _(n):
        offset = pl.multiple_of(n * TILE, TILE)
        out[:, pl.ds(offset, TILE)] = times_basis(
            lambda k: rows[k], panels, BLOCKS, pl.ds(pl.multiple_of(start + offset, TILE), TILE)
        )


def ours(columns, activations, panels, start, width):
    tokens, depth = activations.shape[0], panels[0].shape[0]
    return pl.pallas_call(
        lambda *refs: ours_kernel(start, *refs),
        out_shape=jax.ShapeDtypeStruct((tokens, width), jnp.float32),
        in_specs=[space(pltpu.SMEM), space(pl.ANY)] + [space(pltpu.VMEM)] * len(panels),
        out_specs=space(pltpu.VMEM),
        scratch_shapes=[
            pltpu.VMEM((len(BLOCKS), tokens, depth), activations.dtype),
            pltpu.SemaphoreType.DMA((len(BLOCKS),)),
        ],
        compiler_params=pltpu.CompilerParams(vmem_limit_bytes=VMEM),
        cost_estimate=pl.CostEstimate(
            flops=2 * tokens * width * 7168, bytes_accessed=2**22, transcendentals=0
        ),
    )(columns, activations, *panels)


def squares_kernel(where_ref, out_rows, *refs):
    in_rows, total_ref = refs[:-1], refs[-1]
    half = total_ref.shape[0] // 2

    @pl.loop(0, total_ref.shape[1] // TILE)
    def _(n):
        columns = pl.ds(pl.multiple_of(n * TILE, TILE), TILE)
        for part in range(2):
            rows = pl.ds(part * half, half)
            total = None
            for k, block in enumerate(in_rows):
                at = where_ref[k]
                for example in range(EXAMPLES):
                    tokens = pl.ds(example * TOK, TOK)
                    rotated = dot(out_rows[at, rows, tokens], block[tokens, columns])
                    squared = rotated * rotated
                    total = squared if total is None else total + squared
            total_ref[rows, columns] = total


def sums_of_squares(where, out_rows, in_rows):
    rows, width = out_rows.shape[1], in_rows[0].shape[1]
    return pl.pallas_call(
        squares_kernel,
        out_shape=jax.ShapeDtypeStruct((rows, width), jnp.float32),
        in_specs=[space(pltpu.SMEM)] + [space(pltpu.VMEM)] * (1 + len(in_rows)),
        out_specs=space(pltpu.VMEM),
        compiler_params=pltpu.CompilerParams(vmem_limit_bytes=VMEM),
        cost_estimate=pl.CostEstimate(
            flops=2 * rows * width * len(in_rows) * EXAMPLES * TOK,
            bytes_accessed=out_rows.size * 2 + rows * width * 4,
            transcendentals=0,
        ),
    )(where, out_rows, *in_rows)


def transposed(block):
    pairs = []
    for sx in range(NX):
        for sy in range(NY):
            for sc in range(NC):
                for t in range(NX * NY * NC):
                    source = ((sx * NY + sy) * NC + sc) * NH * NZ + t
                    target = (t // NC * NC + sc) * NH * NZ + t % NC * NZ + sx * NY + sy
                    pairs.append((source, target))
    return lax.ppermute(block, ("dp", "blk"), pairs)


def on_device(activations, out_grads, basis_in, basis_out):
    d, b = lax.axis_index("dp"), lax.axis_index("blk")
    core, y, x = d % NC, (d // NC) % NY, d // (NC * NY)
    parity = b % 2
    scale = 1.0 / float(EXAMPLES * NX * NY * NC)
    depth = basis_in.shape[0]
    spots = [((y + dy) % NY) * NC + (core + dc) % NC for dy, dc in BLOCKS]
    half = len(BLOCKS)

    left, right = shift(basis_in, dy=1), shift(basis_in, dy=3)
    own_other = shift(basis_in, dc=1)

    block = transposed(dot(out_grads, basis_out).astype(jnp.bfloat16).T)
    other = shift(block, dx=NX)
    mine = (b // NZ) == core
    block = jnp.concatenate([jnp.where(mine, block, other), jnp.where(mine, other, block)], 0)
    out_rows = lax.all_gather(
        block,
        "blk",
        axis=0,
        axis_index_groups=[[h * NZ + z for z in range(NZ)] for h in range(NH)],
    )
    where = jnp.stack([((x + dx) % NX) * NY + (y + dy) % NY for dx, dy in ORDER]).astype(jnp.int32)

    table = jnp.stack(spots)
    give = jnp.concatenate(
        [lax.dynamic_slice_in_dim(table, parity * SPLIT, SPLIT), table[2 * SPLIT :]]
    )
    give = ((half * (1 - x) + give) * depth).astype(jnp.int32)
    near0, near1, rest0, rest1 = pieces(give, activations, depth)
    near0, near1 = shift(near0, dx=3), shift(near1, dx=1)
    rest0, rest1 = shift(rest0, dx=3), shift(rest1, dx=1)
    away0, away1 = shift(near0, dz=NZ - 1), shift(near1, dz=1)

    far_short, far_long = shift(left[:SHORT], dy=1), shift(right[SHORT:], dy=3)
    panels = [basis_in, own_other, left, shift(left, dc=1), right, shift(right, dc=1)]
    panels += [far_short, far_long, shift(far_short, dc=1), shift(far_long, dc=1)]
    keep = ((half * x + table) * depth).astype(jnp.int32)
    parity = parity.reshape(1).astype(jnp.int32)

    results = []
    for start, width in CHUNKS:
        partial = theirs(parity, (near0, near1, away0, away1), (rest0, rest1), panels, start, width)
        arrived = swap((partial * FACTOR).astype(jnp.float16)).astype(jnp.float32) * (1.0 / FACTOR)
        total = ours(keep, activations, panels, start, width)
        proj_in = (total + arrived).astype(jnp.bfloat16)

        p_left, p_right, p_far = shift(proj_in, dy=1), shift(proj_in, dy=3), shift(proj_in, dy=2)
        p_across = swap(proj_in)
        px_left, px_right = shift(p_across, dy=1), shift(p_across, dy=3)
        px_far = swap(p_far)
        sums = sums_of_squares(
            where,
            out_rows,
            (proj_in, p_left, p_right, p_across, p_far, px_left, px_right, px_far),
        )
        rows = sums.shape[0] // 2
        results.append((sums[:rows] + shift(sums[rows:], dc=1)) * jnp.float32(scale))
    return jnp.concatenate(results, 1) if len(results) > 1 else results[0]


def solution(mesh):
    return jax.shard_map(
        on_device,
        mesh=mesh,
        in_specs=(P("dp", None), P("dp", None), P("dp", "blk"), P(None, "blk")),
        out_specs=P("dp", "blk"),
        check_vma=False,
    )
```

time: 281 us -> 235 us (0.84)
  waiting for transfers between devices: 234 us -> 44.9 us
  Pallas kernels: 0 us -> 85.7 us
  starting transfers between devices: 0.08 us -> 68.9 us
  matrix products: 28.2 us -> 2.34 us
  local copies, waits for them, and re-layouts: 0.82 us -> 16.4 us
    all_gather x2 -> x1, waiting for transfers between devices: 160 us -> 0.01 us  [on_device(): lax.all_gather(block, 'blk', axis=0, axis_index_groups=[[h * NZ + z for z...]
    pallas_call x0 -> x4, Pallas kernels: none -> 85.7 us  [the longest x1 71.3 us: pieces(): pl.pallas_call(pieces_kernel, out_shape=[jax.ShapeDtypeStruct((n, TOK, de...]
    reduce_scatter x1 -> x0, waiting for transfers between devices: 73.3 us -> none  [on_device(): lax.psum_scatter(lax.fori_loop(0, EXAMPLES, add_example, jnp.zeros((lax.a...]
    ppermute x0 -> x26, starting transfers between devices: none -> 68.9 us  [the longest x22 65.3 us: shift(): return lax.ppermute(value, ('dp', 'blk'), pairs)]
    ppermute x0 -> x26, waiting for transfers between devices: none -> 44.9 us  [the longest x22 43.9 us: shift(): return lax.ppermute(value, ('dp', 'blk'), pairs)]
    dot_general x4 -> x1, matrix products: 28.2 us -> 2.34 us  [dot(): return jnp.dot(a, b, preferred_element_type=jnp.float32)]
    unnamed x2 -> x28, local copies, waits for them, and re-layouts: 0.82 us -> 15.1 us
  transfers between devices with their start and end apart: 3 -> 27, of which waited for: 3 -> 8; matrix products, arithmetic and copies ran while one was open for 5% -> 1% of each run, Pallas kernels for 0% -> 35%
where the time goes in v2:
time: 235 us; the launch traced here: 234 us
  Pallas kernels  85.7 us (36%)
  starting transfers between devices  68.9 us (29%)
  waiting for transfers between devices  44.9 us (19%)
  local copies, waits for them, and re-layouts  16.4 us (7%)
  between operations  13.6 us (6%)
  other arithmetic  2.36 us (1%)
    pallas_call x1, Pallas kernels, pieces(): pl.pallas_call(pieces_kernel, out_shape=[jax.ShapeDtypeStruct((n, TOK, de...  71.3 us
    ppermute x22, starting transfers between devices, shift(): return lax.ppermute(value, ('dp', 'blk'), pairs)  65.3 us
    ppermute x22, waiting for transfers between devices, shift(): return lax.ppermute(value, ('dp', 'blk'), pairs)  43.9 us
    unnamed x28, local copies, waits for them, and re-layouts  15.1 us
    pallas_call x1, Pallas kernels, theirs(): pl.pallas_call(lambda *refs: theirs_kernel(start, *refs), out_shape=jax.S...  5.37 us
    pallas_call x1, Pallas kernels, ours(): pl.pallas_call(lambda *refs: ours_kernel(start, *refs), out_shape=jax.Sha...  5.34 us
  transfers between devices with their start and end apart: 27, of which 8 were waited for; matrix products, arithmetic and copies ran while one was open for 1% of the time, Pallas kernels for 35%

profile of v2, /device:TPU:1, one launch (start us, length us, event | category | flops | bytes accessed | tf_op | source)
XLA Modules:
  0.0 234.3 jit_solution(2429927252464423857)
XLA Ops:
  6.5 1.6 copy-done
  8.1 2.3 convolution_convert_fusion
  11.2 18.4 %collective-permute-start.1 = (bf16[256,256]{1,0:T(8,128)(2,1)S(1)}, bf16[256,256]{1,0:T(8,128)(2,1)S(1)}, u32[]{:S(2)}, u32[]{:S(2)}) collective-permute-start(bf16[256,256]{1,0:T(8,128)(2,1)S(1)} %collective-permute-done), channel_id=1, source_target_pairs={{0,8},{16,24},{1,9},{17,25},{2,10},{18,26},{3,11},{19,27},{4,12},{... | collective-permute-start | bytes 393224 | tf_op jit(solution)/shard_map/ppermute | solution.py:34
  29.7 5.0 %collective-permute-done.1 = bf16[256,256]{1,0:T(8,128)(2,1)S(1)} collective-permute-done((bf16[256,256]{1,0:T(8,128)(2,1)S(1)}, bf16[256,256]{1,0:T(8,128)(2,1)S(1)}, u32[]{:S(2)}, u32[]{:S(2)}) %collective-permute-start.1) | collective-permute-done | bytes 131104 | tf_op jit(solution)/shard_map/ppermute | solution.py:34
  36.1 71.3 %shard_map.47 = (bf16[3,128,896]{2,1,0:T(8,128)(2,1)}, bf16[3,128,896]{2,1,0:T(8,128)(2,1)}, bf16[2,128,896]{2,1,0:T(8,128)(2,1)}, bf16[2,128,896]{2,1,0:T(8,128)(2,1)}) custom-call(s32[5]{0:T(128)} %fusion.1.columns_ref, bf16[256,14336]{1,0:T(8,128)(2,1)} %source.1), custom_call_target="tpu_custom_call" | custom-call | bytes 8388608 | tf_op jit(solution)/shard_map/pallas_call | solution.py:80
  107.5 9.0 %collective-permute-start.5 = (bf16[896,512]{1,0:T(8,128)(2,1)}, bf16[896,512]{1,0:T(8,128)(2,1)S(1)}, u32[]{:S(2)}, u32[]{:S(2)}) collective-permute-start(bf16[896,512]{1,0:T(8,128)(2,1)} %refs_7_.1), channel_id=1, source_target_pairs={{0,96},{16,112},{1,97},{17,113},{2,98},{18,114},{3,99},{19,115},{4... | collective-permute-start | bytes 2752520 | tf_op jit(solution)/shard_map/ppermute | solution.py:34
  116.5 2.0 collective-permute-start.2
  119.3 2.0 collective-permute-start.12
  121.3 1.1 collective-permute-start.16
  122.4 1.0 slice.18
  123.5 12.4 %collective-permute-done.11.refs_1_ = bf16[3,128,896]{2,1,0:T(8,128)(2,1)S(1)} collective-permute-done((bf16[3,128,896]{2,1,0:T(8,128)(2,1)}, bf16[3,128,896]{2,1,0:T(8,128)(2,1)S(1)}, u32[]{:S(2)}, u32[]{:S(2)}) %collective-permute-start.11) | collective-permute-done | bytes 688160 | tf_op jit(solution)/shard_map/ppermute | solution.py:34
  135.9 8.7 %collective-permute-start.13 = (bf16[3,128,896]{2,1,0:T(8,128)(2,1)S(1)}, bf16[3,128,896]{2,1,0:T(8,128)(2,1)S(1)}, u32[]{:S(2)}, u32[]{:S(2)}) collective-permute-start(bf16[3,128,896]{2,1,0:T(8,128)(2,1)S(1)} %collective-permute-done.11.refs_1_), channel_id=1, source_target_pairs={{0,7},{16,23},{1,0},{17,16},{2,1},{18,17},{3,2},{19,18},{4,3},{20,... | collective-permute-start | bytes 2064392 | tf_op jit(solution)/shard_map/ppermute | solution.py:34
  146.2 5.4 %collective-permute-start.8 = (bf16[512,512]{1,0:T(8,128)(2,1)S(1)}, bf16[512,512]{1,0:T(8,128)(2,1)S(1)}, u32[]{:S(2)}, u32[]{:S(2)}) collective-permute-start(bf16[512,512]{1,0:T(8,128)(2,1)S(1)} %slice.19), channel_id=1, source_target_pairs={{0,96},{16,112},{1,97},{17,113},{2,98},{18,114},{3,99},{19,115},{4... | collective-permute-start | bytes 1572872 | tf_op jit(solution)/shard_map/ppermute | solution.py:34
  151.7 5.2 %collective-permute-start.4 = (bf16[896,512]{1,0:T(8,128)(2,1)}, bf16[896,512]{1,0:T(8,128)(2,1)}, u32[]{:S(2)}, u32[]{:S(2)}) collective-permute-start(bf16[896,512]{1,0:T(8,128)(2,1)} %collective-permute-done.3.refs_4_.refs_9_), channel_id=1, source_target_pairs={{0,16},{16,0},{1,17},{17,1},{2,18},{18,2},{3,19},{19,3},{4,20},{20... | collective-permute-start | bytes 2752520 | tf_op jit(solution)/shard_map/ppermute | solution.py:34
  157.8 6.0 %collective-permute-start.10 = (bf16[512,512]{1,0:T(8,128)(2,1)S(1)}, bf16[512,512]{1,0:T(8,128)(2,1)}, u32[]{:S(2)}, u32[]{:S(2)}) collective-permute-start(bf16[512,512]{1,0:T(8,128)(2,1)S(1)} %collective-permute-done.8.refs_9_.refs_14_), channel_id=1, source_target_pairs={{0,16},{16,0},{1,17},{17,1},{2,18},{18,2},{3,19},{19,3},{4,20},{20... | collective-permute-start | bytes 1572872 | tf_op jit(solution)/shard_map/ppermute | solution.py:34
  164.7 12.3 %collective-permute-done.14.refs_4_ = bf16[3,128,896]{2,1,0:T(8,128)(2,1)} collective-permute-done((bf16[3,128,896]{2,1,0:T(8,128)(2,1)}, bf16[3,128,896]{2,1,0:T(8,128)(2,1)}, u32[]{:S(2)}, u32[]{:S(2)}) %collective-permute-start.14) | collective-permute-done | bytes 688160 | tf_op jit(solution)/shard_map/ppermute | solution.py:34
  177.0 1.2 copy-done.3
  178.2 1.1 copy-done.7
  179.3 1.1 copy-done.9
  182.4 5.4 %shard_map.48 = f32[256,512]{1,0:T(8,128)S(1)} custom-call(s32[1]{0:T(128)} %bitcast.17.refs_0_, bf16[3,128,896]{2,1,0:T(8,128)(2,1)S(1)} %copy-done.7, bf16[3,128,896]{2,1,0:T(8,128)(2,1)} %collective-permute-done.12.refs_2_, bf16[3,128,896]{2,1,0:T(8,128)(2,1)S(1)} %copy-done.9, bf16[3,128,896]{2,1,0:T(8,128)(2,1)} %collective-permute-done.14.refs_4_, ...), custom_call_target="tpu_custom_call" | custom-call | flops 1879048192 | bytes 4194304 | tf_op jit(solution)/shard_map/pallas_call | solution.py:132
  188.0 3.1 %copy-done.1 = bf16[256,14336]{1,0:T(8,128)(2,1)S(1)} copy-done((bf16[256,14336]{1,0:T(8,128)(2,1)S(1)}, bf16[256,14336]{1,0:T(8,128)(2,1)}, u32[]{:S(2)}) %copy-start.1) | copy-done | bytes 7340056
  191.1 5.3 %shard_map.46 = f32[256,512]{1,0:T(8,128)S(1)} custom-call(s32[8]{0:T(128)S(1)} %add_multiply_fusion.refs_0_, bf16[256,14336]{1,0:T(8,128)(2,1)S(1)} %copy-done.1, bf16[896,512]{1,0:T(8,128)(2,1)} %refs_7_.1, bf16[896,512]{1,0:T(8,128)(2,1)S(1)} %copy-done.4, bf16[896,512]{1,0:T(8,128)(2,1)} %collective-permute-done.3.refs_4_.refs_9_, ...), custom_call_target="tpu_custom_call" | custom-call | flops 1879048192 | bytes 4194304 | tf_op jit(solution)/shard_map/pallas_call | solution.py:169
  196.6 1.5 collective-permute-start.20
  198.1 1.7 collective-permute-start.18
  199.8 2.4 %collective-permute-start.19 = (bf16[256,512]{1,0:T(8,128)(2,1)S(1)}, bf16[256,512]{1,0:T(8,128)(2,1)S(1)}, u32[]{:S(2)}, u32[]{:S(2)}) collective-permute-start(bf16[256,512]{1,0:T(8,128)(2,1)S(1)} %add_convert_fusion.refs_0_), channel_id=1, source_target_pairs={{0,96},{16,112},{1,97},{17,113},{2,98},{18,114},{3,99},{19,115},{4... | collective-permute-start | bytes 786440 | tf_op jit(solution)/shard_map/ppermute | solution.py:34
  203.2 1.7 collective-permute-start.22
  205.9 1.4 collective-permute-start.24
  207.3 6.1 %collective-permute-done.18.refs_1_ = bf16[256,512]{1,0:T(8,128)(2,1)S(1)} collective-permute-done((bf16[256,512]{1,0:T(8,128)(2,1)S(1)}, bf16[256,512]{1,0:T(8,128)(2,1)S(1)}, u32[]{:S(2)}, u32[]{:S(2)}) %collective-permute-start.18) | collective-permute-done | bytes 262176 | tf_op jit(solution)/shard_map/ppermute | solution.py:34
  213.4 5.7 %collective-permute-done.22.refs_5_ = bf16[256,512]{1,0:T(8,128)(2,1)} collective-permute-done((bf16[256,512]{1,0:T(8,128)(2,1)S(1)}, bf16[256,512]{1,0:T(8,128)(2,1)}, u32[]{:S(2)}, u32[]{:S(2)}) %collective-permute-start.22) | collective-permute-done | bytes 262176 | tf_op jit(solution)/shard_map/ppermute | solution.py:34
  219.2 1.6 copy-done.5
  220.8 3.6 %shard_map.49 = f32[512,512]{1,0:T(8,128)S(1)} custom-call(s32[8]{0:T(128)S(1)} %stack.62.where_ref, bf16[8,512,256]{2,1,0:T(8,128)(2,1)S(1)} %bitcast.20, bf16[256,512]{1,0:T(8,128)(2,1)S(1)} %add_convert_fusion.refs_0_, bf16[256,512]{1,0:T(8,128)(2,1)S(1)} %collective-permute-done.18.refs_1_, bf16[256,512]{1,0:T(8,128)(2,1)S(1)} %collective-permute-done.19.refs_2_, ...), custom_call_target="tpu_custom_call" | custom-call | flops 1073741824 | bytes 3145728 | tf_op jit(solution)/shard_map/pallas_call | solution.py:207
  225.0 1.5 collective-permute-done.25
  (69 shorter events, 12.4 us)
Async XLA Ops:
  6.5 1.6 copy-start
  6.5 212.6 %all-gather.3.cloned.1.call-start = ((), (), s32[]{:S(2)}) async-start(), calls=%async_computation | async-start | bytes 2359296 | tf_op jit(solution)/shard_map/all_gather | solution.py:249
  10.5 0.7 collective-permute-start
  11.2 23.5 %collective-permute-start.1 = (bf16[256,256]{1,0:T(8,128)(2,1)S(1)}, bf16[256,256]{1,0:T(8,128)(2,1)S(1)}, u32[]{:S(2)}, u32[]{:S(2)}) collective-permute-start(bf16[256,256]{1,0:T(8,128)(2,1)S(1)} %collective-permute-done), channel_id=1, source_target_pairs={{0,8},{16,24},{1,9},{17,25},{2,10},{18,26},{3,11},{19,27},{4,12},{... | collective-permute-start | bytes 393224 | tf_op jit(solution)/shard_map/ppermute | solution.py:34
  29.5 91.8 %collective-permute-start.3 = (bf16[896,512]{1,0:T(8,128)(2,1)}, bf16[896,512]{1,0:T(8,128)(2,1)}, u32[]{:S(2)}, u32[]{:S(2)}) collective-permute-start(bf16[896,512]{1,0:T(8,128)(2,1)} %refs_7_.1), channel_id=1, source_target_pairs={{0,32},{16,48},{1,33},{17,49},{2,34},{18,50},{3,35},{19,51},{4,36}... | collective-permute-start | bytes 2752520 | tf_op jit(solution)/shard_map/ppermute | solution.py:34
  107.4 11.1 %collective-permute-start.15 = (bf16[2,128,896]{2,1,0:T(8,128)(2,1)}, bf16[2,128,896]{2,1,0:T(8,128)(2,1)S(1)}, u32[]{:S(2)}, u32[]{:S(2)}) collective-permute-start(bf16[2,128,896]{2,1,0:T(8,128)(2,1)} %get-tuple-element.11), channel_id=1, source_target_pairs={{0,136},{16,152},{1,137},{17,153},{2,138},{18,154},{3,139},{19,155... | collective-permute-start | bytes 1376264 | tf_op jit(solution)/shard_map/ppermute | solution.py:34
  107.5 28.4 %collective-permute-start.5 = (bf16[896,512]{1,0:T(8,128)(2,1)}, bf16[896,512]{1,0:T(8,128)(2,1)S(1)}, u32[]{:S(2)}, u32[]{:S(2)}) collective-permute-start(bf16[896,512]{1,0:T(8,128)(2,1)} %refs_7_.1), channel_id=1, source_target_pairs={{0,96},{16,112},{1,97},{17,113},{2,98},{18,114},{3,99},{19,115},{4... | collective-permute-start | bytes 2752520 | tf_op jit(solution)/shard_map/ppermute | solution.py:34
  116.5 40.3 %collective-permute-start.2 = (bf16[896,512]{1,0:T(8,128)(2,1)}, bf16[896,512]{1,0:T(8,128)(2,1)S(1)}, u32[]{:S(2)}, u32[]{:S(2)}) collective-permute-start(bf16[896,512]{1,0:T(8,128)(2,1)} %refs_7_.1), channel_id=1, source_target_pairs={{0,16},{16,0},{1,17},{17,1},{2,18},{18,2},{3,19},{19,3},{4,20},{20... | collective-permute-start | bytes 2752520 | tf_op jit(solution)/shard_map/ppermute | solution.py:34
  118.5 17.4 %collective-permute-start.11 = (bf16[3,128,896]{2,1,0:T(8,128)(2,1)}, bf16[3,128,896]{2,1,0:T(8,128)(2,1)S(1)}, u32[]{:S(2)}, u32[]{:S(2)}) collective-permute-start(bf16[3,128,896]{2,1,0:T(8,128)(2,1)} %get-tuple-element.9), channel_id=1, source_target_pairs={{0,136},{16,152},{1,137},{17,153},{2,138},{18,154},{3,139},{19,155... | collective-permute-start | bytes 2064392 | tf_op jit(solution)/shard_map/ppermute | solution.py:34
  119.3 32.4 %collective-permute-start.12 = (bf16[3,128,896]{2,1,0:T(8,128)(2,1)}, bf16[3,128,896]{2,1,0:T(8,128)(2,1)}, u32[]{:S(2)}, u32[]{:S(2)}) collective-permute-start(bf16[3,128,896]{2,1,0:T(8,128)(2,1)} %get-tuple-element.10), channel_id=1, source_target_pairs={{0,128},{16,144},{1,129},{17,145},{2,130},{18,146},{3,131},{19,147... | collective-permute-start | bytes 2064392 | tf_op jit(solution)/shard_map/ppermute | solution.py:34
  121.3 24.1 %collective-permute-start.16 = (bf16[2,128,896]{2,1,0:T(8,128)(2,1)}, bf16[2,128,896]{2,1,0:T(8,128)(2,1)S(1)}, u32[]{:S(2)}, u32[]{:S(2)}) collective-permute-start(bf16[2,128,896]{2,1,0:T(8,128)(2,1)} %get-tuple-element.12), channel_id=1, source_target_pairs={{0,128},{16,144},{1,129},{17,145},{2,130},{18,146},{3,131},{19,147... | collective-permute-start | bytes 1376264 | tf_op jit(solution)/shard_map/ppermute | solution.py:34
  135.9 21.9 %copy-start.6 = (bf16[3,128,896]{2,1,0:T(8,128)(2,1)}, bf16[3,128,896]{2,1,0:T(8,128)(2,1)S(1)}, u32[]{:S(2)}) copy-start(bf16[3,128,896]{2,1,0:T(8,128)(2,1)S(1)} %collective-permute-done.11.refs_1_) | copy-start | bytes 2064388
  135.9 21.9 %collective-permute-start.7 = (bf16[384,512]{1,0:T(8,128)(2,1)S(1)}, bf16[384,512]{1,0:T(8,128)(2,1)}, u32[]{:S(2)}, u32[]{:S(2)}) collective-permute-start(bf16[384,512]{1,0:T(8,128)(2,1)S(1)} %slice.18), channel_id=1, source_target_pairs={{0,32},{16,48},{1,33},{17,49},{2,34},{18,50},{3,35},{19,51},{4,36}... | collective-permute-start | bytes 1179656 | tf_op jit(solution)/shard_map/ppermute | solution.py:34
  135.9 27.9 %collective-permute-start.13 = (bf16[3,128,896]{2,1,0:T(8,128)(2,1)S(1)}, bf16[3,128,896]{2,1,0:T(8,128)(2,1)S(1)}, u32[]{:S(2)}, u32[]{:S(2)}) collective-permute-start(bf16[3,128,896]{2,1,0:T(8,128)(2,1)S(1)} %collective-permute-done.11.refs_1_), channel_id=1, source_target_pairs={{0,7},{16,23},{1,0},{17,16},{2,1},{18,17},{3,2},{19,18},{4,3},{20,... | collective-permute-start | bytes 2064392 | tf_op jit(solution)/shard_map/ppermute | solution.py:34
  146.2 11.6 %collective-permute-start.8 = (bf16[512,512]{1,0:T(8,128)(2,1)S(1)}, bf16[512,512]{1,0:T(8,128)(2,1)S(1)}, u32[]{:S(2)}, u32[]{:S(2)}) collective-permute-start(bf16[512,512]{1,0:T(8,128)(2,1)S(1)} %slice.19), channel_id=1, source_target_pairs={{0,96},{16,112},{1,97},{17,113},{2,98},{18,114},{3,99},{19,115},{4... | collective-permute-start | bytes 1572872 | tf_op jit(solution)/shard_map/ppermute | solution.py:34
  151.7 25.3 %collective-permute-start.4 = (bf16[896,512]{1,0:T(8,128)(2,1)}, bf16[896,512]{1,0:T(8,128)(2,1)}, u32[]{:S(2)}, u32[]{:S(2)}) collective-permute-start(bf16[896,512]{1,0:T(8,128)(2,1)} %collective-permute-done.3.refs_4_.refs_9_), channel_id=1, source_target_pairs={{0,16},{16,0},{1,17},{17,1},{2,18},{18,2},{3,19},{19,3},{4,20},{20... | collective-permute-start | bytes 2752520 | tf_op jit(solution)/shard_map/ppermute | solution.py:34
  157.8 19.2 %collective-permute-start.6 = (bf16[896,512]{1,0:T(8,128)(2,1)S(1)}, bf16[896,512]{1,0:T(8,128)(2,1)}, u32[]{:S(2)}, u32[]{:S(2)}) collective-permute-start(bf16[896,512]{1,0:T(8,128)(2,1)S(1)} %collective-permute-done.5.refs_6_.refs_11_), channel_id=1, source_target_pairs={{0,16},{16,0},{1,17},{17,1},{2,18},{18,2},{3,19},{19,3},{4,20},{20... | collective-permute-start | bytes 2752520 | tf_op jit(solution)/shard_map/ppermute | solution.py:34
  157.8 19.2 %collective-permute-start.14 = (bf16[3,128,896]{2,1,0:T(8,128)(2,1)}, bf16[3,128,896]{2,1,0:T(8,128)(2,1)}, u32[]{:S(2)}, u32[]{:S(2)}) collective-permute-start(bf16[3,128,896]{2,1,0:T(8,128)(2,1)} %collective-permute-done.12.refs_2_), channel_id=1, source_target_pairs={{0,1},{16,17},{1,2},{17,18},{2,3},{18,19},{3,4},{19,20},{4,5},{20,... | collective-permute-start | bytes 2064392 | tf_op jit(solution)/shard_map/ppermute | solution.py:34
  157.8 19.2 %collective-permute-start.10 = (bf16[512,512]{1,0:T(8,128)(2,1)S(1)}, bf16[512,512]{1,0:T(8,128)(2,1)}, u32[]{:S(2)}, u32[]{:S(2)}) collective-permute-start(bf16[512,512]{1,0:T(8,128)(2,1)S(1)} %collective-permute-done.8.refs_9_.refs_14_), channel_id=1, source_target_pairs={{0,16},{16,0},{1,17},{17,1},{2,18},{18,2},{3,19},{19,3},{4,20},{20... | collective-permute-start | bytes 1572872 | tf_op jit(solution)/shard_map/ppermute | solution.py:34
  164.7 12.3 %collective-permute-start.9 = (bf16[384,512]{1,0:T(8,128)(2,1)}, bf16[384,512]{1,0:T(8,128)(2,1)}, u32[]{:S(2)}, u32[]{:S(2)}) collective-permute-start(bf16[384,512]{1,0:T(8,128)(2,1)} %collective-permute-done.7.refs_8_.refs_13_), channel_id=1, source_target_pairs={{0,16},{16,0},{1,17},{17,1},{2,18},{18,2},{3,19},{19,3},{4,20},{20... | collective-permute-start | bytes 1179656 | tf_op jit(solution)/shard_map/ppermute | solution.py:34
  182.4 5.6 %copy-start.4 = (bf16[896,512]{1,0:T(8,128)(2,1)S(1)}, bf16[896,512]{1,0:T(8,128)(2,1)}, u32[]{:S(2)}) copy-start(bf16[896,512]{1,0:T(8,128)(2,1)} %copy-done.2) | copy-start | bytes 2752516
  187.9 8.6 %collective-permute-start.17 = (f16[256,512]{1,0:T(8,128)(2,1)S(1)}, f16[256,512]{1,0:T(8,128)(2,1)S(1)}, u32[]{:S(2)}, u32[]{:S(2)}) collective-permute-start(f16[256,512]{1,0:T(8,128)(2,1)S(1)} %multiply_convert_fusion), channel_id=1, source_target_pairs={{0,128},{16,144},{1,129},{17,145},{2,130},{18,146},{3,131},{19,147... | collective-permute-start | bytes 786440 | tf_op jit(solution)/shard_map/ppermute | solution.py:45
  188.0 3.1 %copy-start.1 = (bf16[256,14336]{1,0:T(8,128)(2,1)S(1)}, bf16[256,14336]{1,0:T(8,128)(2,1)}, u32[]{:S(2)}) copy-start(bf16[256,14336]{1,0:T(8,128)(2,1)} %source.1) | copy-start | bytes 22020100
  196.6 6.6 %collective-permute-start.20 = (bf16[256,512]{1,0:T(8,128)(2,1)S(1)}, bf16[256,512]{1,0:T(8,128)(2,1)S(1)}, u32[]{:S(2)}, u32[]{:S(2)}) collective-permute-start(bf16[256,512]{1,0:T(8,128)(2,1)S(1)} %add_convert_fusion.refs_0_), channel_id=1, source_target_pairs={{0,128},{16,144},{1,129},{17,145},{2,130},{18,146},{3,131},{19,147... | collective-permute-start | bytes 786440 | tf_op jit(solution)/shard_map/ppermute | solution.py:45
  198.1 7.8 %collective-permute-start.21 = (bf16[256,512]{1,0:T(8,128)(2,1)S(1)}, bf16[256,512]{1,0:T(8,128)(2,1)S(1)}, u32[]{:S(2)}, u32[]{:S(2)}) collective-permute-start(bf16[256,512]{1,0:T(8,128)(2,1)S(1)} %add_convert_fusion.refs_0_), channel_id=1, source_target_pairs={{0,64},{16,80},{1,65},{17,81},{2,66},{18,82},{3,67},{19,83},{4,68}... | collective-permute-start | bytes 786440 | tf_op jit(solution)/shard_map/ppermute | solution.py:34
  198.1 15.3 %collective-permute-start.18 = (bf16[256,512]{1,0:T(8,128)(2,1)S(1)}, bf16[256,512]{1,0:T(8,128)(2,1)S(1)}, u32[]{:S(2)}, u32[]{:S(2)}) collective-permute-start(bf16[256,512]{1,0:T(8,128)(2,1)S(1)} %add_convert_fusion.refs_0_), channel_id=1, source_target_pairs={{0,32},{16,48},{1,33},{17,49},{2,34},{18,50},{3,35},{19,51},{4,36}... | collective-permute-start | bytes 786440 | tf_op jit(solution)/shard_map/ppermute | solution.py:34
  199.8 13.6 %collective-permute-start.19 = (bf16[256,512]{1,0:T(8,128)(2,1)S(1)}, bf16[256,512]{1,0:T(8,128)(2,1)S(1)}, u32[]{:S(2)}, u32[]{:S(2)}) collective-permute-start(bf16[256,512]{1,0:T(8,128)(2,1)S(1)} %add_convert_fusion.refs_0_), channel_id=1, source_target_pairs={{0,96},{16,112},{1,97},{17,113},{2,98},{18,114},{3,99},{19,115},{4... | collective-permute-start | bytes 786440 | tf_op jit(solution)/shard_map/ppermute | solution.py:34
  203.2 15.9 %collective-permute-start.22 = (bf16[256,512]{1,0:T(8,128)(2,1)S(1)}, bf16[256,512]{1,0:T(8,128)(2,1)}, u32[]{:S(2)}, u32[]{:S(2)}) collective-permute-start(bf16[256,512]{1,0:T(8,128)(2,1)S(1)} %collective-permute-done.20.refs_3_), channel_id=1, source_target_pairs={{0,32},{16,48},{1,33},{17,49},{2,34},{18,50},{3,35},{19,51},{4,36}... | collective-permute-start | bytes 786440 | tf_op jit(solution)/shard_map/ppermute | solution.py:34
  204.9 14.2 %collective-permute-start.23 = (bf16[256,512]{1,0:T(8,128)(2,1)S(1)}, bf16[256,512]{1,0:T(8,128)(2,1)}, u32[]{:S(2)}, u32[]{:S(2)}) collective-permute-start(bf16[256,512]{1,0:T(8,128)(2,1)S(1)} %collective-permute-done.20.refs_3_), channel_id=1, source_target_pairs={{0,96},{16,112},{1,97},{17,113},{2,98},{18,114},{3,99},{19,115},{4... | collective-permute-start | bytes 786440 | tf_op jit(solution)/shard_map/ppermute | solution.py:34
  205.9 13.3 %collective-permute-start.24 = (bf16[256,512]{1,0:T(8,128)(2,1)S(1)}, bf16[256,512]{1,0:T(8,128)(2,1)}, u32[]{:S(2)}, u32[]{:S(2)}) collective-permute-start(bf16[256,512]{1,0:T(8,128)(2,1)S(1)} %collective-permute-done.21.refs_4_), channel_id=1, source_target_pairs={{0,128},{16,144},{1,129},{17,145},{2,130},{18,146},{3,131},{19,147... | collective-permute-start | bytes 786440 | tf_op jit(solution)/shard_map/ppermute | solution.py:45
  219.2 1.6 copy-start.5
  224.4 2.1 collective-permute-start.25
  (9 other events, 8.8 us)
Sparse Core Ops, SparseCore 0:
  35.6 79.9 all-gather.2

commit v3 on v0

v3 whole, which is shorter than its diff:
```python
import jax
import jax.numpy as jnp
from jax import lax
from jax.experimental import pallas as pl
from jax.experimental.pallas import tpu as pltpu
from jax.sharding import PartitionSpec as P

TOK = 128
EXAMPLES = 2
NX, NY, NC = 2, 4, 2
NH, NZ = 2, 8
SPLIT = 2
FACTOR = 32.0
VMEM = 60 * 1024 * 1024
BLOCKS = ((0, 0), (0, 1), (3, 0), (3, 1), (1, 0), (1, 1), (2, 0), (2, 1))
ORDER = ((0, 0), (0, 3), (0, 1), (1, 0), (0, 2), (1, 3), (1, 1), (1, 2))


def index(x, y, z, c):
    return ((x % NX * NY + y) * NC + c) * NH * NZ + x // NX * NZ + z


def shift(value, dx=0, dy=0, dz=0, dc=0):
    size = NX * NH
    pairs = [
        (index(x, y, z, c), index((x + dx) % size, (y + dy) % NY, (z + dz) % NZ, (c + dc) % NC))
        for x in range(size)
        for y in range(NY)
        for z in range(NZ)
        for c in range(NC)
    ]
    return lax.ppermute(value, ("dp", "blk"), pairs)


def by_core(value, dx=0, dy=0, dz=0):
    size = NX * NH
    pairs = []
    for x in range(size):
        for y in range(NY):
            for z in range(NZ):
                for c, way in ((0, 1), (1, -1)):
                    target = ((x + way * dx) % size, (y + way * dy) % NY, (z + way * dz) % NZ, c)
                    pairs.append((index(x, y, z, c), index(*target)))
    return lax.ppermute(value, ("dp", "blk"), pairs)


def swap(value, dy=0):
    pairs = [
        (index(x, y, z, c), index(x ^ 1, (y + dy) % NY, z, c))
        for x in range(NX * NH)
        for y in range(NY)
        for z in range(NZ)
        for c in range(NC)
    ]
    return lax.ppermute(value, ("dp", "blk"), pairs)


def dot(a, b):
    return jnp.dot(a, b, preferred_element_type=jnp.float32)


def space(kind):
    return pl.BlockSpec(memory_space=kind)


def pieces_kernel(columns_ref, source, near, rest, held, arrived, left):
    moves = []
    for k in range(held.shape[0]):
        column = pl.multiple_of(columns_ref[k], 128)
        out = near.at[k] if k < SPLIT else rest.at[k - SPLIT]
        moves.append(
            (
                pltpu.make_async_copy(
                    source.at[:, pl.ds(column, held.shape[2])], held.at[k], arrived.at[k]
                ),
                pltpu.make_async_copy(held.at[k], out, left.at[k]),
            )
        )
    for get, put in moves:
        get.start()
    for get, put in moves:
        get.wait()
        put.start()
    for get, put in moves:
        put.wait()


def pieces(columns, activations, depth):
    tokens, count = activations.shape[0], len(BLOCKS) - SPLIT
    return pl.pallas_call(
        pieces_kernel,
        out_shape=[
            jax.ShapeDtypeStruct((n, tokens, depth), activations.dtype)
            for n in (SPLIT, count - SPLIT)
        ],
        in_specs=[space(pltpu.SMEM), space(pltpu.HBM)],
        out_specs=[space(pltpu.HBM)] * 2,
        scratch_shapes=[
            pltpu.VMEM((count, tokens, depth), activations.dtype),
            pltpu.SemaphoreType.DMA((count,)),
            pltpu.SemaphoreType.DMA((count,)),
        ],
        compiler_params=pltpu.CompilerParams(vmem_limit_bytes=VMEM),
        cost_estimate=pl.CostEstimate(flops=0, bytes_accessed=2**23, transcendentals=0),
    )(columns, activations)


def product_kernel(moves, layout, *refs):
    table, sources, refs = refs[0], refs[1 : 1 + layout[0]], refs[1 + layout[0] :]
    parts, refs = refs[: sum(layout[1])], refs[sum(layout[1]) :]
    before, (out, rows, panels, semaphore) = refs[:-4], refs[-4:]
    pairs = moves(table, sources, rows)
    for_rows = [pltpu.make_async_copy(*pair, semaphore.at[n]) for n, pair in enumerate(pairs)]
    for_panels, at = [], 0
    for k, count in enumerate(layout[1]):
        filled, copies = 0, []
        for part in parts[at : at + count]:
            target = panels.at[k, pl.ds(filled, part.shape[0])]
            number = len(pairs) + at + len(copies)
            copies.append(pltpu.make_async_copy(part, target, semaphore.at[number]))
            filled += part.shape[0]
        at += count
        for_panels.append(copies)
    for copy in for_rows + sum(for_panels, []):
        copy.start()
    for copy in for_rows:
        copy.wait()
    for k, copies in enumerate(for_panels):
        for copy in copies:
            copy.wait()
        term = dot(rows[k], panels[k])
        if k:
            out[...] += term
        else:
            out[...] = before[0][...] + term if before else term


def product(moves, count, table, sources, panels, before=None):
    tokens, blocks = EXAMPLES * TOK, len(panels)
    depth, width = panels[0][0].shape[0] if len(panels[0]) == 1 else sum(
        part.shape[0] for part in panels[0]
    ), panels[0][0].shape[1]
    parts = sum(panels, [])
    layout = (len(sources), [len(panel) for panel in panels])
    extra = [] if before is None else [before]
    return pl.pallas_call(
        lambda *refs: product_kernel(moves, layout, *refs),
        out_shape=jax.ShapeDtypeStruct((tokens, width), jnp.float32),
        in_specs=[space(pltpu.SMEM)]
        + [space(pl.ANY)] * (len(sources) + len(parts))
        + [space(pltpu.VMEM)] * len(extra),
        out_specs=space(pltpu.VMEM),
        scratch_shapes=[
            pltpu.VMEM((blocks, tokens, depth), jnp.bfloat16),
            pltpu.VMEM((blocks, depth, width), jnp.bfloat16),
            pltpu.SemaphoreType.DMA((count + len(parts),)),
        ],
        compiler_params=pltpu.CompilerParams(vmem_limit_bytes=VMEM),
        cost_estimate=pl.CostEstimate(
            flops=2 * tokens * width * blocks * depth, bytes_accessed=2**22, transcendentals=0
        ),
    )(table, *sources, *parts, *extra)


def near_moves(table, sources, rows):
    return [
        (source, rows.at[pl.ds(start * SPLIT, SPLIT)])
        for start, source in zip((table[0], 1 - table[0]), sources)
    ]


def rest_moves(table, sources, rows):
    return [(sources[0], rows)]


def own_moves(table, sources, rows):
    return [
        (sources[0].at[:, pl.ds(pl.multiple_of(table[k], 128), rows.shape[2])], rows.at[k])
        for k in range(rows.shape[0])
    ]


def squares_kernel(where_ref, out_rows, *refs):
    blocks = (len(refs) - 4)
    in_rows, (total_ref, outer, inner, semaphore) = refs[:-4], refs[-4:]
    copies = [
        (
            pltpu.make_async_copy(out_rows.at[where_ref[k]], outer.at[k], semaphore.at[2 * k]),
            pltpu.make_async_copy(in_rows[k], inner.at[k], semaphore.at[2 * k + 1]),
        )
        for k in range(blocks)
    ]
    for pair in copies:
        pair[0].start()
        pair[1].start()
    for pair in copies:
        pair[0].wait()
        pair[1].wait()
    half = total_ref.shape[0] // 2

    @pl.loop(0, total_ref.shape[1] // TILE)
    def _(n):
        columns = pl.ds(pl.multiple_of(n * TILE, TILE), TILE)
        for part in range(2):
            rows = pl.ds(part * half, half)
            total = None
            for k in range(blocks):
                for example in range(EXAMPLES):
                    tokens = pl.ds(example * TOK, TOK)
                    rotated = dot(outer[k, rows, tokens], inner[k, tokens, columns])
                    squared = rotated * rotated
                    total = squared if total is None else total + squared
            total_ref[rows, columns] = total


TILE = 256


def sums_of_squares(where, out_rows, in_rows):
    rows, tokens = out_rows.shape[1:]
    width, blocks = in_rows[0].shape[1], len(in_rows)
    return pl.pallas_call(
        squares_kernel,
        out_shape=jax.ShapeDtypeStruct((rows, width), jnp.float32),
        in_specs=[space(pltpu.SMEM)] + [space(pl.ANY)] * (1 + blocks),
        out_specs=space(pltpu.VMEM),
        scratch_shapes=[
            pltpu.VMEM((blocks, rows, tokens), jnp.bfloat16),
            pltpu.VMEM((blocks, tokens, width), jnp.bfloat16),
            pltpu.SemaphoreType.DMA((2 * blocks,)),
        ],
        compiler_params=pltpu.CompilerParams(vmem_limit_bytes=VMEM),
        cost_estimate=pl.CostEstimate(
            flops=2 * rows * width * blocks * tokens,
            bytes_accessed=out_rows.size * 2 + rows * width * 4,
            transcendentals=0,
        ),
    )(where, out_rows, *in_rows)


def transposed(block):
    pairs = []
    for sx in range(NX):
        for sy in range(NY):
            for sc in range(NC):
                for t in range(NX * NY * NC):
                    source = ((sx * NY + sy) * NC + sc) * NH * NZ + t
                    target = (t // NC * NC + sc) * NH * NZ + t % NC * NZ + sx * NY + sy
                    pairs.append((source, target))
    return lax.ppermute(block, ("dp", "blk"), pairs)


def on_device(activations, out_grads, basis_in, basis_out):
    d, b = lax.axis_index("dp"), lax.axis_index("blk")
    core, y, x = d % NC, (d // NC) % NY, d // (NC * NY)
    parity = b % 2
    scale = 1.0 / float(EXAMPLES * NX * NY * NC)
    depth = basis_in.shape[0]
    spots = [((y + dy) % NY) * NC + (core + dc) % NC for dy, dc in BLOCKS]
    half = len(BLOCKS)

    table = jnp.stack(spots)
    give = jnp.concatenate(
        [lax.dynamic_slice_in_dim(table, parity * SPLIT, SPLIT), table[2 * SPLIT :]]
    )
    give = ((half * (1 - x) + give) * depth).astype(jnp.int32)
    keep = ((half * x + table) * depth).astype(jnp.int32)
    near, rest = pieces(give, activations, depth)
    left, right = shift(basis_in, dy=1), shift(basis_in, dy=3)
    near, own_other = by_core(near, dx=1), shift(basis_in, dc=1)
    block = transposed(dot(out_grads, basis_out).astype(jnp.bfloat16).T)

    near, left, right, rest, block, own_other = lax.optimization_barrier(
        (near, left, right, rest, block, own_other)
    )
    far = by_core(jnp.where(core == 0, left, right), dy=1)
    rest, away = by_core(rest, dx=1), by_core(near, dz=1)
    left_other, right_other = shift(left, dc=1), shift(right, dc=1)

    other = shift(block, dx=NX)
    mine = (b // NZ) == core
    block = jnp.concatenate([jnp.where(mine, block, other), jnp.where(mine, other, block)], 0)
    out_rows = lax.all_gather(
        block,
        "blk",
        axis=0,
        axis_index_groups=[[h * NZ + z for z in range(NZ)] for h in range(NH)],
    )
    where = jnp.stack([((x + dx) % NX) * NY + (y + dy) % NY for dx, dy in ORDER]).astype(jnp.int32)

    panels = [basis_in, own_other, left, left_other, right, right_other, far, shift(far, dc=1)]
    panels = [[panel] for panel in panels]
    parity = parity.reshape(1).astype(jnp.int32)
    partial = product(near_moves, 2, parity, (near, away), panels[: 2 * SPLIT])
    partial = product(rest_moves, 1, parity, (rest,), panels[2 * SPLIT :], partial)
    arrived = swap((partial * FACTOR).astype(jnp.float16))
    total = product(own_moves, len(BLOCKS), keep, (activations,), panels)
    proj_in = (total + arrived.astype(jnp.float32) * (1.0 / FACTOR)).astype(jnp.bfloat16)

    p_left, p_right, p_far = shift(proj_in, dy=1), shift(proj_in, dy=3), shift(proj_in, dy=2)
    p_across = swap(proj_in)
    px_left, px_right = shift(p_across, dy=1), shift(p_across, dy=3)
    px_far = swap(p_far)
    sums = sums_of_squares(
        where,
        out_rows,
        (proj_in, p_left, p_right, p_across, p_far, px_left, px_right, px_far),
    )
    rows = sums.shape[0] // 2
    return (sums[:rows] + shift(sums[rows:], dc=1)) * jnp.float32(scale)


def solution(mesh):
    return jax.shard_map(
        on_device,
        mesh=mesh,
        in_specs=(P("dp", None), P("dp", None), P("dp", "blk"), P(None, "blk")),
        out_specs=P("dp", "blk"),
        check_vma=False,
    )
```

time: 281 us -> 139 us (0.49)
  waiting for transfers between devices: 234 us -> 60 us
  starting transfers between devices: 0.08 us -> 28 us
  matrix products: 28.2 us -> 2.34 us
  Pallas kernels: 0 us -> 25.4 us
  other arithmetic: 1.88 us -> 7.16 us
    all_gather x2 -> x1, waiting for transfers between devices: 160 us -> 0.01 us  [on_device(): lax.all_gather(block, 'blk', axis=0, axis_index_groups=[[h * NZ + z for z...]
    reduce_scatter x1 -> x0, waiting for transfers between devices: 73.3 us -> none  [on_device(): lax.psum_scatter(lax.fori_loop(0, EXAMPLES, add_example, jnp.zeros((lax.a...]
    ppermute x0 -> x21, waiting for transfers between devices: none -> 59.9 us  [the longest x13 34.5 us: shift(): return lax.ppermute(value, ('dp', 'blk'), pairs)]
    ppermute x0 -> x21, starting transfers between devices: none -> 28 us  [the longest x13 12.4 us: shift(): return lax.ppermute(value, ('dp', 'blk'), pairs)]
    dot_general x4 -> x1, matrix products: 28.2 us -> 2.34 us  [dot(): return jnp.dot(a, b, preferred_element_type=jnp.float32)]
    pallas_call x0 -> x5, Pallas kernels: none -> 25.4 us  [the longest x3 15.7 us: product(): pl.pallas_call(lambda *refs: product_kernel(moves, layout, *refs), out_sh...]
  transfers between devices with their start and end apart: 3 -> 22, of which waited for: 3 -> 11; matrix products, arithmetic and copies ran while one was open for 5% -> 5% of each run, Pallas kernels for 0% -> 11%
where the time goes in v3:
time: 139 us
  waiting for transfers between devices  60 us (43%)
  starting transfers between devices  28 us (20%)
  Pallas kernels  25.4 us (18%)
  between operations  13.6 us (10%)
  other arithmetic  7.16 us (5%)
  matrix products  2.34 us (2%)
  local copies, waits for them, and re-layouts  2.02 us (1%)
    ppermute x13, waiting for transfers between devices, shift(): return lax.ppermute(value, ('dp', 'blk'), pairs)  34.5 us
    ppermute x4, waiting for transfers between devices, by_core(): return lax.ppermute(value, ('dp', 'blk'), pairs)  22.9 us
    pallas_call x3, Pallas kernels, product(): pl.pallas_call(lambda *refs: product_kernel(moves, layout, *refs), out_sh...  15.7 us
    ppermute x13, starting transfers between devices, shift(): return lax.ppermute(value, ('dp', 'blk'), pairs)  12.4 us
    ppermute x4, starting transfers between devices, by_core(): return lax.ppermute(value, ('dp', 'blk'), pairs)  11.4 us
    pallas_call x1, Pallas kernels, sums_of_squares(): pl.pallas_call(squares_kernel, out_shape=jax.ShapeDtypeStruct((rows, widt...  6.42 us
    ppermute x3, starting transfers between devices, swap(): return lax.ppermute(value, ('dp', 'blk'), pairs)  3.57 us
    pallas_call x1, Pallas kernels, pieces(): pl.pallas_call(pieces_kernel, out_shape=[jax.ShapeDtypeStruct((n, tokens,...  3.33 us
  transfers between devices with their start and end apart: 22, of which 11 were waited for; matrix products, arithmetic and copies ran while one was open for 5% of the time, Pallas kernels for 11%

profile of v3, /device:TPU:1, one launch (start us, length us, event | category | flops | bytes accessed | tf_op | source)
XLA Modules:
  0.0 138.5 jit_solution(2547692906845374490)
XLA Ops:
  7.3 3.3 %shard_map.46 = (bf16[2,256,896]{2,1,0:T(8,128)(2,1)}, bf16[4,256,896]{2,1,0:T(8,128)(2,1)}) custom-call(s32[6]{0:T(128)} %add_multiply_fusion.1.columns_ref, bf16[256,14336]{1,0:T(8,128)(2,1)} %refs_1_.1), custom_call_target="tpu_custom_call" | custom-call | bytes 8388608 | tf_op jit(solution)/shard_map/pallas_call | solution.py:90
  10.6 3.4 %collective-permute-start = (bf16[2,256,896]{2,1,0:T(8,128)(2,1)}, bf16[2,256,896]{2,1,0:T(8,128)(2,1)}, u32[]{:S(2)}, u32[]{:S(2)}) collective-permute-start(bf16[2,256,896]{2,1,0:T(8,128)(2,1)} %get-tuple-element.13), channel_id=1, source_target_pairs={{0,128},{16,152},{1,129},{17,153},{2,130},{18,154},{3,131},{19,155... | collective-permute-start | bytes 2752520 | tf_op jit(solution)/shard_map/ppermute | solution.py:44
  14.0 1.3 collective-permute-start.1
  15.3 1.4 %collective-permute-start.2 = (bf16[896,512]{1,0:T(8,128)(2,1)}, bf16[896,512]{1,0:T(8,128)(2,1)}, u32[]{:S(2)}, u32[]{:S(2)}) collective-permute-start(bf16[896,512]{1,0:T(8,128)(2,1)} %refs_3_.1), channel_id=1, source_target_pairs={{0,96},{16,112},{1,97},{17,113},{2,98},{18,114},{3,99},{19,115},{4... | collective-permute-start | bytes 2752520 | tf_op jit(solution)/shard_map/ppermute | solution.py:32
  17.3 2.3 %convolution_convert_fusion = bf16[256,256]{1,0:T(8,128)(2,1)S(1)} fusion(bf16[4096,256]{1,0:T(8,128)(2,1)S(1)} %copy-done, bf16[256,4096]{1,0:T(8,128)(2,1)} %param.5), kind=kOutput, calls=%fused_computation | convolution fusion | flops 536936448 | bytes 4325376 | tf_op jit(solution)/shard_map/dot_general | solution.py:59
  20.3 4.4 %collective-permute-done.refs_1_ = bf16[2,256,896]{2,1,0:T(8,128)(2,1)} collective-permute-done((bf16[2,256,896]{2,1,0:T(8,128)(2,1)}, bf16[2,256,896]{2,1,0:T(8,128)(2,1)}, u32[]{:S(2)}, u32[]{:S(2)}) %collective-permute-start) | collective-permute-done | bytes 917536 | tf_op jit(solution)/shard_map/ppermute | solution.py:44
  24.7 16.6 %collective-permute-done.1.refs_4_.refs_5_ = bf16[896,512]{1,0:T(8,128)(2,1)S(1)} collective-permute-done((bf16[896,512]{1,0:T(8,128)(2,1)}, bf16[896,512]{1,0:T(8,128)(2,1)S(1)}, u32[]{:S(2)}, u32[]{:S(2)}) %collective-permute-start.1) | collective-permute-done | bytes 917536 | tf_op jit(solution)/shard_map/ppermute | solution.py:32
  41.4 6.0 %collective-permute-done.5 = bf16[256,256]{1,0:T(8,128)(2,1)S(1)} collective-permute-done((bf16[256,256]{1,0:T(8,128)(2,1)S(1)}, bf16[256,256]{1,0:T(8,128)(2,1)S(1)}, u32[]{:S(2)}, u32[]{:S(2)}) %collective-permute-start.5) | collective-permute-done | bytes 131104 | tf_op jit(solution)/shard_map/ppermute | solution.py:32
  48.2 1.3 broadcast_select_fusion
  50.3 2.1 %collective-permute-start.10 = (bf16[4,256,896]{2,1,0:T(8,128)(2,1)}, bf16[4,256,896]{2,1,0:T(8,128)(2,1)}, u32[]{:S(2)}, u32[]{:S(2)}) collective-permute-start(bf16[4,256,896]{2,1,0:T(8,128)(2,1)} %get-tuple-element.19), channel_id=1, source_target_pairs={{0,128},{16,152},{1,129},{17,153},{2,130},{18,154},{3,131},{19,155... | collective-permute-start | bytes 5505032 | tf_op jit(solution)/shard_map/ppermute | solution.py:44
  52.4 5.1 %collective-permute-start.11 = (bf16[2,256,896]{2,1,0:T(8,128)(2,1)}, bf16[2,256,896]{2,1,0:T(8,128)(2,1)}, u32[]{:S(2)}, u32[]{:S(2)}) collective-permute-start(bf16[2,256,896]{2,1,0:T(8,128)(2,1)} %collective-permute-done.refs_1_), channel_id=1, source_target_pairs={{0,1},{16,23},{1,2},{17,16},{2,3},{18,17},{3,4},{19,18},{4,5},{20,... | collective-permute-start | bytes 2752520 | tf_op jit(solution)/shard_map/ppermute | solution.py:44
  58.0 4.8 %collective-permute-done.8.refs_8_.refs_4_ = bf16[896,512]{1,0:T(8,128)(2,1)} collective-permute-done((bf16[896,512]{1,0:T(8,128)(2,1)S(1)}, bf16[896,512]{1,0:T(8,128)(2,1)}, u32[]{:S(2)}, u32[]{:S(2)}) %collective-permute-start.8) | collective-permute-done | bytes 917536 | tf_op jit(solution)/shard_map/ppermute | solution.py:44
  62.8 1.6 %collective-permute-start.9 = (bf16[896,512]{1,0:T(8,128)(2,1)}, bf16[896,512]{1,0:T(8,128)(2,1)}, u32[]{:S(2)}, u32[]{:S(2)}) collective-permute-start(bf16[896,512]{1,0:T(8,128)(2,1)} %collective-permute-done.8.refs_8_.refs_4_), channel_id=1, source_target_pairs={{0,16},{16,0},{1,17},{17,1},{2,18},{18,2},{3,19},{19,3},{4,20},{20... | collective-permute-start | bytes 2752520 | tf_op jit(solution)/shard_map/ppermute | solution.py:32
  64.5 13.7 %collective-permute-done.11.refs_2_ = bf16[2,256,896]{2,1,0:T(8,128)(2,1)} collective-permute-done((bf16[2,256,896]{2,1,0:T(8,128)(2,1)}, bf16[2,256,896]{2,1,0:T(8,128)(2,1)}, u32[]{:S(2)}, u32[]{:S(2)}) %collective-permute-start.11) | collective-permute-done | bytes 917536 | tf_op jit(solution)/shard_map/ppermute | solution.py:44
  78.2 4.0 %shard_map.48.refs_6_ = f32[256,512]{1,0:T(8,128)} custom-call(s32[1]{0:T(128)} %bitcast.17.refs_0_, bf16[2,256,896]{2,1,0:T(8,128)(2,1)} %collective-permute-done.refs_1_, bf16[2,256,896]{2,1,0:T(8,128)(2,1)} %collective-permute-done.11.refs_2_, bf16[896,512]{1,0:T(8,128)(2,1)} %refs_3_.1, bf16[896,512]{1,0:T(8,128)(2,1)} %collective-permute-done.4.refs_3_.refs_4_, ...), custom_call_target="tpu_custom_call" | custom-call | flops 939524096 | bytes 4194304 | tf_op jit(solution)/shard_map/pallas_call | solution.py:146
  82.2 5.1 %shard_map.49 = f32[256,512]{1,0:T(8,128)} custom-call(s32[1]{0:T(128)} %bitcast.17.refs_0_, bf16[4,256,896]{2,1,0:T(8,128)(2,1)} %collective-permute-done.10.refs_1_, bf16[896,512]{1,0:T(8,128)(2,1)} %collective-permute-done.2.refs_6_.refs_2_, bf16[896,512]{1,0:T(8,128)(2,1)} %collective-permute-done.7.refs_7_.refs_3_, ...), custom_call_target="tpu_custom_call" | custom-call | flops 939524096 | bytes 4194304 | tf_op jit(solution)/shard_map/pallas_call | solution.py:146
  87.3 1.1 multiply_convert_fusion
  88.4 2.7 %collective-permute-start.12 = (f16[256,512]{1,0:T(8,128)(2,1)S(1)}, f16[256,512]{1,0:T(8,128)(2,1)S(1)}, u32[]{:S(2)}, u32[]{:S(2)}) collective-permute-start(f16[256,512]{1,0:T(8,128)(2,1)S(1)} %multiply_convert_fusion), channel_id=1, source_target_pairs={{0,128},{16,144},{1,129},{17,145},{2,130},{18,146},{3,131},{19,147... | collective-permute-start | bytes 786440 | tf_op jit(solution)/shard_map/ppermute | solution.py:55
  91.5 6.6 %shard_map.47 = f32[256,512]{1,0:T(8,128)} custom-call(s32[8]{0:T(128)} %add_multiply_fusion.refs_0_, bf16[256,14336]{1,0:T(8,128)(2,1)} %refs_1_.1, bf16[896,512]{1,0:T(8,128)(2,1)} %refs_3_.1, bf16[896,512]{1,0:T(8,128)(2,1)} %collective-permute-done.4.refs_3_.refs_4_, bf16[896,512]{1,0:T(8,128)(2,1)} %copy-done.1, ...), custom_call_target="tpu_custom_call" | custom-call | flops 1879048192 | bytes 4194304 | tf_op jit(solution)/shard_map/pallas_call | solution.py:146
  98.2 1.1 add_convert_fusion.refs_0_
  99.7 2.2 %collective-permute-start.13 = (bf16[256,512]{1,0:T(8,128)(2,1)S(1)}, bf16[256,512]{1,0:T(8,128)(2,1)S(1)}, u32[]{:S(2)}, u32[]{:S(2)}) collective-permute-start(bf16[256,512]{1,0:T(8,128)(2,1)S(1)} %add_convert_fusion.refs_0_), channel_id=1, source_target_pairs={{0,32},{16,48},{1,33},{17,49},{2,34},{18,50},{3,35},{19,51},{4,36}... | collective-permute-start | bytes 786440 | tf_op jit(solution)/shard_map/ppermute | solution.py:32
  102.4 2.5 %collective-permute-done.15.refs_3_ = bf16[256,512]{1,0:T(8,128)(2,1)S(1)} collective-permute-done((bf16[256,512]{1,0:T(8,128)(2,1)S(1)}, bf16[256,512]{1,0:T(8,128)(2,1)S(1)}, u32[]{:S(2)}, u32[]{:S(2)}) %collective-permute-start.15) | collective-permute-done | bytes 262176 | tf_op jit(solution)/shard_map/ppermute | solution.py:55
  104.9 2.7 %collective-permute-start.18 = (bf16[256,512]{1,0:T(8,128)(2,1)S(1)}, bf16[256,512]{1,0:T(8,128)(2,1)}, u32[]{:S(2)}, u32[]{:S(2)}) collective-permute-start(bf16[256,512]{1,0:T(8,128)(2,1)S(1)} %collective-permute-done.15.refs_3_), channel_id=1, source_target_pairs={{0,96},{16,112},{1,97},{17,113},{2,98},{18,114},{3,99},{19,115},{4... | collective-permute-start | bytes 786440 | tf_op jit(solution)/shard_map/ppermute | solution.py:32
  109.0 3.7 %collective-permute-done.13.refs_1_ = bf16[256,512]{1,0:T(8,128)(2,1)S(1)} collective-permute-done((bf16[256,512]{1,0:T(8,128)(2,1)S(1)}, bf16[256,512]{1,0:T(8,128)(2,1)S(1)}, u32[]{:S(2)}, u32[]{:S(2)}) %collective-permute-start.13) | collective-permute-done | bytes 262176 | tf_op jit(solution)/shard_map/ppermute | solution.py:32
  112.7 1.1 collective-permute-done.14.refs_2_
  113.8 4.6 %collective-permute-done.17.refs_5_ = bf16[256,512]{1,0:T(8,128)(2,1)} collective-permute-done((bf16[256,512]{1,0:T(8,128)(2,1)S(1)}, bf16[256,512]{1,0:T(8,128)(2,1)}, u32[]{:S(2)}, u32[]{:S(2)}) %collective-permute-start.17) | collective-permute-done | bytes 262176 | tf_op jit(solution)/shard_map/ppermute | solution.py:32
  118.5 1.0 collective-permute-done.18.refs_6_
  119.5 6.4 %shard_map.50 = f32[512,512]{1,0:T(8,128)} custom-call(s32[8]{0:T(128)} %stack.62.where_ref, bf16[8,512,256]{2,1,0:T(8,128)(2,1)} %bitcast.20, bf16[256,512]{1,0:T(8,128)(2,1)} %copy-done.2, bf16[256,512]{1,0:T(8,128)(2,1)} %copy-done.5, bf16[256,512]{1,0:T(8,128)(2,1)} %copy-done.6, bf16[256,512]{1,0:T(8,128)(2,1)} %copy-done.3, ...), custom_call_target="tpu_custom_call" | custom-call | flops 1073741824 | bytes 3145728 | tf_op jit(solution)/shard_map/pallas_call | solution.py:222
  125.9 1.1 slice.11
  127.0 1.2 collective-permute-start.20
  128.2 1.5 %collective-permute-done.20 = f32[256,512]{1,0:T(8,128)S(1)} collective-permute-done((f32[256,512]{1,0:T(8,128)S(1)}, f32[256,512]{1,0:T(8,128)S(1)}, u32[]{:S(2)}, u32[]{:S(2)}) %collective-permute-start.20) | collective-permute-done | bytes 524320 | tf_op jit(solution)/shard_map/ppermute | solution.py:32
  129.7 1.9 %fusion = f32[256,512]{1,0:T(8,128)} fusion(f32[256,512]{1,0:T(8,128)S(1)} %collective-permute-done.20, f32[512,512]{1,0:T(8,128)} %shard_map.50), kind=kLoop, calls=%fused_computation.3 | loop fusion | flops 262144 | bytes 1572864 | tf_op jit(solution)/shard_map/mul | solution.py:310
  (46 shorter events, 7.0 us)
Async XLA Ops:
  6.5 10.8 %copy-start = (bf16[4096,256]{1,0:T(8,128)(2,1)S(1)}, bf16[4096,256]{1,0:T(8,128)(2,1)}, u32[]{:S(2)}) copy-start(bf16[4096,256]{1,0:T(8,128)(2,1)} %param.7) | copy-start | bytes 6291460
  6.5 112.9 %all-gather.3.cloned.1.call-start = ((), (), s32[]{:S(2)}) async-start(), calls=%async_computation | async-start | bytes 2359296 | tf_op jit(solution)/shard_map/all_gather | solution.py:283
  10.6 14.0 %collective-permute-start = (bf16[2,256,896]{2,1,0:T(8,128)(2,1)}, bf16[2,256,896]{2,1,0:T(8,128)(2,1)}, u32[]{:S(2)}, u32[]{:S(2)}) collective-permute-start(bf16[2,256,896]{2,1,0:T(8,128)(2,1)} %get-tuple-element.13), channel_id=1, source_target_pairs={{0,128},{16,152},{1,129},{17,153},{2,130},{18,154},{3,131},{19,155... | collective-permute-start | bytes 2752520 | tf_op jit(solution)/shard_map/ppermute | solution.py:44
  14.0 27.3 %collective-permute-start.1 = (bf16[896,512]{1,0:T(8,128)(2,1)}, bf16[896,512]{1,0:T(8,128)(2,1)S(1)}, u32[]{:S(2)}, u32[]{:S(2)}) collective-permute-start(bf16[896,512]{1,0:T(8,128)(2,1)} %refs_3_.1), channel_id=1, source_target_pairs={{0,32},{16,48},{1,33},{17,49},{2,34},{18,50},{3,35},{19,51},{4,36}... | collective-permute-start | bytes 2752520 | tf_op jit(solution)/shard_map/ppermute | solution.py:32
  15.3 26.0 %collective-permute-start.2 = (bf16[896,512]{1,0:T(8,128)(2,1)}, bf16[896,512]{1,0:T(8,128)(2,1)}, u32[]{:S(2)}, u32[]{:S(2)}) collective-permute-start(bf16[896,512]{1,0:T(8,128)(2,1)} %refs_3_.1), channel_id=1, source_target_pairs={{0,96},{16,112},{1,97},{17,113},{2,98},{18,114},{3,99},{19,115},{4... | collective-permute-start | bytes 2752520 | tf_op jit(solution)/shard_map/ppermute | solution.py:32
  16.8 24.5 %collective-permute-start.4 = (bf16[896,512]{1,0:T(8,128)(2,1)}, bf16[896,512]{1,0:T(8,128)(2,1)}, u32[]{:S(2)}, u32[]{:S(2)}) collective-permute-start(bf16[896,512]{1,0:T(8,128)(2,1)} %refs_3_.1), channel_id=1, source_target_pairs={{0,16},{16,0},{1,17},{17,1},{2,18},{18,2},{3,19},{19,3},{4,20},{20... | collective-permute-start | bytes 2752520 | tf_op jit(solution)/shard_map/ppermute | solution.py:32
  19.6 0.7 collective-permute-start.3
  41.3 36.9 %copy-start.1 = (bf16[896,512]{1,0:T(8,128)(2,1)}, bf16[896,512]{1,0:T(8,128)(2,1)S(1)}, u32[]{:S(2)}) copy-start(bf16[896,512]{1,0:T(8,128)(2,1)S(1)} %collective-permute-done.1.refs_4_.refs_5_) | copy-start | bytes 2752516
  41.3 6.1 %collective-permute-start.5 = (bf16[256,256]{1,0:T(8,128)(2,1)S(1)}, bf16[256,256]{1,0:T(8,128)(2,1)S(1)}, u32[]{:S(2)}, u32[]{:S(2)}) collective-permute-start(bf16[256,256]{1,0:T(8,128)(2,1)S(1)} %collective-permute-done.3), channel_id=1, source_target_pairs={{0,8},{16,24},{1,9},{17,25},{2,10},{18,26},{3,11},{19,27},{4,12},{... | collective-permute-start | bytes 393224 | tf_op jit(solution)/shard_map/ppermute | solution.py:32
  49.4 13.4 %collective-permute-start.8 = (bf16[896,512]{1,0:T(8,128)(2,1)S(1)}, bf16[896,512]{1,0:T(8,128)(2,1)}, u32[]{:S(2)}, u32[]{:S(2)}) collective-permute-start(bf16[896,512]{1,0:T(8,128)(2,1)S(1)} %broadcast_select_fusion), channel_id=1, source_target_pairs={{0,32},{16,112},{1,33},{17,113},{2,34},{18,114},{3,35},{19,115},{4... | collective-permute-start | bytes 2752520 | tf_op jit(solution)/shard_map/ppermute | solution.py:44
  50.3 31.9 %collective-permute-start.10 = (bf16[4,256,896]{2,1,0:T(8,128)(2,1)}, bf16[4,256,896]{2,1,0:T(8,128)(2,1)}, u32[]{:S(2)}, u32[]{:S(2)}) collective-permute-start(bf16[4,256,896]{2,1,0:T(8,128)(2,1)} %get-tuple-element.19), channel_id=1, source_target_pairs={{0,128},{16,152},{1,129},{17,153},{2,130},{18,154},{3,131},{19,155... | collective-permute-start | bytes 5505032 | tf_op jit(solution)/shard_map/ppermute | solution.py:44
  52.4 25.8 %collective-permute-start.11 = (bf16[2,256,896]{2,1,0:T(8,128)(2,1)}, bf16[2,256,896]{2,1,0:T(8,128)(2,1)}, u32[]{:S(2)}, u32[]{:S(2)}) collective-permute-start(bf16[2,256,896]{2,1,0:T(8,128)(2,1)} %collective-permute-done.refs_1_), channel_id=1, source_target_pairs={{0,1},{16,23},{1,2},{17,16},{2,3},{18,17},{3,4},{19,18},{4,5},{20,... | collective-permute-start | bytes 2752520 | tf_op jit(solution)/shard_map/ppermute | solution.py:44
  57.5 20.7 %collective-permute-start.6 = (bf16[896,512]{1,0:T(8,128)(2,1)S(1)}, bf16[896,512]{1,0:T(8,128)(2,1)}, u32[]{:S(2)}, u32[]{:S(2)}) collective-permute-start(bf16[896,512]{1,0:T(8,128)(2,1)S(1)} %collective-permute-done.1.refs_4_.refs_5_), channel_id=1, source_target_pairs={{0,16},{16,0},{1,17},{17,1},{2,18},{18,2},{3,19},{19,3},{4,20},{20... | collective-permute-start | bytes 2752520 | tf_op jit(solution)/shard_map/ppermute | solution.py:32
  57.5 24.7 %collective-permute-start.7 = (bf16[896,512]{1,0:T(8,128)(2,1)}, bf16[896,512]{1,0:T(8,128)(2,1)}, u32[]{:S(2)}, u32[]{:S(2)}) collective-permute-start(bf16[896,512]{1,0:T(8,128)(2,1)} %collective-permute-done.2.refs_6_.refs_2_), channel_id=1, source_target_pairs={{0,16},{16,0},{1,17},{17,1},{2,18},{18,2},{3,19},{19,3},{4,20},{20... | collective-permute-start | bytes 2752520 | tf_op jit(solution)/shard_map/ppermute | solution.py:32
  62.8 19.4 %collective-permute-start.9 = (bf16[896,512]{1,0:T(8,128)(2,1)}, bf16[896,512]{1,0:T(8,128)(2,1)}, u32[]{:S(2)}, u32[]{:S(2)}) collective-permute-start(bf16[896,512]{1,0:T(8,128)(2,1)} %collective-permute-done.8.refs_8_.refs_4_), channel_id=1, source_target_pairs={{0,16},{16,0},{1,17},{17,1},{2,18},{18,2},{3,19},{19,3},{4,20},{20... | collective-permute-start | bytes 2752520 | tf_op jit(solution)/shard_map/ppermute | solution.py:32
  88.4 9.8 %collective-permute-start.12 = (f16[256,512]{1,0:T(8,128)(2,1)S(1)}, f16[256,512]{1,0:T(8,128)(2,1)S(1)}, u32[]{:S(2)}, u32[]{:S(2)}) collective-permute-start(f16[256,512]{1,0:T(8,128)(2,1)S(1)} %multiply_convert_fusion), channel_id=1, source_target_pairs={{0,128},{16,144},{1,129},{17,145},{2,130},{18,146},{3,131},{19,147... | collective-permute-start | bytes 786440 | tf_op jit(solution)/shard_map/ppermute | solution.py:55
  99.3 20.2 %copy-start.2 = (bf16[256,512]{1,0:T(8,128)(2,1)}, bf16[256,512]{1,0:T(8,128)(2,1)S(1)}, u32[]{:S(2)}) copy-start(bf16[256,512]{1,0:T(8,128)(2,1)S(1)} %add_convert_fusion.refs_0_) | copy-start | bytes 786436
  99.3 5.6 %collective-permute-start.15 = (bf16[256,512]{1,0:T(8,128)(2,1)S(1)}, bf16[256,512]{1,0:T(8,128)(2,1)S(1)}, u32[]{:S(2)}, u32[]{:S(2)}) collective-permute-start(bf16[256,512]{1,0:T(8,128)(2,1)S(1)} %add_convert_fusion.refs_0_), channel_id=1, source_target_pairs={{0,128},{16,144},{1,129},{17,145},{2,130},{18,146},{3,131},{19,147... | collective-permute-start | bytes 786440 | tf_op jit(solution)/shard_map/ppermute | solution.py:55
  99.4 8.2 %collective-permute-start.16 = (bf16[256,512]{1,0:T(8,128)(2,1)S(1)}, bf16[256,512]{1,0:T(8,128)(2,1)S(1)}, u32[]{:S(2)}, u32[]{:S(2)}) collective-permute-start(bf16[256,512]{1,0:T(8,128)(2,1)S(1)} %add_convert_fusion.refs_0_), channel_id=1, source_target_pairs={{0,64},{16,80},{1,65},{17,81},{2,66},{18,82},{3,67},{19,83},{4,68}... | collective-permute-start | bytes 786440 | tf_op jit(solution)/shard_map/ppermute | solution.py:32
  99.7 13.0 %collective-permute-start.13 = (bf16[256,512]{1,0:T(8,128)(2,1)S(1)}, bf16[256,512]{1,0:T(8,128)(2,1)S(1)}, u32[]{:S(2)}, u32[]{:S(2)}) collective-permute-start(bf16[256,512]{1,0:T(8,128)(2,1)S(1)} %add_convert_fusion.refs_0_), channel_id=1, source_target_pairs={{0,32},{16,48},{1,33},{17,49},{2,34},{18,50},{3,35},{19,51},{4,36}... | collective-permute-start | bytes 786440 | tf_op jit(solution)/shard_map/ppermute | solution.py:32
  101.9 11.9 %collective-permute-start.14 = (bf16[256,512]{1,0:T(8,128)(2,1)S(1)}, bf16[256,512]{1,0:T(8,128)(2,1)S(1)}, u32[]{:S(2)}, u32[]{:S(2)}) collective-permute-start(bf16[256,512]{1,0:T(8,128)(2,1)S(1)} %add_convert_fusion.refs_0_), channel_id=1, source_target_pairs={{0,96},{16,112},{1,97},{17,113},{2,98},{18,114},{3,99},{19,115},{4... | collective-permute-start | bytes 786440 | tf_op jit(solution)/shard_map/ppermute | solution.py:32
  104.9 14.6 %copy-start.3 = (bf16[256,512]{1,0:T(8,128)(2,1)}, bf16[256,512]{1,0:T(8,128)(2,1)S(1)}, u32[]{:S(2)}) copy-start(bf16[256,512]{1,0:T(8,128)(2,1)S(1)} %collective-permute-done.15.refs_3_) | copy-start | bytes 786436
  104.9 13.5 %collective-permute-start.17 = (bf16[256,512]{1,0:T(8,128)(2,1)S(1)}, bf16[256,512]{1,0:T(8,128)(2,1)}, u32[]{:S(2)}, u32[]{:S(2)}) collective-permute-start(bf16[256,512]{1,0:T(8,128)(2,1)S(1)} %collective-permute-done.15.refs_3_), channel_id=1, source_target_pairs={{0,32},{16,48},{1,33},{17,49},{2,34},{18,50},{3,35},{19,51},{4,36}... | collective-permute-start | bytes 786440 | tf_op jit(solution)/shard_map/ppermute | solution.py:32
  104.9 14.5 %collective-permute-start.18 = (bf16[256,512]{1,0:T(8,128)(2,1)S(1)}, bf16[256,512]{1,0:T(8,128)(2,1)}, u32[]{:S(2)}, u32[]{:S(2)}) collective-permute-start(bf16[256,512]{1,0:T(8,128)(2,1)S(1)} %collective-permute-done.15.refs_3_), channel_id=1, source_target_pairs={{0,96},{16,112},{1,97},{17,113},{2,98},{18,114},{3,99},{19,115},{4... | collective-permute-start | bytes 786440 | tf_op jit(solution)/shard_map/ppermute | solution.py:32
  107.6 11.9 %copy-start.4 = (bf16[256,512]{1,0:T(8,128)(2,1)}, bf16[256,512]{1,0:T(8,128)(2,1)S(1)}, u32[]{:S(2)}) copy-start(bf16[256,512]{1,0:T(8,128)(2,1)S(1)} %collective-permute-done.16.refs_4_) | copy-start | bytes 786436
  107.6 11.9 %collective-permute-start.19 = (bf16[256,512]{1,0:T(8,128)(2,1)S(1)}, bf16[256,512]{1,0:T(8,128)(2,1)}, u32[]{:S(2)}, u32[]{:S(2)}) collective-permute-start(bf16[256,512]{1,0:T(8,128)(2,1)S(1)} %collective-permute-done.16.refs_4_), channel_id=1, source_target_pairs={{0,128},{16,144},{1,129},{17,145},{2,130},{18,146},{3,131},{19,147... | collective-permute-start | bytes 786440 | tf_op jit(solution)/shard_map/ppermute | solution.py:55
  112.7 6.8 %copy-start.5 = (bf16[256,512]{1,0:T(8,128)(2,1)}, bf16[256,512]{1,0:T(8,128)(2,1)S(1)}, u32[]{:S(2)}) copy-start(bf16[256,512]{1,0:T(8,128)(2,1)S(1)} %collective-permute-done.13.refs_1_) | copy-start | bytes 786436
  113.8 5.7 %copy-start.6 = (bf16[256,512]{1,0:T(8,128)(2,1)}, bf16[256,512]{1,0:T(8,128)(2,1)S(1)}, u32[]{:S(2)}) copy-start(bf16[256,512]{1,0:T(8,128)(2,1)S(1)} %collective-permute-done.14.refs_2_) | copy-start | bytes 786436
  127.0 2.7 %collective-permute-start.20 = (f32[256,512]{1,0:T(8,128)S(1)}, f32[256,512]{1,0:T(8,128)S(1)}, u32[]{:S(2)}, u32[]{:S(2)}) collective-permute-start(f32[256,512]{1,0:T(8,128)S(1)} %slice.11), channel_id=1, source_target_pairs={{0,16},{16,0},{1,17},{17,1},{2,18},{18,2},{3,19},{19,3},{4,20},{20... | collective-permute-start | bytes 1572872 | tf_op jit(solution)/shard_map/ppermute | solution.py:32
Sparse Core Ops, SparseCore 0:
  48.3 41.8 all-gather.2

commit v4 on v3

--- a/solution.py
+++ b/solution.py
@@ -12,6 +12,8 @@
 SPLIT = 2
 FACTOR = 32.0
 VMEM = 60 * 1024 * 1024
+FOLLOWED = 6 * 10**9
+TAIL_VMEM = 16 * 1024 * 1024
 BLOCKS = ((0, 0), (0, 1), (3, 0), (3, 1), (1, 0), (1, 1), (2, 0), (2, 1))
 ORDER = ((0, 0), (0, 3), (0, 1), (1, 0), (0, 2), (1, 3), (1, 1), (1, 2))
 
@@ -63,17 +65,15 @@
     return pl.BlockSpec(memory_space=kind)
 
 
-def pieces_kernel(columns_ref, source, near, rest, held, arrived, left):
+def pieces_kernel(columns_ref, source, out, held, arrived, left):
     moves = []
     for k in range(held.shape[0]):
         column = pl.multiple_of(columns_ref[k], 128)
-        out = near.at[k] if k < SPLIT else rest.at[k - SPLIT]
+        get = source.at[:, pl.ds(column, held.shape[2])]
         moves.append(
             (
-                pltpu.make_async_copy(
-                    source.at[:, pl.ds(column, held.shape[2])], held.at[k], arrived.at[k]
-                ),
-                pltpu.make_async_copy(held.at[k], out, left.at[k]),
+                pltpu.make_async_copy(get, held.at[k], arrived.at[k]),
+                pltpu.make_async_copy(held.at[k], out.at[k], left.at[k]),
             )
         )
     for get, put in moves:
@@ -86,22 +86,20 @@
 
 
 def pieces(columns, activations, depth):
-    tokens, count = activations.shape[0], len(BLOCKS) - SPLIT
+    tokens, count = activations.shape[0], columns.shape[0]
+    shape = (count, tokens, depth)
     return pl.pallas_call(
         pieces_kernel,
-        out_shape=[
-            jax.ShapeDtypeStruct((n, tokens, depth), activations.dtype)
-            for n in (SPLIT, count - SPLIT)
-        ],
+        out_shape=jax.ShapeDtypeStruct(shape, activations.dtype),
         in_specs=[space(pltpu.SMEM), space(pltpu.HBM)],
-        out_specs=[space(pltpu.HBM)] * 2,
+        out_specs=space(pltpu.HBM),
         scratch_shapes=[
-            pltpu.VMEM((count, tokens, depth), activations.dtype),
+            pltpu.VMEM(shape, activations.dtype),
             pltpu.SemaphoreType.DMA((count,)),
             pltpu.SemaphoreType.DMA((count,)),
         ],
         compiler_params=pltpu.CompilerParams(vmem_limit_bytes=VMEM),
-        cost_estimate=pl.CostEstimate(flops=0, bytes_accessed=2**23, transcendentals=0),
+        cost_estimate=pl.CostEstimate(flops=0, bytes_accessed=2**22, transcendentals=0),
     )(columns, activations)
 
 
@@ -135,7 +133,7 @@
             out[...] = before[0][...] + term if before else term
 
 
-def product(moves, count, table, sources, panels, before=None):
+def product(moves, count, table, sources, panels, before=None, followed_by=0):
     tokens, blocks = EXAMPLES * TOK, len(panels)
     depth, width = panels[0][0].shape[0] if len(panels[0]) == 1 else sum(
         part.shape[0] for part in panels[0]
@@ -157,20 +155,24 @@
         ],
         compiler_params=pltpu.CompilerParams(vmem_limit_bytes=VMEM),
         cost_estimate=pl.CostEstimate(
-            flops=2 * tokens * width * blocks * depth, bytes_accessed=2**22, transcendentals=0
+            flops=2 * tokens * width * blocks * depth + followed_by,
+            bytes_accessed=2**22,
+            transcendentals=0,
         ),
     )(table, *sources, *parts, *extra)
 
 
 def near_moves(table, sources, rows):
+    near, away, rest = sources
     return [
-        (source, rows.at[pl.ds(start * SPLIT, SPLIT)])
-        for start, source in zip((table[0], 1 - table[0]), sources)
+        (near, rows.at[pl.ds(table[0] * SPLIT, SPLIT)]),
+        (away, rows.at[pl.ds((1 - table[0]) * SPLIT, SPLIT)]),
+        (rest.at[pl.ds(0, 2)], rows.at[pl.ds(2 * SPLIT, 2)]),
     ]
 
 
-def rest_moves(table, sources, rows):
-    return [(sources[0], rows)]
+def last_moves(table, sources, rows):
+    return [(sources[0].at[pl.ds(2, 2)], rows)]
 
 
 def own_moves(table, sources, rows):
@@ -181,58 +183,54 @@
 
 
 def squares_kernel(where_ref, out_rows, *refs):
-    blocks = (len(refs) - 4)
-    in_rows, (total_ref, outer, inner, semaphore) = refs[:-4], refs[-4:]
-    copies = [
-        (
-            pltpu.make_async_copy(out_rows.at[where_ref[k]], outer.at[k], semaphore.at[2 * k]),
-            pltpu.make_async_copy(in_rows[k], inner.at[k], semaphore.at[2 * k + 1]),
+    blocks = out_rows.shape[0]
+    in_rows, refs = refs[:blocks], refs[blocks:]
+    totals, (outer, inner, semaphore) = refs[:2], refs[2:]
+    copies = [pltpu.make_async_copy(out_rows, outer, semaphore.at[blocks])]
+    for k in range(blocks):
+        copies.append(
+            pltpu.make_async_copy(in_rows[k], inner.at[where_ref[k]], semaphore.at[k])
         )
-        for k in range(blocks)
-    ]
-    for pair in copies:
-        pair[0].start()
-        pair[1].start()
-    for pair in copies:
-        pair[0].wait()
-        pair[1].wait()
-    half = total_ref.shape[0] // 2
-
-    @pl.loop(0, total_ref.shape[1] // TILE)
+    for copy in copies:
+        copy.start()
+    for copy in copies:
+        copy.wait()
+
+    @pl.loop(0, inner.shape[2] // TILE)
     def _(n):
         columns = pl.ds(pl.multiple_of(n * TILE, TILE), TILE)
-        for part in range(2):
-            rows = pl.ds(part * half, half)
+        for part, total_ref in enumerate(totals):
+            half = where_ref[blocks + part]
             total = None
             for k in range(blocks):
                 for example in range(EXAMPLES):
                     tokens = pl.ds(example * TOK, TOK)
-                    rotated = dot(outer[k, rows, tokens], inner[k, tokens, columns])
+                    rotated = dot(outer[k, half, :, tokens], inner[k, tokens, columns])
                     squared = rotated * rotated
                     total = squared if total is None else total + squared
-            total_ref[rows, columns] = total
+            total_ref[:, columns] = total
 
 
 TILE = 256
 
 
 def sums_of_squares(where, out_rows, in_rows):
-    rows, tokens = out_rows.shape[1:]
+    rows, tokens = out_rows.shape[2:]
     width, blocks = in_rows[0].shape[1], len(in_rows)
     return pl.pallas_call(
         squares_kernel,
-        out_shape=jax.ShapeDtypeStruct((rows, width), jnp.float32),
+        out_shape=[jax.ShapeDtypeStruct((rows, width), jnp.float32)] * 2,
         in_specs=[space(pltpu.SMEM)] + [space(pl.ANY)] * (1 + blocks),
-        out_specs=space(pltpu.VMEM),
+        out_specs=[space(pltpu.VMEM)] * 2,
         scratch_shapes=[
-            pltpu.VMEM((blocks, rows, tokens), jnp.bfloat16),
+            pltpu.VMEM(out_rows.shape, jnp.bfloat16),
             pltpu.VMEM((blocks, tokens, width), jnp.bfloat16),
-            pltpu.SemaphoreType.DMA((2 * blocks,)),
+            pltpu.SemaphoreType.DMA((blocks + 1,)),
         ],
-        compiler_params=pltpu.CompilerParams(vmem_limit_bytes=VMEM),
+        compiler_params=pltpu.CompilerParams(vmem_limit_bytes=TAIL_VMEM),
         cost_estimate=pl.CostEstimate(
-            flops=2 * rows * width * blocks * tokens,
-            bytes_accessed=out_rows.size * 2 + rows * width * 4,
+            flops=4 * rows * width * blocks * tokens,
+            bytes_accessed=out_rows.size * 2 + rows * width * 8,
             transcendentals=0,
         ),
     )(where, out_rows, *in_rows)
@@ -259,40 +257,37 @@
     spots = [((y + dy) % NY) * NC + (core + dc) % NC for dy, dc in BLOCKS]
     half = len(BLOCKS)
 
-    table = jnp.stack(spots)
-    give = jnp.concatenate(
-        [lax.dynamic_slice_in_dim(table, parity * SPLIT, SPLIT), table[2 * SPLIT :]]
-    )
-    give = ((half * (1 - x) + give) * depth).astype(jnp.int32)
+    table = jnp.stack(spots).astype(jnp.int32)
+    give = (half * (1 - x) + table) * depth
     keep = ((half * x + table) * depth).astype(jnp.int32)
-    near, rest = pieces(give, activations, depth)
+    near = lax.dynamic_slice_in_dim(give, parity * SPLIT, SPLIT)
+    near = by_core(pieces(near.astype(jnp.int32), activations, depth), dx=1)
     left, right = shift(basis_in, dy=1), shift(basis_in, dy=3)
-    near, own_other = by_core(near, dx=1), shift(basis_in, dc=1)
+    own_other = shift(basis_in, dc=1)
     block = transposed(dot(out_grads, basis_out).astype(jnp.bfloat16).T)
 
-    near, left, right, rest, block, own_other = lax.optimization_barrier(
-        (near, left, right, rest, block, own_other)
-    )
+    rest = pieces(give[2 * SPLIT :].astype(jnp.int32), activations, depth)
+    near, rest, block = lax.optimization_barrier((near, rest, block))
+    rest, away = by_core(rest, dx=1), by_core(near, dz=1)
     far = by_core(jnp.where(core == 0, left, right), dy=1)
-    rest, away = by_core(rest, dx=1), by_core(near, dz=1)
     left_other, right_other = shift(left, dc=1), shift(right, dc=1)
 
-    other = shift(block, dx=NX)
-    mine = (b // NZ) == core
-    block = jnp.concatenate([jnp.where(mine, block, other), jnp.where(mine, other, block)], 0)
     out_rows = lax.all_gather(
-        block,
+        jnp.stack([block, shift(block, dx=NX)]),
         "blk",
         axis=0,
         axis_index_groups=[[h * NZ + z for z in range(NZ)] for h in range(NH)],
     )
-    where = jnp.stack([((x + dx) % NX) * NY + (y + dy) % NY for dx, dy in ORDER]).astype(jnp.int32)
+    flip = (b // NZ + core) % 2
+    where = jnp.stack(
+        [((x + dx) % NX) * NY + (y + dy) % NY for dx, dy in ORDER] + [flip, 1 - flip]
+    ).astype(jnp.int32)
 
     panels = [basis_in, own_other, left, left_other, right, right_other, far, shift(far, dc=1)]
     panels = [[panel] for panel in panels]
     parity = parity.reshape(1).astype(jnp.int32)
-    partial = product(near_moves, 2, parity, (near, away), panels[: 2 * SPLIT])
-    partial = product(rest_moves, 1, parity, (rest,), panels[2 * SPLIT :], partial)
+    partial = product(near_moves, 3, parity, (near, away, rest), panels[:-2])
+    partial = product(last_moves, 1, parity, (rest,), panels[-2:], partial, FOLLOWED)
     arrived = swap((partial * FACTOR).astype(jnp.float16))
     total = product(own_moves, len(BLOCKS), keep, (activations,), panels)
     proj_in = (total + arrived.astype(jnp.float32) * (1.0 / FACTOR)).astype(jnp.bfloat16)
@@ -301,13 +296,12 @@
     p_across = swap(proj_in)
     px_left, px_right = shift(p_across, dy=1), shift(p_across, dy=3)
     px_far = swap(p_far)
-    sums = sums_of_squares(
+    kept, given = sums_of_squares(
         where,
         out_rows,
         (proj_in, p_left, p_right, p_across, p_far, px_left, px_right, px_far),
     )
-    rows = sums.shape[0] // 2
-    return (sums[:rows] + shift(sums[rows:], dc=1)) * jnp.float32(scale)
+    return (kept + shift(given, dc=1)) * jnp.float32(scale)
 
 
 def solution(mesh):

time: 139 us -> 142 us (1.022); the launches traced: 139 us -> 139 us
  waiting for transfers between devices: 60 us -> 24.8 us
  starting transfers between devices: 28 us -> 61.1 us
  local copies, waits for them, and re-layouts: 2.02 us -> 4.89 us
    ppermute x4, waiting for transfers between devices: 22.9 us -> 0.67 us  [by_core(): return lax.ppermute(value, ('dp', 'blk'), pairs)]
    ppermute x13, starting transfers between devices: 12.4 us -> 27 us  [shift(): return lax.ppermute(value, ('dp', 'blk'), pairs)]
    ppermute x13, waiting for transfers between devices: 34.5 us -> 20.5 us  [shift(): return lax.ppermute(value, ('dp', 'blk'), pairs)]
    ppermute x4, starting transfers between devices: 11.4 us -> 22.2 us  [by_core(): return lax.ppermute(value, ('dp', 'blk'), pairs)]
    ppermute x3, starting transfers between devices: 3.57 us -> 11.1 us  [swap(): return lax.ppermute(value, ('dp', 'blk'), pairs)]
    unnamed x14 -> x12, local copies, waits for them, and re-layouts: 0.03 us -> 3.55 us
    mul x2 -> x1, other arithmetic: 2.45 us -> 0.9 us  [on_device(): return (kept + shift(given, dc=1)) * jnp.float32(scale)]
    pallas_call x2 -> x3, Pallas kernels: 9.75 us -> 10.2 us  [the longest x2 5.74 us: pieces(): pl.pallas_call(pieces_kernel, out_shape=jax.ShapeDtypeStruct(shape, activ...]
  transfers between devices with their start and end apart: 22 -> 22, of which waited for: 11 -> 8; matrix products, arithmetic and copies ran while one was open for 5% -> 6% of each run, Pallas kernels for 11% -> 13%
where the time goes in v4:
time: 142 us; the launch traced here: 139 us
  starting transfers between devices  61.1 us (43%)
  Pallas kernels  25.9 us (18%)
  waiting for transfers between devices  24.8 us (17%)
  between operations  13.5 us (10%)
  other arithmetic  6.96 us (5%)
  local copies, waits for them, and re-layouts  4.89 us (3%)
  matrix products  2.34 us (2%)
    ppermute x13, starting transfers between devices, shift(): return lax.ppermute(value, ('dp', 'blk'), pairs)  27 us
    ppermute x4, starting transfers between devices, by_core(): return lax.ppermute(value, ('dp', 'blk'), pairs)  22.2 us
    ppermute x13, waiting for transfers between devices, shift(): return lax.ppermute(value, ('dp', 'blk'), pairs)  20.5 us
    pallas_call x3, Pallas kernels, product(): pl.pallas_call(lambda *refs: product_kernel(moves, layout, *refs), out_sh...  15.7 us
    ppermute x3, starting transfers between devices, swap(): return lax.ppermute(value, ('dp', 'blk'), pairs)  11.1 us
    pallas_call x2, Pallas kernels, pieces(): pl.pallas_call(pieces_kernel, out_shape=jax.ShapeDtypeStruct(shape, activ...  5.74 us
    pallas_call x1, Pallas kernels, sums_of_squares(): pl.pallas_call(squares_kernel, out_shape=[jax.ShapeDtypeStruct((rows, wid...  4.45 us
    ppermute x3, waiting for transfers between devices, swap(): return lax.ppermute(value, ('dp', 'blk'), pairs)  3.62 us
  transfers between devices with their start and end apart: 22, of which 8 were waited for; matrix products, arithmetic and copies ran while one was open for 6% of the time, Pallas kernels for 13%

profile of v4, /device:TPU:1, one launch (start us, length us, event | category | flops | bytes accessed | tf_op | source)
XLA Modules:
  0.0 139.4 jit_solution(4942346014594289278)
XLA Ops:
  7.8 2.7 %shard_map.46 = bf16[2,256,896]{2,1,0:T(8,128)(2,1)} custom-call(s32[2]{0:T(128)} %dynamic_slice.3.columns_ref, bf16[256,14336]{1,0:T(8,128)(2,1)} %refs_1_.1), custom_call_target="tpu_custom_call" | custom-call | bytes 4194304 | tf_op jit(solution)/shard_map/pallas_call | solution.py:91
  10.5 3.4 %collective-permute-start = (bf16[2,256,896]{2,1,0:T(8,128)(2,1)}, bf16[2,256,896]{2,1,0:T(8,128)(2,1)}, u32[]{:S(2)}, u32[]{:S(2)}) collective-permute-start(bf16[2,256,896]{2,1,0:T(8,128)(2,1)} %shard_map.46), channel_id=1, source_target_pairs={{0,128},{16,152},{1,129},{17,153},{2,130},{18,154},{3,131},{19,155... | collective-permute-start | bytes 2752520 | tf_op jit(solution)/shard_map/ppermute | solution.py:46
  13.9 1.3 collective-permute-start.4
  15.2 1.4 %collective-permute-start.6 = (bf16[896,512]{1,0:T(8,128)(2,1)}, bf16[896,512]{1,0:T(8,128)(2,1)}, u32[]{:S(2)}, u32[]{:S(2)}) collective-permute-start(bf16[896,512]{1,0:T(8,128)(2,1)} %refs_4_.1), channel_id=1, source_target_pairs={{0,96},{16,112},{1,97},{17,113},{2,98},{18,114},{3,99},{19,115},{4... | collective-permute-start | bytes 2752520 | tf_op jit(solution)/shard_map/ppermute | solution.py:34
  16.7 2.3 %convolution_convert_fusion = bf16[256,256]{1,0:T(8,128)(2,1)S(1)} fusion(bf16[4096,256]{1,0:T(8,128)(2,1)S(1)} %copy-done, bf16[256,4096]{1,0:T(8,128)(2,1)} %param.5), kind=kOutput, calls=%fused_computation | convolution fusion | flops 536936448 | bytes 4325376 | tf_op jit(solution)/shard_map/dot_general | solution.py:61
  20.9 3.0 %shard_map.47 = bf16[4,256,896]{2,1,0:T(8,128)(2,1)} custom-call(s32[4]{0:T(128)} %slice.3.columns_ref, bf16[256,14336]{1,0:T(8,128)(2,1)} %refs_1_.1), custom_call_target="tpu_custom_call" | custom-call | bytes 4194304 | tf_op jit(solution)/shard_map/pallas_call | solution.py:91
  24.6 10.8 %collective-permute-start.10 = (bf16[4,256,896]{2,1,0:T(8,128)(2,1)}, bf16[4,256,896]{2,1,0:T(8,128)(2,1)}, u32[]{:S(2)}, u32[]{:S(2)}) collective-permute-start(bf16[4,256,896]{2,1,0:T(8,128)(2,1)} %shard_map.47), channel_id=1, source_target_pairs={{0,128},{16,152},{1,129},{17,153},{2,130},{18,154},{3,131},{19,155... | collective-permute-start | bytes 5505032 | tf_op jit(solution)/shard_map/ppermute | solution.py:46
  35.4 1.2 collective-permute-start.2
  36.6 4.6 %collective-permute-done.4.refs_4_.refs_6_ = bf16[896,512]{1,0:T(8,128)(2,1)S(1)} collective-permute-done((bf16[896,512]{1,0:T(8,128)(2,1)}, bf16[896,512]{1,0:T(8,128)(2,1)S(1)}, u32[]{:S(2)}, u32[]{:S(2)}) %collective-permute-start.4) | collective-permute-done | bytes 917536 | tf_op jit(solution)/shard_map/ppermute | solution.py:34
  41.2 2.5 %broadcast_select_fusion = bf16[896,512]{1,0:T(8,128)(2,1)} fusion(bf16[896,512]{1,0:T(8,128)(2,1)S(1)} %collective-permute-done.4.refs_4_.refs_6_, bf16[896,512]{1,0:T(8,128)(2,1)} %collective-permute-done.6.refs_6_.refs_8_, pred[]{:T(512)S(6)} %eq.40), kind=kLoop, calls=%fused_computation.1 | loop fusion | flops 458752 | bytes 2752513 | tf_op jit(solution)/shard_map/jit(_where)/select_n | solution.py:272
  43.7 2.4 %collective-permute-start.8 = (bf16[896,512]{1,0:T(8,128)(2,1)}, bf16[896,512]{1,0:T(8,128)(2,1)}, u32[]{:S(2)}, u32[]{:S(2)}) collective-permute-start(bf16[896,512]{1,0:T(8,128)(2,1)} %broadcast_select_fusion), channel_id=1, source_target_pairs={{0,32},{16,112},{1,33},{17,113},{2,34},{18,114},{3,35},{19,115},{4... | collective-permute-start | bytes 2752520 | tf_op jit(solution)/shard_map/ppermute | solution.py:46
  46.9 5.6 %collective-permute-start.11 = (bf16[2,256,896]{2,1,0:T(8,128)(2,1)}, bf16[2,256,896]{2,1,0:T(8,128)(2,1)S(1)}, u32[]{:S(2)}, u32[]{:S(2)}) collective-permute-start(bf16[2,256,896]{2,1,0:T(8,128)(2,1)} %collective-permute-done.refs_1_), channel_id=1, source_target_pairs={{0,1},{16,23},{1,2},{17,16},{2,3},{18,17},{3,4},{19,18},{4,5},{20,... | collective-permute-start | bytes 2752520 | tf_op jit(solution)/shard_map/ppermute | solution.py:46
  52.5 15.4 %collective-permute-start.5 = (bf16[896,512]{1,0:T(8,128)(2,1)S(1)}, bf16[896,512]{1,0:T(8,128)(2,1)S(1)}, u32[]{:S(2)}, u32[]{:S(2)}) collective-permute-start(bf16[896,512]{1,0:T(8,128)(2,1)S(1)} %collective-permute-done.4.refs_4_.refs_6_), channel_id=1, source_target_pairs={{0,16},{16,0},{1,17},{17,1},{2,18},{18,2},{3,19},{19,3},{4,20},{20... | collective-permute-start | bytes 2752520 | tf_op jit(solution)/shard_map/ppermute | solution.py:34
  68.4 2.8 %collective-permute-done.5.refs_5_.refs_7_ = bf16[896,512]{1,0:T(8,128)(2,1)S(1)} collective-permute-done((bf16[896,512]{1,0:T(8,128)(2,1)S(1)}, bf16[896,512]{1,0:T(8,128)(2,1)S(1)}, u32[]{:S(2)}, u32[]{:S(2)}) %collective-permute-start.5) | collective-permute-done | bytes 917536 | tf_op jit(solution)/shard_map/ppermute | solution.py:34
  71.2 1.0 copy-done.3
  72.7 1.0 copy-done.4
  73.7 4.9 %shard_map.49.refs_4_ = f32[256,512]{1,0:T(8,128)} custom-call(s32[1]{0:T(128)} %bitcast.21.refs_0_, bf16[2,256,896]{2,1,0:T(8,128)(2,1)} %collective-permute-done.refs_1_, bf16[2,256,896]{2,1,0:T(8,128)(2,1)} %copy-done.5, bf16[4,256,896]{2,1,0:T(8,128)(2,1)} %collective-permute-done.10.refs_3_.refs_1_, bf16[896,512]{1,0:T(8,128)(2,1)} %refs_4_.1, ...), custom_call_target="tpu_custom_call" | custom-call | flops 1409286144 | bytes 4194304 | tf_op jit(solution)/shard_map/pallas_call | solution.py:144
  78.6 4.1 %shard_map.50 = f32[256,512]{1,0:T(8,128)} custom-call(s32[1]{0:T(128)} %bitcast.21.refs_0_, bf16[4,256,896]{2,1,0:T(8,128)(2,1)} %collective-permute-done.10.refs_3_.refs_1_, bf16[896,512]{1,0:T(8,128)(2,1)} %collective-permute-done.8.refs_8_.refs_2_, bf16[896,512]{1,0:T(8,128)(2,1)} %collective-permute-done.9.refs_9_.refs_3_, f32[256,512]{1,0:T(8,128)} %shard_map.49.refs_4_), custom_call_target="tpu_custom_call" | custom-call | flops 6469762048 | bytes 4194304 | tf_op jit(solution)/shard_map/pallas_call | solution.py:144
  82.7 1.1 multiply_convert_fusion
  83.8 10.8 %collective-permute-start.12 = (f16[256,512]{1,0:T(8,128)(2,1)S(1)}, f16[256,512]{1,0:T(8,128)(2,1)S(1)}, u32[]{:S(2)}, u32[]{:S(2)}) collective-permute-start(f16[256,512]{1,0:T(8,128)(2,1)S(1)} %multiply_convert_fusion), channel_id=1, source_target_pairs={{0,128},{16,144},{1,129},{17,145},{2,130},{18,146},{3,131},{19,147... | collective-permute-start | bytes 786440 | tf_op jit(solution)/shard_map/ppermute | solution.py:57
  94.6 6.6 %shard_map.48 = f32[256,512]{1,0:T(8,128)} custom-call(s32[8]{0:T(128)} %get-tuple-element.15.refs_0_, bf16[256,14336]{1,0:T(8,128)(2,1)} %refs_1_.1, bf16[896,512]{1,0:T(8,128)(2,1)} %refs_4_.1, bf16[896,512]{1,0:T(8,128)(2,1)} %collective-permute-done.3.refs_3_.refs_5_, bf16[896,512]{1,0:T(8,128)(2,1)} %copy-done.2, bf16[896,512]{1,0:T(8,128)(2,1)} %copy-done.3, ...), custom_call_target="tpu_custom_call" | custom-call | flops 1879048192 | bytes 4194304 | tf_op jit(solution)/shard_map/pallas_call | solution.py:144
  101.3 1.1 add_convert_fusion.refs_0_
  102.7 2.7 %collective-permute-start.14 = (bf16[256,512]{1,0:T(8,128)(2,1)S(1)}, bf16[256,512]{1,0:T(8,128)(2,1)S(1)}, u32[]{:S(2)}, u32[]{:S(2)}) collective-permute-start(bf16[256,512]{1,0:T(8,128)(2,1)S(1)} %add_convert_fusion.refs_0_), channel_id=1, source_target_pairs={{0,96},{16,112},{1,97},{17,113},{2,98},{18,114},{3,99},{19,115},{4... | collective-permute-start | bytes 786440 | tf_op jit(solution)/shard_map/ppermute | solution.py:34
  105.4 3.6 %collective-permute-done.15.refs_3_ = bf16[256,512]{1,0:T(8,128)(2,1)S(1)} collective-permute-done((bf16[256,512]{1,0:T(8,128)(2,1)S(1)}, bf16[256,512]{1,0:T(8,128)(2,1)S(1)}, u32[]{:S(2)}, u32[]{:S(2)}) %collective-permute-start.15) | collective-permute-done | bytes 262176 | tf_op jit(solution)/shard_map/ppermute | solution.py:57
  109.0 2.7 %collective-permute-start.18 = (bf16[256,512]{1,0:T(8,128)(2,1)S(1)}, bf16[256,512]{1,0:T(8,128)(2,1)}, u32[]{:S(2)}, u32[]{:S(2)}) collective-permute-start(bf16[256,512]{1,0:T(8,128)(2,1)S(1)} %collective-permute-done.15.refs_3_), channel_id=1, source_target_pairs={{0,96},{16,112},{1,97},{17,113},{2,98},{18,114},{3,99},{19,115},{4... | collective-permute-start | bytes 786440 | tf_op jit(solution)/shard_map/ppermute | solution.py:34
  111.8 5.3 %collective-permute-done.13.refs_1_ = bf16[256,512]{1,0:T(8,128)(2,1)S(1)} collective-permute-done((bf16[256,512]{1,0:T(8,128)(2,1)S(1)}, bf16[256,512]{1,0:T(8,128)(2,1)S(1)}, u32[]{:S(2)}, u32[]{:S(2)}) %collective-permute-start.13) | collective-permute-done | bytes 262176 | tf_op jit(solution)/shard_map/ppermute | solution.py:34
  117.1 5.7 %collective-permute-done.17.refs_5_ = bf16[256,512]{1,0:T(8,128)(2,1)} collective-permute-done((bf16[256,512]{1,0:T(8,128)(2,1)S(1)}, bf16[256,512]{1,0:T(8,128)(2,1)}, u32[]{:S(2)}, u32[]{:S(2)}) %collective-permute-start.17) | collective-permute-done | bytes 262176 | tf_op jit(solution)/shard_map/ppermute | solution.py:34
  122.8 1.6 %copy-done.1 = bf16[16,256,256]{2,1,0:T(8,128)(2,1)S(1)} copy-done((bf16[16,256,256]{2,1,0:T(8,128)(2,1)S(1)}, bf16[16,256,256]{2,1,0:T(8,128)(2,1)}, u32[]{:S(2)}) %copy-start.1) | copy-done | bytes 2097176
  124.4 4.5 %shard_map.51 = (f32[256,512]{1,0:T(8,128)S(1)}, f32[256,512]{1,0:T(8,128)S(1)}) custom-call(s32[10]{0:T(128)S(1)} %stack.79.where_ref, bf16[8,2,256,256]{3,2,1,0:T(8,128)(2,1)S(1)} %bitcast.24, bf16[256,512]{1,0:T(8,128)(2,1)S(1)} %add_convert_fusion.refs_0_, bf16[256,512]{1,0:T(8,128)(2,1)S(1)} %collective-permute-done.13.refs_1_, ...), custom_call_target="tpu_custom_call" | custom-call | flops 1073741824 | bytes 3145728 | tf_op jit(solution)/shard_map/pallas_call | solution.py:220
  128.9 1.3 collective-permute-start.20
  130.2 1.5 %collective-permute-done.20 = f32[256,512]{1,0:T(8,128)S(1)} collective-permute-done((f32[256,512]{1,0:T(8,128)S(1)}, f32[256,512]{1,0:T(8,128)S(1)}, u32[]{:S(2)}, u32[]{:S(2)}) %collective-permute-start.20) | collective-permute-done | bytes 524320 | tf_op jit(solution)/shard_map/ppermute | solution.py:34
  131.7 0.9 add_multiply_fusion
  (42 shorter events, 6.0 us)
Async XLA Ops:
  6.5 10.1 %copy-start = (bf16[4096,256]{1,0:T(8,128)(2,1)S(1)}, bf16[4096,256]{1,0:T(8,128)(2,1)}, u32[]{:S(2)}) copy-start(bf16[4096,256]{1,0:T(8,128)(2,1)} %param.7) | copy-start | bytes 6291460
  6.5 116.3 %all-gather.3.cloned.1.call-start = ((), (), s32[]{:S(2)}) async-start(), calls=%async_computation | async-start | bytes 2359296 | tf_op jit(solution)/shard_map/all_gather | solution.py:275
  10.5 14.0 %collective-permute-start = (bf16[2,256,896]{2,1,0:T(8,128)(2,1)}, bf16[2,256,896]{2,1,0:T(8,128)(2,1)}, u32[]{:S(2)}, u32[]{:S(2)}) collective-permute-start(bf16[2,256,896]{2,1,0:T(8,128)(2,1)} %shard_map.46), channel_id=1, source_target_pairs={{0,128},{16,152},{1,129},{17,153},{2,130},{18,154},{3,131},{19,155... | collective-permute-start | bytes 2752520 | tf_op jit(solution)/shard_map/ppermute | solution.py:46
  13.9 27.3 %collective-permute-start.4 = (bf16[896,512]{1,0:T(8,128)(2,1)}, bf16[896,512]{1,0:T(8,128)(2,1)S(1)}, u32[]{:S(2)}, u32[]{:S(2)}) collective-permute-start(bf16[896,512]{1,0:T(8,128)(2,1)} %refs_4_.1), channel_id=1, source_target_pairs={{0,32},{16,48},{1,33},{17,49},{2,34},{18,50},{3,35},{19,51},{4,36}... | collective-permute-start | bytes 2752520 | tf_op jit(solution)/shard_map/ppermute | solution.py:34
  15.2 26.0 %collective-permute-start.6 = (bf16[896,512]{1,0:T(8,128)(2,1)}, bf16[896,512]{1,0:T(8,128)(2,1)}, u32[]{:S(2)}, u32[]{:S(2)}) collective-permute-start(bf16[896,512]{1,0:T(8,128)(2,1)} %refs_4_.1), channel_id=1, source_target_pairs={{0,96},{16,112},{1,97},{17,113},{2,98},{18,114},{3,99},{19,115},{4... | collective-permute-start | bytes 2752520 | tf_op jit(solution)/shard_map/ppermute | solution.py:34
  19.0 4.9 %collective-permute-start.1 = (bf16[256,256]{1,0:T(8,128)(2,1)S(1)}, bf16[256,256]{1,0:T(8,128)(2,1)S(1)}, u32[]{:S(2)}, u32[]{:S(2)}) collective-permute-start(bf16[256,256]{1,0:T(8,128)(2,1)S(1)} %convolution_convert_fusion), channel_id=1, source_target_pairs={{0,0},{1,8},{2,32},{3,40},{4,64},{5,72},{6,96},{7,104},{8,128},{9,... | collective-permute-start | bytes 393224 | tf_op jit(solution)/shard_map/ppermute | solution.py:248
  19.7 48.2 %collective-permute-start.3 = (bf16[896,512]{1,0:T(8,128)(2,1)}, bf16[896,512]{1,0:T(8,128)(2,1)}, u32[]{:S(2)}, u32[]{:S(2)}) collective-permute-start(bf16[896,512]{1,0:T(8,128)(2,1)} %refs_4_.1), channel_id=1, source_target_pairs={{0,16},{16,0},{1,17},{17,1},{2,18},{18,2},{3,19},{19,3},{4,20},{20... | collective-permute-start | bytes 2752520 | tf_op jit(solution)/shard_map/ppermute | solution.py:34
  24.6 49.1 %collective-permute-start.10 = (bf16[4,256,896]{2,1,0:T(8,128)(2,1)}, bf16[4,256,896]{2,1,0:T(8,128)(2,1)}, u32[]{:S(2)}, u32[]{:S(2)}) collective-permute-start(bf16[4,256,896]{2,1,0:T(8,128)(2,1)} %shard_map.47), channel_id=1, source_target_pairs={{0,128},{16,152},{1,129},{17,153},{2,130},{18,154},{3,131},{19,155... | collective-permute-start | bytes 5505032 | tf_op jit(solution)/shard_map/ppermute | solution.py:46
  35.4 10.7 %collective-permute-start.2 = (bf16[256,256]{1,0:T(8,128)(2,1)S(1)}, bf16[256,256]{1,0:T(8,128)(2,1)S(1)}, u32[]{:S(2)}, u32[]{:S(2)}) collective-permute-start(bf16[256,256]{1,0:T(8,128)(2,1)S(1)} %collective-permute-done.1), channel_id=1, source_target_pairs={{0,8},{16,24},{1,9},{17,25},{2,10},{18,26},{3,11},{19,27},{4,12},{... | collective-permute-start | bytes 393224 | tf_op jit(solution)/shard_map/ppermute | solution.py:34
  41.2 32.5 %copy-start.2 = (bf16[896,512]{1,0:T(8,128)(2,1)}, bf16[896,512]{1,0:T(8,128)(2,1)S(1)}, u32[]{:S(2)}) copy-start(bf16[896,512]{1,0:T(8,128)(2,1)S(1)} %collective-permute-done.4.refs_4_.refs_6_) | copy-start | bytes 2752516
  43.7 24.1 %collective-permute-start.8 = (bf16[896,512]{1,0:T(8,128)(2,1)}, bf16[896,512]{1,0:T(8,128)(2,1)}, u32[]{:S(2)}, u32[]{:S(2)}) collective-permute-start(bf16[896,512]{1,0:T(8,128)(2,1)} %broadcast_select_fusion), channel_id=1, source_target_pairs={{0,32},{16,112},{1,33},{17,113},{2,34},{18,114},{3,35},{19,115},{4... | collective-permute-start | bytes 2752520 | tf_op jit(solution)/shard_map/ppermute | solution.py:46
  46.9 21.5 %collective-permute-start.11 = (bf16[2,256,896]{2,1,0:T(8,128)(2,1)}, bf16[2,256,896]{2,1,0:T(8,128)(2,1)S(1)}, u32[]{:S(2)}, u32[]{:S(2)}) collective-permute-start(bf16[2,256,896]{2,1,0:T(8,128)(2,1)} %collective-permute-done.refs_1_), channel_id=1, source_target_pairs={{0,1},{16,23},{1,2},{17,16},{2,3},{18,17},{3,4},{19,18},{4,5},{20,... | collective-permute-start | bytes 2752520 | tf_op jit(solution)/shard_map/ppermute | solution.py:46
  52.5 18.7 %collective-permute-start.5 = (bf16[896,512]{1,0:T(8,128)(2,1)S(1)}, bf16[896,512]{1,0:T(8,128)(2,1)S(1)}, u32[]{:S(2)}, u32[]{:S(2)}) collective-permute-start(bf16[896,512]{1,0:T(8,128)(2,1)S(1)} %collective-permute-done.4.refs_4_.refs_6_), channel_id=1, source_target_pairs={{0,16},{16,0},{1,17},{17,1},{2,18},{18,2},{3,19},{19,3},{4,20},{20... | collective-permute-start | bytes 2752520 | tf_op jit(solution)/shard_map/ppermute | solution.py:34
  67.9 4.8 %collective-permute-start.7 = (bf16[896,512]{1,0:T(8,128)(2,1)}, bf16[896,512]{1,0:T(8,128)(2,1)S(1)}, u32[]{:S(2)}, u32[]{:S(2)}) collective-permute-start(bf16[896,512]{1,0:T(8,128)(2,1)} %collective-permute-done.6.refs_6_.refs_8_), channel_id=1, source_target_pairs={{0,16},{16,0},{1,17},{17,1},{2,18},{18,2},{3,19},{19,3},{4,20},{20... | collective-permute-start | bytes 2752520 | tf_op jit(solution)/shard_map/ppermute | solution.py:34
  67.9 10.7 %collective-permute-start.9 = (bf16[896,512]{1,0:T(8,128)(2,1)}, bf16[896,512]{1,0:T(8,128)(2,1)}, u32[]{:S(2)}, u32[]{:S(2)}) collective-permute-start(bf16[896,512]{1,0:T(8,128)(2,1)} %collective-permute-done.8.refs_8_.refs_2_), channel_id=1, source_target_pairs={{0,16},{16,0},{1,17},{17,1},{2,18},{18,2},{3,19},{19,3},{4,20},{20... | collective-permute-start | bytes 2752520 | tf_op jit(solution)/shard_map/ppermute | solution.py:34
  68.4 5.3 %copy-start.5 = (bf16[2,256,896]{2,1,0:T(8,128)(2,1)}, bf16[2,256,896]{2,1,0:T(8,128)(2,1)S(1)}, u32[]{:S(2)}) copy-start(bf16[2,256,896]{2,1,0:T(8,128)(2,1)S(1)} %collective-permute-done.11.refs_2_) | copy-start | bytes 2752516
  71.2 1.0 copy-start.3
  72.6 1.0 copy-start.4
  83.8 17.5 %collective-permute-start.12 = (f16[256,512]{1,0:T(8,128)(2,1)S(1)}, f16[256,512]{1,0:T(8,128)(2,1)S(1)}, u32[]{:S(2)}, u32[]{:S(2)}) collective-permute-start(f16[256,512]{1,0:T(8,128)(2,1)S(1)} %multiply_convert_fusion), channel_id=1, source_target_pairs={{0,128},{16,144},{1,129},{17,145},{2,130},{18,146},{3,131},{19,147... | collective-permute-start | bytes 786440 | tf_op jit(solution)/shard_map/ppermute | solution.py:57
  102.4 6.6 %collective-permute-start.15 = (bf16[256,512]{1,0:T(8,128)(2,1)S(1)}, bf16[256,512]{1,0:T(8,128)(2,1)S(1)}, u32[]{:S(2)}, u32[]{:S(2)}) collective-permute-start(bf16[256,512]{1,0:T(8,128)(2,1)S(1)} %add_convert_fusion.refs_0_), channel_id=1, source_target_pairs={{0,128},{16,144},{1,129},{17,145},{2,130},{18,146},{3,131},{19,147... | collective-permute-start | bytes 786440 | tf_op jit(solution)/shard_map/ppermute | solution.py:57
  102.7 9.0 %collective-permute-start.16 = (bf16[256,512]{1,0:T(8,128)(2,1)S(1)}, bf16[256,512]{1,0:T(8,128)(2,1)S(1)}, u32[]{:S(2)}, u32[]{:S(2)}) collective-permute-start(bf16[256,512]{1,0:T(8,128)(2,1)S(1)} %add_convert_fusion.refs_0_), channel_id=1, source_target_pairs={{0,64},{16,80},{1,65},{17,81},{2,66},{18,82},{3,67},{19,83},{4,68}... | collective-permute-start | bytes 786440 | tf_op jit(solution)/shard_map/ppermute | solution.py:34
  102.7 14.3 %collective-permute-start.13 = (bf16[256,512]{1,0:T(8,128)(2,1)S(1)}, bf16[256,512]{1,0:T(8,128)(2,1)S(1)}, u32[]{:S(2)}, u32[]{:S(2)}) collective-permute-start(bf16[256,512]{1,0:T(8,128)(2,1)S(1)} %add_convert_fusion.refs_0_), channel_id=1, source_target_pairs={{0,32},{16,48},{1,33},{17,49},{2,34},{18,50},{3,35},{19,51},{4,36}... | collective-permute-start | bytes 786440 | tf_op jit(solution)/shard_map/ppermute | solution.py:34
  102.7 14.3 %collective-permute-start.14 = (bf16[256,512]{1,0:T(8,128)(2,1)S(1)}, bf16[256,512]{1,0:T(8,128)(2,1)S(1)}, u32[]{:S(2)}, u32[]{:S(2)}) collective-permute-start(bf16[256,512]{1,0:T(8,128)(2,1)S(1)} %add_convert_fusion.refs_0_), channel_id=1, source_target_pairs={{0,96},{16,112},{1,97},{17,113},{2,98},{18,114},{3,99},{19,115},{4... | collective-permute-start | bytes 786440 | tf_op jit(solution)/shard_map/ppermute | solution.py:34
  109.0 13.8 %collective-permute-start.17 = (bf16[256,512]{1,0:T(8,128)(2,1)S(1)}, bf16[256,512]{1,0:T(8,128)(2,1)}, u32[]{:S(2)}, u32[]{:S(2)}) collective-permute-start(bf16[256,512]{1,0:T(8,128)(2,1)S(1)} %collective-permute-done.15.refs_3_), channel_id=1, source_target_pairs={{0,32},{16,48},{1,33},{17,49},{2,34},{18,50},{3,35},{19,51},{4,36}... | collective-permute-start | bytes 786440 | tf_op jit(solution)/shard_map/ppermute | solution.py:34
  109.0 13.8 %collective-permute-start.18 = (bf16[256,512]{1,0:T(8,128)(2,1)S(1)}, bf16[256,512]{1,0:T(8,128)(2,1)}, u32[]{:S(2)}, u32[]{:S(2)}) collective-permute-start(bf16[256,512]{1,0:T(8,128)(2,1)S(1)} %collective-permute-done.15.refs_3_), channel_id=1, source_target_pairs={{0,96},{16,112},{1,97},{17,113},{2,98},{18,114},{3,99},{19,115},{4... | collective-permute-start | bytes 786440 | tf_op jit(solution)/shard_map/ppermute | solution.py:34
  111.7 11.1 %collective-permute-start.19 = (bf16[256,512]{1,0:T(8,128)(2,1)S(1)}, bf16[256,512]{1,0:T(8,128)(2,1)}, u32[]{:S(2)}, u32[]{:S(2)}) collective-permute-start(bf16[256,512]{1,0:T(8,128)(2,1)S(1)} %collective-permute-done.16.refs_4_), channel_id=1, source_target_pairs={{0,128},{16,144},{1,129},{17,145},{2,130},{18,146},{3,131},{19,147... | collective-permute-start | bytes 786440 | tf_op jit(solution)/shard_map/ppermute | solution.py:57
  122.8 1.6 %copy-start.1 = (bf16[16,256,256]{2,1,0:T(8,128)(2,1)S(1)}, bf16[16,256,256]{2,1,0:T(8,128)(2,1)}, u32[]{:S(2)}) copy-start(bf16[16,256,256]{2,1,0:T(8,128)(2,1)} %all-gather.3.cloned.1.call-done) | copy-start | bytes 6291460
  128.9 2.8 %collective-permute-start.20 = (f32[256,512]{1,0:T(8,128)S(1)}, f32[256,512]{1,0:T(8,128)S(1)}, u32[]{:S(2)}, u32[]{:S(2)}) collective-permute-start(f32[256,512]{1,0:T(8,128)S(1)} %get-tuple-element.14), channel_id=1, source_target_pairs={{0,16},{16,0},{1,17},{17,1},{2,18},{18,2},{3,19},{19,3},{4,20},{20... | collective-permute-start | bytes 1572872 | tf_op jit(solution)/shard_map/ppermute | solution.py:34
Sparse Core Ops, SparseCore 0:
  47.0 58.1 all-gather.2

commit v5 on v4

--- a/solution.py
+++ b/solution.py
@@ -14,7 +14,7 @@
 VMEM = 60 * 1024 * 1024
 FOLLOWED = 6 * 10**9
 TAIL_VMEM = 16 * 1024 * 1024
-BLOCKS = ((0, 0), (0, 1), (3, 0), (3, 1), (1, 0), (1, 1), (2, 0), (2, 1))
+BLOCKS = ((0, 0), (0, 1), (3, 0), (1, 1), (1, 0), (3, 1), (2, 0), (2, 1))
 ORDER = ((0, 0), (0, 3), (0, 1), (1, 0), (0, 2), (1, 3), (1, 1), (1, 2))
 
 
@@ -133,7 +133,7 @@
             out[...] = before[0][...] + term if before else term
 
 
-def product(moves, count, table, sources, panels, before=None, followed_by=0):
+def product(moves, count, table, sources, panels, before=None, followed_by=0, grant=VMEM):
     tokens, blocks = EXAMPLES * TOK, len(panels)
     depth, width = panels[0][0].shape[0] if len(panels[0]) == 1 else sum(
         part.shape[0] for part in panels[0]
@@ -153,7 +153,7 @@
             pltpu.VMEM((blocks, depth, width), jnp.bfloat16),
             pltpu.SemaphoreType.DMA((count + len(parts),)),
         ],
-        compiler_params=pltpu.CompilerParams(vmem_limit_bytes=VMEM),
+        compiler_params=pltpu.CompilerParams(vmem_limit_bytes=grant),
         cost_estimate=pl.CostEstimate(
             flops=2 * tokens * width * blocks * depth + followed_by,
             bytes_accessed=2**22,
@@ -236,6 +236,14 @@
     )(where, out_rows, *in_rows)
 
 
+def z_swap(value):
+    pairs = []
+    for d in range(NX * NY * NC):
+        for b in range(NH * NZ):
+            pairs.append((d * NH * NZ + b, d * NH * NZ + (b ^ 1)))
+    return lax.ppermute(value, ("dp", "blk"), pairs)
+
+
 def transposed(block):
     pairs = []
     for sx in range(NX):
@@ -254,7 +262,8 @@
     parity = b % 2
     scale = 1.0 / float(EXAMPLES * NX * NY * NC)
     depth = basis_in.shape[0]
-    spots = [((y + dy) % NY) * NC + (core + dc) % NC for dy, dc in BLOCKS]
+    mirror = 1 - 2 * core
+    spots = [((y + mirror * dy) % NY) * NC + (core + dc) % NC for dy, dc in BLOCKS]
     half = len(BLOCKS)
 
     table = jnp.stack(spots).astype(jnp.int32)
@@ -262,18 +271,19 @@
     keep = ((half * x + table) * depth).astype(jnp.int32)
     near = lax.dynamic_slice_in_dim(give, parity * SPLIT, SPLIT)
     near = by_core(pieces(near.astype(jnp.int32), activations, depth), dx=1)
-    left, right = shift(basis_in, dy=1), shift(basis_in, dy=3)
-    own_other = shift(basis_in, dc=1)
-    block = transposed(dot(out_grads, basis_out).astype(jnp.bfloat16).T)
-
+    first, own_other = by_core(basis_in, dy=1), shift(basis_in, dc=1)
     rest = pieces(give[2 * SPLIT :].astype(jnp.int32), activations, depth)
-    near, rest, block = lax.optimization_barrier((near, rest, block))
+    block = dot(out_grads, basis_out).astype(jnp.bfloat16).T
+    block = transposed(jnp.stack([block, z_swap(block)]))
+
+    first, near, rest, again, own_other = lax.optimization_barrier(
+        (first, near, rest, basis_in, own_other)
+    )
+    second, far = by_core(again, dy=NY - 1), by_core(first, dy=1)
     rest, away = by_core(rest, dx=1), by_core(near, dz=1)
-    far = by_core(jnp.where(core == 0, left, right), dy=1)
-    left_other, right_other = shift(left, dc=1), shift(right, dc=1)
 
     out_rows = lax.all_gather(
-        jnp.stack([block, shift(block, dx=NX)]),
+        block,
         "blk",
         axis=0,
         axis_index_groups=[[h * NZ + z for z in range(NZ)] for h in range(NH)],
@@ -283,11 +293,14 @@
         [((x + dx) % NX) * NY + (y + dy) % NY for dx, dy in ORDER] + [flip, 1 - flip]
     ).astype(jnp.int32)
 
-    panels = [basis_in, own_other, left, left_other, right, right_other, far, shift(far, dc=1)]
+    panels = []
+    for panel in (first, second, far):
+        panels += [panel, shift(panel, dc=1)]
+    panels = [basis_in, own_other] + panels
     panels = [[panel] for panel in panels]
     parity = parity.reshape(1).astype(jnp.int32)
     partial = product(near_moves, 3, parity, (near, away, rest), panels[:-2])
-    partial = product(last_moves, 1, parity, (rest,), panels[-2:], partial, FOLLOWED)
+    partial = product(last_moves, 1, parity, (rest,), panels[-2:], partial, FOLLOWED, TAIL_VMEM)
     arrived = swap((partial * FACTOR).astype(jnp.float16))
     total = product(own_moves, len(BLOCKS), keep, (activations,), panels)
     proj_in = (total + arrived.astype(jnp.float32) * (1.0 / FACTOR)).astype(jnp.bfloat16)

time: 142 us -> 139 us (0.979); the launches traced: 139 us -> 139 us
  waiting for transfers between devices: 24.8 us -> 34.7 us
  starting transfers between devices: 61.1 us -> 56.4 us
  other arithmetic: 6.96 us -> 3.39 us
  Pallas kernels: 25.9 us -> 23.7 us
    ppermute x13 -> x10, starting transfers between devices: 27 us -> 6.38 us  [shift(): return lax.ppermute(value, ('dp', 'blk'), pairs)]
    ppermute x4 -> x6, waiting for transfers between devices: 0.67 us -> 15.9 us  [by_core(): return lax.ppermute(value, ('dp', 'blk'), pairs)]
    ppermute x4 -> x6, starting transfers between devices: 22.2 us -> 36.6 us  [by_core(): return lax.ppermute(value, ('dp', 'blk'), pairs)]
    ppermute x13 -> x10, waiting for transfers between devices: 20.5 us -> 11.5 us  [shift(): return lax.ppermute(value, ('dp', 'blk'), pairs)]
    ppermute x0 -> x1, waiting for transfers between devices: none -> 3.4 us  [z_swap(): return lax.ppermute(value, ('dp', 'blk'), pairs)]
    ppermute x3, starting transfers between devices: 11.1 us -> 8.14 us  [swap(): return lax.ppermute(value, ('dp', 'blk'), pairs)]
    ppermute x1, starting transfers between devices: 0.67 us -> 3.57 us  [transposed(): return lax.ppermute(block, ('dp', 'blk'), pairs)]
    select_n x1 -> x0, other arithmetic: 2.55 us -> none  [on_device(): far = by_core(jnp.where(core == 0, left, right), dy=1)]
  transfers between devices with their start and end apart: 22 -> 22, of which waited for: 8 -> 7; matrix products, arithmetic and copies ran while one was open for 6% -> 4% of each run, Pallas kernels for 13% -> 12%
where the time goes in v5:
time: 139 us
  starting transfers between devices  56.4 us (41%)
  waiting for transfers between devices  34.7 us (25%)
  Pallas kernels  23.7 us (17%)
  between operations  13.6 us (10%)
  local copies, waits for them, and re-layouts  4.38 us (3%)
  other arithmetic  3.39 us (2%)
  matrix products  2.34 us (2%)
    ppermute x6, starting transfers between devices, by_core(): return lax.ppermute(value, ('dp', 'blk'), pairs)  36.6 us
    ppermute x6, waiting for transfers between devices, by_core(): return lax.ppermute(value, ('dp', 'blk'), pairs)  15.9 us
    pallas_call x3, Pallas kernels, product(): pl.pallas_call(lambda *refs: product_kernel(moves, layout, *refs), out_sh...  13.6 us
    ppermute x10, waiting for transfers between devices, shift(): return lax.ppermute(value, ('dp', 'blk'), pairs)  11.5 us
    ppermute x3, starting transfers between devices, swap(): return lax.ppermute(value, ('dp', 'blk'), pairs)  8.14 us
    ppermute x10, starting transfers between devices, shift(): return lax.ppermute(value, ('dp', 'blk'), pairs)  6.38 us
    pallas_call x2, Pallas kernels, pieces(): pl.pallas_call(pieces_kernel, out_shape=jax.ShapeDtypeStruct(shape, activ...  5.63 us
    pallas_call x1, Pallas kernels, sums_of_squares(): pl.pallas_call(squares_kernel, out_shape=[jax.ShapeDtypeStruct((rows, wid...  4.45 us
  transfers between devices with their start and end apart: 22, of which 7 were waited for; matrix products, arithmetic and copies ran while one was open for 4% of the time, Pallas kernels for 12%

profile of v5, /device:TPU:1, one launch (start us, length us, event | category | flops | bytes accessed | tf_op | source)
XLA Modules:
  0.0 138.5 jit_solution(9005684491470545070)
XLA Ops:
  7.8 2.6 %shard_map.46 = bf16[2,256,896]{2,1,0:T(8,128)(2,1)} custom-call(s32[2]{0:T(128)} %dynamic_slice.3.columns_ref, bf16[256,14336]{1,0:T(8,128)(2,1)} %refs_1_.1), custom_call_target="tpu_custom_call" | custom-call | bytes 4194304 | tf_op jit(solution)/shard_map/pallas_call | solution.py:91
  10.5 3.4 %collective-permute-start.3 = (bf16[2,256,896]{2,1,0:T(8,128)(2,1)}, bf16[2,256,896]{2,1,0:T(8,128)(2,1)}, u32[]{:S(2)}, u32[]{:S(2)}) collective-permute-start(bf16[2,256,896]{2,1,0:T(8,128)(2,1)} %shard_map.46), channel_id=1, source_target_pairs={{0,128},{16,152},{1,129},{17,153},{2,130},{18,154},{3,131},{19,155... | collective-permute-start | bytes 2752520 | tf_op jit(solution)/shard_map/ppermute | solution.py:46
  13.8 2.7 %collective-permute-start.2 = (bf16[896,512]{1,0:T(8,128)(2,1)}, bf16[896,512]{1,0:T(8,128)(2,1)S(1)}, u32[]{:S(2)}, u32[]{:S(2)}) collective-permute-start(bf16[896,512]{1,0:T(8,128)(2,1)} %refs_4_.1), channel_id=1, source_target_pairs={{0,32},{16,112},{1,33},{17,113},{2,34},{18,114},{3,35},{19,115},{4... | collective-permute-start | bytes 2752520 | tf_op jit(solution)/shard_map/ppermute | solution.py:46
  16.6 2.3 %convolution_convert_fusion = bf16[256,256]{1,0:T(8,128)(2,1)S(1)} fusion(bf16[4096,256]{1,0:T(8,128)(2,1)S(1)} %copy-done, bf16[256,4096]{1,0:T(8,128)(2,1)} %param.5), kind=kOutput, calls=%fused_computation | convolution fusion | flops 536936448 | bytes 4325376 | tf_op jit(solution)/shard_map/dot_general | solution.py:61
  18.9 1.7 %collective-permute-start = (bf16[256,256]{1,0:T(8,128)(2,1)S(1)}, bf16[256,256]{1,0:T(8,128)(2,1)S(1)}, u32[]{:S(2)}, u32[]{:S(2)}) collective-permute-start(bf16[256,256]{1,0:T(8,128)(2,1)S(1)} %convolution_convert_fusion), channel_id=1, source_target_pairs={{0,1},{1,0},{2,3},{3,2},{4,5},{5,4},{6,7},{7,6},{8,9},{9,8},{10,11... | collective-permute-start | bytes 393224 | tf_op jit(solution)/shard_map/ppermute | solution.py:244
  20.7 3.4 %collective-permute-done = bf16[256,256]{1,0:T(8,128)(2,1)S(1)} collective-permute-done((bf16[256,256]{1,0:T(8,128)(2,1)S(1)}, bf16[256,256]{1,0:T(8,128)(2,1)S(1)}, u32[]{:S(2)}, u32[]{:S(2)}) %collective-permute-start) | collective-permute-done | bytes 131104 | tf_op jit(solution)/shard_map/ppermute | solution.py:244
  24.1 0.7 pad_maximum_fusion
  24.8 3.6 %collective-permute-start.1 = (bf16[2,256,256]{2,1,0:T(8,128)(2,1)}, bf16[2,256,256]{2,1,0:T(8,128)(2,1)}, u32[]{:S(2)}, u32[]{:S(2)}) collective-permute-start(bf16[2,256,256]{2,1,0:T(8,128)(2,1)} %pad_maximum_fusion), channel_id=1, source_target_pairs={{0,0},{1,8},{2,32},{3,40},{4,64},{5,72},{6,96},{7,104},{8,128},{9,... | collective-permute-start | bytes 786440 | tf_op jit(solution)/shard_map/ppermute | solution.py:256
  28.9 3.0 %shard_map.47 = bf16[4,256,896]{2,1,0:T(8,128)(2,1)} custom-call(s32[4]{0:T(128)} %slice.3.columns_ref, bf16[256,14336]{1,0:T(8,128)(2,1)} %refs_1_.1), custom_call_target="tpu_custom_call" | custom-call | bytes 4194304 | tf_op jit(solution)/shard_map/pallas_call | solution.py:91
  32.0 0.9 collective-permute-start.6
  33.3 7.3 %collective-permute-start.10 = (bf16[4,256,896]{2,1,0:T(8,128)(2,1)}, bf16[4,256,896]{2,1,0:T(8,128)(2,1)}, u32[]{:S(2)}, u32[]{:S(2)}) collective-permute-start(bf16[4,256,896]{2,1,0:T(8,128)(2,1)} %shard_map.47), channel_id=1, source_target_pairs={{0,128},{16,152},{1,129},{17,153},{2,130},{18,154},{3,131},{19,155... | collective-permute-start | bytes 5505032 | tf_op jit(solution)/shard_map/ppermute | solution.py:46
  40.5 1.5 %collective-permute-start.8 = (bf16[896,512]{1,0:T(8,128)(2,1)}, bf16[896,512]{1,0:T(8,128)(2,1)S(1)}, u32[]{:S(2)}, u32[]{:S(2)}) collective-permute-start(bf16[896,512]{1,0:T(8,128)(2,1)} %copy-done.4), channel_id=1, source_target_pairs={{0,32},{16,112},{1,33},{17,113},{2,34},{18,114},{3,35},{19,115},{4... | collective-permute-start | bytes 2752520 | tf_op jit(solution)/shard_map/ppermute | solution.py:46
  42.2 20.9 %collective-permute-start.11 = (bf16[2,256,896]{2,1,0:T(8,128)(2,1)}, bf16[2,256,896]{2,1,0:T(8,128)(2,1)}, u32[]{:S(2)}, u32[]{:S(2)}) collective-permute-start(bf16[2,256,896]{2,1,0:T(8,128)(2,1)} %collective-permute-done.3.refs_1_), channel_id=1, source_target_pairs={{0,1},{16,23},{1,2},{17,16},{2,3},{18,17},{3,4},{19,18},{4,5},{20,... | collective-permute-start | bytes 2752520 | tf_op jit(solution)/shard_map/ppermute | solution.py:46
  63.8 15.3 %collective-permute-done.11.refs_2_ = bf16[2,256,896]{2,1,0:T(8,128)(2,1)} collective-permute-done((bf16[2,256,896]{2,1,0:T(8,128)(2,1)}, bf16[2,256,896]{2,1,0:T(8,128)(2,1)}, u32[]{:S(2)}, u32[]{:S(2)}) %collective-permute-start.11) | collective-permute-done | bytes 917536 | tf_op jit(solution)/shard_map/ppermute | solution.py:46
  79.1 5.0 %shard_map.49.refs_4_ = f32[256,512]{1,0:T(8,128)} custom-call(s32[1]{0:T(128)} %bitcast.21.refs_0_, bf16[2,256,896]{2,1,0:T(8,128)(2,1)} %collective-permute-done.3.refs_1_, bf16[2,256,896]{2,1,0:T(8,128)(2,1)} %collective-permute-done.11.refs_2_, bf16[4,256,896]{2,1,0:T(8,128)(2,1)} %collective-permute-done.10.refs_3_.refs_1_, bf16[896,512]{1,0:T(8,128)(2,1)} %refs_4_.1, ...), custom_call_target="tpu_custom_call" | custom-call | flops 1409286144 | bytes 4194304 | tf_op jit(solution)/shard_map/pallas_call | solution.py:144
  84.0 1.0 copy-done.3
  85.1 2.0 %shard_map.50 = f32[256,512]{1,0:T(8,128)S(1)} custom-call(s32[1]{0:T(128)} %bitcast.21.refs_0_, bf16[4,256,896]{2,1,0:T(8,128)(2,1)} %collective-permute-done.10.refs_3_.refs_1_, bf16[896,512]{1,0:T(8,128)(2,1)S(1)} %collective-permute-done.8.refs_8_.refs_2_, bf16[896,512]{1,0:T(8,128)(2,1)} %collective-permute-done.9.refs_9_.refs_3_, f32[256,512]{1,0:T(8,128)S(1)} %copy-done.3), custom_call_target="tpu_custom_call" | custom-call | flops 6469762048 | bytes 4194304 | tf_op jit(solution)/shard_map/pallas_call | solution.py:144
  87.2 5.1 %collective-permute-start.12 = (f16[256,512]{1,0:T(8,128)(2,1)S(1)}, f16[256,512]{1,0:T(8,128)(2,1)S(1)}, u32[]{:S(2)}, u32[]{:S(2)}) collective-permute-start(f16[256,512]{1,0:T(8,128)(2,1)S(1)} %multiply_convert_fusion), channel_id=1, source_target_pairs={{0,128},{16,144},{1,129},{17,145},{2,130},{18,146},{3,131},{19,147... | collective-permute-start | bytes 786440 | tf_op jit(solution)/shard_map/ppermute | solution.py:57
  92.3 6.6 %shard_map.48 = f32[256,512]{1,0:T(8,128)} custom-call(s32[8]{0:T(128)} %get-tuple-element.20.refs_0_, bf16[256,14336]{1,0:T(8,128)(2,1)} %refs_1_.1, bf16[896,512]{1,0:T(8,128)(2,1)} %refs_4_.1, bf16[896,512]{1,0:T(8,128)(2,1)} %copy-done.5, bf16[896,512]{1,0:T(8,128)(2,1)} %copy-done.4, bf16[896,512]{1,0:T(8,128)(2,1)} %collective-permute-done.5.refs_5_.refs_7_, ...), custom_call_target="tpu_custom_call" | custom-call | flops 1879048192 | bytes 4194304 | tf_op jit(solution)/shard_map/pallas_call | solution.py:144
  99.0 1.1 add_convert_fusion.refs_0_
  100.1 1.7 %collective-permute-start.15 = (bf16[256,512]{1,0:T(8,128)(2,1)S(1)}, bf16[256,512]{1,0:T(8,128)(2,1)S(1)}, u32[]{:S(2)}, u32[]{:S(2)}) collective-permute-start(bf16[256,512]{1,0:T(8,128)(2,1)S(1)} %add_convert_fusion.refs_0_), channel_id=1, source_target_pairs={{0,128},{16,144},{1,129},{17,145},{2,130},{18,146},{3,131},{19,147... | collective-permute-start | bytes 786440 | tf_op jit(solution)/shard_map/ppermute | solution.py:57
  101.8 2.7 %collective-permute-start.14 = (bf16[256,512]{1,0:T(8,128)(2,1)S(1)}, bf16[256,512]{1,0:T(8,128)(2,1)S(1)}, u32[]{:S(2)}, u32[]{:S(2)}) collective-permute-start(bf16[256,512]{1,0:T(8,128)(2,1)S(1)} %add_convert_fusion.refs_0_), channel_id=1, source_target_pairs={{0,96},{16,112},{1,97},{17,113},{2,98},{18,114},{3,99},{19,115},{4... | collective-permute-start | bytes 786440 | tf_op jit(solution)/shard_map/ppermute | solution.py:34
  104.5 3.9 %collective-permute-done.15.refs_3_ = bf16[256,512]{1,0:T(8,128)(2,1)S(1)} collective-permute-done((bf16[256,512]{1,0:T(8,128)(2,1)S(1)}, bf16[256,512]{1,0:T(8,128)(2,1)S(1)}, u32[]{:S(2)}, u32[]{:S(2)}) %collective-permute-start.15) | collective-permute-done | bytes 262176 | tf_op jit(solution)/shard_map/ppermute | solution.py:57
  108.3 2.7 %collective-permute-start.18 = (bf16[256,512]{1,0:T(8,128)(2,1)S(1)}, bf16[256,512]{1,0:T(8,128)(2,1)}, u32[]{:S(2)}, u32[]{:S(2)}) collective-permute-start(bf16[256,512]{1,0:T(8,128)(2,1)S(1)} %collective-permute-done.15.refs_3_), channel_id=1, source_target_pairs={{0,96},{16,112},{1,97},{17,113},{2,98},{18,114},{3,99},{19,115},{4... | collective-permute-start | bytes 786440 | tf_op jit(solution)/shard_map/ppermute | solution.py:34
  111.0 1.3 collective-permute-start.19
  112.4 4.2 %collective-permute-done.13.refs_1_ = bf16[256,512]{1,0:T(8,128)(2,1)S(1)} collective-permute-done((bf16[256,512]{1,0:T(8,128)(2,1)S(1)}, bf16[256,512]{1,0:T(8,128)(2,1)S(1)}, u32[]{:S(2)}, u32[]{:S(2)}) %collective-permute-start.13) | collective-permute-done | bytes 262176 | tf_op jit(solution)/shard_map/ppermute | solution.py:34
  116.6 5.7 %collective-permute-done.17.refs_5_ = bf16[256,512]{1,0:T(8,128)(2,1)} collective-permute-done((bf16[256,512]{1,0:T(8,128)(2,1)S(1)}, bf16[256,512]{1,0:T(8,128)(2,1)}, u32[]{:S(2)}, u32[]{:S(2)}) %collective-permute-start.17) | collective-permute-done | bytes 262176 | tf_op jit(solution)/shard_map/ppermute | solution.py:34
  122.3 1.6 %copy-done.1 = bf16[16,256,256]{2,1,0:T(8,128)(2,1)S(1)} copy-done((bf16[16,256,256]{2,1,0:T(8,128)(2,1)S(1)}, bf16[16,256,256]{2,1,0:T(8,128)(2,1)}, u32[]{:S(2)}) %copy-start.1) | copy-done | bytes 2097176
  123.9 4.5 %shard_map.51 = (f32[256,512]{1,0:T(8,128)S(1)}, f32[256,512]{1,0:T(8,128)S(1)}) custom-call(s32[10]{0:T(128)S(1)} %stack.79.where_ref, bf16[8,2,256,256]{3,2,1,0:T(8,128)(2,1)S(1)} %bitcast.24, bf16[256,512]{1,0:T(8,128)(2,1)S(1)} %add_convert_fusion.refs_0_, bf16[256,512]{1,0:T(8,128)(2,1)S(1)} %collective-permute-done.13.refs_1_, ...), custom_call_target="tpu_custom_call" | custom-call | flops 1073741824 | bytes 3145728 | tf_op jit(solution)/shard_map/pallas_call | solution.py:220
  128.4 0.8 collective-permute-start.20
  129.2 1.5 %collective-permute-done.20 = f32[256,512]{1,0:T(8,128)S(1)} collective-permute-done((f32[256,512]{1,0:T(8,128)S(1)}, f32[256,512]{1,0:T(8,128)S(1)}, u32[]{:S(2)}, u32[]{:S(2)}) %collective-permute-start.20) | collective-permute-done | bytes 524320 | tf_op jit(solution)/shard_map/ppermute | solution.py:34
  130.8 0.9 add_multiply_fusion
  (41 shorter events, 3.3 us)
Async XLA Ops:
  6.5 10.0 %copy-start = (bf16[4096,256]{1,0:T(8,128)(2,1)S(1)}, bf16[4096,256]{1,0:T(8,128)(2,1)}, u32[]{:S(2)}) copy-start(bf16[4096,256]{1,0:T(8,128)(2,1)} %param.7) | copy-start | bytes 6291460
  6.5 115.8 %all-gather.3.cloned.1.call-start = ((), (), s32[]{:S(2)}) async-start(), calls=%async_computation | async-start | bytes 2359296 | tf_op jit(solution)/shard_map/all_gather | solution.py:285
  10.5 21.5 %collective-permute-start.3 = (bf16[2,256,896]{2,1,0:T(8,128)(2,1)}, bf16[2,256,896]{2,1,0:T(8,128)(2,1)}, u32[]{:S(2)}, u32[]{:S(2)}) collective-permute-start(bf16[2,256,896]{2,1,0:T(8,128)(2,1)} %shard_map.46), channel_id=1, source_target_pairs={{0,128},{16,152},{1,129},{17,153},{2,130},{18,154},{3,131},{19,155... | collective-permute-start | bytes 2752520 | tf_op jit(solution)/shard_map/ppermute | solution.py:46
  13.8 18.1 %collective-permute-start.2 = (bf16[896,512]{1,0:T(8,128)(2,1)}, bf16[896,512]{1,0:T(8,128)(2,1)S(1)}, u32[]{:S(2)}, u32[]{:S(2)}) collective-permute-start(bf16[896,512]{1,0:T(8,128)(2,1)} %refs_4_.1), channel_id=1, source_target_pairs={{0,32},{16,112},{1,33},{17,113},{2,34},{18,114},{3,35},{19,115},{4... | collective-permute-start | bytes 2752520 | tf_op jit(solution)/shard_map/ppermute | solution.py:46
  16.6 15.4 %collective-permute-start.4 = (bf16[896,512]{1,0:T(8,128)(2,1)}, bf16[896,512]{1,0:T(8,128)(2,1)S(1)}, u32[]{:S(2)}, u32[]{:S(2)}) collective-permute-start(bf16[896,512]{1,0:T(8,128)(2,1)} %refs_4_.1), channel_id=1, source_target_pairs={{0,16},{16,0},{1,17},{17,1},{2,18},{18,2},{3,19},{19,3},{4,20},{20... | collective-permute-start | bytes 2752520 | tf_op jit(solution)/shard_map/ppermute | solution.py:34
  18.9 5.1 %collective-permute-start = (bf16[256,256]{1,0:T(8,128)(2,1)S(1)}, bf16[256,256]{1,0:T(8,128)(2,1)S(1)}, u32[]{:S(2)}, u32[]{:S(2)}) collective-permute-start(bf16[256,256]{1,0:T(8,128)(2,1)S(1)} %convolution_convert_fusion), channel_id=1, source_target_pairs={{0,1},{1,0},{2,3},{3,2},{4,5},{5,4},{6,7},{7,6},{8,9},{9,8},{10,11... | collective-permute-start | bytes 393224 | tf_op jit(solution)/shard_map/ppermute | solution.py:244
  24.8 17.3 %collective-permute-start.1 = (bf16[2,256,256]{2,1,0:T(8,128)(2,1)}, bf16[2,256,256]{2,1,0:T(8,128)(2,1)}, u32[]{:S(2)}, u32[]{:S(2)}) collective-permute-start(bf16[2,256,256]{2,1,0:T(8,128)(2,1)} %pad_maximum_fusion), channel_id=1, source_target_pairs={{0,0},{1,8},{2,32},{3,40},{4,64},{5,72},{6,96},{7,104},{8,128},{9,... | collective-permute-start | bytes 786440 | tf_op jit(solution)/shard_map/ppermute | solution.py:256
  32.0 1.0 copy-start.4
  32.0 1.3 copy-start.5
  32.0 31.1 %collective-permute-start.6 = (bf16[896,512]{1,0:T(8,128)(2,1)}, bf16[896,512]{1,0:T(8,128)(2,1)}, u32[]{:S(2)}, u32[]{:S(2)}) collective-permute-start(bf16[896,512]{1,0:T(8,128)(2,1)} %refs_4_.1), channel_id=1, source_target_pairs={{0,96},{16,48},{1,97},{17,49},{2,98},{18,50},{3,99},{19,51},{4,100... | collective-permute-start | bytes 2752520 | tf_op jit(solution)/shard_map/ppermute | solution.py:46
  33.3 45.8 %collective-permute-start.10 = (bf16[4,256,896]{2,1,0:T(8,128)(2,1)}, bf16[4,256,896]{2,1,0:T(8,128)(2,1)}, u32[]{:S(2)}, u32[]{:S(2)}) collective-permute-start(bf16[4,256,896]{2,1,0:T(8,128)(2,1)} %shard_map.47), channel_id=1, source_target_pairs={{0,128},{16,152},{1,129},{17,153},{2,130},{18,154},{3,131},{19,155... | collective-permute-start | bytes 5505032 | tf_op jit(solution)/shard_map/ppermute | solution.py:46
  40.5 23.2 %collective-permute-start.8 = (bf16[896,512]{1,0:T(8,128)(2,1)}, bf16[896,512]{1,0:T(8,128)(2,1)S(1)}, u32[]{:S(2)}, u32[]{:S(2)}) collective-permute-start(bf16[896,512]{1,0:T(8,128)(2,1)} %copy-done.4), channel_id=1, source_target_pairs={{0,32},{16,112},{1,33},{17,113},{2,34},{18,114},{3,35},{19,115},{4... | collective-permute-start | bytes 2752520 | tf_op jit(solution)/shard_map/ppermute | solution.py:46
  42.1 37.0 %collective-permute-start.5 = (bf16[896,512]{1,0:T(8,128)(2,1)}, bf16[896,512]{1,0:T(8,128)(2,1)}, u32[]{:S(2)}, u32[]{:S(2)}) collective-permute-start(bf16[896,512]{1,0:T(8,128)(2,1)} %copy-done.4), channel_id=1, source_target_pairs={{0,16},{16,0},{1,17},{17,1},{2,18},{18,2},{3,19},{19,3},{4,20},{20... | collective-permute-start | bytes 2752520 | tf_op jit(solution)/shard_map/ppermute | solution.py:34
  42.2 36.8 %collective-permute-start.11 = (bf16[2,256,896]{2,1,0:T(8,128)(2,1)}, bf16[2,256,896]{2,1,0:T(8,128)(2,1)}, u32[]{:S(2)}, u32[]{:S(2)}) collective-permute-start(bf16[2,256,896]{2,1,0:T(8,128)(2,1)} %collective-permute-done.3.refs_1_), channel_id=1, source_target_pairs={{0,1},{16,23},{1,2},{17,16},{2,3},{18,17},{3,4},{19,18},{4,5},{20,... | collective-permute-start | bytes 2752520 | tf_op jit(solution)/shard_map/ppermute | solution.py:46
  63.1 15.9 %collective-permute-start.7 = (bf16[896,512]{1,0:T(8,128)(2,1)}, bf16[896,512]{1,0:T(8,128)(2,1)}, u32[]{:S(2)}, u32[]{:S(2)}) collective-permute-start(bf16[896,512]{1,0:T(8,128)(2,1)} %collective-permute-done.6.refs_6_.refs_8_), channel_id=1, source_target_pairs={{0,16},{16,0},{1,17},{17,1},{2,18},{18,2},{3,19},{19,3},{4,20},{20... | collective-permute-start | bytes 2752520 | tf_op jit(solution)/shard_map/ppermute | solution.py:34
  63.8 20.3 %copy-start.2 = (bf16[896,512]{1,0:T(8,128)(2,1)}, bf16[896,512]{1,0:T(8,128)(2,1)S(1)}, u32[]{:S(2)}) copy-start(bf16[896,512]{1,0:T(8,128)(2,1)S(1)} %collective-permute-done.8.refs_8_.refs_2_) | copy-start | bytes 2752516
  63.8 20.3 %collective-permute-start.9 = (bf16[896,512]{1,0:T(8,128)(2,1)S(1)}, bf16[896,512]{1,0:T(8,128)(2,1)}, u32[]{:S(2)}, u32[]{:S(2)}) collective-permute-start(bf16[896,512]{1,0:T(8,128)(2,1)S(1)} %collective-permute-done.8.refs_8_.refs_2_), channel_id=1, source_target_pairs={{0,16},{16,0},{1,17},{17,1},{2,18},{18,2},{3,19},{19,3},{4,20},{20... | collective-permute-start | bytes 2752520 | tf_op jit(solution)/shard_map/ppermute | solution.py:34
  84.0 1.1 copy-start.3
  87.2 11.8 %collective-permute-start.12 = (f16[256,512]{1,0:T(8,128)(2,1)S(1)}, f16[256,512]{1,0:T(8,128)(2,1)S(1)}, u32[]{:S(2)}, u32[]{:S(2)}) collective-permute-start(f16[256,512]{1,0:T(8,128)(2,1)S(1)} %multiply_convert_fusion), channel_id=1, source_target_pairs={{0,128},{16,144},{1,129},{17,145},{2,130},{18,146},{3,131},{19,147... | collective-permute-start | bytes 786440 | tf_op jit(solution)/shard_map/ppermute | solution.py:57
  100.1 8.3 %collective-permute-start.15 = (bf16[256,512]{1,0:T(8,128)(2,1)S(1)}, bf16[256,512]{1,0:T(8,128)(2,1)S(1)}, u32[]{:S(2)}, u32[]{:S(2)}) collective-permute-start(bf16[256,512]{1,0:T(8,128)(2,1)S(1)} %add_convert_fusion.refs_0_), channel_id=1, source_target_pairs={{0,128},{16,144},{1,129},{17,145},{2,130},{18,146},{3,131},{19,147... | collective-permute-start | bytes 786440 | tf_op jit(solution)/shard_map/ppermute | solution.py:57
  101.8 9.2 %collective-permute-start.16 = (bf16[256,512]{1,0:T(8,128)(2,1)S(1)}, bf16[256,512]{1,0:T(8,128)(2,1)S(1)}, u32[]{:S(2)}, u32[]{:S(2)}) collective-permute-start(bf16[256,512]{1,0:T(8,128)(2,1)S(1)} %add_convert_fusion.refs_0_), channel_id=1, source_target_pairs={{0,64},{16,80},{1,65},{17,81},{2,66},{18,82},{3,67},{19,83},{4,68}... | collective-permute-start | bytes 786440 | tf_op jit(solution)/shard_map/ppermute | solution.py:34
  101.8 14.8 %collective-permute-start.13 = (bf16[256,512]{1,0:T(8,128)(2,1)S(1)}, bf16[256,512]{1,0:T(8,128)(2,1)S(1)}, u32[]{:S(2)}, u32[]{:S(2)}) collective-permute-start(bf16[256,512]{1,0:T(8,128)(2,1)S(1)} %add_convert_fusion.refs_0_), channel_id=1, source_target_pairs={{0,32},{16,48},{1,33},{17,49},{2,34},{18,50},{3,35},{19,51},{4,36}... | collective-permute-start | bytes 786440 | tf_op jit(solution)/shard_map/ppermute | solution.py:34
  101.8 14.8 %collective-permute-start.14 = (bf16[256,512]{1,0:T(8,128)(2,1)S(1)}, bf16[256,512]{1,0:T(8,128)(2,1)S(1)}, u32[]{:S(2)}, u32[]{:S(2)}) collective-permute-start(bf16[256,512]{1,0:T(8,128)(2,1)S(1)} %add_convert_fusion.refs_0_), channel_id=1, source_target_pairs={{0,96},{16,112},{1,97},{17,113},{2,98},{18,114},{3,99},{19,115},{4... | collective-permute-start | bytes 786440 | tf_op jit(solution)/shard_map/ppermute | solution.py:34
  108.3 14.0 %collective-permute-start.17 = (bf16[256,512]{1,0:T(8,128)(2,1)S(1)}, bf16[256,512]{1,0:T(8,128)(2,1)}, u32[]{:S(2)}, u32[]{:S(2)}) collective-permute-start(bf16[256,512]{1,0:T(8,128)(2,1)S(1)} %collective-permute-done.15.refs_3_), channel_id=1, source_target_pairs={{0,32},{16,48},{1,33},{17,49},{2,34},{18,50},{3,35},{19,51},{4,36}... | collective-permute-start | bytes 786440 | tf_op jit(solution)/shard_map/ppermute | solution.py:34
  108.3 14.0 %collective-permute-start.18 = (bf16[256,512]{1,0:T(8,128)(2,1)S(1)}, bf16[256,512]{1,0:T(8,128)(2,1)}, u32[]{:S(2)}, u32[]{:S(2)}) collective-permute-start(bf16[256,512]{1,0:T(8,128)(2,1)S(1)} %collective-permute-done.15.refs_3_), channel_id=1, source_target_pairs={{0,96},{16,112},{1,97},{17,113},{2,98},{18,114},{3,99},{19,115},{4... | collective-permute-start | bytes 786440 | tf_op jit(solution)/shard_map/ppermute | solution.py:34
  111.0 11.3 %collective-permute-start.19 = (bf16[256,512]{1,0:T(8,128)(2,1)S(1)}, bf16[256,512]{1,0:T(8,128)(2,1)}, u32[]{:S(2)}, u32[]{:S(2)}) collective-permute-start(bf16[256,512]{1,0:T(8,128)(2,1)S(1)} %collective-permute-done.16.refs_4_), channel_id=1, source_target_pairs={{0,128},{16,144},{1,129},{17,145},{2,130},{18,146},{3,131},{19,147... | collective-permute-start | bytes 786440 | tf_op jit(solution)/shard_map/ppermute | solution.py:57
  122.3 1.6 %copy-start.1 = (bf16[16,256,256]{2,1,0:T(8,128)(2,1)S(1)}, bf16[16,256,256]{2,1,0:T(8,128)(2,1)}, u32[]{:S(2)}) copy-start(bf16[16,256,256]{2,1,0:T(8,128)(2,1)} %all-gather.3.cloned.1.call-done) | copy-start | bytes 6291460
  128.4 2.4 %collective-permute-start.20 = (f32[256,512]{1,0:T(8,128)S(1)}, f32[256,512]{1,0:T(8,128)S(1)}, u32[]{:S(2)}, u32[]{:S(2)}) collective-permute-start(f32[256,512]{1,0:T(8,128)S(1)} %get-tuple-element.18), channel_id=1, source_target_pairs={{0,16},{16,0},{1,17},{17,1},{2,18},{18,2},{3,19},{19,3},{4,20},{20... | collective-permute-start | bytes 1572872 | tf_op jit(solution)/shard_map/ppermute | solution.py:34
Sparse Core Ops, SparseCore 0:
  42.2 54.2 all-gather.2

commit v6 on v5

--- a/solution.py
+++ b/solution.py
@@ -163,16 +163,15 @@
 
 
 def near_moves(table, sources, rows):
-    near, away, rest = sources
+    near, away = sources
     return [
         (near, rows.at[pl.ds(table[0] * SPLIT, SPLIT)]),
         (away, rows.at[pl.ds((1 - table[0]) * SPLIT, SPLIT)]),
-        (rest.at[pl.ds(0, 2)], rows.at[pl.ds(2 * SPLIT, 2)]),
     ]
 
 
-def last_moves(table, sources, rows):
-    return [(sources[0].at[pl.ds(2, 2)], rows)]
+def rest_moves(table, sources, rows):
+    return [(source, rows.at[pl.ds(n * SPLIT, SPLIT)]) for n, source in enumerate(sources)]
 
 
 def own_moves(table, sources, rows):
@@ -182,15 +181,15 @@
     ]
 
 
-def squares_kernel(where_ref, out_rows, *refs):
-    blocks = out_rows.shape[0]
-    in_rows, refs = refs[:blocks], refs[blocks:]
+def squares_kernel(blocks, where_ref, *refs):
+    sources, refs = refs[: 2 * blocks], refs[2 * blocks :]
     totals, (outer, inner, semaphore) = refs[:2], refs[2:]
-    copies = [pltpu.make_async_copy(out_rows, outer, semaphore.at[blocks])]
+    copies = []
     for k in range(blocks):
-        copies.append(
-            pltpu.make_async_copy(in_rows[k], inner.at[where_ref[k]], semaphore.at[k])
-        )
+        for n, target in ((k, outer), (blocks + k, inner)):
+            copies.append(
+                pltpu.make_async_copy(sources[n], target.at[where_ref[n]], semaphore.at[n])
+            )
     for copy in copies:
         copy.start()
     for copy in copies:
@@ -200,7 +199,7 @@
     def _(n):
         columns = pl.ds(pl.multiple_of(n * TILE, TILE), TILE)
         for part, total_ref in enumerate(totals):
-            half = where_ref[blocks + part]
+            half = where_ref[2 * blocks + part]
             total = None
             for k in range(blocks):
                 for example in range(EXAMPLES):
@@ -215,25 +214,25 @@
 
 
 def sums_of_squares(where, out_rows, in_rows):
-    rows, tokens = out_rows.shape[2:]
+    rows, tokens = out_rows[0].shape[1:]
     width, blocks = in_rows[0].shape[1], len(in_rows)
     return pl.pallas_call(
-        squares_kernel,
+        lambda *refs: squares_kernel(blocks, *refs),
         out_shape=[jax.ShapeDtypeStruct((rows, width), jnp.float32)] * 2,
-        in_specs=[space(pltpu.SMEM)] + [space(pl.ANY)] * (1 + blocks),
+        in_specs=[space(pltpu.SMEM)] + [space(pl.ANY)] * (2 * blocks),
         out_specs=[space(pltpu.VMEM)] * 2,
         scratch_shapes=[
-            pltpu.VMEM(out_rows.shape, jnp.bfloat16),
+            pltpu.VMEM((blocks, *out_rows[0].shape), jnp.bfloat16),
             pltpu.VMEM((blocks, tokens, width), jnp.bfloat16),
-            pltpu.SemaphoreType.DMA((blocks + 1,)),
+            pltpu.SemaphoreType.DMA((2 * blocks,)),
         ],
         compiler_params=pltpu.CompilerParams(vmem_limit_bytes=TAIL_VMEM),
         cost_estimate=pl.CostEstimate(
             flops=4 * rows * width * blocks * tokens,
-            bytes_accessed=out_rows.size * 2 + rows * width * 8,
+            bytes_accessed=2**22,
             transcendentals=0,
         ),
-    )(where, out_rows, *in_rows)
+    )(where, *out_rows, *in_rows)
 
 
 def z_swap(value):
@@ -269,46 +268,60 @@
     table = jnp.stack(spots).astype(jnp.int32)
     give = (half * (1 - x) + table) * depth
     keep = ((half * x + table) * depth).astype(jnp.int32)
+    first, own_other = by_core(basis_in, dy=1), shift(basis_in, dc=1)
+    block = dot(out_grads, basis_out).astype(jnp.bfloat16).T
+    block, source = lax.optimization_barrier((block, activations))
     near = lax.dynamic_slice_in_dim(give, parity * SPLIT, SPLIT)
-    near = by_core(pieces(near.astype(jnp.int32), activations, depth), dx=1)
-    first, own_other = by_core(basis_in, dy=1), shift(basis_in, dc=1)
-    rest = pieces(give[2 * SPLIT :].astype(jnp.int32), activations, depth)
-    block = dot(out_grads, basis_out).astype(jnp.bfloat16).T
-    block = transposed(jnp.stack([block, z_swap(block)]))
-
-    first, near, rest, again, own_other = lax.optimization_barrier(
-        (first, near, rest, basis_in, own_other)
-    )
-    second, far = by_core(again, dy=NY - 1), by_core(first, dy=1)
-    rest, away = by_core(rest, dx=1), by_core(near, dz=1)
-
-    out_rows = lax.all_gather(
-        block,
-        "blk",
-        axis=0,
-        axis_index_groups=[[h * NZ + z for z in range(NZ)] for h in range(NH)],
-    )
-    flip = (b // NZ + core) % 2
+    near = by_core(pieces(near.astype(jnp.int32), source, depth), dx=1)
+    block, source = lax.optimization_barrier((jnp.stack([block, z_swap(block)]), source))
+    later = give[2 * SPLIT :].astype(jnp.int32)
+    rest_a = pieces(later[:SPLIT], source, depth)
+    rest_b = pieces(later[SPLIT:], source, depth)
+
+    first, near, rest_a, again, block, own_other = lax.optimization_barrier(
+        (first, near, rest_a, basis_in, block, own_other)
+    )
+    second, rest_a, away = by_core(again, dy=NY - 1), by_core(rest_a, dx=1), by_core(near, dz=1)
+    block, first_other = transposed(block), shift(first, dc=1)
+    second, rest_a, away, block, onward, rest_b = lax.optimization_barrier(
+        (second, rest_a, away, block, first, rest_b)
+    )
+    far, rest_b, second_other = by_core(onward, dy=1), by_core(rest_b, dx=1), shift(second, dc=1)
+
+    up1, down1 = shift(block, dz=1), shift(block, dz=NZ - 1)
+    far, up1, down1 = lax.optimization_barrier((far, up1, down1))
+    up2, down2 = shift(up1, dz=1), shift(down1, dz=NZ - 1)
+    h, z = b // NZ, b % NZ
+    flip = (h + core) % 2
     where = jnp.stack(
-        [((x + dx) % NX) * NY + (y + dy) % NY for dx, dy in ORDER] + [flip, 1 - flip]
+        [(z - step) % NZ for step in range(NZ)]
+        + [((x + dx) % NX) * NY + (y + dy) % NY for dx, dy in ORDER]
+        + [flip, 1 - flip]
     ).astype(jnp.int32)
 
-    panels = []
-    for panel in (first, second, far):
-        panels += [panel, shift(panel, dc=1)]
-    panels = [basis_in, own_other] + panels
+    panels = [basis_in, own_other, first, first_other]
+    panels += [second, second_other, far, shift(far, dc=1)]
     panels = [[panel] for panel in panels]
     parity = parity.reshape(1).astype(jnp.int32)
-    partial = product(near_moves, 3, parity, (near, away, rest), panels[:-2])
-    partial = product(last_moves, 1, parity, (rest,), panels[-2:], partial, FOLLOWED, TAIL_VMEM)
+    partial = product(near_moves, 2, parity, (near, away), panels[: 2 * SPLIT])
+    partial = product(
+        rest_moves, 2, parity, (rest_a, rest_b), panels[2 * SPLIT :], partial, FOLLOWED, TAIL_VMEM
+    )
     arrived = swap((partial * FACTOR).astype(jnp.float16))
+    arrived, up2, down2 = lax.optimization_barrier((arrived, up2, down2))
+    up3, down3 = shift(up2, dz=1), shift(down2, dz=NZ - 1)
     total = product(own_moves, len(BLOCKS), keep, (activations,), panels)
     proj_in = (total + arrived.astype(jnp.float32) * (1.0 / FACTOR)).astype(jnp.bfloat16)
 
     p_left, p_right, p_far = shift(proj_in, dy=1), shift(proj_in, dy=3), shift(proj_in, dy=2)
     p_across = swap(proj_in)
+    p_across, p_far, p_left, p_right, up3, down3 = lax.optimization_barrier(
+        (p_across, p_far, p_left, p_right, up3, down3)
+    )
     px_left, px_right = shift(p_across, dy=1), shift(p_across, dy=3)
     px_far = swap(p_far)
+    opposite = by_core(jnp.where(core == 0, up3, down3), dz=1)
+    out_rows = (block, up1, up2, up3, opposite, down3, down2, down1)
     kept, given = sums_of_squares(
         where,
         out_rows,

time: 139 us -> 140 us (level)
  between operations: 13.6 us -> 0.22 us
  waiting for transfers between devices: 34.7 us -> 47.3 us
  Pallas kernels: 23.7 us -> 26.6 us
  local copies, waits for them, and re-layouts: 4.38 us -> 2.84 us
    ppermute x10 -> x16, starting transfers between devices: 6.38 us -> 30.1 us  [shift(): return lax.ppermute(value, ('dp', 'blk'), pairs)]
    ppermute x6 -> x8, starting transfers between devices: 36.6 us -> 20.3 us  [by_core(): return lax.ppermute(value, ('dp', 'blk'), pairs)]
    ppermute x6 -> x8, waiting for transfers between devices: 15.9 us -> 23.1 us  [by_core(): return lax.ppermute(value, ('dp', 'blk'), pairs)]
    ppermute x10 -> x16, waiting for transfers between devices: 11.5 us -> 17.3 us  [shift(): return lax.ppermute(value, ('dp', 'blk'), pairs)]
    ppermute x3, starting transfers between devices: 8.14 us -> 3.62 us  [swap(): return lax.ppermute(value, ('dp', 'blk'), pairs)]
    ppermute x1, starting transfers between devices: 3.57 us -> 0.67 us  [transposed(): return lax.ppermute(block, ('dp', 'blk'), pairs)]
    pallas_call x2 -> x3, Pallas kernels: 5.63 us -> 8.14 us  [pieces(): pl.pallas_call(pieces_kernel, out_shape=jax.ShapeDtypeStruct(shape, activ...]
  transfers between devices with their start and end apart: 22 -> 29, of which waited for: 7 -> 11; matrix products, arithmetic and copies ran while one was open for 4% -> 3% of each run, Pallas kernels for 12% -> 16%
where the time goes in v6:
time: 140 us; the launch traced here: 139 us
  starting transfers between devices  56.2 us (40%)
  waiting for transfers between devices  47.3 us (34%)
  Pallas kernels  26.6 us (19%)
  other arithmetic  3.32 us (2%)
  local copies, waits for them, and re-layouts  2.84 us (2%)
  matrix products  2.34 us (2%)
    ppermute x16, starting transfers between devices, shift(): return lax.ppermute(value, ('dp', 'blk'), pairs)  30.1 us
    ppermute x8, waiting for transfers between devices, by_core(): return lax.ppermute(value, ('dp', 'blk'), pairs)  23.1 us
    ppermute x8, starting transfers between devices, by_core(): return lax.ppermute(value, ('dp', 'blk'), pairs)  20.3 us
    ppermute x16, waiting for transfers between devices, shift(): return lax.ppermute(value, ('dp', 'blk'), pairs)  17.3 us
    pallas_call x3, Pallas kernels, product(): pl.pallas_call(lambda *refs: product_kernel(moves, layout, *refs), out_sh...  13.5 us
    pallas_call x3, Pallas kernels, pieces(): pl.pallas_call(pieces_kernel, out_shape=jax.ShapeDtypeStruct(shape, activ...  8.14 us
    pallas_call x1, Pallas kernels, sums_of_squares(): pl.pallas_call(lambda *refs: squares_kernel(blocks, *refs), out_shape=[ja...  4.91 us
    ppermute x3, starting transfers between devices, swap(): return lax.ppermute(value, ('dp', 'blk'), pairs)  3.62 us
  transfers between devices with their start and end apart: 29, of which 11 were waited for; matrix products, arithmetic and copies ran while one was open for 3% of the time, Pallas kernels for 16%

profile of v6, /device:TPU:1, one launch (start us, length us, event | category | flops | bytes accessed | tf_op | source)
XLA Modules:
  0.0 138.9 jit_solution(1891709481264563537)
XLA Ops:
  0.0 3.6 %collective-permute-start = (bf16[896,512]{1,0:T(8,128)(2,1)}, bf16[896,512]{1,0:T(8,128)(2,1)}, u32[]{:S(2)}, u32[]{:S(2)}) collective-permute-start(bf16[896,512]{1,0:T(8,128)(2,1)} %refs_2_.1), channel_id=1, source_target_pairs={{0,32},{16,112},{1,33},{17,113},{2,34},{18,114},{3,35},{19,115},{4... | collective-permute-start | bytes 2752520 | tf_op jit(solution)/shard_map/ppermute | solution.py:46
  3.6 2.3 %convolution_convert_fusion = bf16[256,256]{1,0:T(8,128)(2,1)S(1)} fusion(bf16[4096,256]{1,0:T(8,128)(2,1)S(1)} %copy-done, bf16[256,4096]{1,0:T(8,128)(2,1)} %param.5), kind=kOutput, calls=%fused_computation | convolution fusion | flops 536936448 | bytes 4325376 | tf_op jit(solution)/shard_map/dot_general | solution.py:61
  7.2 2.8 %shard_map.46 = bf16[2,256,896]{2,1,0:T(8,128)(2,1)} custom-call(s32[2]{0:T(128)} %get-tuple-element.69.columns_ref, bf16[256,14336]{1,0:T(8,128)(2,1)} %refs_1_.1), custom_call_target="tpu_custom_call" | custom-call | bytes 4194304 | tf_op jit(solution)/shard_map/pallas_call | solution.py:91
  10.0 2.6 %collective-permute-start.1 = (bf16[2,256,896]{2,1,0:T(8,128)(2,1)}, bf16[2,256,896]{2,1,0:T(8,128)(2,1)}, u32[]{:S(2)}, u32[]{:S(2)}) collective-permute-start(bf16[2,256,896]{2,1,0:T(8,128)(2,1)} %shard_map.46), channel_id=1, source_target_pairs={{0,128},{16,152},{1,129},{17,153},{2,130},{18,154},{3,131},{19,155... | collective-permute-start | bytes 2752520 | tf_op jit(solution)/shard_map/ppermute | solution.py:46
  12.5 1.6 %collective-permute-start.2 = (bf16[256,256]{1,0:T(8,128)(2,1)S(1)}, bf16[256,256]{1,0:T(8,128)(2,1)S(1)}, u32[]{:S(2)}, u32[]{:S(2)}) collective-permute-start(bf16[256,256]{1,0:T(8,128)(2,1)S(1)} %convolution_convert_fusion), channel_id=1, source_target_pairs={{0,1},{1,0},{2,3},{3,2},{4,5},{5,4},{6,7},{7,6},{8,9},{9,8},{10,11... | collective-permute-start | bytes 393224 | tf_op jit(solution)/shard_map/ppermute | solution.py:243
  14.2 3.4 %collective-permute-done.2 = bf16[256,256]{1,0:T(8,128)(2,1)S(1)} collective-permute-done((bf16[256,256]{1,0:T(8,128)(2,1)S(1)}, bf16[256,256]{1,0:T(8,128)(2,1)S(1)}, u32[]{:S(2)}, u32[]{:S(2)}) %collective-permute-start.2) | collective-permute-done | bytes 131104 | tf_op jit(solution)/shard_map/ppermute | solution.py:243
  17.6 2.6 %shard_map.47 = bf16[2,256,896]{2,1,0:T(8,128)(2,1)} custom-call(s32[2]{0:T(128)} %get-tuple-element.68.columns_ref, bf16[256,14336]{1,0:T(8,128)(2,1)} %refs_1_.1), custom_call_target="tpu_custom_call" | custom-call | bytes 4194304 | tf_op jit(solution)/shard_map/pallas_call | solution.py:91
  20.2 2.9 %collective-permute-done.1.refs_1_ = bf16[2,256,896]{2,1,0:T(8,128)(2,1)} collective-permute-done((bf16[2,256,896]{2,1,0:T(8,128)(2,1)}, bf16[2,256,896]{2,1,0:T(8,128)(2,1)}, u32[]{:S(2)}, u32[]{:S(2)}) %collective-permute-start.1) | collective-permute-done | bytes 917536 | tf_op jit(solution)/shard_map/ppermute | solution.py:46
  23.3 3.1 %collective-permute-start.5 = (bf16[2,256,896]{2,1,0:T(8,128)(2,1)}, bf16[2,256,896]{2,1,0:T(8,128)(2,1)}, u32[]{:S(2)}, u32[]{:S(2)}) collective-permute-start(bf16[2,256,896]{2,1,0:T(8,128)(2,1)} %shard_map.47), channel_id=1, source_target_pairs={{0,128},{16,152},{1,129},{17,153},{2,130},{18,154},{3,131},{19,155... | collective-permute-start | bytes 2752520 | tf_op jit(solution)/shard_map/ppermute | solution.py:46
  26.5 5.6 %collective-permute-start.6 = (bf16[2,256,896]{2,1,0:T(8,128)(2,1)}, bf16[2,256,896]{2,1,0:T(8,128)(2,1)}, u32[]{:S(2)}, u32[]{:S(2)}) collective-permute-start(bf16[2,256,896]{2,1,0:T(8,128)(2,1)} %collective-permute-done.1.refs_1_), channel_id=1, source_target_pairs={{0,1},{16,23},{1,2},{17,16},{2,3},{18,17},{3,4},{19,18},{4,5},{20,... | collective-permute-start | bytes 2752520 | tf_op jit(solution)/shard_map/ppermute | solution.py:46
  32.7 2.7 %shard_map.48 = bf16[2,256,896]{2,1,0:T(8,128)(2,1)} custom-call(s32[2]{0:T(128)} %get-tuple-element.67.columns_ref, bf16[256,14336]{1,0:T(8,128)(2,1)} %refs_1_.1), custom_call_target="tpu_custom_call" | custom-call | bytes 4194304 | tf_op jit(solution)/shard_map/pallas_call | solution.py:91
  35.5 1.8 %collective-permute-done.4.refs_3_.refs_6_ = bf16[896,512]{1,0:T(8,128)(2,1)S(1)} collective-permute-done((bf16[896,512]{1,0:T(8,128)(2,1)}, bf16[896,512]{1,0:T(8,128)(2,1)S(1)}, u32[]{:S(2)}, u32[]{:S(2)}) %collective-permute-start.4) | collective-permute-done | bytes 917536 | tf_op jit(solution)/shard_map/ppermute | solution.py:46
  37.3 17.2 %collective-permute-done.6.refs_2_ = bf16[2,256,896]{2,1,0:T(8,128)(2,1)} collective-permute-done((bf16[2,256,896]{2,1,0:T(8,128)(2,1)}, bf16[2,256,896]{2,1,0:T(8,128)(2,1)}, u32[]{:S(2)}, u32[]{:S(2)}) %collective-permute-start.6) | collective-permute-done | bytes 917536 | tf_op jit(solution)/shard_map/ppermute | solution.py:46
  54.4 2.9 %collective-permute-start.8 = (bf16[896,512]{1,0:T(8,128)(2,1)}, bf16[896,512]{1,0:T(8,128)(2,1)}, u32[]{:S(2)}, u32[]{:S(2)}) collective-permute-start(bf16[896,512]{1,0:T(8,128)(2,1)} %collective-permute-done.refs_5_.refs_4_), channel_id=1, source_target_pairs={{0,32},{16,112},{1,33},{17,113},{2,34},{18,114},{3,35},{19,115},{4... | collective-permute-start | bytes 2752520 | tf_op jit(solution)/shard_map/ppermute | solution.py:46
  57.9 12.3 %collective-permute-start.10 = (bf16[2,256,256]{2,1,0:T(8,128)(2,1)S(1)}, bf16[2,256,256]{2,1,0:T(8,128)(2,1)S(1)}, u32[]{:S(2)}, u32[]{:S(2)}) collective-permute-start(bf16[2,256,256]{2,1,0:T(8,128)(2,1)S(1)} %collective-permute-done.7.refs_1_), channel_id=1, source_target_pairs={{0,7},{16,23},{1,0},{17,16},{2,1},{18,17},{3,2},{19,18},{4,3},{20,... | collective-permute-start | bytes 786440 | tf_op jit(solution)/shard_map/ppermute | solution.py:34
  70.1 1.7 %collective-permute-start.11 = (bf16[2,256,896]{2,1,0:T(8,128)(2,1)}, bf16[2,256,896]{2,1,0:T(8,128)(2,1)}, u32[]{:S(2)}, u32[]{:S(2)}) collective-permute-start(bf16[2,256,896]{2,1,0:T(8,128)(2,1)} %shard_map.48), channel_id=1, source_target_pairs={{0,128},{16,152},{1,129},{17,153},{2,130},{18,154},{3,131},{19,155... | collective-permute-start | bytes 2752520 | tf_op jit(solution)/shard_map/ppermute | solution.py:46
  71.9 4.0 %collective-permute-done.9.refs_2_ = bf16[2,256,256]{2,1,0:T(8,128)(2,1)S(1)} collective-permute-done((bf16[2,256,256]{2,1,0:T(8,128)(2,1)S(1)}, bf16[2,256,256]{2,1,0:T(8,128)(2,1)S(1)}, u32[]{:S(2)}, u32[]{:S(2)}) %collective-permute-start.9) | collective-permute-done | bytes 262176 | tf_op jit(solution)/shard_map/ppermute | solution.py:34
  75.9 4.8 %collective-permute-start.13 = (bf16[896,512]{1,0:T(8,128)(2,1)}, bf16[896,512]{1,0:T(8,128)(2,1)}, u32[]{:S(2)}, u32[]{:S(2)}) collective-permute-start(bf16[896,512]{1,0:T(8,128)(2,1)} %collective-permute-done.8.refs_5_.refs_8_), channel_id=1, source_target_pairs={{0,16},{16,0},{1,17},{17,1},{2,18},{18,2},{3,19},{19,3},{4,20},{20... | collective-permute-start | bytes 2752520 | tf_op jit(solution)/shard_map/ppermute | solution.py:34
  80.7 4.0 %shard_map.49.refs_7_ = f32[256,512]{1,0:T(8,128)} custom-call(s32[1]{0:T(128)} %bitcast.28.refs_0_, bf16[2,256,896]{2,1,0:T(8,128)(2,1)} %collective-permute-done.1.refs_1_, bf16[2,256,896]{2,1,0:T(8,128)(2,1)} %collective-permute-done.6.refs_2_, bf16[896,512]{1,0:T(8,128)(2,1)} %refs_2_.1, bf16[896,512]{1,0:T(8,128)(2,1)} %collective-permute-done.3.refs_4_.refs_3_, ...), custom_call_target="tpu_custom_call" | custom-call | flops 939524096 | bytes 4194304 | tf_op jit(solution)/shard_map/pallas_call | solution.py:144
  84.9 2.7 %collective-permute-start.17 = (bf16[2,256,256]{2,1,0:T(8,128)(2,1)S(1)}, bf16[2,256,256]{2,1,0:T(8,128)(2,1)}, u32[]{:S(2)}, u32[]{:S(2)}) collective-permute-start(bf16[2,256,256]{2,1,0:T(8,128)(2,1)S(1)} %collective-permute-done.10.refs_8_), channel_id=1, source_target_pairs={{0,7},{16,23},{1,0},{17,16},{2,1},{18,17},{3,2},{19,18},{4,3},{20,... | collective-permute-start | bytes 786440 | tf_op jit(solution)/shard_map/ppermute | solution.py:34
  88.7 2.9 %shard_map.50 = f32[256,512]{1,0:T(8,128)S(1)} custom-call(s32[1]{0:T(128)} %bitcast.28.refs_0_, bf16[2,256,896]{2,1,0:T(8,128)(2,1)} %collective-permute-done.5.refs_1_, bf16[2,256,896]{2,1,0:T(8,128)(2,1)} %collective-permute-done.11.refs_2_, bf16[896,512]{1,0:T(8,128)(2,1)S(1)} %collective-permute-done.4.refs_3_.refs_6_, ...), custom_call_target="tpu_custom_call" | custom-call | flops 6939524096 | bytes 4194304 | tf_op jit(solution)/shard_map/pallas_call | solution.py:144
  91.7 2.0 %collective-permute-start.15 = (f16[256,512]{1,0:T(8,128)(2,1)S(1)}, f16[256,512]{1,0:T(8,128)(2,1)S(1)}, u32[]{:S(2)}, u32[]{:S(2)}) collective-permute-start(f16[256,512]{1,0:T(8,128)(2,1)S(1)} %multiply_convert_fusion), channel_id=1, source_target_pairs={{0,128},{16,144},{1,129},{17,145},{2,130},{18,146},{3,131},{19,147... | collective-permute-start | bytes 786440 | tf_op jit(solution)/shard_map/ppermute | solution.py:57
  93.7 6.6 %shard_map.51 = f32[256,512]{1,0:T(8,128)} custom-call(s32[8]{0:T(128)} %get-tuple-element.65.refs_0_, bf16[256,14336]{1,0:T(8,128)(2,1)} %refs_1_.1, bf16[896,512]{1,0:T(8,128)(2,1)} %refs_2_.1, bf16[896,512]{1,0:T(8,128)(2,1)} %collective-permute-done.3.refs_4_.refs_3_, bf16[896,512]{1,0:T(8,128)(2,1)} %collective-permute-done.refs_5_.refs_4_, ...), custom_call_target="tpu_custom_call" | custom-call | flops 1879048192 | bytes 4194304 | tf_op jit(solution)/shard_map/pallas_call | solution.py:144
  103.4 2.2 %collective-permute-start.21 = (bf16[256,512]{1,0:T(8,128)(2,1)S(1)}, bf16[256,512]{1,0:T(8,128)(2,1)}, u32[]{:S(2)}, u32[]{:S(2)}) collective-permute-start(bf16[256,512]{1,0:T(8,128)(2,1)S(1)} %add_convert_fusion.refs_9_), channel_id=1, source_target_pairs={{0,96},{16,112},{1,97},{17,113},{2,98},{18,114},{3,99},{19,115},{4... | collective-permute-start | bytes 786440 | tf_op jit(solution)/shard_map/ppermute | solution.py:34
  105.7 2.7 %collective-permute-done.18.refs_12_ = bf16[256,512]{1,0:T(8,128)(2,1)} collective-permute-done((bf16[256,512]{1,0:T(8,128)(2,1)S(1)}, bf16[256,512]{1,0:T(8,128)(2,1)}, u32[]{:S(2)}, u32[]{:S(2)}) %collective-permute-start.18) | collective-permute-done | bytes 262176 | tf_op jit(solution)/shard_map/ppermute | solution.py:57
  109.4 7.9 %collective-permute-done.20.refs_10_ = bf16[256,512]{1,0:T(8,128)(2,1)} collective-permute-done((bf16[256,512]{1,0:T(8,128)(2,1)S(1)}, bf16[256,512]{1,0:T(8,128)(2,1)}, u32[]{:S(2)}, u32[]{:S(2)}) %collective-permute-start.20) | collective-permute-done | bytes 262176 | tf_op jit(solution)/shard_map/ppermute | solution.py:34
  118.8 2.7 %collective-permute-start.26 = (bf16[256,512]{1,0:T(8,128)(2,1)}, bf16[256,512]{1,0:T(8,128)(2,1)}, u32[]{:S(2)}, u32[]{:S(2)}) collective-permute-start(bf16[256,512]{1,0:T(8,128)(2,1)} %collective-permute-done.18.refs_12_), channel_id=1, source_target_pairs={{0,96},{16,112},{1,97},{17,113},{2,98},{18,114},{3,99},{19,115},{4... | collective-permute-start | bytes 786440 | tf_op jit(solution)/shard_map/ppermute | solution.py:34
  122.7 1.2 collective-permute-done.24.refs_5_
  123.9 3.8 %collective-permute-done.25.refs_14_ = bf16[256,512]{1,0:T(8,128)(2,1)} collective-permute-done((bf16[256,512]{1,0:T(8,128)(2,1)}, bf16[256,512]{1,0:T(8,128)(2,1)}, u32[]{:S(2)}, u32[]{:S(2)}) %collective-permute-start.25) | collective-permute-done | bytes 262176 | tf_op jit(solution)/shard_map/ppermute | solution.py:34
  129.5 4.9 %shard_map.52 = (f32[256,512]{1,0:T(8,128)S(1)}, f32[256,512]{1,0:T(8,128)S(1)}) custom-call(s32[18]{0:T(128)S(1)} %stack.111.refs_0_, bf16[2,256,256]{2,1,0:T(8,128)(2,1)S(1)} %collective-permute-done.7.refs_1_, bf16[2,256,256]{2,1,0:T(8,128)(2,1)S(1)} %collective-permute-done.9.refs_2_, bf16[2,256,256]{2,1,0:T(8,128)(2,1)} %collective-permute-done.16.refs_3_, ...), custom_call_target="tpu_custom_call" | custom-call | flops 1073741824 | bytes 4194304 | tf_op jit(solution)/shard_map/pallas_call | solution.py:219
  134.4 2.0 %collective-permute-start.28 = (f32[256,512]{1,0:T(8,128)S(1)}, f32[256,512]{1,0:T(8,128)S(1)}, u32[]{:S(2)}, u32[]{:S(2)}) collective-permute-start(f32[256,512]{1,0:T(8,128)S(1)} %get-tuple-element.64), channel_id=1, source_target_pairs={{0,16},{16,0},{1,17},{17,1},{2,18},{18,2},{3,19},{19,3},{4,20},{20... | collective-permute-start | bytes 1572872 | tf_op jit(solution)/shard_map/ppermute | solution.py:34
  136.5 1.5 %collective-permute-done.28 = f32[256,512]{1,0:T(8,128)S(1)} collective-permute-done((f32[256,512]{1,0:T(8,128)S(1)}, f32[256,512]{1,0:T(8,128)S(1)}, u32[]{:S(2)}, u32[]{:S(2)}) %collective-permute-start.28) | collective-permute-done | bytes 524320 | tf_op jit(solution)/shard_map/ppermute | solution.py:34
  (55 shorter events, 13.6 us)
Async XLA Ops:
  0.0 20.2 %collective-permute-start = (bf16[896,512]{1,0:T(8,128)(2,1)}, bf16[896,512]{1,0:T(8,128)(2,1)}, u32[]{:S(2)}, u32[]{:S(2)}) collective-permute-start(bf16[896,512]{1,0:T(8,128)(2,1)} %refs_2_.1), channel_id=1, source_target_pairs={{0,32},{16,112},{1,33},{17,113},{2,34},{18,114},{3,35},{19,115},{4... | collective-permute-start | bytes 2752520 | tf_op jit(solution)/shard_map/ppermute | solution.py:46
  7.2 5.3 %copy-start.5 = (bf16[896,512]{1,0:T(8,128)(2,1)S(1)}, bf16[896,512]{1,0:T(8,128)(2,1)}, u32[]{:S(2)}) copy-start(bf16[896,512]{1,0:T(8,128)(2,1)} %refs_2_.1) | copy-start | bytes 2752516
  10.0 13.2 %collective-permute-start.1 = (bf16[2,256,896]{2,1,0:T(8,128)(2,1)}, bf16[2,256,896]{2,1,0:T(8,128)(2,1)}, u32[]{:S(2)}, u32[]{:S(2)}) collective-permute-start(bf16[2,256,896]{2,1,0:T(8,128)(2,1)} %shard_map.46), channel_id=1, source_target_pairs={{0,128},{16,152},{1,129},{17,153},{2,130},{18,154},{3,131},{19,155... | collective-permute-start | bytes 2752520 | tf_op jit(solution)/shard_map/ppermute | solution.py:46
  12.5 10.7 %collective-permute-start.3 = (bf16[896,512]{1,0:T(8,128)(2,1)S(1)}, bf16[896,512]{1,0:T(8,128)(2,1)}, u32[]{:S(2)}, u32[]{:S(2)}) collective-permute-start(bf16[896,512]{1,0:T(8,128)(2,1)S(1)} %copy-done.5), channel_id=1, source_target_pairs={{0,16},{16,0},{1,17},{17,1},{2,18},{18,2},{3,19},{19,3},{4,20},{20... | collective-permute-start | bytes 2752520 | tf_op jit(solution)/shard_map/ppermute | solution.py:34
  12.5 5.0 %collective-permute-start.2 = (bf16[256,256]{1,0:T(8,128)(2,1)S(1)}, bf16[256,256]{1,0:T(8,128)(2,1)S(1)}, u32[]{:S(2)}, u32[]{:S(2)}) collective-permute-start(bf16[256,256]{1,0:T(8,128)(2,1)S(1)} %convolution_convert_fusion), channel_id=1, source_target_pairs={{0,1},{1,0},{2,3},{3,2},{4,5},{5,4},{6,7},{7,6},{8,9},{9,8},{10,11... | collective-permute-start | bytes 393224 | tf_op jit(solution)/shard_map/ppermute | solution.py:243
  23.2 14.1 %collective-permute-start.4 = (bf16[896,512]{1,0:T(8,128)(2,1)}, bf16[896,512]{1,0:T(8,128)(2,1)S(1)}, u32[]{:S(2)}, u32[]{:S(2)}) collective-permute-start(bf16[896,512]{1,0:T(8,128)(2,1)} %refs_2_.1), channel_id=1, source_target_pairs={{0,96},{16,48},{1,97},{17,49},{2,98},{18,50},{3,99},{19,51},{4,100... | collective-permute-start | bytes 2752520 | tf_op jit(solution)/shard_map/ppermute | solution.py:46
  23.3 13.9 %collective-permute-start.5 = (bf16[2,256,896]{2,1,0:T(8,128)(2,1)}, bf16[2,256,896]{2,1,0:T(8,128)(2,1)}, u32[]{:S(2)}, u32[]{:S(2)}) collective-permute-start(bf16[2,256,896]{2,1,0:T(8,128)(2,1)} %shard_map.47), channel_id=1, source_target_pairs={{0,128},{16,152},{1,129},{17,153},{2,130},{18,154},{3,131},{19,155... | collective-permute-start | bytes 2752520 | tf_op jit(solution)/shard_map/ppermute | solution.py:46
  26.5 28.0 %collective-permute-start.6 = (bf16[2,256,896]{2,1,0:T(8,128)(2,1)}, bf16[2,256,896]{2,1,0:T(8,128)(2,1)}, u32[]{:S(2)}, u32[]{:S(2)}) collective-permute-start(bf16[2,256,896]{2,1,0:T(8,128)(2,1)} %collective-permute-done.1.refs_1_), channel_id=1, source_target_pairs={{0,1},{16,23},{1,2},{17,16},{2,3},{18,17},{3,4},{19,18},{4,5},{20,... | collective-permute-start | bytes 2752520 | tf_op jit(solution)/shard_map/ppermute | solution.py:46
  32.0 3.4 %collective-permute-start.7 = (bf16[2,256,256]{2,1,0:T(8,128)(2,1)S(1)}, bf16[2,256,256]{2,1,0:T(8,128)(2,1)S(1)}, u32[]{:S(2)}, u32[]{:S(2)}) collective-permute-start(bf16[2,256,256]{2,1,0:T(8,128)(2,1)S(1)} %pad_maximum_fusion), channel_id=1, source_target_pairs={{0,0},{1,8},{2,32},{3,40},{4,64},{5,72},{6,96},{7,104},{8,128},{9,... | collective-permute-start | bytes 786440 | tf_op jit(solution)/shard_map/ppermute | solution.py:255
  37.2 50.4 %copy-start.1 = (bf16[896,512]{1,0:T(8,128)(2,1)}, bf16[896,512]{1,0:T(8,128)(2,1)S(1)}, u32[]{:S(2)}) copy-start(bf16[896,512]{1,0:T(8,128)(2,1)S(1)} %collective-permute-done.4.refs_3_.refs_6_) | copy-start | bytes 2752516
  54.4 21.5 %collective-permute-start.8 = (bf16[896,512]{1,0:T(8,128)(2,1)}, bf16[896,512]{1,0:T(8,128)(2,1)}, u32[]{:S(2)}, u32[]{:S(2)}) collective-permute-start(bf16[896,512]{1,0:T(8,128)(2,1)} %collective-permute-done.refs_5_.refs_4_), channel_id=1, source_target_pairs={{0,32},{16,112},{1,33},{17,113},{2,34},{18,114},{3,35},{19,115},{4... | collective-permute-start | bytes 2752520 | tf_op jit(solution)/shard_map/ppermute | solution.py:46
  57.3 18.6 %collective-permute-start.9 = (bf16[2,256,256]{2,1,0:T(8,128)(2,1)S(1)}, bf16[2,256,256]{2,1,0:T(8,128)(2,1)S(1)}, u32[]{:S(2)}, u32[]{:S(2)}) collective-permute-start(bf16[2,256,256]{2,1,0:T(8,128)(2,1)S(1)} %collective-permute-done.7.refs_1_), channel_id=1, source_target_pairs={{0,1},{16,17},{1,2},{17,18},{2,3},{18,19},{3,4},{19,20},{4,5},{20,... | collective-permute-start | bytes 786440 | tf_op jit(solution)/shard_map/ppermute | solution.py:34
  57.9 18.0 %collective-permute-start.10 = (bf16[2,256,256]{2,1,0:T(8,128)(2,1)S(1)}, bf16[2,256,256]{2,1,0:T(8,128)(2,1)S(1)}, u32[]{:S(2)}, u32[]{:S(2)}) collective-permute-start(bf16[2,256,256]{2,1,0:T(8,128)(2,1)S(1)} %collective-permute-done.7.refs_1_), channel_id=1, source_target_pairs={{0,7},{16,23},{1,0},{17,16},{2,1},{18,17},{3,2},{19,18},{4,3},{20,... | collective-permute-start | bytes 786440 | tf_op jit(solution)/shard_map/ppermute | solution.py:34
  70.1 10.6 %collective-permute-start.14 = (bf16[896,512]{1,0:T(8,128)(2,1)}, bf16[896,512]{1,0:T(8,128)(2,1)}, u32[]{:S(2)}, u32[]{:S(2)}) collective-permute-start(bf16[896,512]{1,0:T(8,128)(2,1)} %collective-permute-done.refs_5_.refs_4_), channel_id=1, source_target_pairs={{0,16},{16,0},{1,17},{17,1},{2,18},{18,2},{3,19},{19,3},{4,20},{20... | collective-permute-start | bytes 2752520 | tf_op jit(solution)/shard_map/ppermute | solution.py:34
  70.1 17.5 %collective-permute-start.11 = (bf16[2,256,896]{2,1,0:T(8,128)(2,1)}, bf16[2,256,896]{2,1,0:T(8,128)(2,1)}, u32[]{:S(2)}, u32[]{:S(2)}) collective-permute-start(bf16[2,256,896]{2,1,0:T(8,128)(2,1)} %shard_map.48), channel_id=1, source_target_pairs={{0,128},{16,152},{1,129},{17,153},{2,130},{18,154},{3,131},{19,155... | collective-permute-start | bytes 2752520 | tf_op jit(solution)/shard_map/ppermute | solution.py:46
  75.8 11.7 %collective-permute-start.12 = (bf16[896,512]{1,0:T(8,128)(2,1)S(1)}, bf16[896,512]{1,0:T(8,128)(2,1)}, u32[]{:S(2)}, u32[]{:S(2)}) collective-permute-start(bf16[896,512]{1,0:T(8,128)(2,1)S(1)} %collective-permute-done.4.refs_3_.refs_6_), channel_id=1, source_target_pairs={{0,16},{16,0},{1,17},{17,1},{2,18},{18,2},{3,19},{19,3},{4,20},{20... | collective-permute-start | bytes 2752520 | tf_op jit(solution)/shard_map/ppermute | solution.py:34
  75.9 9.1 %copy-start.3 = (bf16[2,256,256]{2,1,0:T(8,128)(2,1)}, bf16[2,256,256]{2,1,0:T(8,128)(2,1)S(1)}, u32[]{:S(2)}) copy-start(bf16[2,256,256]{2,1,0:T(8,128)(2,1)S(1)} %collective-permute-done.10.refs_8_) | copy-start | bytes 786436
  75.9 11.7 %collective-permute-start.13 = (bf16[896,512]{1,0:T(8,128)(2,1)}, bf16[896,512]{1,0:T(8,128)(2,1)}, u32[]{:S(2)}, u32[]{:S(2)}) collective-permute-start(bf16[896,512]{1,0:T(8,128)(2,1)} %collective-permute-done.8.refs_5_.refs_8_), channel_id=1, source_target_pairs={{0,16},{16,0},{1,17},{17,1},{2,18},{18,2},{3,19},{19,3},{4,20},{20... | collective-permute-start | bytes 2752520 | tf_op jit(solution)/shard_map/ppermute | solution.py:34
  84.7 15.6 %collective-permute-start.16 = (bf16[2,256,256]{2,1,0:T(8,128)(2,1)S(1)}, bf16[2,256,256]{2,1,0:T(8,128)(2,1)}, u32[]{:S(2)}, u32[]{:S(2)}) collective-permute-start(bf16[2,256,256]{2,1,0:T(8,128)(2,1)S(1)} %collective-permute-done.9.refs_2_), channel_id=1, source_target_pairs={{0,1},{16,17},{1,2},{17,18},{2,3},{18,19},{3,4},{19,20},{4,5},{20,... | collective-permute-start | bytes 786440 | tf_op jit(solution)/shard_map/ppermute | solution.py:34
  84.9 15.4 %collective-permute-start.17 = (bf16[2,256,256]{2,1,0:T(8,128)(2,1)S(1)}, bf16[2,256,256]{2,1,0:T(8,128)(2,1)}, u32[]{:S(2)}, u32[]{:S(2)}) collective-permute-start(bf16[2,256,256]{2,1,0:T(8,128)(2,1)S(1)} %collective-permute-done.10.refs_8_), channel_id=1, source_target_pairs={{0,7},{16,23},{1,0},{17,16},{2,1},{18,17},{3,2},{19,18},{4,3},{20,... | collective-permute-start | bytes 786440 | tf_op jit(solution)/shard_map/ppermute | solution.py:34
  91.7 8.6 %collective-permute-start.15 = (f16[256,512]{1,0:T(8,128)(2,1)S(1)}, f16[256,512]{1,0:T(8,128)(2,1)S(1)}, u32[]{:S(2)}, u32[]{:S(2)}) collective-permute-start(f16[256,512]{1,0:T(8,128)(2,1)S(1)} %multiply_convert_fusion), channel_id=1, source_target_pairs={{0,128},{16,144},{1,129},{17,145},{2,130},{18,146},{3,131},{19,147... | collective-permute-start | bytes 786440 | tf_op jit(solution)/shard_map/ppermute | solution.py:57
  101.4 6.9 %collective-permute-start.18 = (bf16[256,512]{1,0:T(8,128)(2,1)S(1)}, bf16[256,512]{1,0:T(8,128)(2,1)}, u32[]{:S(2)}, u32[]{:S(2)}) collective-permute-start(bf16[256,512]{1,0:T(8,128)(2,1)S(1)} %add_convert_fusion.refs_9_), channel_id=1, source_target_pairs={{0,128},{16,144},{1,129},{17,145},{2,130},{18,146},{3,131},{19,147... | collective-permute-start | bytes 786440 | tf_op jit(solution)/shard_map/ppermute | solution.py:57
  101.9 7.5 %collective-permute-start.19 = (bf16[256,512]{1,0:T(8,128)(2,1)S(1)}, bf16[256,512]{1,0:T(8,128)(2,1)}, u32[]{:S(2)}, u32[]{:S(2)}) collective-permute-start(bf16[256,512]{1,0:T(8,128)(2,1)S(1)} %add_convert_fusion.refs_9_), channel_id=1, source_target_pairs={{0,64},{16,80},{1,65},{17,81},{2,66},{18,82},{3,67},{19,83},{4,68}... | collective-permute-start | bytes 786440 | tf_op jit(solution)/shard_map/ppermute | solution.py:34
  103.0 14.4 %collective-permute-start.20 = (bf16[256,512]{1,0:T(8,128)(2,1)S(1)}, bf16[256,512]{1,0:T(8,128)(2,1)}, u32[]{:S(2)}, u32[]{:S(2)}) collective-permute-start(bf16[256,512]{1,0:T(8,128)(2,1)S(1)} %add_convert_fusion.refs_9_), channel_id=1, source_target_pairs={{0,32},{16,48},{1,33},{17,49},{2,34},{18,50},{3,35},{19,51},{4,36}... | collective-permute-start | bytes 786440 | tf_op jit(solution)/shard_map/ppermute | solution.py:34
  103.4 13.9 %collective-permute-start.21 = (bf16[256,512]{1,0:T(8,128)(2,1)S(1)}, bf16[256,512]{1,0:T(8,128)(2,1)}, u32[]{:S(2)}, u32[]{:S(2)}) collective-permute-start(bf16[256,512]{1,0:T(8,128)(2,1)S(1)} %add_convert_fusion.refs_9_), channel_id=1, source_target_pairs={{0,96},{16,112},{1,97},{17,113},{2,98},{18,114},{3,99},{19,115},{4... | collective-permute-start | bytes 786440 | tf_op jit(solution)/shard_map/ppermute | solution.py:34
  105.7 11.7 %collective-permute-start.22 = (bf16[2,256,256]{2,1,0:T(8,128)(2,1)}, bf16[2,256,256]{2,1,0:T(8,128)(2,1)S(1)}, u32[]{:S(2)}, u32[]{:S(2)}) collective-permute-start(bf16[2,256,256]{2,1,0:T(8,128)(2,1)} %collective-permute-done.16.refs_3_), channel_id=1, source_target_pairs={{0,1},{16,17},{1,2},{17,18},{2,3},{18,19},{3,4},{19,20},{4,5},{20,... | collective-permute-start | bytes 786440 | tf_op jit(solution)/shard_map/ppermute | solution.py:34
  108.4 9.0 %collective-permute-start.23 = (bf16[2,256,256]{2,1,0:T(8,128)(2,1)}, bf16[2,256,256]{2,1,0:T(8,128)(2,1)S(1)}, u32[]{:S(2)}, u32[]{:S(2)}) collective-permute-start(bf16[2,256,256]{2,1,0:T(8,128)(2,1)} %collective-permute-done.17.refs_7_), channel_id=1, source_target_pairs={{0,7},{16,23},{1,0},{17,16},{2,1},{18,17},{3,2},{19,18},{4,3},{20,... | collective-permute-start | bytes 786440 | tf_op jit(solution)/shard_map/ppermute | solution.py:34
  118.1 5.8 %collective-permute-start.24 = (bf16[2,256,256]{2,1,0:T(8,128)(2,1)}, bf16[2,256,256]{2,1,0:T(8,128)(2,1)}, u32[]{:S(2)}, u32[]{:S(2)}) collective-permute-start(bf16[2,256,256]{2,1,0:T(8,128)(2,1)} %broadcast_select_fusion), channel_id=1, source_target_pairs={{0,1},{16,23},{1,2},{17,16},{2,3},{18,17},{3,4},{19,18},{4,5},{20,... | collective-permute-start | bytes 786440 | tf_op jit(solution)/shard_map/ppermute | solution.py:46
  118.8 9.0 %collective-permute-start.25 = (bf16[256,512]{1,0:T(8,128)(2,1)}, bf16[256,512]{1,0:T(8,128)(2,1)}, u32[]{:S(2)}, u32[]{:S(2)}) collective-permute-start(bf16[256,512]{1,0:T(8,128)(2,1)} %collective-permute-done.18.refs_12_), channel_id=1, source_target_pairs={{0,32},{16,48},{1,33},{17,49},{2,34},{18,50},{3,35},{19,51},{4,36}... | collective-permute-start | bytes 786440 | tf_op jit(solution)/shard_map/ppermute | solution.py:34
  118.8 9.0 %collective-permute-start.26 = (bf16[256,512]{1,0:T(8,128)(2,1)}, bf16[256,512]{1,0:T(8,128)(2,1)}, u32[]{:S(2)}, u32[]{:S(2)}) collective-permute-start(bf16[256,512]{1,0:T(8,128)(2,1)} %collective-permute-done.18.refs_12_), channel_id=1, source_target_pairs={{0,96},{16,112},{1,97},{17,113},{2,98},{18,114},{3,99},{19,115},{4... | collective-permute-start | bytes 786440 | tf_op jit(solution)/shard_map/ppermute | solution.py:34
  121.5 7.1 %collective-permute-start.27 = (bf16[256,512]{1,0:T(8,128)(2,1)}, bf16[256,512]{1,0:T(8,128)(2,1)}, u32[]{:S(2)}, u32[]{:S(2)}) collective-permute-start(bf16[256,512]{1,0:T(8,128)(2,1)} %collective-permute-done.19.refs_13_), channel_id=1, source_target_pairs={{0,128},{16,144},{1,129},{17,145},{2,130},{18,146},{3,131},{19,147... | collective-permute-start | bytes 786440 | tf_op jit(solution)/shard_map/ppermute | solution.py:57
  134.4 3.5 %collective-permute-start.28 = (f32[256,512]{1,0:T(8,128)S(1)}, f32[256,512]{1,0:T(8,128)S(1)}, u32[]{:S(2)}, u32[]{:S(2)}) collective-permute-start(f32[256,512]{1,0:T(8,128)S(1)} %get-tuple-element.64), channel_id=1, source_target_pairs={{0,16},{16,0},{1,17},{17,1},{2,18},{18,2},{3,19},{19,3},{4,20},{20... | collective-permute-start | bytes 1572872 | tf_op jit(solution)/shard_map/ppermute | solution.py:34
  (3 other events, 5.6 us)

commit v7 on v6

--- a/solution.py
+++ b/solution.py
@@ -171,7 +171,7 @@
 
 
 def rest_moves(table, sources, rows):
-    return [(source, rows.at[pl.ds(n * SPLIT, SPLIT)]) for n, source in enumerate(sources)]
+    return [(sources[0], rows)]
 
 
 def own_moves(table, sources, rows):
@@ -235,14 +235,6 @@
     )(where, *out_rows, *in_rows)
 
 
-def z_swap(value):
-    pairs = []
-    for d in range(NX * NY * NC):
-        for b in range(NH * NZ):
-            pairs.append((d * NH * NZ + b, d * NH * NZ + (b ^ 1)))
-    return lax.ppermute(value, ("dp", "blk"), pairs)
-
-
 def transposed(block):
     pairs = []
     for sx in range(NX):
@@ -269,28 +261,25 @@
     give = (half * (1 - x) + table) * depth
     keep = ((half * x + table) * depth).astype(jnp.int32)
     first, own_other = by_core(basis_in, dy=1), shift(basis_in, dc=1)
-    block = dot(out_grads, basis_out).astype(jnp.bfloat16).T
-    block, source = lax.optimization_barrier((block, activations))
     near = lax.dynamic_slice_in_dim(give, parity * SPLIT, SPLIT)
-    near = by_core(pieces(near.astype(jnp.int32), source, depth), dx=1)
-    block, source = lax.optimization_barrier((jnp.stack([block, z_swap(block)]), source))
-    later = give[2 * SPLIT :].astype(jnp.int32)
-    rest_a = pieces(later[:SPLIT], source, depth)
-    rest_b = pieces(later[SPLIT:], source, depth)
-
-    first, near, rest_a, again, block, own_other = lax.optimization_barrier(
-        (first, near, rest_a, basis_in, block, own_other)
+    near = pieces(near.astype(jnp.int32), activations, depth)
+    block = transposed(dot(out_grads, basis_out).astype(jnp.bfloat16).T)
+    near, block = lax.optimization_barrier((near, block))
+    near, other = by_core(near, dx=1), shift(block, dx=NX)
+    rest = pieces(give[2 * SPLIT :].astype(jnp.int32), activations, depth)
+    first, again = lax.optimization_barrier((first, basis_in))
+    second, first_other = by_core(again, dy=NY - 1), shift(first, dc=1)
+
+    block = jnp.stack([block, other])
+    up1, down1 = shift(block, dz=1), shift(block, dz=NZ - 1)
+    near, second, up1, down1, rest, first = lax.optimization_barrier(
+        (near, second, up1, down1, rest, first)
     )
-    second, rest_a, away = by_core(again, dy=NY - 1), by_core(rest_a, dx=1), by_core(near, dz=1)
-    block, first_other = transposed(block), shift(first, dc=1)
-    second, rest_a, away, block, onward, rest_b = lax.optimization_barrier(
-        (second, rest_a, away, block, first, rest_b)
-    )
-    far, rest_b, second_other = by_core(onward, dy=1), by_core(rest_b, dx=1), shift(second, dc=1)
-
-    up1, down1 = shift(block, dz=1), shift(block, dz=NZ - 1)
-    far, up1, down1 = lax.optimization_barrier((far, up1, down1))
+    far, rest, away = by_core(first, dy=1), by_core(rest, dx=1), by_core(near, dz=1)
     up2, down2 = shift(up1, dz=1), shift(down1, dz=NZ - 1)
+    second_other = shift(second, dc=1)
+    far, away, up2, down2 = lax.optimization_barrier((far, away, up2, down2))
+    up3, down3 = shift(up2, dz=1), shift(down2, dz=NZ - 1)
     h, z = b // NZ, b % NZ
     flip = (h + core) % 2
     where = jnp.stack(
@@ -304,24 +293,20 @@
     panels = [[panel] for panel in panels]
     parity = parity.reshape(1).astype(jnp.int32)
     partial = product(near_moves, 2, parity, (near, away), panels[: 2 * SPLIT])
+    rest, up3, down3 = lax.optimization_barrier((rest, up3, down3))
+    opposite = by_core(jnp.where(core == 0, up3, down3), dz=1)
+    out_rows = (block, up1, up2, up3, opposite, down3, down2, down1)
     partial = product(
-        rest_moves, 2, parity, (rest_a, rest_b), panels[2 * SPLIT :], partial, FOLLOWED, TAIL_VMEM
+        rest_moves, 1, parity, (rest,), panels[2 * SPLIT :], partial, FOLLOWED, TAIL_VMEM
     )
     arrived = swap((partial * FACTOR).astype(jnp.float16))
-    arrived, up2, down2 = lax.optimization_barrier((arrived, up2, down2))
-    up3, down3 = shift(up2, dz=1), shift(down2, dz=NZ - 1)
     total = product(own_moves, len(BLOCKS), keep, (activations,), panels)
     proj_in = (total + arrived.astype(jnp.float32) * (1.0 / FACTOR)).astype(jnp.bfloat16)
 
     p_left, p_right, p_far = shift(proj_in, dy=1), shift(proj_in, dy=3), shift(proj_in, dy=2)
     p_across = swap(proj_in)
-    p_across, p_far, p_left, p_right, up3, down3 = lax.optimization_barrier(
-        (p_across, p_far, p_left, p_right, up3, down3)
-    )
     px_left, px_right = shift(p_across, dy=1), shift(p_across, dy=3)
     px_far = swap(p_far)
-    opposite = by_core(jnp.where(core == 0, up3, down3), dz=1)
-    out_rows = (block, up1, up2, up3, opposite, down3, down2, down1)
     kept, given = sums_of_squares(
         where,
         out_rows,

time: 140 us -> 139 us (level)
  waiting for transfers between devices: 47.3 us -> 30.6 us
  starting transfers between devices: 56.2 us -> 69.3 us
  local copies, waits for them, and re-layouts: 2.84 us -> 8.9 us
  Pallas kernels: 26.6 us -> 24.1 us
    ppermute x8 -> x7, waiting for transfers between devices: 23.1 us -> 0.02 us  [by_core(): return lax.ppermute(value, ('dp', 'blk'), pairs)]
    ppermute x16 -> x17, waiting for transfers between devices: 17.3 us -> 30.5 us  [shift(): return lax.ppermute(value, ('dp', 'blk'), pairs)]
    ppermute x8 -> x7, starting transfers between devices: 20.3 us -> 32.5 us  [by_core(): return lax.ppermute(value, ('dp', 'blk'), pairs)]
    unnamed x12 -> x28, local copies, waits for them, and re-layouts: 2 us -> 7.56 us
    ppermute x3, waiting for transfers between devices: 3.52 us -> 0.08 us  [swap(): return lax.ppermute(value, ('dp', 'blk'), pairs)]
    ppermute x1 -> x0, waiting for transfers between devices: 3.4 us -> none  [z_swap(): return lax.ppermute(value, ('dp', 'blk'), pairs)]
    pallas_call x3 -> x2, Pallas kernels: 8.14 us -> 5.64 us  [pieces(): pl.pallas_call(pieces_kernel, out_shape=jax.ShapeDtypeStruct(shape, activ...]
    ppermute x16 -> x17, starting transfers between devices: 30.1 us -> 32.5 us  [shift(): return lax.ppermute(value, ('dp', 'blk'), pairs)]
  transfers between devices with their start and end apart: 29 -> 28, of which waited for: 11 -> 12; matrix products, arithmetic and copies ran while one was open for 3% -> 3% of each run, Pallas kernels for 16% -> 12%
where the time goes in v7:
time: 139 us; the launch traced here: 138 us
  starting transfers between devices  69.3 us (50%)
  waiting for transfers between devices  30.6 us (22%)
  Pallas kernels  24.1 us (17%)
  local copies, waits for them, and re-layouts  8.9 us (6%)
  other arithmetic  2.76 us (2%)
  matrix products  2.34 us (2%)
    ppermute x17, starting transfers between devices, shift(): return lax.ppermute(value, ('dp', 'blk'), pairs)  32.5 us
    ppermute x7, starting transfers between devices, by_core(): return lax.ppermute(value, ('dp', 'blk'), pairs)  32.5 us
    ppermute x17, waiting for transfers between devices, shift(): return lax.ppermute(value, ('dp', 'blk'), pairs)  30.5 us
    pallas_call x3, Pallas kernels, product(): pl.pallas_call(lambda *refs: product_kernel(moves, layout, *refs), out_sh...  13.8 us
    unnamed x28, local copies, waits for them, and re-layouts  7.56 us
    pallas_call x2, Pallas kernels, pieces(): pl.pallas_call(pieces_kernel, out_shape=jax.ShapeDtypeStruct(shape, activ...  5.64 us
    pallas_call x1, Pallas kernels, sums_of_squares(): pl.pallas_call(lambda *refs: squares_kernel(blocks, *refs), out_shape=[ja...  4.69 us
    ppermute x3, starting transfers between devices, swap(): return lax.ppermute(value, ('dp', 'blk'), pairs)  3.58 us
  transfers between devices with their start and end apart: 28, of which 12 were waited for; matrix products, arithmetic and copies ran while one was open for 3% of the time, Pallas kernels for 12%

profile of v7, /device:TPU:1, one launch (start us, length us, event | category | flops | bytes accessed | tf_op | source)
XLA Modules:
  0.0 138.4 jit_solution(15828085801525425965)
XLA Ops:
  0.0 3.6 %collective-permute-start.3 = (bf16[896,512]{1,0:T(8,128)(2,1)}, bf16[896,512]{1,0:T(8,128)(2,1)S(1)}, u32[]{:S(2)}, u32[]{:S(2)}) collective-permute-start(bf16[896,512]{1,0:T(8,128)(2,1)} %refs_3_.1), channel_id=1, source_target_pairs={{0,32},{16,112},{1,33},{17,113},{2,34},{18,114},{3,35},{19,115},{4... | collective-permute-start | bytes 2752520 | tf_op jit(solution)/shard_map/ppermute | solution.py:46
  3.6 2.3 %convolution_convert_fusion = bf16[256,256]{1,0:T(8,128)(2,1)S(1)} fusion(bf16[4096,256]{1,0:T(8,128)(2,1)S(1)} %copy-done, bf16[256,4096]{1,0:T(8,128)(2,1)} %param.5), kind=kOutput, calls=%fused_computation | convolution fusion | flops 536936448 | bytes 4325376 | tf_op jit(solution)/shard_map/dot_general | solution.py:61
  8.0 2.6 %shard_map.46 = bf16[2,256,896]{2,1,0:T(8,128)(2,1)} custom-call(s32[2]{0:T(128)} %dynamic_slice.3.columns_ref, bf16[256,14336]{1,0:T(8,128)(2,1)} %refs_1_.1), custom_call_target="tpu_custom_call" | custom-call | bytes 4194304 | tf_op jit(solution)/shard_map/pallas_call | solution.py:91
  10.7 12.8 %collective-permute-start.2 = (bf16[2,256,896]{2,1,0:T(8,128)(2,1)}, bf16[2,256,896]{2,1,0:T(8,128)(2,1)}, u32[]{:S(2)}, u32[]{:S(2)}) collective-permute-start(bf16[2,256,896]{2,1,0:T(8,128)(2,1)} %shard_map.46), channel_id=1, source_target_pairs={{0,128},{16,152},{1,129},{17,153},{2,130},{18,154},{3,131},{19,155... | collective-permute-start | bytes 2752520 | tf_op jit(solution)/shard_map/ppermute | solution.py:46
  23.5 1.4 %collective-permute-start.4 = (bf16[896,512]{1,0:T(8,128)(2,1)}, bf16[896,512]{1,0:T(8,128)(2,1)}, u32[]{:S(2)}, u32[]{:S(2)}) collective-permute-start(bf16[896,512]{1,0:T(8,128)(2,1)} %refs_3_.1), channel_id=1, source_target_pairs={{0,96},{16,48},{1,97},{17,49},{2,98},{18,50},{3,99},{19,51},{4,100... | collective-permute-start | bytes 2752520 | tf_op jit(solution)/shard_map/ppermute | solution.py:46
  25.0 2.7 %collective-permute-start.1 = (bf16[256,256]{1,0:T(8,128)(2,1)S(1)}, bf16[256,256]{1,0:T(8,128)(2,1)S(1)}, u32[]{:S(2)}, u32[]{:S(2)}) collective-permute-start(bf16[256,256]{1,0:T(8,128)(2,1)S(1)} %collective-permute-done), channel_id=1, source_target_pairs={{0,8},{16,24},{1,9},{17,25},{2,10},{18,26},{3,11},{19,27},{4,12},{... | collective-permute-start | bytes 393224 | tf_op jit(solution)/shard_map/ppermute | solution.py:34
  27.6 4.1 %collective-permute-done.1 = bf16[256,256]{1,0:T(8,128)(2,1)S(1)} collective-permute-done((bf16[256,256]{1,0:T(8,128)(2,1)S(1)}, bf16[256,256]{1,0:T(8,128)(2,1)S(1)}, u32[]{:S(2)}, u32[]{:S(2)}) %collective-permute-start.1) | collective-permute-done | bytes 131104 | tf_op jit(solution)/shard_map/ppermute | solution.py:34
  31.8 8.8 %collective-permute-start.6 = (bf16[2,256,256]{2,1,0:T(8,128)(2,1)S(1)}, bf16[2,256,256]{2,1,0:T(8,128)(2,1)S(1)}, u32[]{:S(2)}, u32[]{:S(2)}) collective-permute-start(bf16[2,256,256]{2,1,0:T(8,128)(2,1)S(1)} %pad_maximum_fusion.refs_1_), channel_id=1, source_target_pairs={{0,7},{16,23},{1,0},{17,16},{2,1},{18,17},{3,2},{19,18},{4,3},{20,... | collective-permute-start | bytes 786440 | tf_op jit(solution)/shard_map/ppermute | solution.py:34
  41.1 3.0 %shard_map.47 = bf16[4,256,896]{2,1,0:T(8,128)(2,1)} custom-call(s32[4]{0:T(128)} %slice.3.columns_ref, bf16[256,14336]{1,0:T(8,128)(2,1)} %refs_1_.1), custom_call_target="tpu_custom_call" | custom-call | bytes 4194304 | tf_op jit(solution)/shard_map/pallas_call | solution.py:91
  44.2 2.8 %collective-permute-done.5.refs_2_ = bf16[2,256,256]{2,1,0:T(8,128)(2,1)S(1)} collective-permute-done((bf16[2,256,256]{2,1,0:T(8,128)(2,1)S(1)}, bf16[2,256,256]{2,1,0:T(8,128)(2,1)S(1)}, u32[]{:S(2)}, u32[]{:S(2)}) %collective-permute-start.5) | collective-permute-done | bytes 262176 | tf_op jit(solution)/shard_map/ppermute | solution.py:34
  47.7 12.0 %collective-permute-start.11 = (bf16[4,256,896]{2,1,0:T(8,128)(2,1)}, bf16[4,256,896]{2,1,0:T(8,128)(2,1)}, u32[]{:S(2)}, u32[]{:S(2)}) collective-permute-start(bf16[4,256,896]{2,1,0:T(8,128)(2,1)} %shard_map.47), channel_id=1, source_target_pairs={{0,128},{16,152},{1,129},{17,153},{2,130},{18,154},{3,131},{19,155... | collective-permute-start | bytes 5505032 | tf_op jit(solution)/shard_map/ppermute | solution.py:46
  59.8 1.3 collective-permute-start.9
  61.1 1.4 %collective-permute-start.10 = (bf16[2,256,256]{2,1,0:T(8,128)(2,1)S(1)}, bf16[2,256,256]{2,1,0:T(8,128)(2,1)S(1)}, u32[]{:S(2)}, u32[]{:S(2)}) collective-permute-start(bf16[2,256,256]{2,1,0:T(8,128)(2,1)S(1)} %collective-permute-done.6.refs_8_), channel_id=1, source_target_pairs={{0,7},{16,23},{1,0},{17,16},{2,1},{18,17},{3,2},{19,18},{4,3},{20,... | collective-permute-start | bytes 786440 | tf_op jit(solution)/shard_map/ppermute | solution.py:34
  62.5 6.9 %collective-permute-done.9.refs_3_ = bf16[2,256,256]{2,1,0:T(8,128)(2,1)S(1)} collective-permute-done((bf16[2,256,256]{2,1,0:T(8,128)(2,1)S(1)}, bf16[2,256,256]{2,1,0:T(8,128)(2,1)S(1)}, u32[]{:S(2)}, u32[]{:S(2)}) %collective-permute-start.9) | collective-permute-done | bytes 262176 | tf_op jit(solution)/shard_map/ppermute | solution.py:34
  69.4 9.6 %collective-permute-start.15 = (bf16[896,512]{1,0:T(8,128)(2,1)}, bf16[896,512]{1,0:T(8,128)(2,1)S(1)}, u32[]{:S(2)}, u32[]{:S(2)}) collective-permute-start(bf16[896,512]{1,0:T(8,128)(2,1)} %refs_3_.1), channel_id=1, source_target_pairs={{0,16},{16,0},{1,17},{17,1},{2,18},{18,2},{3,19},{19,3},{4,20},{20... | collective-permute-start | bytes 2752520 | tf_op jit(solution)/shard_map/ppermute | solution.py:34
  79.6 1.7 %collective-permute-done.15.refs_3_.refs_4_ = bf16[896,512]{1,0:T(8,128)(2,1)S(1)} collective-permute-done((bf16[896,512]{1,0:T(8,128)(2,1)}, bf16[896,512]{1,0:T(8,128)(2,1)S(1)}, u32[]{:S(2)}, u32[]{:S(2)}) %collective-permute-start.15) | collective-permute-done | bytes 917536 | tf_op jit(solution)/shard_map/ppermute | solution.py:34
  82.3 1.6 %collective-permute-done.16.refs_5_.refs_6_ = bf16[896,512]{1,0:T(8,128)(2,1)S(1)} collective-permute-done((bf16[896,512]{1,0:T(8,128)(2,1)}, bf16[896,512]{1,0:T(8,128)(2,1)S(1)}, u32[]{:S(2)}, u32[]{:S(2)}) %collective-permute-start.16) | collective-permute-done | bytes 917536 | tf_op jit(solution)/shard_map/ppermute | solution.py:34
  85.5 4.0 %shard_map.49.refs_6_ = f32[256,512]{1,0:T(8,128)} custom-call(s32[1]{0:T(128)} %bitcast.28.refs_0_, bf16[2,256,896]{2,1,0:T(8,128)(2,1)} %collective-permute-done.2.refs_1_, bf16[2,256,896]{2,1,0:T(8,128)(2,1)} %copy-done.13, bf16[896,512]{1,0:T(8,128)(2,1)} %refs_3_.1, bf16[896,512]{1,0:T(8,128)(2,1)} %copy-done.11, bf16[896,512]{1,0:T(8,128)(2,1)} %copy-done.10, ...), custom_call_target="tpu_custom_call" | custom-call | flops 939524096 | bytes 4194304 | tf_op jit(solution)/shard_map/pallas_call | solution.py:144
  90.0 2.4 %collective-permute-done.13.refs_6_ = bf16[2,256,256]{2,1,0:T(8,128)(2,1)S(1)} collective-permute-done((bf16[2,256,256]{2,1,0:T(8,128)(2,1)S(1)}, bf16[2,256,256]{2,1,0:T(8,128)(2,1)S(1)}, u32[]{:S(2)}, u32[]{:S(2)}) %collective-permute-start.13) | collective-permute-done | bytes 262176 | tf_op jit(solution)/shard_map/ppermute | solution.py:34
  93.4 3.2 %shard_map.50 = f32[256,512]{1,0:T(8,128)S(1)} custom-call(s32[1]{0:T(128)} %bitcast.28.refs_0_, bf16[4,256,896]{2,1,0:T(8,128)(2,1)} %collective-permute-done.11.refs_1_, bf16[896,512]{1,0:T(8,128)(2,1)} %collective-permute-done.4.refs_6_.refs_2_, bf16[896,512]{1,0:T(8,128)(2,1)} %collective-permute-done.17.refs_7_.refs_3_, ...), custom_call_target="tpu_custom_call" | custom-call | flops 6939524096 | bytes 4194304 | tf_op jit(solution)/shard_map/pallas_call | solution.py:144
  96.8 6.6 %shard_map.48 = f32[256,512]{1,0:T(8,128)} custom-call(s32[8]{0:T(128)} %get-tuple-element.43.refs_0_, bf16[256,14336]{1,0:T(8,128)(2,1)} %refs_1_.1, bf16[896,512]{1,0:T(8,128)(2,1)} %refs_3_.1, bf16[896,512]{1,0:T(8,128)(2,1)} %copy-done.11, bf16[896,512]{1,0:T(8,128)(2,1)} %copy-done.10, bf16[896,512]{1,0:T(8,128)(2,1)} %copy-done.12, ...), custom_call_target="tpu_custom_call" | custom-call | flops 1879048192 | bytes 4194304 | tf_op jit(solution)/shard_map/pallas_call | solution.py:144
  103.5 1.2 add_convert_fusion.refs_9_
  104.8 1.5 %collective-permute-start.22 = (bf16[256,512]{1,0:T(8,128)(2,1)S(1)}, bf16[256,512]{1,0:T(8,128)(2,1)}, u32[]{:S(2)}, u32[]{:S(2)}) collective-permute-start(bf16[256,512]{1,0:T(8,128)(2,1)S(1)} %add_convert_fusion.refs_9_), channel_id=1, source_target_pairs={{0,128},{16,144},{1,129},{17,145},{2,130},{18,146},{3,131},{19,147... | collective-permute-start | bytes 786440 | tf_op jit(solution)/shard_map/ppermute | solution.py:57
  106.3 1.9 %collective-permute-start.14 = (bf16[2,256,256]{2,1,0:T(8,128)(2,1)S(1)}, bf16[2,256,256]{2,1,0:T(8,128)(2,1)S(1)}, u32[]{:S(2)}, u32[]{:S(2)}) collective-permute-start(bf16[2,256,256]{2,1,0:T(8,128)(2,1)S(1)} %broadcast_select_fusion), channel_id=1, source_target_pairs={{0,1},{16,23},{1,2},{17,16},{2,3},{18,17},{3,4},{19,18},{4,5},{20,... | collective-permute-start | bytes 786440 | tf_op jit(solution)/shard_map/ppermute | solution.py:46
  109.6 2.4 %collective-permute-done.23.refs_13_ = bf16[256,512]{1,0:T(8,128)(2,1)} collective-permute-done((bf16[256,512]{1,0:T(8,128)(2,1)S(1)}, bf16[256,512]{1,0:T(8,128)(2,1)}, u32[]{:S(2)}, u32[]{:S(2)}) %collective-permute-start.23) | collective-permute-done | bytes 262176 | tf_op jit(solution)/shard_map/ppermute | solution.py:34
  112.1 2.0 %collective-permute-start.26 = (bf16[256,512]{1,0:T(8,128)(2,1)}, bf16[256,512]{1,0:T(8,128)(2,1)}, u32[]{:S(2)}, u32[]{:S(2)}) collective-permute-start(bf16[256,512]{1,0:T(8,128)(2,1)} %collective-permute-done.23.refs_13_), channel_id=1, source_target_pairs={{0,128},{16,144},{1,129},{17,145},{2,130},{18,146},{3,131},{19,147... | collective-permute-start | bytes 786440 | tf_op jit(solution)/shard_map/ppermute | solution.py:57
  114.8 1.5 %collective-permute-start.24 = (bf16[256,512]{1,0:T(8,128)(2,1)}, bf16[256,512]{1,0:T(8,128)(2,1)}, u32[]{:S(2)}, u32[]{:S(2)}) collective-permute-start(bf16[256,512]{1,0:T(8,128)(2,1)} %collective-permute-done.22.refs_12_), channel_id=1, source_target_pairs={{0,32},{16,48},{1,33},{17,49},{2,34},{18,50},{3,35},{19,51},{4,36}... | collective-permute-start | bytes 786440 | tf_op jit(solution)/shard_map/ppermute | solution.py:34
  116.4 3.9 %collective-permute-done.20.refs_10_ = bf16[256,512]{1,0:T(8,128)(2,1)} collective-permute-done((bf16[256,512]{1,0:T(8,128)(2,1)S(1)}, bf16[256,512]{1,0:T(8,128)(2,1)}, u32[]{:S(2)}, u32[]{:S(2)}) %collective-permute-start.20) | collective-permute-done | bytes 262176 | tf_op jit(solution)/shard_map/ppermute | solution.py:34
  120.3 2.6 %collective-permute-done.24.refs_14_ = bf16[256,512]{1,0:T(8,128)(2,1)} collective-permute-done((bf16[256,512]{1,0:T(8,128)(2,1)}, bf16[256,512]{1,0:T(8,128)(2,1)}, u32[]{:S(2)}, u32[]{:S(2)}) %collective-permute-start.24) | collective-permute-done | bytes 262176 | tf_op jit(solution)/shard_map/ppermute | solution.py:34
  126.7 4.7 %shard_map.51 = (f32[256,512]{1,0:T(8,128)S(1)}, f32[256,512]{1,0:T(8,128)S(1)}) custom-call(s32[18]{0:T(128)S(1)} %stack.111.refs_0_, bf16[2,256,256]{2,1,0:T(8,128)(2,1)S(1)} %pad_maximum_fusion.refs_1_, bf16[2,256,256]{2,1,0:T(8,128)(2,1)S(1)} %copy-done.3, bf16[2,256,256]{2,1,0:T(8,128)(2,1)S(1)} %copy-done.5, ...), custom_call_target="tpu_custom_call" | custom-call | flops 1073741824 | bytes 4194304 | tf_op jit(solution)/shard_map/pallas_call | solution.py:219
  131.4 4.6 %collective-permute-start.27 = (f32[256,512]{1,0:T(8,128)S(1)}, f32[256,512]{1,0:T(8,128)S(1)}, u32[]{:S(2)}, u32[]{:S(2)}) collective-permute-start(f32[256,512]{1,0:T(8,128)S(1)} %get-tuple-element.42), channel_id=1, source_target_pairs={{0,16},{16,0},{1,17},{17,1},{2,18},{18,2},{3,19},{19,3},{4,20},{20... | collective-permute-start | bytes 1572872 | tf_op jit(solution)/shard_map/ppermute | solution.py:34
  136.0 1.5 %collective-permute-done.27 = f32[256,512]{1,0:T(8,128)S(1)} collective-permute-done((f32[256,512]{1,0:T(8,128)S(1)}, f32[256,512]{1,0:T(8,128)S(1)}, u32[]{:S(2)}, u32[]{:S(2)}) %collective-permute-start.27) | collective-permute-done | bytes 524320 | tf_op jit(solution)/shard_map/ppermute | solution.py:34
  (69 shorter events, 15.4 us)
Async XLA Ops:
  0.0 23.5 %collective-permute-start.3 = (bf16[896,512]{1,0:T(8,128)(2,1)}, bf16[896,512]{1,0:T(8,128)(2,1)S(1)}, u32[]{:S(2)}, u32[]{:S(2)}) collective-permute-start(bf16[896,512]{1,0:T(8,128)(2,1)} %refs_3_.1), channel_id=1, source_target_pairs={{0,32},{16,112},{1,33},{17,113},{2,34},{18,114},{3,35},{19,115},{4... | collective-permute-start | bytes 2752520 | tf_op jit(solution)/shard_map/ppermute | solution.py:46
  5.9 4.7 %collective-permute-start = (bf16[256,256]{1,0:T(8,128)(2,1)S(1)}, bf16[256,256]{1,0:T(8,128)(2,1)S(1)}, u32[]{:S(2)}, u32[]{:S(2)}) collective-permute-start(bf16[256,256]{1,0:T(8,128)(2,1)S(1)} %convolution_convert_fusion), channel_id=1, source_target_pairs={{0,0},{1,8},{2,32},{3,40},{4,64},{5,72},{6,96},{7,104},{8,128},{9,... | collective-permute-start | bytes 393224 | tf_op jit(solution)/shard_map/ppermute | solution.py:247
  10.7 36.3 %collective-permute-start.2 = (bf16[2,256,896]{2,1,0:T(8,128)(2,1)}, bf16[2,256,896]{2,1,0:T(8,128)(2,1)}, u32[]{:S(2)}, u32[]{:S(2)}) collective-permute-start(bf16[2,256,896]{2,1,0:T(8,128)(2,1)} %shard_map.46), channel_id=1, source_target_pairs={{0,128},{16,152},{1,129},{17,153},{2,130},{18,154},{3,131},{19,155... | collective-permute-start | bytes 2752520 | tf_op jit(solution)/shard_map/ppermute | solution.py:46
  23.5 8.2 %copy-start.10 = (bf16[896,512]{1,0:T(8,128)(2,1)}, bf16[896,512]{1,0:T(8,128)(2,1)S(1)}, u32[]{:S(2)}) copy-start(bf16[896,512]{1,0:T(8,128)(2,1)S(1)} %collective-permute-done.3.refs_4_.refs_5_) | copy-start | bytes 2752516
  23.5 23.5 %collective-permute-start.4 = (bf16[896,512]{1,0:T(8,128)(2,1)}, bf16[896,512]{1,0:T(8,128)(2,1)}, u32[]{:S(2)}, u32[]{:S(2)}) collective-permute-start(bf16[896,512]{1,0:T(8,128)(2,1)} %refs_3_.1), channel_id=1, source_target_pairs={{0,96},{16,48},{1,97},{17,49},{2,98},{18,50},{3,99},{19,51},{4,100... | collective-permute-start | bytes 2752520 | tf_op jit(solution)/shard_map/ppermute | solution.py:46
  25.0 6.8 %collective-permute-start.1 = (bf16[256,256]{1,0:T(8,128)(2,1)S(1)}, bf16[256,256]{1,0:T(8,128)(2,1)S(1)}, u32[]{:S(2)}, u32[]{:S(2)}) collective-permute-start(bf16[256,256]{1,0:T(8,128)(2,1)S(1)} %collective-permute-done), channel_id=1, source_target_pairs={{0,8},{16,24},{1,9},{17,25},{2,10},{18,26},{3,11},{19,27},{4,12},{... | collective-permute-start | bytes 393224 | tf_op jit(solution)/shard_map/ppermute | solution.py:34
  31.8 12.4 %collective-permute-start.6 = (bf16[2,256,256]{2,1,0:T(8,128)(2,1)S(1)}, bf16[2,256,256]{2,1,0:T(8,128)(2,1)S(1)}, u32[]{:S(2)}, u32[]{:S(2)}) collective-permute-start(bf16[2,256,256]{2,1,0:T(8,128)(2,1)S(1)} %pad_maximum_fusion.refs_1_), channel_id=1, source_target_pairs={{0,7},{16,23},{1,0},{17,16},{2,1},{18,17},{3,2},{19,18},{4,3},{20,... | collective-permute-start | bytes 786440 | tf_op jit(solution)/shard_map/ppermute | solution.py:34
  40.5 6.4 %collective-permute-start.5 = (bf16[2,256,256]{2,1,0:T(8,128)(2,1)S(1)}, bf16[2,256,256]{2,1,0:T(8,128)(2,1)S(1)}, u32[]{:S(2)}, u32[]{:S(2)}) collective-permute-start(bf16[2,256,256]{2,1,0:T(8,128)(2,1)S(1)} %pad_maximum_fusion.refs_1_), channel_id=1, source_target_pairs={{0,1},{16,17},{1,2},{17,18},{2,3},{18,19},{3,4},{19,20},{4,5},{20,... | collective-permute-start | bytes 786440 | tf_op jit(solution)/shard_map/ppermute | solution.py:34
  47.0 42.5 %copy-start.2 = (bf16[2,256,256]{2,1,0:T(8,128)(2,1)}, bf16[2,256,256]{2,1,0:T(8,128)(2,1)S(1)}, u32[]{:S(2)}) copy-start(bf16[2,256,256]{2,1,0:T(8,128)(2,1)S(1)} %collective-permute-done.5.refs_2_) | copy-start | bytes 786436
  47.0 32.1 %collective-permute-start.8 = (bf16[2,256,896]{2,1,0:T(8,128)(2,1)}, bf16[2,256,896]{2,1,0:T(8,128)(2,1)S(1)}, u32[]{:S(2)}, u32[]{:S(2)}) collective-permute-start(bf16[2,256,896]{2,1,0:T(8,128)(2,1)} %collective-permute-done.2.refs_1_), channel_id=1, source_target_pairs={{0,1},{16,23},{1,2},{17,16},{2,3},{18,17},{3,4},{19,18},{4,5},{20,... | collective-permute-start | bytes 2752520 | tf_op jit(solution)/shard_map/ppermute | solution.py:46
  47.7 44.7 %collective-permute-start.11 = (bf16[4,256,896]{2,1,0:T(8,128)(2,1)}, bf16[4,256,896]{2,1,0:T(8,128)(2,1)}, u32[]{:S(2)}, u32[]{:S(2)}) collective-permute-start(bf16[4,256,896]{2,1,0:T(8,128)(2,1)} %shard_map.47), channel_id=1, source_target_pairs={{0,128},{16,152},{1,129},{17,153},{2,130},{18,154},{3,131},{19,155... | collective-permute-start | bytes 5505032 | tf_op jit(solution)/shard_map/ppermute | solution.py:46
  59.7 19.8 %collective-permute-start.7 = (bf16[896,512]{1,0:T(8,128)(2,1)}, bf16[896,512]{1,0:T(8,128)(2,1)}, u32[]{:S(2)}, u32[]{:S(2)}) collective-permute-start(bf16[896,512]{1,0:T(8,128)(2,1)} %copy-done.10), channel_id=1, source_target_pairs={{0,32},{16,112},{1,33},{17,113},{2,34},{18,114},{3,35},{19,115},{4... | collective-permute-start | bytes 2752520 | tf_op jit(solution)/shard_map/ppermute | solution.py:46
  59.8 9.6 %collective-permute-start.9 = (bf16[2,256,256]{2,1,0:T(8,128)(2,1)S(1)}, bf16[2,256,256]{2,1,0:T(8,128)(2,1)S(1)}, u32[]{:S(2)}, u32[]{:S(2)}) collective-permute-start(bf16[2,256,256]{2,1,0:T(8,128)(2,1)S(1)} %collective-permute-done.5.refs_2_), channel_id=1, source_target_pairs={{0,1},{16,17},{1,2},{17,18},{2,3},{18,19},{3,4},{19,20},{4,5},{20,... | collective-permute-start | bytes 786440 | tf_op jit(solution)/shard_map/ppermute | solution.py:34
  61.1 17.9 %collective-permute-start.10 = (bf16[2,256,256]{2,1,0:T(8,128)(2,1)S(1)}, bf16[2,256,256]{2,1,0:T(8,128)(2,1)S(1)}, u32[]{:S(2)}, u32[]{:S(2)}) collective-permute-start(bf16[2,256,256]{2,1,0:T(8,128)(2,1)S(1)} %collective-permute-done.6.refs_8_), channel_id=1, source_target_pairs={{0,7},{16,23},{1,0},{17,16},{2,1},{18,17},{3,2},{19,18},{4,3},{20,... | collective-permute-start | bytes 786440 | tf_op jit(solution)/shard_map/ppermute | solution.py:34
  69.4 20.1 %copy-start.4 = (bf16[2,256,256]{2,1,0:T(8,128)(2,1)}, bf16[2,256,256]{2,1,0:T(8,128)(2,1)S(1)}, u32[]{:S(2)}) copy-start(bf16[2,256,256]{2,1,0:T(8,128)(2,1)S(1)} %collective-permute-done.9.refs_3_) | copy-start | bytes 786436
  69.4 11.9 %collective-permute-start.15 = (bf16[896,512]{1,0:T(8,128)(2,1)}, bf16[896,512]{1,0:T(8,128)(2,1)S(1)}, u32[]{:S(2)}, u32[]{:S(2)}) collective-permute-start(bf16[896,512]{1,0:T(8,128)(2,1)} %refs_3_.1), channel_id=1, source_target_pairs={{0,16},{16,0},{1,17},{17,1},{2,18},{18,2},{3,19},{19,3},{4,20},{20... | collective-permute-start | bytes 2752520 | tf_op jit(solution)/shard_map/ppermute | solution.py:34
  78.9 10.5 %copy-start.6 = (bf16[2,256,256]{2,1,0:T(8,128)(2,1)}, bf16[2,256,256]{2,1,0:T(8,128)(2,1)S(1)}, u32[]{:S(2)}) copy-start(bf16[2,256,256]{2,1,0:T(8,128)(2,1)S(1)} %collective-permute-done.10.refs_7_) | copy-start | bytes 786436
  78.9 4.9 %collective-permute-start.16 = (bf16[896,512]{1,0:T(8,128)(2,1)}, bf16[896,512]{1,0:T(8,128)(2,1)S(1)}, u32[]{:S(2)}, u32[]{:S(2)}) collective-permute-start(bf16[896,512]{1,0:T(8,128)(2,1)} %copy-done.10), channel_id=1, source_target_pairs={{0,16},{16,0},{1,17},{17,1},{2,18},{18,2},{3,19},{19,3},{4,20},{20... | collective-permute-start | bytes 2752520 | tf_op jit(solution)/shard_map/ppermute | solution.py:34
  79.1 13.3 %collective-permute-start.17 = (bf16[896,512]{1,0:T(8,128)(2,1)}, bf16[896,512]{1,0:T(8,128)(2,1)}, u32[]{:S(2)}, u32[]{:S(2)}) collective-permute-start(bf16[896,512]{1,0:T(8,128)(2,1)} %collective-permute-done.4.refs_6_.refs_2_), channel_id=1, source_target_pairs={{0,16},{16,0},{1,17},{17,1},{2,18},{18,2},{3,19},{19,3},{4,20},{20... | collective-permute-start | bytes 2752520 | tf_op jit(solution)/shard_map/ppermute | solution.py:34
  79.5 12.9 %collective-permute-start.18 = (bf16[896,512]{1,0:T(8,128)(2,1)}, bf16[896,512]{1,0:T(8,128)(2,1)}, u32[]{:S(2)}, u32[]{:S(2)}) collective-permute-start(bf16[896,512]{1,0:T(8,128)(2,1)} %collective-permute-done.7.refs_8_.refs_4_), channel_id=1, source_target_pairs={{0,16},{16,0},{1,17},{17,1},{2,18},{18,2},{3,19},{19,3},{4,20},{20... | collective-permute-start | bytes 2752520 | tf_op jit(solution)/shard_map/ppermute | solution.py:34
  81.3 8.7 %collective-permute-start.12 = (bf16[2,256,256]{2,1,0:T(8,128)(2,1)S(1)}, bf16[2,256,256]{2,1,0:T(8,128)(2,1)S(1)}, u32[]{:S(2)}, u32[]{:S(2)}) collective-permute-start(bf16[2,256,256]{2,1,0:T(8,128)(2,1)S(1)} %collective-permute-done.9.refs_3_), channel_id=1, source_target_pairs={{0,1},{16,17},{1,2},{17,18},{2,3},{18,19},{3,4},{19,20},{4,5},{20,... | collective-permute-start | bytes 786440 | tf_op jit(solution)/shard_map/ppermute | solution.py:34
  84.9 7.5 %collective-permute-start.13 = (bf16[2,256,256]{2,1,0:T(8,128)(2,1)S(1)}, bf16[2,256,256]{2,1,0:T(8,128)(2,1)S(1)}, u32[]{:S(2)}, u32[]{:S(2)}) collective-permute-start(bf16[2,256,256]{2,1,0:T(8,128)(2,1)S(1)} %collective-permute-done.10.refs_7_), channel_id=1, source_target_pairs={{0,7},{16,23},{1,0},{17,16},{2,1},{18,17},{3,2},{19,18},{4,3},{20,... | collective-permute-start | bytes 786440 | tf_op jit(solution)/shard_map/ppermute | solution.py:34
  96.7 6.8 %collective-permute-start.19 = (f16[256,512]{1,0:T(8,128)(2,1)S(1)}, f16[256,512]{1,0:T(8,128)(2,1)}, u32[]{:S(2)}, u32[]{:S(2)}) collective-permute-start(f16[256,512]{1,0:T(8,128)(2,1)S(1)} %multiply_convert_fusion), channel_id=1, source_target_pairs={{0,128},{16,144},{1,129},{17,145},{2,130},{18,146},{3,131},{19,147... | collective-permute-start | bytes 786440 | tf_op jit(solution)/shard_map/ppermute | solution.py:57
  104.7 7.4 %collective-permute-start.23 = (bf16[256,512]{1,0:T(8,128)(2,1)S(1)}, bf16[256,512]{1,0:T(8,128)(2,1)}, u32[]{:S(2)}, u32[]{:S(2)}) collective-permute-start(bf16[256,512]{1,0:T(8,128)(2,1)S(1)} %add_convert_fusion.refs_9_), channel_id=1, source_target_pairs={{0,64},{16,80},{1,65},{17,81},{2,66},{18,82},{3,67},{19,83},{4,68}... | collective-permute-start | bytes 786440 | tf_op jit(solution)/shard_map/ppermute | solution.py:34
  104.8 9.3 %collective-permute-start.22 = (bf16[256,512]{1,0:T(8,128)(2,1)S(1)}, bf16[256,512]{1,0:T(8,128)(2,1)}, u32[]{:S(2)}, u32[]{:S(2)}) collective-permute-start(bf16[256,512]{1,0:T(8,128)(2,1)S(1)} %add_convert_fusion.refs_9_), channel_id=1, source_target_pairs={{0,128},{16,144},{1,129},{17,145},{2,130},{18,146},{3,131},{19,147... | collective-permute-start | bytes 786440 | tf_op jit(solution)/shard_map/ppermute | solution.py:57
  106.3 7.8 %collective-permute-start.14 = (bf16[2,256,256]{2,1,0:T(8,128)(2,1)S(1)}, bf16[2,256,256]{2,1,0:T(8,128)(2,1)S(1)}, u32[]{:S(2)}, u32[]{:S(2)}) collective-permute-start(bf16[2,256,256]{2,1,0:T(8,128)(2,1)S(1)} %broadcast_select_fusion), channel_id=1, source_target_pairs={{0,1},{16,23},{1,2},{17,16},{2,3},{18,17},{3,4},{19,18},{4,5},{20,... | collective-permute-start | bytes 786440 | tf_op jit(solution)/shard_map/ppermute | solution.py:46
  108.2 8.2 %collective-permute-start.21 = (bf16[256,512]{1,0:T(8,128)(2,1)S(1)}, bf16[256,512]{1,0:T(8,128)(2,1)}, u32[]{:S(2)}, u32[]{:S(2)}) collective-permute-start(bf16[256,512]{1,0:T(8,128)(2,1)S(1)} %add_convert_fusion.refs_9_), channel_id=1, source_target_pairs={{0,96},{16,112},{1,97},{17,113},{2,98},{18,114},{3,99},{19,115},{4... | collective-permute-start | bytes 786440 | tf_op jit(solution)/shard_map/ppermute | solution.py:34
  108.5 11.8 %collective-permute-start.20 = (bf16[256,512]{1,0:T(8,128)(2,1)S(1)}, bf16[256,512]{1,0:T(8,128)(2,1)}, u32[]{:S(2)}, u32[]{:S(2)}) collective-permute-start(bf16[256,512]{1,0:T(8,128)(2,1)S(1)} %add_convert_fusion.refs_9_), channel_id=1, source_target_pairs={{0,32},{16,48},{1,33},{17,49},{2,34},{18,50},{3,35},{19,51},{4,36}... | collective-permute-start | bytes 786440 | tf_op jit(solution)/shard_map/ppermute | solution.py:34
  112.1 8.2 %collective-permute-start.26 = (bf16[256,512]{1,0:T(8,128)(2,1)}, bf16[256,512]{1,0:T(8,128)(2,1)}, u32[]{:S(2)}, u32[]{:S(2)}) collective-permute-start(bf16[256,512]{1,0:T(8,128)(2,1)} %collective-permute-done.23.refs_13_), channel_id=1, source_target_pairs={{0,128},{16,144},{1,129},{17,145},{2,130},{18,146},{3,131},{19,147... | collective-permute-start | bytes 786440 | tf_op jit(solution)/shard_map/ppermute | solution.py:57
  114.1 6.2 %collective-permute-start.25 = (bf16[256,512]{1,0:T(8,128)(2,1)}, bf16[256,512]{1,0:T(8,128)(2,1)}, u32[]{:S(2)}, u32[]{:S(2)}) collective-permute-start(bf16[256,512]{1,0:T(8,128)(2,1)} %collective-permute-done.22.refs_12_), channel_id=1, source_target_pairs={{0,96},{16,112},{1,97},{17,113},{2,98},{18,114},{3,99},{19,115},{4... | collective-permute-start | bytes 786440 | tf_op jit(solution)/shard_map/ppermute | solution.py:34
  114.8 8.0 %collective-permute-start.24 = (bf16[256,512]{1,0:T(8,128)(2,1)}, bf16[256,512]{1,0:T(8,128)(2,1)}, u32[]{:S(2)}, u32[]{:S(2)}) collective-permute-start(bf16[256,512]{1,0:T(8,128)(2,1)} %collective-permute-done.22.refs_12_), channel_id=1, source_target_pairs={{0,32},{16,48},{1,33},{17,49},{2,34},{18,50},{3,35},{19,51},{4,36}... | collective-permute-start | bytes 786440 | tf_op jit(solution)/shard_map/ppermute | solution.py:34
  131.4 6.2 %collective-permute-start.27 = (f32[256,512]{1,0:T(8,128)S(1)}, f32[256,512]{1,0:T(8,128)S(1)}, u32[]{:S(2)}, u32[]{:S(2)}) collective-permute-start(f32[256,512]{1,0:T(8,128)S(1)} %get-tuple-element.42), channel_id=1, source_target_pairs={{0,16},{16,0},{1,17},{17,1},{2,18},{18,2},{3,19},{19,3},{4,20},{20... | collective-permute-start | bytes 1572872 | tf_op jit(solution)/shard_map/ppermute | solution.py:34
  (10 other events, 17.5 us)

commit v8 on v5

--- a/solution.py
+++ b/solution.py
@@ -163,16 +163,15 @@
 
 
 def near_moves(table, sources, rows):
-    near, away, rest = sources
+    near, away = sources
     return [
         (near, rows.at[pl.ds(table[0] * SPLIT, SPLIT)]),
         (away, rows.at[pl.ds((1 - table[0]) * SPLIT, SPLIT)]),
-        (rest.at[pl.ds(0, 2)], rows.at[pl.ds(2 * SPLIT, 2)]),
     ]
 
 
-def last_moves(table, sources, rows):
-    return [(sources[0].at[pl.ds(2, 2)], rows)]
+def rest_moves(table, sources, rows):
+    return [(sources[0], rows)]
 
 
 def own_moves(table, sources, rows):
@@ -189,7 +188,7 @@
     copies = [pltpu.make_async_copy(out_rows, outer, semaphore.at[blocks])]
     for k in range(blocks):
         copies.append(
-            pltpu.make_async_copy(in_rows[k], inner.at[where_ref[k]], semaphore.at[k])
+            pltpu.make_async_copy(in_rows[k], inner.at[k], semaphore.at[k])
         )
     for copy in copies:
         copy.start()
@@ -200,12 +199,12 @@
     def _(n):
         columns = pl.ds(pl.multiple_of(n * TILE, TILE), TILE)
         for part, total_ref in enumerate(totals):
-            half = where_ref[blocks + part]
             total = None
             for k in range(blocks):
+                at, half = where_ref[k] + where_ref[2 * blocks + part], where_ref[blocks + k]
                 for example in range(EXAMPLES):
                     tokens = pl.ds(example * TOK, TOK)
-                    rotated = dot(outer[k, half, :, tokens], inner[k, tokens, columns])
+                    rotated = dot(outer[at, half, :, tokens], inner[k, tokens, columns])
                     squared = rotated * rotated
                     total = squared if total is None else total + squared
             total_ref[:, columns] = total
@@ -236,14 +235,6 @@
     )(where, out_rows, *in_rows)
 
 
-def z_swap(value):
-    pairs = []
-    for d in range(NX * NY * NC):
-        for b in range(NH * NZ):
-            pairs.append((d * NH * NZ + b, d * NH * NZ + (b ^ 1)))
-    return lax.ppermute(value, ("dp", "blk"), pairs)
-
-
 def transposed(block):
     pairs = []
     for sx in range(NX):
@@ -251,7 +242,7 @@
             for sc in range(NC):
                 for t in range(NX * NY * NC):
                     source = ((sx * NY + sy) * NC + sc) * NH * NZ + t
-                    target = (t // NC * NC + sc) * NH * NZ + t % NC * NZ + sx * NY + sy
+                    target = (t // NC * NC + sc) * NH * NZ + sx * NZ + sy * NC + t % NC
                     pairs.append((source, target))
     return lax.ppermute(block, ("dp", "blk"), pairs)
 
@@ -269,38 +260,41 @@
     table = jnp.stack(spots).astype(jnp.int32)
     give = (half * (1 - x) + table) * depth
     keep = ((half * x + table) * depth).astype(jnp.int32)
+    first, own_other = by_core(basis_in, dy=1), shift(basis_in, dc=1)
+    block = dot(out_grads, basis_out).astype(jnp.bfloat16).T
+    block, source = lax.optimization_barrier((block, activations))
     near = lax.dynamic_slice_in_dim(give, parity * SPLIT, SPLIT)
-    near = by_core(pieces(near.astype(jnp.int32), activations, depth), dx=1)
-    first, own_other = by_core(basis_in, dy=1), shift(basis_in, dc=1)
-    rest = pieces(give[2 * SPLIT :].astype(jnp.int32), activations, depth)
-    block = dot(out_grads, basis_out).astype(jnp.bfloat16).T
-    block = transposed(jnp.stack([block, z_swap(block)]))
-
-    first, near, rest, again, own_other = lax.optimization_barrier(
-        (first, near, rest, basis_in, own_other)
+    near = by_core(pieces(near.astype(jnp.int32), source, depth), dx=1)
+    rest = pieces(give[2 * SPLIT :].astype(jnp.int32), source, depth)
+    first, near, rest, again, own_other, block = lax.optimization_barrier(
+        (first, near, rest, basis_in, own_other, transposed(block))
     )
     second, far = by_core(again, dy=NY - 1), by_core(first, dy=1)
     rest, away = by_core(rest, dx=1), by_core(near, dz=1)
-
+    first_other = shift(first, dc=1)
+
+    other = lax.optimization_barrier((shift(block, dx=NX), second, away))[0]
     out_rows = lax.all_gather(
-        block,
+        jnp.stack([block, other]),
         "blk",
         axis=0,
         axis_index_groups=[[h * NZ + z for z in range(NZ)] for h in range(NH)],
     )
-    flip = (b // NZ + core) % 2
     where = jnp.stack(
-        [((x + dx) % NX) * NY + (y + dy) % NY for dx, dy in ORDER] + [flip, 1 - flip]
+        [(y + dy) % NY * NC for dx, dy in ORDER]
+        + [(x + dx + b // NZ) % 2 for dx, dy in ORDER]
+        + [core, 1 - core]
     ).astype(jnp.int32)
 
-    panels = []
-    for panel in (first, second, far):
+    panels = [basis_in, own_other, first, first_other]
+    for panel in (second, far):
         panels += [panel, shift(panel, dc=1)]
-    panels = [basis_in, own_other] + panels
     panels = [[panel] for panel in panels]
     parity = parity.reshape(1).astype(jnp.int32)
-    partial = product(near_moves, 3, parity, (near, away, rest), panels[:-2])
-    partial = product(last_moves, 1, parity, (rest,), panels[-2:], partial, FOLLOWED, TAIL_VMEM)
+    partial = product(near_moves, 2, parity, (near, away), panels[: 2 * SPLIT])
+    partial = product(
+        rest_moves, 1, parity, (rest,), panels[2 * SPLIT :], partial, FOLLOWED, TAIL_VMEM
+    )
     arrived = swap((partial * FACTOR).astype(jnp.float16))
     total = product(own_moves, len(BLOCKS), keep, (activations,), panels)
     proj_in = (total + arrived.astype(jnp.float32) * (1.0 / FACTOR)).astype(jnp.bfloat16)

time: 139 us -> 128 us (0.921)
  starting transfers between devices: 56.4 us -> 40.6 us
  local copies, waits for them, and re-layouts: 4.38 us -> 6.57 us
  waiting for transfers between devices: 34.7 us -> 36.3 us
    ppermute x6, starting transfers between devices: 36.6 us -> 21.6 us  [by_core(): return lax.ppermute(value, ('dp', 'blk'), pairs)]
    ppermute x10 -> x11, starting transfers between devices: 6.38 us -> 11.2 us  [shift(): return lax.ppermute(value, ('dp', 'blk'), pairs)]
    ppermute x6, waiting for transfers between devices: 15.9 us -> 20.4 us  [by_core(): return lax.ppermute(value, ('dp', 'blk'), pairs)]
    ppermute x1 -> x0, waiting for transfers between devices: 3.4 us -> none  [z_swap(): return lax.ppermute(value, ('dp', 'blk'), pairs)]
    unnamed x12 -> x14, local copies, waits for them, and re-layouts: 3.04 us -> 5.15 us
    ppermute x1, starting transfers between devices: 3.57 us -> 1.55 us  [transposed(): return lax.ppermute(block, ('dp', 'blk'), pairs)]
    ppermute x3, starting transfers between devices: 8.14 us -> 6.22 us  [swap(): return lax.ppermute(value, ('dp', 'blk'), pairs)]
    ppermute x1 -> x0, starting transfers between devices: 1.72 us -> none  [z_swap(): return lax.ppermute(value, ('dp', 'blk'), pairs)]
  transfers between devices with their start and end apart: 22 -> 22, of which waited for: 7 -> 9; matrix products, arithmetic and copies ran while one was open for 4% -> 2% of each run, Pallas kernels for 12% -> 13%
where the time goes in v8:
time: 128 us; the launch traced here: 127 us
  starting transfers between devices  40.6 us (32%)
  waiting for transfers between devices  36.3 us (28%)
  Pallas kernels  23.8 us (19%)
  between operations  13.5 us (11%)
  local copies, waits for them, and re-layouts  6.57 us (5%)
  other arithmetic  3.43 us (3%)
  matrix products  3 us (2%)
    ppermute x6, starting transfers between devices, by_core(): return lax.ppermute(value, ('dp', 'blk'), pairs)  21.6 us
    ppermute x6, waiting for transfers between devices, by_core(): return lax.ppermute(value, ('dp', 'blk'), pairs)  20.4 us
    pallas_call x3, Pallas kernels, product(): pl.pallas_call(lambda *refs: product_kernel(moves, layout, *refs), out_sh...  13.6 us
    ppermute x11, waiting for transfers between devices, shift(): return lax.ppermute(value, ('dp', 'blk'), pairs)  12.3 us
    ppermute x11, starting transfers between devices, shift(): return lax.ppermute(value, ('dp', 'blk'), pairs)  11.2 us
    ppermute x3, starting transfers between devices, swap(): return lax.ppermute(value, ('dp', 'blk'), pairs)  6.22 us
    pallas_call x2, Pallas kernels, pieces(): pl.pallas_call(pieces_kernel, out_shape=jax.ShapeDtypeStruct(shape, activ...  5.78 us
    unnamed x14, local copies, waits for them, and re-layouts  5.15 us
  transfers between devices with their start and end apart: 22, of which 9 were waited for; matrix products, arithmetic and copies ran while one was open for 2% of the time, Pallas kernels for 13%

profile of v8, /device:TPU:1, one launch (start us, length us, event | category | flops | bytes accessed | tf_op | source)
XLA Modules:
  0.0 127.3 jit_solution(15049522722074369680)
XLA Ops:
  6.5 1.6 %copy-done = bf16[4096,256]{1,0:T(8,128)(2,1)S(1)} copy-done((bf16[4096,256]{1,0:T(8,128)(2,1)S(1)}, bf16[4096,256]{1,0:T(8,128)(2,1)}, u32[]{:S(2)}) %copy-start) | copy-done | bytes 2097176
  8.1 3.0 %convolution_convert_fusion = bf16[256,256]{1,0:T(8,128)(2,1)} fusion(bf16[4096,256]{1,0:T(8,128)(2,1)S(1)} %copy-done, bf16[256,4096]{1,0:T(8,128)(2,1)} %param.5), kind=kOutput, calls=%fused_computation | convolution fusion | flops 536936448 | bytes 4325376 | tf_op jit(solution)/shard_map/dot_general | solution.py:61
  12.4 2.8 %shard_map.46 = bf16[2,256,896]{2,1,0:T(8,128)(2,1)} custom-call(s32[2]{0:T(128)} %dynamic_slice.3.columns_ref, bf16[256,14336]{1,0:T(8,128)(2,1)} %refs_1_.1), custom_call_target="tpu_custom_call" | custom-call | bytes 4194304 | tf_op jit(solution)/shard_map/pallas_call | solution.py:91
  15.1 3.4 %collective-permute-start.1 = (bf16[2,256,896]{2,1,0:T(8,128)(2,1)}, bf16[2,256,896]{2,1,0:T(8,128)(2,1)}, u32[]{:S(2)}, u32[]{:S(2)}) collective-permute-start(bf16[2,256,896]{2,1,0:T(8,128)(2,1)} %shard_map.46), channel_id=1, source_target_pairs={{0,128},{16,152},{1,129},{17,153},{2,130},{18,154},{3,131},{19,155... | collective-permute-start | bytes 2752520 | tf_op jit(solution)/shard_map/ppermute | solution.py:46
  18.5 2.7 %collective-permute-start = (bf16[896,512]{1,0:T(8,128)(2,1)S(1)}, bf16[896,512]{1,0:T(8,128)(2,1)S(1)}, u32[]{:S(2)}, u32[]{:S(2)}) collective-permute-start(bf16[896,512]{1,0:T(8,128)(2,1)S(1)} %copy-done.4), channel_id=1, source_target_pairs={{0,32},{16,112},{1,33},{17,113},{2,34},{18,114},{3,35},{19,115},{4... | collective-permute-start | bytes 2752520 | tf_op jit(solution)/shard_map/ppermute | solution.py:46
  21.3 1.6 %collective-permute-start.3 = (bf16[256,256]{1,0:T(8,128)(2,1)}, bf16[256,256]{1,0:T(8,128)(2,1)S(1)}, u32[]{:S(2)}, u32[]{:S(2)}) collective-permute-start(bf16[256,256]{1,0:T(8,128)(2,1)} %convolution_convert_fusion), channel_id=1, source_target_pairs={{0,0},{1,1},{2,32},{3,33},{4,64},{5,65},{6,96},{7,97},{8,128},{9,1... | collective-permute-start | bytes 393224 | tf_op jit(solution)/shard_map/ppermute | solution.py:247
  23.5 3.0 %shard_map.47 = bf16[4,256,896]{2,1,0:T(8,128)(2,1)} custom-call(s32[4]{0:T(128)} %slice.3.columns_ref, bf16[256,14336]{1,0:T(8,128)(2,1)} %refs_1_.1), custom_call_target="tpu_custom_call" | custom-call | bytes 4194304 | tf_op jit(solution)/shard_map/pallas_call | solution.py:91
  26.5 2.7 %collective-permute-done.1.refs_1_ = bf16[2,256,896]{2,1,0:T(8,128)(2,1)} collective-permute-done((bf16[2,256,896]{2,1,0:T(8,128)(2,1)}, bf16[2,256,896]{2,1,0:T(8,128)(2,1)}, u32[]{:S(2)}, u32[]{:S(2)}) %collective-permute-start.1) | collective-permute-done | bytes 917536 | tf_op jit(solution)/shard_map/ppermute | solution.py:46
  29.2 3.4 %collective-permute-done.refs_4_.refs_5_ = bf16[896,512]{1,0:T(8,128)(2,1)S(1)} collective-permute-done((bf16[896,512]{1,0:T(8,128)(2,1)S(1)}, bf16[896,512]{1,0:T(8,128)(2,1)S(1)}, u32[]{:S(2)}, u32[]{:S(2)}) %collective-permute-start) | collective-permute-done | bytes 917536 | tf_op jit(solution)/shard_map/ppermute | solution.py:46
  33.5 8.2 %collective-permute-start.6 = (bf16[2,256,896]{2,1,0:T(8,128)(2,1)}, bf16[2,256,896]{2,1,0:T(8,128)(2,1)S(1)}, u32[]{:S(2)}, u32[]{:S(2)}) collective-permute-start(bf16[2,256,896]{2,1,0:T(8,128)(2,1)} %collective-permute-done.1.refs_1_), channel_id=1, source_target_pairs={{0,1},{16,23},{1,2},{17,16},{2,3},{18,17},{3,4},{19,18},{4,5},{20,... | collective-permute-start | bytes 2752520 | tf_op jit(solution)/shard_map/ppermute | solution.py:46
  41.7 3.6 %collective-permute-start.4 = (bf16[256,256]{1,0:T(8,128)(2,1)S(1)}, bf16[256,256]{1,0:T(8,128)(2,1)S(1)}, u32[]{:S(2)}, u32[]{:S(2)}) collective-permute-start(bf16[256,256]{1,0:T(8,128)(2,1)S(1)} %collective-permute-done.3), channel_id=1, source_target_pairs={{0,8},{16,24},{1,9},{17,25},{2,10},{18,26},{3,11},{19,27},{4,12},{... | collective-permute-start | bytes 393224 | tf_op jit(solution)/shard_map/ppermute | solution.py:34
  45.3 4.9 %collective-permute-start.9 = (bf16[896,512]{1,0:T(8,128)(2,1)}, bf16[896,512]{1,0:T(8,128)(2,1)}, u32[]{:S(2)}, u32[]{:S(2)}) collective-permute-start(bf16[896,512]{1,0:T(8,128)(2,1)} %copy-done.5), channel_id=1, source_target_pairs={{0,32},{16,112},{1,33},{17,113},{2,34},{18,114},{3,35},{19,115},{4... | collective-permute-start | bytes 2752520 | tf_op jit(solution)/shard_map/ppermute | solution.py:46
  50.2 2.4 %collective-permute-start.11 = (bf16[4,256,896]{2,1,0:T(8,128)(2,1)}, bf16[4,256,896]{2,1,0:T(8,128)(2,1)}, u32[]{:S(2)}, u32[]{:S(2)}) collective-permute-start(bf16[4,256,896]{2,1,0:T(8,128)(2,1)} %shard_map.47), channel_id=1, source_target_pairs={{0,128},{16,152},{1,129},{17,153},{2,130},{18,154},{3,131},{19,155... | collective-permute-start | bytes 5505032 | tf_op jit(solution)/shard_map/ppermute | solution.py:46
  52.6 6.7 %collective-permute-done.5.refs_6_.refs_2_ = bf16[896,512]{1,0:T(8,128)(2,1)S(1)} collective-permute-done((bf16[896,512]{1,0:T(8,128)(2,1)}, bf16[896,512]{1,0:T(8,128)(2,1)S(1)}, u32[]{:S(2)}, u32[]{:S(2)}) %collective-permute-start.5) | collective-permute-done | bytes 917536 | tf_op jit(solution)/shard_map/ppermute | solution.py:46
  60.2 4.5 %collective-permute-done.9.refs_8_.refs_4_ = bf16[896,512]{1,0:T(8,128)(2,1)} collective-permute-done((bf16[896,512]{1,0:T(8,128)(2,1)}, bf16[896,512]{1,0:T(8,128)(2,1)}, u32[]{:S(2)}, u32[]{:S(2)}) %collective-permute-start.9) | collective-permute-done | bytes 917536 | tf_op jit(solution)/shard_map/ppermute | solution.py:46
  64.8 1.2 collective-permute-start.10
  66.0 4.0 %shard_map.49.refs_6_ = f32[256,512]{1,0:T(8,128)} custom-call(s32[1]{0:T(128)} %bitcast.19.refs_0_, bf16[2,256,896]{2,1,0:T(8,128)(2,1)} %collective-permute-done.1.refs_1_, bf16[2,256,896]{2,1,0:T(8,128)(2,1)} %copy-done.6, bf16[896,512]{1,0:T(8,128)(2,1)} %refs_3_.1, bf16[896,512]{1,0:T(8,128)(2,1)} %collective-permute-done.2.refs_3_.refs_4_, ...), custom_call_target="tpu_custom_call" | custom-call | flops 939524096 | bytes 4194304 | tf_op jit(solution)/shard_map/pallas_call | solution.py:144
  70.0 3.1 %collective-permute-done.11.refs_1_ = bf16[4,256,896]{2,1,0:T(8,128)(2,1)} collective-permute-done((bf16[4,256,896]{2,1,0:T(8,128)(2,1)}, bf16[4,256,896]{2,1,0:T(8,128)(2,1)}, u32[]{:S(2)}, u32[]{:S(2)}) %collective-permute-start.11) | collective-permute-done | bytes 1835040 | tf_op jit(solution)/shard_map/ppermute | solution.py:46
  73.1 1.0 copy-done.3
  74.1 3.0 %shard_map.50 = f32[256,512]{1,0:T(8,128)S(1)} custom-call(s32[1]{0:T(128)} %bitcast.19.refs_0_, bf16[4,256,896]{2,1,0:T(8,128)(2,1)} %collective-permute-done.11.refs_1_, bf16[896,512]{1,0:T(8,128)(2,1)S(1)} %collective-permute-done.5.refs_6_.refs_2_, bf16[896,512]{1,0:T(8,128)(2,1)} %collective-permute-done.8.refs_7_.refs_3_, ...), custom_call_target="tpu_custom_call" | custom-call | flops 6939524096 | bytes 4194304 | tf_op jit(solution)/shard_map/pallas_call | solution.py:144
  77.2 4.4 %collective-permute-start.12 = (f16[256,512]{1,0:T(8,128)(2,1)S(1)}, f16[256,512]{1,0:T(8,128)(2,1)S(1)}, u32[]{:S(2)}, u32[]{:S(2)}) collective-permute-start(f16[256,512]{1,0:T(8,128)(2,1)S(1)} %multiply_convert_fusion), channel_id=1, source_target_pairs={{0,128},{16,144},{1,129},{17,145},{2,130},{18,146},{3,131},{19,147... | collective-permute-start | bytes 786440 | tf_op jit(solution)/shard_map/ppermute | solution.py:57
  81.6 6.6 %shard_map.48 = f32[256,512]{1,0:T(8,128)} custom-call(s32[8]{0:T(128)} %get-tuple-element.27.refs_0_, bf16[256,14336]{1,0:T(8,128)(2,1)} %refs_1_.1, bf16[896,512]{1,0:T(8,128)(2,1)} %refs_3_.1, bf16[896,512]{1,0:T(8,128)(2,1)} %collective-permute-done.2.refs_3_.refs_4_, bf16[896,512]{1,0:T(8,128)(2,1)} %copy-done.5, ...), custom_call_target="tpu_custom_call" | custom-call | flops 1879048192 | bytes 4194304 | tf_op jit(solution)/shard_map/pallas_call | solution.py:144
  88.2 1.1 add_convert_fusion.refs_0_
  89.4 1.2 collective-permute-start.15
  90.9 2.4 %collective-permute-start.14 = (bf16[256,512]{1,0:T(8,128)(2,1)S(1)}, bf16[256,512]{1,0:T(8,128)(2,1)S(1)}, u32[]{:S(2)}, u32[]{:S(2)}) collective-permute-start(bf16[256,512]{1,0:T(8,128)(2,1)S(1)} %add_convert_fusion.refs_0_), channel_id=1, source_target_pairs={{0,96},{16,112},{1,97},{17,113},{2,98},{18,114},{3,99},{19,115},{4... | collective-permute-start | bytes 786440 | tf_op jit(solution)/shard_map/ppermute | solution.py:34
  93.2 3.6 %collective-permute-done.15.refs_3_ = bf16[256,512]{1,0:T(8,128)(2,1)S(1)} collective-permute-done((bf16[256,512]{1,0:T(8,128)(2,1)S(1)}, bf16[256,512]{1,0:T(8,128)(2,1)S(1)}, u32[]{:S(2)}, u32[]{:S(2)}) %collective-permute-start.15) | collective-permute-done | bytes 262176 | tf_op jit(solution)/shard_map/ppermute | solution.py:57
  96.8 2.7 %collective-permute-start.18 = (bf16[256,512]{1,0:T(8,128)(2,1)S(1)}, bf16[256,512]{1,0:T(8,128)(2,1)}, u32[]{:S(2)}, u32[]{:S(2)}) collective-permute-start(bf16[256,512]{1,0:T(8,128)(2,1)S(1)} %collective-permute-done.15.refs_3_), channel_id=1, source_target_pairs={{0,96},{16,112},{1,97},{17,113},{2,98},{18,114},{3,99},{19,115},{4... | collective-permute-start | bytes 786440 | tf_op jit(solution)/shard_map/ppermute | solution.py:34
  100.3 5.0 %collective-permute-done.13.refs_1_ = bf16[256,512]{1,0:T(8,128)(2,1)S(1)} collective-permute-done((bf16[256,512]{1,0:T(8,128)(2,1)S(1)}, bf16[256,512]{1,0:T(8,128)(2,1)S(1)}, u32[]{:S(2)}, u32[]{:S(2)}) %collective-permute-start.13) | collective-permute-done | bytes 262176 | tf_op jit(solution)/shard_map/ppermute | solution.py:34
  105.2 5.7 %collective-permute-done.17.refs_5_ = bf16[256,512]{1,0:T(8,128)(2,1)} collective-permute-done((bf16[256,512]{1,0:T(8,128)(2,1)S(1)}, bf16[256,512]{1,0:T(8,128)(2,1)}, u32[]{:S(2)}, u32[]{:S(2)}) %collective-permute-start.17) | collective-permute-done | bytes 262176 | tf_op jit(solution)/shard_map/ppermute | solution.py:34
  111.0 1.6 %copy-done.1 = bf16[16,256,256]{2,1,0:T(8,128)(2,1)S(1)} copy-done((bf16[16,256,256]{2,1,0:T(8,128)(2,1)S(1)}, bf16[16,256,256]{2,1,0:T(8,128)(2,1)}, u32[]{:S(2)}) %copy-start.1) | copy-done | bytes 2097176
  112.6 4.4 %shard_map.51 = (f32[256,512]{1,0:T(8,128)S(1)}, f32[256,512]{1,0:T(8,128)S(1)}) custom-call(s32[18]{0:T(128)S(1)} %stack.81.where_ref, bf16[8,2,256,256]{3,2,1,0:T(8,128)(2,1)S(1)} %bitcast.22, bf16[256,512]{1,0:T(8,128)(2,1)S(1)} %add_convert_fusion.refs_0_, bf16[256,512]{1,0:T(8,128)(2,1)S(1)} %collective-permute-done.13.refs_1_, ...), custom_call_target="tpu_custom_call" | custom-call | flops 1073741824 | bytes 3145728 | tf_op jit(solution)/shard_map/pallas_call | solution.py:219
  118.0 1.5 %collective-permute-done.20 = f32[256,512]{1,0:T(8,128)S(1)} collective-permute-done((f32[256,512]{1,0:T(8,128)S(1)}, f32[256,512]{1,0:T(8,128)S(1)}, u32[]{:S(2)}, u32[]{:S(2)}) %collective-permute-start.20) | collective-permute-done | bytes 524320 | tf_op jit(solution)/shard_map/ppermute | solution.py:34
  (43 shorter events, 6.7 us)
Async XLA Ops:
  6.5 1.6 %copy-start = (bf16[4096,256]{1,0:T(8,128)(2,1)S(1)}, bf16[4096,256]{1,0:T(8,128)(2,1)}, u32[]{:S(2)}) copy-start(bf16[4096,256]{1,0:T(8,128)(2,1)} %param.7) | copy-start | bytes 6291460
  6.5 104.4 %all-gather.3.cloned.1.call-start = ((), (), s32[]{:S(2)}) async-start(), calls=%async_computation | async-start | bytes 2359296 | tf_op jit(solution)/shard_map/all_gather | solution.py:277
  12.4 6.2 %copy-start.4 = (bf16[896,512]{1,0:T(8,128)(2,1)S(1)}, bf16[896,512]{1,0:T(8,128)(2,1)}, u32[]{:S(2)}) copy-start(bf16[896,512]{1,0:T(8,128)(2,1)} %refs_3_.1) | copy-start | bytes 2752516
  15.1 14.0 %collective-permute-start.1 = (bf16[2,256,896]{2,1,0:T(8,128)(2,1)}, bf16[2,256,896]{2,1,0:T(8,128)(2,1)}, u32[]{:S(2)}, u32[]{:S(2)}) collective-permute-start(bf16[2,256,896]{2,1,0:T(8,128)(2,1)} %shard_map.46), channel_id=1, source_target_pairs={{0,128},{16,152},{1,129},{17,153},{2,130},{18,154},{3,131},{19,155... | collective-permute-start | bytes 2752520 | tf_op jit(solution)/shard_map/ppermute | solution.py:46
  18.5 14.1 %collective-permute-start = (bf16[896,512]{1,0:T(8,128)(2,1)S(1)}, bf16[896,512]{1,0:T(8,128)(2,1)S(1)}, u32[]{:S(2)}, u32[]{:S(2)}) collective-permute-start(bf16[896,512]{1,0:T(8,128)(2,1)S(1)} %copy-done.4), channel_id=1, source_target_pairs={{0,32},{16,112},{1,33},{17,113},{2,34},{18,114},{3,35},{19,115},{4... | collective-permute-start | bytes 2752520 | tf_op jit(solution)/shard_map/ppermute | solution.py:46
  21.3 11.3 %collective-permute-start.2 = (bf16[896,512]{1,0:T(8,128)(2,1)S(1)}, bf16[896,512]{1,0:T(8,128)(2,1)}, u32[]{:S(2)}, u32[]{:S(2)}) collective-permute-start(bf16[896,512]{1,0:T(8,128)(2,1)S(1)} %copy-done.4), channel_id=1, source_target_pairs={{0,16},{16,0},{1,17},{17,1},{2,18},{18,2},{3,19},{19,3},{4,20},{20... | collective-permute-start | bytes 2752520 | tf_op jit(solution)/shard_map/ppermute | solution.py:34
  21.3 5.2 %collective-permute-start.3 = (bf16[256,256]{1,0:T(8,128)(2,1)}, bf16[256,256]{1,0:T(8,128)(2,1)S(1)}, u32[]{:S(2)}, u32[]{:S(2)}) collective-permute-start(bf16[256,256]{1,0:T(8,128)(2,1)} %convolution_convert_fusion), channel_id=1, source_target_pairs={{0,0},{1,1},{2,32},{3,33},{4,64},{5,65},{6,96},{7,97},{8,128},{9,1... | collective-permute-start | bytes 393224 | tf_op jit(solution)/shard_map/ppermute | solution.py:247
  32.6 0.9 copy-start.5
  33.5 19.1 %collective-permute-start.6 = (bf16[2,256,896]{2,1,0:T(8,128)(2,1)}, bf16[2,256,896]{2,1,0:T(8,128)(2,1)S(1)}, u32[]{:S(2)}, u32[]{:S(2)}) collective-permute-start(bf16[2,256,896]{2,1,0:T(8,128)(2,1)} %collective-permute-done.1.refs_1_), channel_id=1, source_target_pairs={{0,1},{16,23},{1,2},{17,16},{2,3},{18,17},{3,4},{19,18},{4,5},{20,... | collective-permute-start | bytes 2752520 | tf_op jit(solution)/shard_map/ppermute | solution.py:46
  41.7 17.6 %collective-permute-start.5 = (bf16[896,512]{1,0:T(8,128)(2,1)}, bf16[896,512]{1,0:T(8,128)(2,1)S(1)}, u32[]{:S(2)}, u32[]{:S(2)}) collective-permute-start(bf16[896,512]{1,0:T(8,128)(2,1)} %refs_3_.1), channel_id=1, source_target_pairs={{0,96},{16,48},{1,97},{17,49},{2,98},{18,50},{3,99},{19,51},{4,100... | collective-permute-start | bytes 2752520 | tf_op jit(solution)/shard_map/ppermute | solution.py:46
  41.7 10.9 %collective-permute-start.4 = (bf16[256,256]{1,0:T(8,128)(2,1)S(1)}, bf16[256,256]{1,0:T(8,128)(2,1)S(1)}, u32[]{:S(2)}, u32[]{:S(2)}) collective-permute-start(bf16[256,256]{1,0:T(8,128)(2,1)S(1)} %collective-permute-done.3), channel_id=1, source_target_pairs={{0,8},{16,24},{1,9},{17,25},{2,10},{18,26},{3,11},{19,27},{4,12},{... | collective-permute-start | bytes 393224 | tf_op jit(solution)/shard_map/ppermute | solution.py:34
  45.3 19.5 %collective-permute-start.9 = (bf16[896,512]{1,0:T(8,128)(2,1)}, bf16[896,512]{1,0:T(8,128)(2,1)}, u32[]{:S(2)}, u32[]{:S(2)}) collective-permute-start(bf16[896,512]{1,0:T(8,128)(2,1)} %copy-done.5), channel_id=1, source_target_pairs={{0,32},{16,112},{1,33},{17,113},{2,34},{18,114},{3,35},{19,115},{4... | collective-permute-start | bytes 2752520 | tf_op jit(solution)/shard_map/ppermute | solution.py:46
  50.2 22.9 %collective-permute-start.11 = (bf16[4,256,896]{2,1,0:T(8,128)(2,1)}, bf16[4,256,896]{2,1,0:T(8,128)(2,1)}, u32[]{:S(2)}, u32[]{:S(2)}) collective-permute-start(bf16[4,256,896]{2,1,0:T(8,128)(2,1)} %shard_map.47), channel_id=1, source_target_pairs={{0,128},{16,152},{1,129},{17,153},{2,130},{18,154},{3,131},{19,155... | collective-permute-start | bytes 5505032 | tf_op jit(solution)/shard_map/ppermute | solution.py:46
  52.6 6.7 %copy-start.6 = (bf16[2,256,896]{2,1,0:T(8,128)(2,1)}, bf16[2,256,896]{2,1,0:T(8,128)(2,1)S(1)}, u32[]{:S(2)}) copy-start(bf16[2,256,896]{2,1,0:T(8,128)(2,1)S(1)} %collective-permute-done.6.refs_2_) | copy-start | bytes 2752516
  59.3 13.8 %copy-start.2 = (bf16[896,512]{1,0:T(8,128)(2,1)}, bf16[896,512]{1,0:T(8,128)(2,1)S(1)}, u32[]{:S(2)}) copy-start(bf16[896,512]{1,0:T(8,128)(2,1)S(1)} %collective-permute-done.5.refs_6_.refs_2_) | copy-start | bytes 2752516
  60.1 5.9 %collective-permute-start.7 = (bf16[896,512]{1,0:T(8,128)(2,1)}, bf16[896,512]{1,0:T(8,128)(2,1)}, u32[]{:S(2)}, u32[]{:S(2)}) collective-permute-start(bf16[896,512]{1,0:T(8,128)(2,1)} %copy-done.5), channel_id=1, source_target_pairs={{0,16},{16,0},{1,17},{17,1},{2,18},{18,2},{3,19},{19,3},{4,20},{20... | collective-permute-start | bytes 2752520 | tf_op jit(solution)/shard_map/ppermute | solution.py:34
  64.8 5.2 %collective-permute-start.10 = (bf16[896,512]{1,0:T(8,128)(2,1)}, bf16[896,512]{1,0:T(8,128)(2,1)}, u32[]{:S(2)}, u32[]{:S(2)}) collective-permute-start(bf16[896,512]{1,0:T(8,128)(2,1)} %collective-permute-done.9.refs_8_.refs_4_), channel_id=1, source_target_pairs={{0,16},{16,0},{1,17},{17,1},{2,18},{18,2},{3,19},{19,3},{4,20},{20... | collective-permute-start | bytes 2752520 | tf_op jit(solution)/shard_map/ppermute | solution.py:34
  66.0 4.0 %collective-permute-start.8 = (bf16[896,512]{1,0:T(8,128)(2,1)S(1)}, bf16[896,512]{1,0:T(8,128)(2,1)}, u32[]{:S(2)}, u32[]{:S(2)}) collective-permute-start(bf16[896,512]{1,0:T(8,128)(2,1)S(1)} %collective-permute-done.5.refs_6_.refs_2_), channel_id=1, source_target_pairs={{0,16},{16,0},{1,17},{17,1},{2,18},{18,2},{3,19},{19,3},{4,20},{20... | collective-permute-start | bytes 2752520 | tf_op jit(solution)/shard_map/ppermute | solution.py:34
  73.1 1.0 copy-start.3
  77.2 11.1 %collective-permute-start.12 = (f16[256,512]{1,0:T(8,128)(2,1)S(1)}, f16[256,512]{1,0:T(8,128)(2,1)S(1)}, u32[]{:S(2)}, u32[]{:S(2)}) collective-permute-start(f16[256,512]{1,0:T(8,128)(2,1)S(1)} %multiply_convert_fusion), channel_id=1, source_target_pairs={{0,128},{16,144},{1,129},{17,145},{2,130},{18,146},{3,131},{19,147... | collective-permute-start | bytes 786440 | tf_op jit(solution)/shard_map/ppermute | solution.py:57
  89.4 7.4 %collective-permute-start.15 = (bf16[256,512]{1,0:T(8,128)(2,1)S(1)}, bf16[256,512]{1,0:T(8,128)(2,1)S(1)}, u32[]{:S(2)}, u32[]{:S(2)}) collective-permute-start(bf16[256,512]{1,0:T(8,128)(2,1)S(1)} %add_convert_fusion.refs_0_), channel_id=1, source_target_pairs={{0,128},{16,144},{1,129},{17,145},{2,130},{18,146},{3,131},{19,147... | collective-permute-start | bytes 786440 | tf_op jit(solution)/shard_map/ppermute | solution.py:57
  90.5 9.0 %collective-permute-start.16 = (bf16[256,512]{1,0:T(8,128)(2,1)S(1)}, bf16[256,512]{1,0:T(8,128)(2,1)S(1)}, u32[]{:S(2)}, u32[]{:S(2)}) collective-permute-start(bf16[256,512]{1,0:T(8,128)(2,1)S(1)} %add_convert_fusion.refs_0_), channel_id=1, source_target_pairs={{0,64},{16,80},{1,65},{17,81},{2,66},{18,82},{3,67},{19,83},{4,68}... | collective-permute-start | bytes 786440 | tf_op jit(solution)/shard_map/ppermute | solution.py:34
  90.5 14.7 %collective-permute-start.13 = (bf16[256,512]{1,0:T(8,128)(2,1)S(1)}, bf16[256,512]{1,0:T(8,128)(2,1)S(1)}, u32[]{:S(2)}, u32[]{:S(2)}) collective-permute-start(bf16[256,512]{1,0:T(8,128)(2,1)S(1)} %add_convert_fusion.refs_0_), channel_id=1, source_target_pairs={{0,32},{16,48},{1,33},{17,49},{2,34},{18,50},{3,35},{19,51},{4,36}... | collective-permute-start | bytes 786440 | tf_op jit(solution)/shard_map/ppermute | solution.py:34
  90.9 14.4 %collective-permute-start.14 = (bf16[256,512]{1,0:T(8,128)(2,1)S(1)}, bf16[256,512]{1,0:T(8,128)(2,1)S(1)}, u32[]{:S(2)}, u32[]{:S(2)}) collective-permute-start(bf16[256,512]{1,0:T(8,128)(2,1)S(1)} %add_convert_fusion.refs_0_), channel_id=1, source_target_pairs={{0,96},{16,112},{1,97},{17,113},{2,98},{18,114},{3,99},{19,115},{4... | collective-permute-start | bytes 786440 | tf_op jit(solution)/shard_map/ppermute | solution.py:34
  96.8 14.1 %collective-permute-start.17 = (bf16[256,512]{1,0:T(8,128)(2,1)S(1)}, bf16[256,512]{1,0:T(8,128)(2,1)}, u32[]{:S(2)}, u32[]{:S(2)}) collective-permute-start(bf16[256,512]{1,0:T(8,128)(2,1)S(1)} %collective-permute-done.15.refs_3_), channel_id=1, source_target_pairs={{0,32},{16,48},{1,33},{17,49},{2,34},{18,50},{3,35},{19,51},{4,36}... | collective-permute-start | bytes 786440 | tf_op jit(solution)/shard_map/ppermute | solution.py:34
  96.8 14.1 %collective-permute-start.18 = (bf16[256,512]{1,0:T(8,128)(2,1)S(1)}, bf16[256,512]{1,0:T(8,128)(2,1)}, u32[]{:S(2)}, u32[]{:S(2)}) collective-permute-start(bf16[256,512]{1,0:T(8,128)(2,1)S(1)} %collective-permute-done.15.refs_3_), channel_id=1, source_target_pairs={{0,96},{16,112},{1,97},{17,113},{2,98},{18,114},{3,99},{19,115},{4... | collective-permute-start | bytes 786440 | tf_op jit(solution)/shard_map/ppermute | solution.py:34
  99.5 11.5 %collective-permute-start.19 = (bf16[256,512]{1,0:T(8,128)(2,1)S(1)}, bf16[256,512]{1,0:T(8,128)(2,1)}, u32[]{:S(2)}, u32[]{:S(2)}) collective-permute-start(bf16[256,512]{1,0:T(8,128)(2,1)S(1)} %collective-permute-done.16.refs_4_), channel_id=1, source_target_pairs={{0,128},{16,144},{1,129},{17,145},{2,130},{18,146},{3,131},{19,147... | collective-permute-start | bytes 786440 | tf_op jit(solution)/shard_map/ppermute | solution.py:57
  111.0 1.6 %copy-start.1 = (bf16[16,256,256]{2,1,0:T(8,128)(2,1)S(1)}, bf16[16,256,256]{2,1,0:T(8,128)(2,1)}, u32[]{:S(2)}) copy-start(bf16[16,256,256]{2,1,0:T(8,128)(2,1)} %all-gather.3.cloned.1.call-done) | copy-start | bytes 6291460
  117.0 2.5 %collective-permute-start.20 = (f32[256,512]{1,0:T(8,128)S(1)}, f32[256,512]{1,0:T(8,128)S(1)}, u32[]{:S(2)}, u32[]{:S(2)}) collective-permute-start(f32[256,512]{1,0:T(8,128)S(1)} %get-tuple-element.26), channel_id=1, source_target_pairs={{0,16},{16,0},{1,17},{17,1},{2,18},{18,2},{3,19},{19,3},{4,20},{20... | collective-permute-start | bytes 1572872 | tf_op jit(solution)/shard_map/ppermute | solution.py:34
Sparse Core Ops, SparseCore 0:
  60.3 43.0 all-gather.2

commit v9 on v8

--- a/solution.py
+++ b/solution.py
@@ -261,19 +261,19 @@
     give = (half * (1 - x) + table) * depth
     keep = ((half * x + table) * depth).astype(jnp.int32)
     first, own_other = by_core(basis_in, dy=1), shift(basis_in, dc=1)
-    block = dot(out_grads, basis_out).astype(jnp.bfloat16).T
-    block, source = lax.optimization_barrier((block, activations))
     near = lax.dynamic_slice_in_dim(give, parity * SPLIT, SPLIT)
-    near = by_core(pieces(near.astype(jnp.int32), source, depth), dx=1)
-    rest = pieces(give[2 * SPLIT :].astype(jnp.int32), source, depth)
-    first, near, rest, again, own_other, block = lax.optimization_barrier(
-        (first, near, rest, basis_in, own_other, transposed(block))
-    )
+    near = pieces(near.astype(jnp.int32), activations, depth)
+    rest = pieces(give[2 * SPLIT :].astype(jnp.int32), activations, depth)
+    block = transposed(dot(out_grads, basis_out).astype(jnp.bfloat16).T)
+    near, rest, block = lax.optimization_barrier((near, rest, block))
+    near = by_core(near, dx=1)
+    first, again = lax.optimization_barrier((first, basis_in))
     second, far = by_core(again, dy=NY - 1), by_core(first, dy=1)
+    first_other = shift(first, dc=1)
+    near, rest = lax.optimization_barrier((near, rest))
     rest, away = by_core(rest, dx=1), by_core(near, dz=1)
-    first_other = shift(first, dc=1)
-
-    other = lax.optimization_barrier((shift(block, dx=NX), second, away))[0]
+
+    other = shift(block, dx=NX)
     out_rows = lax.all_gather(
         jnp.stack([block, other]),
         "blk",

time: 128 us -> 123 us (0.961)
  waiting for transfers between devices: 36.3 us -> 32.4 us
    ppermute x11, starting transfers between devices: 11.2 us -> 16 us  [shift(): return lax.ppermute(value, ('dp', 'blk'), pairs)]
    ppermute x3, starting transfers between devices: 6.22 us -> 2.31 us  [swap(): return lax.ppermute(value, ('dp', 'blk'), pairs)]
    ppermute x3, waiting for transfers between devices: 3.61 us -> 0.58 us  [swap(): return lax.ppermute(value, ('dp', 'blk'), pairs)]
    ppermute x6, waiting for transfers between devices: 20.4 us -> 18.6 us  [by_core(): return lax.ppermute(value, ('dp', 'blk'), pairs)]
    unnamed x14 -> x8, local copies, waits for them, and re-layouts: 5.15 us -> 4.22 us
  transfers between devices with their start and end apart: 22 -> 22, of which waited for: 9 -> 10; matrix products, arithmetic and copies ran while one was open for 2% -> 3% of each run, Pallas kernels for 13% -> 16%
where the time goes in v9:
time: 123 us; the launch traced here: 122 us
  starting transfers between devices  40.6 us (33%)
  waiting for transfers between devices  32.4 us (26%)
  Pallas kernels  23.9 us (19%)
  between operations  13.6 us (11%)
  local copies, waits for them, and re-layouts  5.57 us (5%)
  other arithmetic  3.38 us (3%)
  matrix products  2.34 us (2%)
    ppermute x6, starting transfers between devices, by_core(): return lax.ppermute(value, ('dp', 'blk'), pairs)  21.6 us
    ppermute x6, waiting for transfers between devices, by_core(): return lax.ppermute(value, ('dp', 'blk'), pairs)  18.6 us
    ppermute x11, starting transfers between devices, shift(): return lax.ppermute(value, ('dp', 'blk'), pairs)  16 us
    pallas_call x3, Pallas kernels, product(): pl.pallas_call(lambda *refs: product_kernel(moves, layout, *refs), out_sh...  13.9 us
    ppermute x11, waiting for transfers between devices, shift(): return lax.ppermute(value, ('dp', 'blk'), pairs)  13.1 us
    pallas_call x2, Pallas kernels, pieces(): pl.pallas_call(pieces_kernel, out_shape=jax.ShapeDtypeStruct(shape, activ...  5.64 us
    pallas_call x1, Pallas kernels, sums_of_squares(): pl.pallas_call(squares_kernel, out_shape=[jax.ShapeDtypeStruct((rows, wid...  4.45 us
    unnamed x8, local copies, waits for them, and re-layouts  4.22 us
  transfers between devices with their start and end apart: 22, of which 10 were waited for; matrix products, arithmetic and copies ran while one was open for 3% of the time, Pallas kernels for 16%

profile of v9, /device:TPU:1, one launch (start us, length us, event | category | flops | bytes accessed | tf_op | source)
XLA Modules:
  0.0 121.7 jit_solution(560669909049261949)
XLA Ops:
  6.5 1.6 %copy-done = bf16[4096,256]{1,0:T(8,128)(2,1)S(1)} copy-done((bf16[4096,256]{1,0:T(8,128)(2,1)S(1)}, bf16[4096,256]{1,0:T(8,128)(2,1)}, u32[]{:S(2)}) %copy-start) | copy-done | bytes 2097176
  8.1 2.3 %convolution_convert_fusion = bf16[256,256]{1,0:T(8,128)(2,1)S(1)} fusion(bf16[4096,256]{1,0:T(8,128)(2,1)S(1)} %copy-done, bf16[256,4096]{1,0:T(8,128)(2,1)} %param.5), kind=kOutput, calls=%fused_computation | convolution fusion | flops 536936448 | bytes 4325376 | tf_op jit(solution)/shard_map/dot_general | solution.py:61
  11.2 10.6 %collective-permute-start.3 = (bf16[896,512]{1,0:T(8,128)(2,1)}, bf16[896,512]{1,0:T(8,128)(2,1)}, u32[]{:S(2)}, u32[]{:S(2)}) collective-permute-start(bf16[896,512]{1,0:T(8,128)(2,1)} %refs_3_.1), channel_id=1, source_target_pairs={{0,32},{16,112},{1,33},{17,113},{2,34},{18,114},{3,35},{19,115},{4... | collective-permute-start | bytes 2752520 | tf_op jit(solution)/shard_map/ppermute | solution.py:46
  23.6 3.0 %shard_map.47 = bf16[4,256,896]{2,1,0:T(8,128)(2,1)} custom-call(s32[4]{0:T(128)} %slice.3.columns_ref, bf16[256,14336]{1,0:T(8,128)(2,1)} %refs_1_.1), custom_call_target="tpu_custom_call" | custom-call | bytes 4194304 | tf_op jit(solution)/shard_map/pallas_call | solution.py:91
  26.6 2.7 %shard_map.46 = bf16[2,256,896]{2,1,0:T(8,128)(2,1)} custom-call(s32[2]{0:T(128)} %dynamic_slice.3.columns_ref, bf16[256,14336]{1,0:T(8,128)(2,1)} %refs_1_.1), custom_call_target="tpu_custom_call" | custom-call | bytes 4194304 | tf_op jit(solution)/shard_map/pallas_call | solution.py:91
  29.2 2.6 %collective-permute-start.9 = (bf16[2,256,896]{2,1,0:T(8,128)(2,1)}, bf16[2,256,896]{2,1,0:T(8,128)(2,1)}, u32[]{:S(2)}, u32[]{:S(2)}) collective-permute-start(bf16[2,256,896]{2,1,0:T(8,128)(2,1)} %shard_map.46), channel_id=1, source_target_pairs={{0,128},{16,152},{1,129},{17,153},{2,130},{18,154},{3,131},{19,155... | collective-permute-start | bytes 2752520 | tf_op jit(solution)/shard_map/ppermute | solution.py:46
  31.8 1.4 %collective-permute-start.1 = (bf16[256,256]{1,0:T(8,128)(2,1)S(1)}, bf16[256,256]{1,0:T(8,128)(2,1)S(1)}, u32[]{:S(2)}, u32[]{:S(2)}) collective-permute-start(bf16[256,256]{1,0:T(8,128)(2,1)S(1)} %collective-permute-done), channel_id=1, source_target_pairs={{0,8},{16,24},{1,9},{17,25},{2,10},{18,26},{3,11},{19,27},{4,12},{... | collective-permute-start | bytes 393224 | tf_op jit(solution)/shard_map/ppermute | solution.py:34
  33.2 3.3 %collective-permute-start.7 = (bf16[896,512]{1,0:T(8,128)(2,1)}, bf16[896,512]{1,0:T(8,128)(2,1)S(1)}, u32[]{:S(2)}, u32[]{:S(2)}) collective-permute-start(bf16[896,512]{1,0:T(8,128)(2,1)} %collective-permute-done.3.refs_4_.refs_5_), channel_id=1, source_target_pairs={{0,32},{16,112},{1,33},{17,113},{2,34},{18,114},{3,35},{19,115},{4... | collective-permute-start | bytes 2752520 | tf_op jit(solution)/shard_map/ppermute | solution.py:46
  36.5 7.4 %collective-permute-done.9.refs_1_ = bf16[2,256,896]{2,1,0:T(8,128)(2,1)} collective-permute-done((bf16[2,256,896]{2,1,0:T(8,128)(2,1)}, bf16[2,256,896]{2,1,0:T(8,128)(2,1)}, u32[]{:S(2)}, u32[]{:S(2)}) %collective-permute-start.9) | collective-permute-done | bytes 917536 | tf_op jit(solution)/shard_map/ppermute | solution.py:46
  43.9 3.3 %collective-permute-start.10 = (bf16[4,256,896]{2,1,0:T(8,128)(2,1)}, bf16[4,256,896]{2,1,0:T(8,128)(2,1)}, u32[]{:S(2)}, u32[]{:S(2)}) collective-permute-start(bf16[4,256,896]{2,1,0:T(8,128)(2,1)} %shard_map.47), channel_id=1, source_target_pairs={{0,128},{16,152},{1,129},{17,153},{2,130},{18,154},{3,131},{19,155... | collective-permute-start | bytes 5505032 | tf_op jit(solution)/shard_map/ppermute | solution.py:46
  48.0 1.9 %collective-permute-start.11 = (bf16[2,256,896]{2,1,0:T(8,128)(2,1)}, bf16[2,256,896]{2,1,0:T(8,128)(2,1)}, u32[]{:S(2)}, u32[]{:S(2)}) collective-permute-start(bf16[2,256,896]{2,1,0:T(8,128)(2,1)} %collective-permute-done.9.refs_1_), channel_id=1, source_target_pairs={{0,1},{16,23},{1,2},{17,16},{2,3},{18,17},{3,4},{19,18},{4,5},{20,... | collective-permute-start | bytes 2752520 | tf_op jit(solution)/shard_map/ppermute | solution.py:46
  49.9 5.5 %collective-permute-done.7.refs_8_.refs_4_ = bf16[896,512]{1,0:T(8,128)(2,1)S(1)} collective-permute-done((bf16[896,512]{1,0:T(8,128)(2,1)}, bf16[896,512]{1,0:T(8,128)(2,1)S(1)}, u32[]{:S(2)}, u32[]{:S(2)}) %collective-permute-start.7) | collective-permute-done | bytes 917536 | tf_op jit(solution)/shard_map/ppermute | solution.py:46
  55.4 2.4 %collective-permute-start.8 = (bf16[896,512]{1,0:T(8,128)(2,1)S(1)}, bf16[896,512]{1,0:T(8,128)(2,1)}, u32[]{:S(2)}, u32[]{:S(2)}) collective-permute-start(bf16[896,512]{1,0:T(8,128)(2,1)S(1)} %collective-permute-done.7.refs_8_.refs_4_), channel_id=1, source_target_pairs={{0,16},{16,0},{1,17},{17,1},{2,18},{18,2},{3,19},{19,3},{4,20},{20... | collective-permute-start | bytes 2752520 | tf_op jit(solution)/shard_map/ppermute | solution.py:34
  57.8 1.2 collective-permute-done.5.refs_6_.refs_2_
  59.0 4.4 %collective-permute-done.11.refs_2_ = bf16[2,256,896]{2,1,0:T(8,128)(2,1)} collective-permute-done((bf16[2,256,896]{2,1,0:T(8,128)(2,1)}, bf16[2,256,896]{2,1,0:T(8,128)(2,1)}, u32[]{:S(2)}, u32[]{:S(2)}) %collective-permute-start.11) | collective-permute-done | bytes 917536 | tf_op jit(solution)/shard_map/ppermute | solution.py:46
  63.4 4.0 %shard_map.49.refs_6_ = f32[256,512]{1,0:T(8,128)} custom-call(s32[1]{0:T(128)} %bitcast.19.refs_0_, bf16[2,256,896]{2,1,0:T(8,128)(2,1)} %collective-permute-done.9.refs_1_, bf16[2,256,896]{2,1,0:T(8,128)(2,1)} %collective-permute-done.11.refs_2_, bf16[896,512]{1,0:T(8,128)(2,1)} %refs_3_.1, bf16[896,512]{1,0:T(8,128)(2,1)} %collective-permute-done.2.refs_3_.refs_4_, ...), custom_call_target="tpu_custom_call" | custom-call | flops 939524096 | bytes 4194304 | tf_op jit(solution)/shard_map/pallas_call | solution.py:144
  67.6 1.0 copy-done.3
  68.7 3.2 %shard_map.50 = f32[256,512]{1,0:T(8,128)S(1)} custom-call(s32[1]{0:T(128)} %bitcast.19.refs_0_, bf16[4,256,896]{2,1,0:T(8,128)(2,1)} %collective-permute-done.10.refs_1_, bf16[896,512]{1,0:T(8,128)(2,1)} %collective-permute-done.5.refs_6_.refs_2_, bf16[896,512]{1,0:T(8,128)(2,1)} %collective-permute-done.6.refs_7_.refs_3_, ...), custom_call_target="tpu_custom_call" | custom-call | flops 6939524096 | bytes 4194304 | tf_op jit(solution)/shard_map/pallas_call | solution.py:144
  72.1 6.6 %shard_map.48 = f32[256,512]{1,0:T(8,128)} custom-call(s32[8]{0:T(128)} %get-tuple-element.23.refs_0_, bf16[256,14336]{1,0:T(8,128)(2,1)} %refs_1_.1, bf16[896,512]{1,0:T(8,128)(2,1)} %refs_3_.1, bf16[896,512]{1,0:T(8,128)(2,1)} %collective-permute-done.2.refs_3_.refs_4_, bf16[896,512]{1,0:T(8,128)(2,1)} %collective-permute-done.3.refs_4_.refs_5_, ...), custom_call_target="tpu_custom_call" | custom-call | flops 1879048192 | bytes 4194304 | tf_op jit(solution)/shard_map/pallas_call | solution.py:144
  79.3 1.1 add_convert_fusion.refs_0_
  80.4 1.1 collective-permute-start.15
  81.6 6.1 %collective-permute-start.16 = (bf16[256,512]{1,0:T(8,128)(2,1)S(1)}, bf16[256,512]{1,0:T(8,128)(2,1)S(1)}, u32[]{:S(2)}, u32[]{:S(2)}) collective-permute-start(bf16[256,512]{1,0:T(8,128)(2,1)S(1)} %add_convert_fusion.refs_0_), channel_id=1, source_target_pairs={{0,64},{16,80},{1,65},{17,81},{2,66},{18,82},{3,67},{19,83},{4,68}... | collective-permute-start | bytes 786440 | tf_op jit(solution)/shard_map/ppermute | solution.py:34
  87.7 2.7 %collective-permute-start.14 = (bf16[256,512]{1,0:T(8,128)(2,1)S(1)}, bf16[256,512]{1,0:T(8,128)(2,1)S(1)}, u32[]{:S(2)}, u32[]{:S(2)}) collective-permute-start(bf16[256,512]{1,0:T(8,128)(2,1)S(1)} %add_convert_fusion.refs_0_), channel_id=1, source_target_pairs={{0,96},{16,112},{1,97},{17,113},{2,98},{18,114},{3,99},{19,115},{4... | collective-permute-start | bytes 786440 | tf_op jit(solution)/shard_map/ppermute | solution.py:34
  90.4 2.7 %collective-permute-start.18 = (bf16[256,512]{1,0:T(8,128)(2,1)S(1)}, bf16[256,512]{1,0:T(8,128)(2,1)}, u32[]{:S(2)}, u32[]{:S(2)}) collective-permute-start(bf16[256,512]{1,0:T(8,128)(2,1)S(1)} %collective-permute-done.15.refs_3_), channel_id=1, source_target_pairs={{0,96},{16,112},{1,97},{17,113},{2,98},{18,114},{3,99},{19,115},{4... | collective-permute-start | bytes 786440 | tf_op jit(solution)/shard_map/ppermute | solution.py:34
  93.1 1.5 %collective-permute-done.16.refs_4_ = bf16[256,512]{1,0:T(8,128)(2,1)S(1)} collective-permute-done((bf16[256,512]{1,0:T(8,128)(2,1)S(1)}, bf16[256,512]{1,0:T(8,128)(2,1)S(1)}, u32[]{:S(2)}, u32[]{:S(2)}) %collective-permute-start.16) | collective-permute-done | bytes 262176 | tf_op jit(solution)/shard_map/ppermute | solution.py:34
  94.6 1.1 collective-permute-start.19
  95.7 4.4 %collective-permute-done.13.refs_1_ = bf16[256,512]{1,0:T(8,128)(2,1)S(1)} collective-permute-done((bf16[256,512]{1,0:T(8,128)(2,1)S(1)}, bf16[256,512]{1,0:T(8,128)(2,1)S(1)}, u32[]{:S(2)}, u32[]{:S(2)}) %collective-permute-start.13) | collective-permute-done | bytes 262176 | tf_op jit(solution)/shard_map/ppermute | solution.py:34
  100.1 5.7 %collective-permute-done.17.refs_5_ = bf16[256,512]{1,0:T(8,128)(2,1)} collective-permute-done((bf16[256,512]{1,0:T(8,128)(2,1)S(1)}, bf16[256,512]{1,0:T(8,128)(2,1)}, u32[]{:S(2)}, u32[]{:S(2)}) %collective-permute-start.17) | collective-permute-done | bytes 262176 | tf_op jit(solution)/shard_map/ppermute | solution.py:34
  105.9 1.6 %copy-done.1 = bf16[16,256,256]{2,1,0:T(8,128)(2,1)S(1)} copy-done((bf16[16,256,256]{2,1,0:T(8,128)(2,1)S(1)}, bf16[16,256,256]{2,1,0:T(8,128)(2,1)}, u32[]{:S(2)}) %copy-start.1) | copy-done | bytes 2097176
  107.5 4.4 %shard_map.51 = (f32[256,512]{1,0:T(8,128)S(1)}, f32[256,512]{1,0:T(8,128)S(1)}) custom-call(s32[18]{0:T(128)S(1)} %stack.81.where_ref, bf16[8,2,256,256]{3,2,1,0:T(8,128)(2,1)S(1)} %bitcast.22, bf16[256,512]{1,0:T(8,128)(2,1)S(1)} %add_convert_fusion.refs_0_, bf16[256,512]{1,0:T(8,128)(2,1)S(1)} %collective-permute-done.13.refs_1_, ...), custom_call_target="tpu_custom_call" | custom-call | flops 1073741824 | bytes 3145728 | tf_op jit(solution)/shard_map/pallas_call | solution.py:219
  112.4 1.5 %collective-permute-done.20 = f32[256,512]{1,0:T(8,128)S(1)} collective-permute-done((f32[256,512]{1,0:T(8,128)S(1)}, f32[256,512]{1,0:T(8,128)S(1)}, u32[]{:S(2)}, u32[]{:S(2)}) %collective-permute-start.20) | collective-permute-done | bytes 524320 | tf_op jit(solution)/shard_map/ppermute | solution.py:34
  114.0 0.9 add_multiply_fusion
  (37 shorter events, 5.0 us)
Async XLA Ops:
  6.5 1.6 %copy-start = (bf16[4096,256]{1,0:T(8,128)(2,1)S(1)}, bf16[4096,256]{1,0:T(8,128)(2,1)}, u32[]{:S(2)}) copy-start(bf16[4096,256]{1,0:T(8,128)(2,1)} %param.7) | copy-start | bytes 6291460
  6.5 99.3 %all-gather.3.cloned.1.call-start = ((), (), s32[]{:S(2)}) async-start(), calls=%async_computation | async-start | bytes 2359296 | tf_op jit(solution)/shard_map/all_gather | solution.py:277
  10.5 18.7 %collective-permute-start = (bf16[256,256]{1,0:T(8,128)(2,1)S(1)}, bf16[256,256]{1,0:T(8,128)(2,1)S(1)}, u32[]{:S(2)}, u32[]{:S(2)}) collective-permute-start(bf16[256,256]{1,0:T(8,128)(2,1)S(1)} %convolution_convert_fusion), channel_id=1, source_target_pairs={{0,0},{1,1},{2,32},{3,33},{4,64},{5,65},{6,96},{7,97},{8,128},{9,1... | collective-permute-start | bytes 393224 | tf_op jit(solution)/shard_map/ppermute | solution.py:247
  11.2 22.1 %collective-permute-start.3 = (bf16[896,512]{1,0:T(8,128)(2,1)}, bf16[896,512]{1,0:T(8,128)(2,1)}, u32[]{:S(2)}, u32[]{:S(2)}) collective-permute-start(bf16[896,512]{1,0:T(8,128)(2,1)} %refs_3_.1), channel_id=1, source_target_pairs={{0,32},{16,112},{1,33},{17,113},{2,34},{18,114},{3,35},{19,115},{4... | collective-permute-start | bytes 2752520 | tf_op jit(solution)/shard_map/ppermute | solution.py:46
  29.2 14.6 %collective-permute-start.9 = (bf16[2,256,896]{2,1,0:T(8,128)(2,1)}, bf16[2,256,896]{2,1,0:T(8,128)(2,1)}, u32[]{:S(2)}, u32[]{:S(2)}) collective-permute-start(bf16[2,256,896]{2,1,0:T(8,128)(2,1)} %shard_map.46), channel_id=1, source_target_pairs={{0,128},{16,152},{1,129},{17,153},{2,130},{18,154},{3,131},{19,155... | collective-permute-start | bytes 2752520 | tf_op jit(solution)/shard_map/ppermute | solution.py:46
  31.8 15.4 %collective-permute-start.1 = (bf16[256,256]{1,0:T(8,128)(2,1)S(1)}, bf16[256,256]{1,0:T(8,128)(2,1)S(1)}, u32[]{:S(2)}, u32[]{:S(2)}) collective-permute-start(bf16[256,256]{1,0:T(8,128)(2,1)S(1)} %collective-permute-done), channel_id=1, source_target_pairs={{0,8},{16,24},{1,9},{17,25},{2,10},{18,26},{3,11},{19,27},{4,12},{... | collective-permute-start | bytes 393224 | tf_op jit(solution)/shard_map/ppermute | solution.py:34
  33.2 14.8 %collective-permute-start.2 = (bf16[896,512]{1,0:T(8,128)(2,1)}, bf16[896,512]{1,0:T(8,128)(2,1)}, u32[]{:S(2)}, u32[]{:S(2)}) collective-permute-start(bf16[896,512]{1,0:T(8,128)(2,1)} %refs_3_.1), channel_id=1, source_target_pairs={{0,16},{16,0},{1,17},{17,1},{2,18},{18,2},{3,19},{19,3},{4,20},{20... | collective-permute-start | bytes 2752520 | tf_op jit(solution)/shard_map/ppermute | solution.py:34
  33.2 22.2 %collective-permute-start.7 = (bf16[896,512]{1,0:T(8,128)(2,1)}, bf16[896,512]{1,0:T(8,128)(2,1)S(1)}, u32[]{:S(2)}, u32[]{:S(2)}) collective-permute-start(bf16[896,512]{1,0:T(8,128)(2,1)} %collective-permute-done.3.refs_4_.refs_5_), channel_id=1, source_target_pairs={{0,32},{16,112},{1,33},{17,113},{2,34},{18,114},{3,35},{19,115},{4... | collective-permute-start | bytes 2752520 | tf_op jit(solution)/shard_map/ppermute | solution.py:46
  36.5 22.5 %collective-permute-start.5 = (bf16[896,512]{1,0:T(8,128)(2,1)}, bf16[896,512]{1,0:T(8,128)(2,1)}, u32[]{:S(2)}, u32[]{:S(2)}) collective-permute-start(bf16[896,512]{1,0:T(8,128)(2,1)} %refs_3_.1), channel_id=1, source_target_pairs={{0,96},{16,48},{1,97},{17,49},{2,98},{18,50},{3,99},{19,51},{4,100... | collective-permute-start | bytes 2752520 | tf_op jit(solution)/shard_map/ppermute | solution.py:46
  43.9 23.8 %collective-permute-start.10 = (bf16[4,256,896]{2,1,0:T(8,128)(2,1)}, bf16[4,256,896]{2,1,0:T(8,128)(2,1)}, u32[]{:S(2)}, u32[]{:S(2)}) collective-permute-start(bf16[4,256,896]{2,1,0:T(8,128)(2,1)} %shard_map.47), channel_id=1, source_target_pairs={{0,128},{16,152},{1,129},{17,153},{2,130},{18,154},{3,131},{19,155... | collective-permute-start | bytes 5505032 | tf_op jit(solution)/shard_map/ppermute | solution.py:46
  47.9 11.1 %collective-permute-start.4 = (bf16[896,512]{1,0:T(8,128)(2,1)}, bf16[896,512]{1,0:T(8,128)(2,1)}, u32[]{:S(2)}, u32[]{:S(2)}) collective-permute-start(bf16[896,512]{1,0:T(8,128)(2,1)} %collective-permute-done.3.refs_4_.refs_5_), channel_id=1, source_target_pairs={{0,16},{16,0},{1,17},{17,1},{2,18},{18,2},{3,19},{19,3},{4,20},{20... | collective-permute-start | bytes 2752520 | tf_op jit(solution)/shard_map/ppermute | solution.py:34
  48.0 15.4 %collective-permute-start.11 = (bf16[2,256,896]{2,1,0:T(8,128)(2,1)}, bf16[2,256,896]{2,1,0:T(8,128)(2,1)}, u32[]{:S(2)}, u32[]{:S(2)}) collective-permute-start(bf16[2,256,896]{2,1,0:T(8,128)(2,1)} %collective-permute-done.9.refs_1_), channel_id=1, source_target_pairs={{0,1},{16,23},{1,2},{17,16},{2,3},{18,17},{3,4},{19,18},{4,5},{20,... | collective-permute-start | bytes 2752520 | tf_op jit(solution)/shard_map/ppermute | solution.py:46
  55.4 12.2 %copy-start.2 = (bf16[896,512]{1,0:T(8,128)(2,1)}, bf16[896,512]{1,0:T(8,128)(2,1)S(1)}, u32[]{:S(2)}) copy-start(bf16[896,512]{1,0:T(8,128)(2,1)S(1)} %collective-permute-done.7.refs_8_.refs_4_) | copy-start | bytes 2752516
  55.4 12.0 %collective-permute-start.8 = (bf16[896,512]{1,0:T(8,128)(2,1)S(1)}, bf16[896,512]{1,0:T(8,128)(2,1)}, u32[]{:S(2)}, u32[]{:S(2)}) collective-permute-start(bf16[896,512]{1,0:T(8,128)(2,1)S(1)} %collective-permute-done.7.refs_8_.refs_4_), channel_id=1, source_target_pairs={{0,16},{16,0},{1,17},{17,1},{2,18},{18,2},{3,19},{19,3},{4,20},{20... | collective-permute-start | bytes 2752520 | tf_op jit(solution)/shard_map/ppermute | solution.py:34
  59.0 8.4 %collective-permute-start.6 = (bf16[896,512]{1,0:T(8,128)(2,1)}, bf16[896,512]{1,0:T(8,128)(2,1)}, u32[]{:S(2)}, u32[]{:S(2)}) collective-permute-start(bf16[896,512]{1,0:T(8,128)(2,1)} %collective-permute-done.5.refs_6_.refs_2_), channel_id=1, source_target_pairs={{0,16},{16,0},{1,17},{17,1},{2,18},{18,2},{3,19},{19,3},{4,20},{20... | collective-permute-start | bytes 2752520 | tf_op jit(solution)/shard_map/ppermute | solution.py:34
  67.6 1.0 copy-start.3
  72.0 7.3 %collective-permute-start.12 = (f16[256,512]{1,0:T(8,128)(2,1)S(1)}, f16[256,512]{1,0:T(8,128)(2,1)S(1)}, u32[]{:S(2)}, u32[]{:S(2)}) collective-permute-start(f16[256,512]{1,0:T(8,128)(2,1)S(1)} %multiply_convert_fusion), channel_id=1, source_target_pairs={{0,128},{16,144},{1,129},{17,145},{2,130},{18,146},{3,131},{19,147... | collective-permute-start | bytes 786440 | tf_op jit(solution)/shard_map/ppermute | solution.py:57
  80.4 10.0 %collective-permute-start.15 = (bf16[256,512]{1,0:T(8,128)(2,1)S(1)}, bf16[256,512]{1,0:T(8,128)(2,1)S(1)}, u32[]{:S(2)}, u32[]{:S(2)}) collective-permute-start(bf16[256,512]{1,0:T(8,128)(2,1)S(1)} %add_convert_fusion.refs_0_), channel_id=1, source_target_pairs={{0,128},{16,144},{1,129},{17,145},{2,130},{18,146},{3,131},{19,147... | collective-permute-start | bytes 786440 | tf_op jit(solution)/shard_map/ppermute | solution.py:57
  81.6 13.0 %collective-permute-start.16 = (bf16[256,512]{1,0:T(8,128)(2,1)S(1)}, bf16[256,512]{1,0:T(8,128)(2,1)S(1)}, u32[]{:S(2)}, u32[]{:S(2)}) collective-permute-start(bf16[256,512]{1,0:T(8,128)(2,1)S(1)} %add_convert_fusion.refs_0_), channel_id=1, source_target_pairs={{0,64},{16,80},{1,65},{17,81},{2,66},{18,82},{3,67},{19,83},{4,68}... | collective-permute-start | bytes 786440 | tf_op jit(solution)/shard_map/ppermute | solution.py:34
  87.7 12.4 %collective-permute-start.13 = (bf16[256,512]{1,0:T(8,128)(2,1)S(1)}, bf16[256,512]{1,0:T(8,128)(2,1)S(1)}, u32[]{:S(2)}, u32[]{:S(2)}) collective-permute-start(bf16[256,512]{1,0:T(8,128)(2,1)S(1)} %add_convert_fusion.refs_0_), channel_id=1, source_target_pairs={{0,32},{16,48},{1,33},{17,49},{2,34},{18,50},{3,35},{19,51},{4,36}... | collective-permute-start | bytes 786440 | tf_op jit(solution)/shard_map/ppermute | solution.py:34
  87.7 12.4 %collective-permute-start.14 = (bf16[256,512]{1,0:T(8,128)(2,1)S(1)}, bf16[256,512]{1,0:T(8,128)(2,1)S(1)}, u32[]{:S(2)}, u32[]{:S(2)}) collective-permute-start(bf16[256,512]{1,0:T(8,128)(2,1)S(1)} %add_convert_fusion.refs_0_), channel_id=1, source_target_pairs={{0,96},{16,112},{1,97},{17,113},{2,98},{18,114},{3,99},{19,115},{4... | collective-permute-start | bytes 786440 | tf_op jit(solution)/shard_map/ppermute | solution.py:34
  90.4 15.4 %collective-permute-start.17 = (bf16[256,512]{1,0:T(8,128)(2,1)S(1)}, bf16[256,512]{1,0:T(8,128)(2,1)}, u32[]{:S(2)}, u32[]{:S(2)}) collective-permute-start(bf16[256,512]{1,0:T(8,128)(2,1)S(1)} %collective-permute-done.15.refs_3_), channel_id=1, source_target_pairs={{0,32},{16,48},{1,33},{17,49},{2,34},{18,50},{3,35},{19,51},{4,36}... | collective-permute-start | bytes 786440 | tf_op jit(solution)/shard_map/ppermute | solution.py:34
  90.4 15.4 %collective-permute-start.18 = (bf16[256,512]{1,0:T(8,128)(2,1)S(1)}, bf16[256,512]{1,0:T(8,128)(2,1)}, u32[]{:S(2)}, u32[]{:S(2)}) collective-permute-start(bf16[256,512]{1,0:T(8,128)(2,1)S(1)} %collective-permute-done.15.refs_3_), channel_id=1, source_target_pairs={{0,96},{16,112},{1,97},{17,113},{2,98},{18,114},{3,99},{19,115},{4... | collective-permute-start | bytes 786440 | tf_op jit(solution)/shard_map/ppermute | solution.py:34
  94.6 11.3 %collective-permute-start.19 = (bf16[256,512]{1,0:T(8,128)(2,1)S(1)}, bf16[256,512]{1,0:T(8,128)(2,1)}, u32[]{:S(2)}, u32[]{:S(2)}) collective-permute-start(bf16[256,512]{1,0:T(8,128)(2,1)S(1)} %collective-permute-done.16.refs_4_), channel_id=1, source_target_pairs={{0,128},{16,144},{1,129},{17,145},{2,130},{18,146},{3,131},{19,147... | collective-permute-start | bytes 786440 | tf_op jit(solution)/shard_map/ppermute | solution.py:57
  105.9 1.6 %copy-start.1 = (bf16[16,256,256]{2,1,0:T(8,128)(2,1)S(1)}, bf16[16,256,256]{2,1,0:T(8,128)(2,1)}, u32[]{:S(2)}) copy-start(bf16[16,256,256]{2,1,0:T(8,128)(2,1)} %all-gather.3.cloned.1.call-done) | copy-start | bytes 6291460
  111.9 2.1 %collective-permute-start.20 = (f32[256,512]{1,0:T(8,128)S(1)}, f32[256,512]{1,0:T(8,128)S(1)}, u32[]{:S(2)}, u32[]{:S(2)}) collective-permute-start(f32[256,512]{1,0:T(8,128)S(1)} %get-tuple-element.22), channel_id=1, source_target_pairs={{0,16},{16,0},{1,17},{17,1},{2,18},{18,2},{3,19},{19,3},{4,20},{20... | collective-permute-start | bytes 1572872 | tf_op jit(solution)/shard_map/ppermute | solution.py:34
Sparse Core Ops, SparseCore 0:
  48.0 39.0 all-gather.2

commit v10 on v9

--- a/solution.py
+++ b/solution.py
@@ -14,6 +14,7 @@
 VMEM = 60 * 1024 * 1024
 FOLLOWED = 6 * 10**9
 TAIL_VMEM = 16 * 1024 * 1024
+OWN_VMEM = 48 * 1024 * 1024
 BLOCKS = ((0, 0), (0, 1), (3, 0), (1, 1), (1, 0), (3, 1), (2, 0), (2, 1))
 ORDER = ((0, 0), (0, 3), (0, 1), (1, 0), (0, 2), (1, 3), (1, 1), (1, 2))
 
@@ -119,6 +120,9 @@
             filled += part.shape[0]
         at += count
         for_panels.append(copies)
+    if before:
+        carry = pltpu.make_async_copy(before[0], out, semaphore.at[len(pairs) + len(parts)])
+        carry.start()
     for copy in for_rows + sum(for_panels, []):
         copy.start()
     for copy in for_rows:
@@ -127,10 +131,12 @@
         for copy in copies:
             copy.wait()
         term = dot(rows[k], panels[k])
-        if k:
+        if before and not k:
+            carry.wait()
+        if k or before:
             out[...] += term
         else:
-            out[...] = before[0][...] + term if before else term
+            out[...] = term
 
 
 def product(moves, count, table, sources, panels, before=None, followed_by=0, grant=VMEM):
@@ -145,13 +151,12 @@
         lambda *refs: product_kernel(moves, layout, *refs),
         out_shape=jax.ShapeDtypeStruct((tokens, width), jnp.float32),
         in_specs=[space(pltpu.SMEM)]
-        + [space(pl.ANY)] * (len(sources) + len(parts))
-        + [space(pltpu.VMEM)] * len(extra),
+        + [space(pl.ANY)] * (len(sources) + len(parts) + len(extra)),
         out_specs=space(pltpu.VMEM),
         scratch_shapes=[
             pltpu.VMEM((blocks, tokens, depth), jnp.bfloat16),
             pltpu.VMEM((blocks, depth, width), jnp.bfloat16),
-            pltpu.SemaphoreType.DMA((count + len(parts),)),
+            pltpu.SemaphoreType.DMA((count + len(parts) + len(extra),)),
         ],
         compiler_params=pltpu.CompilerParams(vmem_limit_bytes=grant),
         cost_estimate=pl.CostEstimate(
@@ -184,12 +189,10 @@
 def squares_kernel(where_ref, out_rows, *refs):
     blocks = out_rows.shape[0]
     in_rows, refs = refs[:blocks], refs[blocks:]
-    totals, (outer, inner, semaphore) = refs[:2], refs[2:]
-    copies = [pltpu.make_async_copy(out_rows, outer, semaphore.at[blocks])]
-    for k in range(blocks):
-        copies.append(
-            pltpu.make_async_copy(in_rows[k], inner.at[k], semaphore.at[k])
-        )
+    totals, (inner, semaphore) = refs[:2], refs[2:]
+    copies = [
+        pltpu.make_async_copy(in_rows[k], inner.at[k], semaphore.at[k]) for k in range(blocks)
+    ]
     for copy in copies:
         copy.start()
     for copy in copies:
@@ -204,7 +207,7 @@
                 at, half = where_ref[k] + where_ref[2 * blocks + part], where_ref[blocks + k]
                 for example in range(EXAMPLES):
                     tokens = pl.ds(example * TOK, TOK)
-                    rotated = dot(outer[at, half, :, tokens], inner[k, tokens, columns])
+                    rotated = dot(out_rows[at, half, :, tokens], inner[k, tokens, columns])
                     squared = rotated * rotated
                     total = squared if total is None else total + squared
             total_ref[:, columns] = total
@@ -219,12 +222,11 @@
     return pl.pallas_call(
         squares_kernel,
         out_shape=[jax.ShapeDtypeStruct((rows, width), jnp.float32)] * 2,
-        in_specs=[space(pltpu.SMEM)] + [space(pl.ANY)] * (1 + blocks),
+        in_specs=[space(pltpu.SMEM), space(pltpu.VMEM)] + [space(pl.ANY)] * blocks,
         out_specs=[space(pltpu.VMEM)] * 2,
         scratch_shapes=[
-            pltpu.VMEM(out_rows.shape, jnp.bfloat16),
             pltpu.VMEM((blocks, tokens, width), jnp.bfloat16),
-            pltpu.SemaphoreType.DMA((blocks + 1,)),
+            pltpu.SemaphoreType.DMA((blocks,)),
         ],
         compiler_params=pltpu.CompilerParams(vmem_limit_bytes=TAIL_VMEM),
         cost_estimate=pl.CostEstimate(
@@ -265,7 +267,7 @@
     near = pieces(near.astype(jnp.int32), activations, depth)
     rest = pieces(give[2 * SPLIT :].astype(jnp.int32), activations, depth)
     block = transposed(dot(out_grads, basis_out).astype(jnp.bfloat16).T)
-    near, rest, block = lax.optimization_barrier((near, rest, block))
+    near, block = lax.optimization_barrier((near, block))
     near = by_core(near, dx=1)
     first, again = lax.optimization_barrier((first, basis_in))
     second, far = by_core(again, dy=NY - 1), by_core(first, dy=1)
@@ -291,12 +293,18 @@
         panels += [panel, shift(panel, dc=1)]
     panels = [[panel] for panel in panels]
     parity = parity.reshape(1).astype(jnp.int32)
-    partial = product(near_moves, 2, parity, (near, away), panels[: 2 * SPLIT])
+    mine = product(own_moves, 2 * SPLIT, keep[: 2 * SPLIT], (activations,), panels[: 2 * SPLIT])
+    mine, away = lax.optimization_barrier((mine, away))
+    partial = product(
+        near_moves, 2, parity, (near, away), panels[: 2 * SPLIT], None, 0, OWN_VMEM
+    )
     partial = product(
         rest_moves, 1, parity, (rest,), panels[2 * SPLIT :], partial, FOLLOWED, TAIL_VMEM
     )
     arrived = swap((partial * FACTOR).astype(jnp.float16))
-    total = product(own_moves, len(BLOCKS), keep, (activations,), panels)
+    total = product(
+        own_moves, 2 * SPLIT, keep[2 * SPLIT :], (activations,), panels[2 * SPLIT :], mine, 0, OWN_VMEM
+    )
     proj_in = (total + arrived.astype(jnp.float32) * (1.0 / FACTOR)).astype(jnp.bfloat16)
 
     p_left, p_right, p_far = shift(proj_in, dy=1), shift(proj_in, dy=3), shift(proj_in, dy=2)

time: 123 us -> 123 us (level)
  waiting for transfers between devices: 32.4 us -> 30.1 us
  starting transfers between devices: 40.6 us -> 42.3 us
  local copies, waits for them, and re-layouts: 5.57 us -> 7.22 us
  other arithmetic: 3.38 us -> 1.76 us
  Pallas kernels: 23.9 us -> 25.4 us
    ppermute x6, waiting for transfers between devices: 18.6 us -> 12.6 us  [by_core(): return lax.ppermute(value, ('dp', 'blk'), pairs)]
    ppermute x6, starting transfers between devices: 21.6 us -> 27.2 us  [by_core(): return lax.ppermute(value, ('dp', 'blk'), pairs)]
    ppermute x11, starting transfers between devices: 16 us -> 13.2 us  [shift(): return lax.ppermute(value, ('dp', 'blk'), pairs)]
    ppermute x3, waiting for transfers between devices: 0.58 us -> 3.27 us  [swap(): return lax.ppermute(value, ('dp', 'blk'), pairs)]
    pallas_call x3 -> x4, Pallas kernels: 13.9 us -> 15.4 us  [product(): pl.pallas_call(lambda *refs: product_kernel(moves, layout, *refs), out_sh...]
    unnamed x8 -> x14, local copies, waits for them, and re-layouts: 4.22 us -> 5.29 us
  transfers between devices with their start and end apart: 22 -> 22, of which waited for: 10 -> 9; matrix products, arithmetic and copies ran while one was open for 3% -> 2% of each run, Pallas kernels for 16% -> 17%
where the time goes in v10:
time: 123 us
  starting transfers between devices  42.3 us (34%)
  waiting for transfers between devices  30.1 us (24%)
  Pallas kernels  25.4 us (21%)
  between operations  13.6 us (11%)
  local copies, waits for them, and re-layouts  7.22 us (6%)
  matrix products  2.34 us (2%)
  other arithmetic  1.76 us (1%)
    ppermute x6, starting transfers between devices, by_core(): return lax.ppermute(value, ('dp', 'blk'), pairs)  27.2 us
    pallas_call x4, Pallas kernels, product(): pl.pallas_call(lambda *refs: product_kernel(moves, layout, *refs), out_sh...  15.4 us
    ppermute x11, waiting for transfers between devices, shift(): return lax.ppermute(value, ('dp', 'blk'), pairs)  14.2 us
    ppermute x11, starting transfers between devices, shift(): return lax.ppermute(value, ('dp', 'blk'), pairs)  13.2 us
    ppermute x6, waiting for transfers between devices, by_core(): return lax.ppermute(value, ('dp', 'blk'), pairs)  12.6 us
    pallas_call x2, Pallas kernels, pieces(): pl.pallas_call(pieces_kernel, out_shape=jax.ShapeDtypeStruct(shape, activ...  5.64 us
    unnamed x14, local copies, waits for them, and re-layouts  5.29 us
    pallas_call x1, Pallas kernels, sums_of_squares(): pl.pallas_call(squares_kernel, out_shape=[jax.ShapeDtypeStruct((rows, wid...  4.3 us
  transfers between devices with their start and end apart: 22, of which 9 were waited for; matrix products, arithmetic and copies ran while one was open for 2% of the time, Pallas kernels for 17%

profile of v10, /device:TPU:1, one launch (start us, length us, event | category | flops | bytes accessed | tf_op | source)
XLA Modules:
  0.0 122.7 jit_solution(10236566875788674854)
XLA Ops:
  6.5 1.6 %copy-done = bf16[4096,256]{1,0:T(8,128)(2,1)S(1)} copy-done((bf16[4096,256]{1,0:T(8,128)(2,1)S(1)}, bf16[4096,256]{1,0:T(8,128)(2,1)}, u32[]{:S(2)}) %copy-start) | copy-done | bytes 2097176
  8.1 2.3 %convolution_convert_fusion = bf16[256,256]{1,0:T(8,128)(2,1)S(1)} fusion(bf16[4096,256]{1,0:T(8,128)(2,1)S(1)} %copy-done, bf16[256,4096]{1,0:T(8,128)(2,1)} %param.5), kind=kOutput, calls=%fused_computation | convolution fusion | flops 536936448 | bytes 4325376 | tf_op jit(solution)/shard_map/dot_general | solution.py:62
  10.5 0.7 collective-permute-start
  11.2 10.6 %collective-permute-start.2 = (bf16[896,512]{1,0:T(8,128)(2,1)S(1)}, bf16[896,512]{1,0:T(8,128)(2,1)}, u32[]{:S(2)}, u32[]{:S(2)}) collective-permute-start(bf16[896,512]{1,0:T(8,128)(2,1)S(1)} %copy-done.1), channel_id=1, source_target_pairs={{0,32},{16,112},{1,33},{17,113},{2,34},{18,114},{3,35},{19,115},{4... | collective-permute-start | bytes 2752520 | tf_op jit(solution)/shard_map/ppermute | solution.py:47
  22.4 2.6 %shard_map.46 = bf16[2,256,896]{2,1,0:T(8,128)(2,1)} custom-call(s32[2]{0:T(128)} %dynamic_slice.3.columns_ref, bf16[256,14336]{1,0:T(8,128)(2,1)} %refs_1_.3), custom_call_target="tpu_custom_call" | custom-call | bytes 4194304 | tf_op jit(solution)/shard_map/pallas_call | solution.py:92
  25.1 2.6 %collective-permute-start.9 = (bf16[2,256,896]{2,1,0:T(8,128)(2,1)}, bf16[2,256,896]{2,1,0:T(8,128)(2,1)}, u32[]{:S(2)}, u32[]{:S(2)}) collective-permute-start(bf16[2,256,896]{2,1,0:T(8,128)(2,1)} %shard_map.46), channel_id=1, source_target_pairs={{0,128},{16,152},{1,129},{17,153},{2,130},{18,154},{3,131},{19,155... | collective-permute-start | bytes 2752520 | tf_op jit(solution)/shard_map/ppermute | solution.py:47
  27.6 1.4 %collective-permute-start.1 = (bf16[256,256]{1,0:T(8,128)(2,1)S(1)}, bf16[256,256]{1,0:T(8,128)(2,1)S(1)}, u32[]{:S(2)}, u32[]{:S(2)}) collective-permute-start(bf16[256,256]{1,0:T(8,128)(2,1)S(1)} %collective-permute-done), channel_id=1, source_target_pairs={{0,8},{16,24},{1,9},{17,25},{2,10},{18,26},{3,11},{19,27},{4,12},{... | collective-permute-start | bytes 393224 | tf_op jit(solution)/shard_map/ppermute | solution.py:35
  29.7 3.0 %shard_map.48 = bf16[4,256,896]{2,1,0:T(8,128)(2,1)} custom-call(s32[4]{0:T(128)} %slice.11.columns_ref, bf16[256,14336]{1,0:T(8,128)(2,1)} %refs_1_.3), custom_call_target="tpu_custom_call" | custom-call | bytes 4194304 | tf_op jit(solution)/shard_map/pallas_call | solution.py:92
  32.8 6.1 %collective-permute-start.5 = (bf16[896,512]{1,0:T(8,128)(2,1)}, bf16[896,512]{1,0:T(8,128)(2,1)}, u32[]{:S(2)}, u32[]{:S(2)}) collective-permute-start(bf16[896,512]{1,0:T(8,128)(2,1)} %collective-permute-done.2.refs_4_.refs_5_), channel_id=1, source_target_pairs={{0,32},{16,112},{1,33},{17,113},{2,34},{18,114},{3,35},{19,115},{4... | collective-permute-start | bytes 2752520 | tf_op jit(solution)/shard_map/ppermute | solution.py:47
  38.9 0.9 collective-permute-done.9.refs_1_
  39.7 3.4 %collective-permute-start.11 = (bf16[4,256,896]{2,1,0:T(8,128)(2,1)}, bf16[4,256,896]{2,1,0:T(8,128)(2,1)}, u32[]{:S(2)}, u32[]{:S(2)}) collective-permute-start(bf16[4,256,896]{2,1,0:T(8,128)(2,1)} %shard_map.48), channel_id=1, source_target_pairs={{0,128},{16,152},{1,129},{17,153},{2,130},{18,154},{3,131},{19,155... | collective-permute-start | bytes 5505032 | tf_op jit(solution)/shard_map/ppermute | solution.py:47
  43.1 0.7 pad_maximum_fusion
  43.9 4.7 %collective-permute-start.10 = (bf16[2,256,896]{2,1,0:T(8,128)(2,1)}, bf16[2,256,896]{2,1,0:T(8,128)(2,1)}, u32[]{:S(2)}, u32[]{:S(2)}) collective-permute-start(bf16[2,256,896]{2,1,0:T(8,128)(2,1)} %collective-permute-done.9.refs_1_), channel_id=1, source_target_pairs={{0,1},{16,23},{1,2},{17,16},{2,3},{18,17},{3,4},{19,18},{4,5},{20,... | collective-permute-start | bytes 2752520 | tf_op jit(solution)/shard_map/ppermute | solution.py:47
  48.6 10.4 %collective-permute-done.5.refs_4_ = bf16[896,512]{1,0:T(8,128)(2,1)} collective-permute-done((bf16[896,512]{1,0:T(8,128)(2,1)}, bf16[896,512]{1,0:T(8,128)(2,1)}, u32[]{:S(2)}, u32[]{:S(2)}) %collective-permute-start.5) | collective-permute-done | bytes 917536 | tf_op jit(solution)/shard_map/ppermute | solution.py:47
  59.0 1.2 %collective-permute-done.3.refs_2_ = bf16[896,512]{1,0:T(8,128)(2,1)} collective-permute-done((bf16[896,512]{1,0:T(8,128)(2,1)S(1)}, bf16[896,512]{1,0:T(8,128)(2,1)}, u32[]{:S(2)}, u32[]{:S(2)}) %collective-permute-start.3) | collective-permute-done | bytes 917536 | tf_op jit(solution)/shard_map/ppermute | solution.py:47
  60.9 0.9 copy-done.3
  61.8 5.4 %shard_map.47.refs_6_ = f32[256,512]{1,0:T(8,128)} custom-call(s32[4]{0:T(128)} %get-tuple-element.25.refs_0_, bf16[256,14336]{1,0:T(8,128)(2,1)} %refs_1_.3, bf16[896,512]{1,0:T(8,128)(2,1)} %refs_3_.1, bf16[896,512]{1,0:T(8,128)(2,1)} %collective-permute-done.7.refs_3_.refs_4_, bf16[896,512]{1,0:T(8,128)(2,1)} %collective-permute-done.2.refs_4_.refs_5_, ...), custom_call_target="tpu_custom_call" | custom-call | flops 939524096 | bytes 4194304 | tf_op jit(solution)/shard_map/pallas_call | solution.py:150
  67.2 1.2 copy-done.4
  68.4 2.9 %shard_map.50.refs_6_ = f32[256,512]{1,0:T(8,128)S(1)} custom-call(s32[1]{0:T(128)} %bitcast.19.refs_0_, bf16[2,256,896]{2,1,0:T(8,128)(2,1)} %collective-permute-done.9.refs_1_, bf16[2,256,896]{2,1,0:T(8,128)(2,1)} %collective-permute-done.10.refs_2_, bf16[896,512]{1,0:T(8,128)(2,1)S(1)} %copy-done.2, ...), custom_call_target="tpu_custom_call" | custom-call | flops 939524096 | bytes 4194304 | tf_op jit(solution)/shard_map/pallas_call | solution.py:150
  71.4 3.3 %shard_map.51 = f32[256,512]{1,0:T(8,128)S(1)} custom-call(s32[1]{0:T(128)} %bitcast.19.refs_0_, bf16[4,256,896]{2,1,0:T(8,128)(2,1)} %collective-permute-done.11.refs_1_, bf16[896,512]{1,0:T(8,128)(2,1)} %collective-permute-done.3.refs_2_, bf16[896,512]{1,0:T(8,128)(2,1)} %collective-permute-done.4.refs_3_, ...), custom_call_target="tpu_custom_call" | custom-call | flops 6939524096 | bytes 4194304 | tf_op jit(solution)/shard_map/pallas_call | solution.py:150
  75.4 3.8 %shard_map.49 = f32[256,512]{1,0:T(8,128)S(1)} custom-call(s32[4]{0:T(128)S(1)} %get-tuple-element.26.refs_0_, bf16[256,14336]{1,0:T(8,128)(2,1)} %refs_1_.3, bf16[896,512]{1,0:T(8,128)(2,1)} %collective-permute-done.3.refs_2_, bf16[896,512]{1,0:T(8,128)(2,1)} %collective-permute-done.4.refs_3_, bf16[896,512]{1,0:T(8,128)(2,1)} %collective-permute-done.5.refs_4_, ...), custom_call_target="tpu_custom_call" | custom-call | flops 939524096 | bytes 4194304 | tf_op jit(solution)/shard_map/pallas_call | solution.py:150
  79.2 3.3 %collective-permute-done.12 = f16[256,512]{1,0:T(8,128)(2,1)S(1)} collective-permute-done((f16[256,512]{1,0:T(8,128)(2,1)S(1)}, f16[256,512]{1,0:T(8,128)(2,1)S(1)}, u32[]{:S(2)}, u32[]{:S(2)}) %collective-permute-start.12) | collective-permute-done | bytes 262176 | tf_op jit(solution)/shard_map/ppermute | solution.py:58
  83.1 5.7 %collective-permute-start.16 = (bf16[256,512]{1,0:T(8,128)(2,1)S(1)}, bf16[256,512]{1,0:T(8,128)(2,1)S(1)}, u32[]{:S(2)}, u32[]{:S(2)}) collective-permute-start(bf16[256,512]{1,0:T(8,128)(2,1)S(1)} %add_convert_fusion.refs_0_), channel_id=1, source_target_pairs={{0,64},{16,80},{1,65},{17,81},{2,66},{18,82},{3,67},{19,83},{4,68}... | collective-permute-start | bytes 786440 | tf_op jit(solution)/shard_map/ppermute | solution.py:35
  88.8 2.7 %collective-permute-start.14 = (bf16[256,512]{1,0:T(8,128)(2,1)S(1)}, bf16[256,512]{1,0:T(8,128)(2,1)S(1)}, u32[]{:S(2)}, u32[]{:S(2)}) collective-permute-start(bf16[256,512]{1,0:T(8,128)(2,1)S(1)} %add_convert_fusion.refs_0_), channel_id=1, source_target_pairs={{0,96},{16,112},{1,97},{17,113},{2,98},{18,114},{3,99},{19,115},{4... | collective-permute-start | bytes 786440 | tf_op jit(solution)/shard_map/ppermute | solution.py:35
  91.5 2.7 %collective-permute-start.18 = (bf16[256,512]{1,0:T(8,128)(2,1)S(1)}, bf16[256,512]{1,0:T(8,128)(2,1)}, u32[]{:S(2)}, u32[]{:S(2)}) collective-permute-start(bf16[256,512]{1,0:T(8,128)(2,1)S(1)} %collective-permute-done.15.refs_3_), channel_id=1, source_target_pairs={{0,96},{16,112},{1,97},{17,113},{2,98},{18,114},{3,99},{19,115},{4... | collective-permute-start | bytes 786440 | tf_op jit(solution)/shard_map/ppermute | solution.py:35
  94.2 1.5 %collective-permute-done.16.refs_4_ = bf16[256,512]{1,0:T(8,128)(2,1)S(1)} collective-permute-done((bf16[256,512]{1,0:T(8,128)(2,1)S(1)}, bf16[256,512]{1,0:T(8,128)(2,1)S(1)}, u32[]{:S(2)}, u32[]{:S(2)}) %collective-permute-start.16) | collective-permute-done | bytes 262176 | tf_op jit(solution)/shard_map/ppermute | solution.py:35
  95.7 5.5 %collective-permute-done.13.refs_1_ = bf16[256,512]{1,0:T(8,128)(2,1)S(1)} collective-permute-done((bf16[256,512]{1,0:T(8,128)(2,1)S(1)}, bf16[256,512]{1,0:T(8,128)(2,1)S(1)}, u32[]{:S(2)}, u32[]{:S(2)}) %collective-permute-start.13) | collective-permute-done | bytes 262176 | tf_op jit(solution)/shard_map/ppermute | solution.py:35
  101.2 5.7 %collective-permute-done.17.refs_5_ = bf16[256,512]{1,0:T(8,128)(2,1)} collective-permute-done((bf16[256,512]{1,0:T(8,128)(2,1)S(1)}, bf16[256,512]{1,0:T(8,128)(2,1)}, u32[]{:S(2)}, u32[]{:S(2)}) %collective-permute-start.17) | collective-permute-done | bytes 262176 | tf_op jit(solution)/shard_map/ppermute | solution.py:35
  107.0 1.6 %copy-done.6 = bf16[16,256,256]{2,1,0:T(8,128)(2,1)S(1)} copy-done((bf16[16,256,256]{2,1,0:T(8,128)(2,1)S(1)}, bf16[16,256,256]{2,1,0:T(8,128)(2,1)}, u32[]{:S(2)}) %copy-start.6) | copy-done | bytes 2097176
  108.6 4.3 %shard_map.52 = (f32[256,512]{1,0:T(8,128)S(1)}, f32[256,512]{1,0:T(8,128)S(1)}) custom-call(s32[18]{0:T(128)S(1)} %stack.81.where_ref, bf16[8,2,256,256]{3,2,1,0:T(8,128)(2,1)S(1)} %bitcast.22, bf16[256,512]{1,0:T(8,128)(2,1)S(1)} %add_convert_fusion.refs_0_, bf16[256,512]{1,0:T(8,128)(2,1)S(1)} %collective-permute-done.13.refs_1_, ...), custom_call_target="tpu_custom_call" | custom-call | flops 1073741824 | bytes 3145728 | tf_op jit(solution)/shard_map/pallas_call | solution.py:222
  113.4 1.5 %collective-permute-done.20 = f32[256,512]{1,0:T(8,128)S(1)} collective-permute-done((f32[256,512]{1,0:T(8,128)S(1)}, f32[256,512]{1,0:T(8,128)S(1)}, u32[]{:S(2)}, u32[]{:S(2)}) %collective-permute-start.20) | collective-permute-done | bytes 524320 | tf_op jit(solution)/shard_map/ppermute | solution.py:35
  115.0 0.9 add_multiply_fusion
  (45 shorter events, 4.1 us)
Async XLA Ops:
  6.5 1.6 %copy-start = (bf16[4096,256]{1,0:T(8,128)(2,1)S(1)}, bf16[4096,256]{1,0:T(8,128)(2,1)}, u32[]{:S(2)}) copy-start(bf16[4096,256]{1,0:T(8,128)(2,1)} %param.7) | copy-start | bytes 6291460
  6.5 4.6 %copy-start.1 = (bf16[896,512]{1,0:T(8,128)(2,1)S(1)}, bf16[896,512]{1,0:T(8,128)(2,1)}, u32[]{:S(2)}) copy-start(bf16[896,512]{1,0:T(8,128)(2,1)} %refs_3_.1) | copy-start | bytes 2752516
  6.5 100.4 %all-gather.3.cloned.1.call-start = ((), (), s32[]{:S(2)}) async-start(), calls=%async_computation | async-start | bytes 2359296 | tf_op jit(solution)/shard_map/all_gather | solution.py:279
  10.5 14.6 %collective-permute-start = (bf16[256,256]{1,0:T(8,128)(2,1)S(1)}, bf16[256,256]{1,0:T(8,128)(2,1)S(1)}, u32[]{:S(2)}, u32[]{:S(2)}) collective-permute-start(bf16[256,256]{1,0:T(8,128)(2,1)S(1)} %convolution_convert_fusion), channel_id=1, source_target_pairs={{0,0},{1,1},{2,32},{3,33},{4,64},{5,65},{6,96},{7,97},{8,128},{9,1... | collective-permute-start | bytes 393224 | tf_op jit(solution)/shard_map/ppermute | solution.py:249
  11.2 21.6 %collective-permute-start.2 = (bf16[896,512]{1,0:T(8,128)(2,1)S(1)}, bf16[896,512]{1,0:T(8,128)(2,1)}, u32[]{:S(2)}, u32[]{:S(2)}) collective-permute-start(bf16[896,512]{1,0:T(8,128)(2,1)S(1)} %copy-done.1), channel_id=1, source_target_pairs={{0,32},{16,112},{1,33},{17,113},{2,34},{18,114},{3,35},{19,115},{4... | collective-permute-start | bytes 2752520 | tf_op jit(solution)/shard_map/ppermute | solution.py:47
  25.1 14.6 %collective-permute-start.9 = (bf16[2,256,896]{2,1,0:T(8,128)(2,1)}, bf16[2,256,896]{2,1,0:T(8,128)(2,1)}, u32[]{:S(2)}, u32[]{:S(2)}) collective-permute-start(bf16[2,256,896]{2,1,0:T(8,128)(2,1)} %shard_map.46), channel_id=1, source_target_pairs={{0,128},{16,152},{1,129},{17,153},{2,130},{18,154},{3,131},{19,155... | collective-permute-start | bytes 2752520 | tf_op jit(solution)/shard_map/ppermute | solution.py:47
  27.6 15.5 %collective-permute-start.1 = (bf16[256,256]{1,0:T(8,128)(2,1)S(1)}, bf16[256,256]{1,0:T(8,128)(2,1)S(1)}, u32[]{:S(2)}, u32[]{:S(2)}) collective-permute-start(bf16[256,256]{1,0:T(8,128)(2,1)S(1)} %collective-permute-done), channel_id=1, source_target_pairs={{0,8},{16,24},{1,9},{17,25},{2,10},{18,26},{3,11},{19,27},{4,12},{... | collective-permute-start | bytes 393224 | tf_op jit(solution)/shard_map/ppermute | solution.py:35
  29.1 14.9 %collective-permute-start.7 = (bf16[896,512]{1,0:T(8,128)(2,1)S(1)}, bf16[896,512]{1,0:T(8,128)(2,1)}, u32[]{:S(2)}, u32[]{:S(2)}) collective-permute-start(bf16[896,512]{1,0:T(8,128)(2,1)S(1)} %copy-done.1), channel_id=1, source_target_pairs={{0,16},{16,0},{1,17},{17,1},{2,18},{18,2},{3,19},{19,3},{4,20},{20... | collective-permute-start | bytes 2752520 | tf_op jit(solution)/shard_map/ppermute | solution.py:35
  32.8 26.2 %collective-permute-start.5 = (bf16[896,512]{1,0:T(8,128)(2,1)}, bf16[896,512]{1,0:T(8,128)(2,1)}, u32[]{:S(2)}, u32[]{:S(2)}) collective-permute-start(bf16[896,512]{1,0:T(8,128)(2,1)} %collective-permute-done.2.refs_4_.refs_5_), channel_id=1, source_target_pairs={{0,32},{16,112},{1,33},{17,113},{2,34},{18,114},{3,35},{19,115},{4... | collective-permute-start | bytes 2752520 | tf_op jit(solution)/shard_map/ppermute | solution.py:47
  38.9 21.4 %collective-permute-start.3 = (bf16[896,512]{1,0:T(8,128)(2,1)S(1)}, bf16[896,512]{1,0:T(8,128)(2,1)}, u32[]{:S(2)}, u32[]{:S(2)}) collective-permute-start(bf16[896,512]{1,0:T(8,128)(2,1)S(1)} %copy-done.1), channel_id=1, source_target_pairs={{0,96},{16,48},{1,97},{17,49},{2,98},{18,50},{3,99},{19,51},{4,100... | collective-permute-start | bytes 2752520 | tf_op jit(solution)/shard_map/ppermute | solution.py:47
  39.7 31.7 %collective-permute-start.11 = (bf16[4,256,896]{2,1,0:T(8,128)(2,1)}, bf16[4,256,896]{2,1,0:T(8,128)(2,1)}, u32[]{:S(2)}, u32[]{:S(2)}) collective-permute-start(bf16[4,256,896]{2,1,0:T(8,128)(2,1)} %shard_map.48), channel_id=1, source_target_pairs={{0,128},{16,152},{1,129},{17,153},{2,130},{18,154},{3,131},{19,155... | collective-permute-start | bytes 5505032 | tf_op jit(solution)/shard_map/ppermute | solution.py:47
  43.8 17.0 %collective-permute-start.8 = (bf16[896,512]{1,0:T(8,128)(2,1)}, bf16[896,512]{1,0:T(8,128)(2,1)S(1)}, u32[]{:S(2)}, u32[]{:S(2)}) collective-permute-start(bf16[896,512]{1,0:T(8,128)(2,1)} %collective-permute-done.2.refs_4_.refs_5_), channel_id=1, source_target_pairs={{0,16},{16,0},{1,17},{17,1},{2,18},{18,2},{3,19},{19,3},{4,20},{20... | collective-permute-start | bytes 2752520 | tf_op jit(solution)/shard_map/ppermute | solution.py:35
  43.9 23.2 %collective-permute-start.10 = (bf16[2,256,896]{2,1,0:T(8,128)(2,1)}, bf16[2,256,896]{2,1,0:T(8,128)(2,1)}, u32[]{:S(2)}, u32[]{:S(2)}) collective-permute-start(bf16[2,256,896]{2,1,0:T(8,128)(2,1)} %collective-permute-done.9.refs_1_), channel_id=1, source_target_pairs={{0,1},{16,23},{1,2},{17,16},{2,3},{18,17},{3,4},{19,18},{4,5},{20,... | collective-permute-start | bytes 2752520 | tf_op jit(solution)/shard_map/ppermute | solution.py:47
  59.0 12.3 %collective-permute-start.6 = (bf16[896,512]{1,0:T(8,128)(2,1)}, bf16[896,512]{1,0:T(8,128)(2,1)}, u32[]{:S(2)}, u32[]{:S(2)}) collective-permute-start(bf16[896,512]{1,0:T(8,128)(2,1)} %collective-permute-done.5.refs_4_), channel_id=1, source_target_pairs={{0,16},{16,0},{1,17},{17,1},{2,18},{18,2},{3,19},{19,3},{4,20},{20... | collective-permute-start | bytes 2752520 | tf_op jit(solution)/shard_map/ppermute | solution.py:35
  60.3 11.1 %collective-permute-start.4 = (bf16[896,512]{1,0:T(8,128)(2,1)}, bf16[896,512]{1,0:T(8,128)(2,1)}, u32[]{:S(2)}, u32[]{:S(2)}) collective-permute-start(bf16[896,512]{1,0:T(8,128)(2,1)} %collective-permute-done.3.refs_2_), channel_id=1, source_target_pairs={{0,16},{16,0},{1,17},{17,1},{2,18},{18,2},{3,19},{19,3},{4,20},{20... | collective-permute-start | bytes 2752520 | tf_op jit(solution)/shard_map/ppermute | solution.py:35
  60.8 0.9 copy-start.3
  61.8 5.4 %copy-start.2 = (bf16[896,512]{1,0:T(8,128)(2,1)S(1)}, bf16[896,512]{1,0:T(8,128)(2,1)}, u32[]{:S(2)}) copy-start(bf16[896,512]{1,0:T(8,128)(2,1)} %refs_3_.1) | copy-start | bytes 2752516
  67.2 1.2 copy-start.4
  71.3 4.1 %copy-start.5 = (f32[256,512]{1,0:T(8,128)S(1)}, f32[256,512]{1,0:T(8,128)}, u32[]{:S(2)}) copy-start(f32[256,512]{1,0:T(8,128)} %shard_map.47.refs_6_) | copy-start | bytes 1572868
  74.7 7.7 %collective-permute-start.12 = (f16[256,512]{1,0:T(8,128)(2,1)S(1)}, f16[256,512]{1,0:T(8,128)(2,1)S(1)}, u32[]{:S(2)}, u32[]{:S(2)}) collective-permute-start(f16[256,512]{1,0:T(8,128)(2,1)S(1)} %multiply_convert_fusion), channel_id=1, source_target_pairs={{0,128},{16,144},{1,129},{17,145},{2,130},{18,146},{3,131},{19,147... | collective-permute-start | bytes 786440 | tf_op jit(solution)/shard_map/ppermute | solution.py:58
  82.6 8.9 %collective-permute-start.15 = (bf16[256,512]{1,0:T(8,128)(2,1)S(1)}, bf16[256,512]{1,0:T(8,128)(2,1)S(1)}, u32[]{:S(2)}, u32[]{:S(2)}) collective-permute-start(bf16[256,512]{1,0:T(8,128)(2,1)S(1)} %add_convert_fusion.refs_0_), channel_id=1, source_target_pairs={{0,128},{16,144},{1,129},{17,145},{2,130},{18,146},{3,131},{19,147... | collective-permute-start | bytes 786440 | tf_op jit(solution)/shard_map/ppermute | solution.py:58
  83.1 12.6 %collective-permute-start.16 = (bf16[256,512]{1,0:T(8,128)(2,1)S(1)}, bf16[256,512]{1,0:T(8,128)(2,1)S(1)}, u32[]{:S(2)}, u32[]{:S(2)}) collective-permute-start(bf16[256,512]{1,0:T(8,128)(2,1)S(1)} %add_convert_fusion.refs_0_), channel_id=1, source_target_pairs={{0,64},{16,80},{1,65},{17,81},{2,66},{18,82},{3,67},{19,83},{4,68}... | collective-permute-start | bytes 786440 | tf_op jit(solution)/shard_map/ppermute | solution.py:35
  88.8 12.4 %collective-permute-start.13 = (bf16[256,512]{1,0:T(8,128)(2,1)S(1)}, bf16[256,512]{1,0:T(8,128)(2,1)S(1)}, u32[]{:S(2)}, u32[]{:S(2)}) collective-permute-start(bf16[256,512]{1,0:T(8,128)(2,1)S(1)} %add_convert_fusion.refs_0_), channel_id=1, source_target_pairs={{0,32},{16,48},{1,33},{17,49},{2,34},{18,50},{3,35},{19,51},{4,36}... | collective-permute-start | bytes 786440 | tf_op jit(solution)/shard_map/ppermute | solution.py:35
  88.8 12.4 %collective-permute-start.14 = (bf16[256,512]{1,0:T(8,128)(2,1)S(1)}, bf16[256,512]{1,0:T(8,128)(2,1)S(1)}, u32[]{:S(2)}, u32[]{:S(2)}) collective-permute-start(bf16[256,512]{1,0:T(8,128)(2,1)S(1)} %add_convert_fusion.refs_0_), channel_id=1, source_target_pairs={{0,96},{16,112},{1,97},{17,113},{2,98},{18,114},{3,99},{19,115},{4... | collective-permute-start | bytes 786440 | tf_op jit(solution)/shard_map/ppermute | solution.py:35
  91.5 15.5 %collective-permute-start.17 = (bf16[256,512]{1,0:T(8,128)(2,1)S(1)}, bf16[256,512]{1,0:T(8,128)(2,1)}, u32[]{:S(2)}, u32[]{:S(2)}) collective-permute-start(bf16[256,512]{1,0:T(8,128)(2,1)S(1)} %collective-permute-done.15.refs_3_), channel_id=1, source_target_pairs={{0,32},{16,48},{1,33},{17,49},{2,34},{18,50},{3,35},{19,51},{4,36}... | collective-permute-start | bytes 786440 | tf_op jit(solution)/shard_map/ppermute | solution.py:35
  91.5 15.5 %collective-permute-start.18 = (bf16[256,512]{1,0:T(8,128)(2,1)S(1)}, bf16[256,512]{1,0:T(8,128)(2,1)}, u32[]{:S(2)}, u32[]{:S(2)}) collective-permute-start(bf16[256,512]{1,0:T(8,128)(2,1)S(1)} %collective-permute-done.15.refs_3_), channel_id=1, source_target_pairs={{0,96},{16,112},{1,97},{17,113},{2,98},{18,114},{3,99},{19,115},{4... | collective-permute-start | bytes 786440 | tf_op jit(solution)/shard_map/ppermute | solution.py:35
  95.6 11.3 %collective-permute-start.19 = (bf16[256,512]{1,0:T(8,128)(2,1)S(1)}, bf16[256,512]{1,0:T(8,128)(2,1)}, u32[]{:S(2)}, u32[]{:S(2)}) collective-permute-start(bf16[256,512]{1,0:T(8,128)(2,1)S(1)} %collective-permute-done.16.refs_4_), channel_id=1, source_target_pairs={{0,128},{16,144},{1,129},{17,145},{2,130},{18,146},{3,131},{19,147... | collective-permute-start | bytes 786440 | tf_op jit(solution)/shard_map/ppermute | solution.py:58
  107.0 1.6 %copy-start.6 = (bf16[16,256,256]{2,1,0:T(8,128)(2,1)S(1)}, bf16[16,256,256]{2,1,0:T(8,128)(2,1)}, u32[]{:S(2)}) copy-start(bf16[16,256,256]{2,1,0:T(8,128)(2,1)} %all-gather.3.cloned.1.call-done) | copy-start | bytes 6291460
  112.9 2.1 %collective-permute-start.20 = (f32[256,512]{1,0:T(8,128)S(1)}, f32[256,512]{1,0:T(8,128)S(1)}, u32[]{:S(2)}, u32[]{:S(2)}) collective-permute-start(f32[256,512]{1,0:T(8,128)S(1)} %get-tuple-element.24), channel_id=1, source_target_pairs={{0,16},{16,0},{1,17},{17,1},{2,18},{18,2},{3,19},{19,3},{4,20},{20... | collective-permute-start | bytes 1572872 | tf_op jit(solution)/shard_map/ppermute | solution.py:35
Sparse Core Ops, SparseCore 0:
  43.9 43.8 all-gather.2

commit v11 on v10

--- a/solution.py
+++ b/solution.py
@@ -271,11 +271,11 @@
     near = by_core(near, dx=1)
     first, again = lax.optimization_barrier((first, basis_in))
     second, far = by_core(again, dy=NY - 1), by_core(first, dy=1)
-    first_other = shift(first, dc=1)
     near, rest = lax.optimization_barrier((near, rest))
     rest, away = by_core(rest, dx=1), by_core(near, dz=1)
 
-    other = shift(block, dx=NX)
+    other, first = lax.optimization_barrier((shift(block, dx=NX), first))
+    first_other = shift(first, dc=1)
     out_rows = lax.all_gather(
         jnp.stack([block, other]),
         "blk",
@@ -288,13 +288,12 @@
         + [core, 1 - core]
     ).astype(jnp.int32)
 
-    panels = [basis_in, own_other, first, first_other]
+    panels = [[panel] for panel in (basis_in, own_other, first, first_other)]
+    mine = product(own_moves, 2 * SPLIT, keep[: 2 * SPLIT], (activations,), panels)
+    mine, second = lax.optimization_barrier((mine, second))
     for panel in (second, far):
-        panels += [panel, shift(panel, dc=1)]
-    panels = [[panel] for panel in panels]
+        panels += [[panel], [shift(panel, dc=1)]]
     parity = parity.reshape(1).astype(jnp.int32)
-    mine = product(own_moves, 2 * SPLIT, keep[: 2 * SPLIT], (activations,), panels[: 2 * SPLIT])
-    mine, away = lax.optimization_barrier((mine, away))
     partial = product(
         near_moves, 2, parity, (near, away), panels[: 2 * SPLIT], None, 0, OWN_VMEM
     )

time: 123 us -> 129 us (1.049)
  waiting for transfers between devices: 30.1 us -> 37.3 us
    ppermute x3, waiting for transfers between devices: 3.27 us -> 7.96 us  [swap(): return lax.ppermute(value, ('dp', 'blk'), pairs)]
    ppermute x6, waiting for transfers between devices: 12.6 us -> 15.5 us  [by_core(): return lax.ppermute(value, ('dp', 'blk'), pairs)]
    ppermute x11, starting transfers between devices: 13.2 us -> 14.7 us  [shift(): return lax.ppermute(value, ('dp', 'blk'), pairs)]
    ppermute x6, starting transfers between devices: 27.2 us -> 25.7 us  [by_core(): return lax.ppermute(value, ('dp', 'blk'), pairs)]
    unnamed x14 -> x10, local copies, waits for them, and re-layouts: 5.29 us -> 4.36 us
  transfers between devices with their start and end apart: 22 -> 22, of which waited for: 9 -> 8; matrix products, arithmetic and copies ran while one was open for 2% -> 2% of each run, Pallas kernels for 17% -> 16%
where the time goes in v11:
time: 129 us; the launch traced here: 128 us
  starting transfers between devices  42.1 us (33%)
  waiting for transfers between devices  37.3 us (29%)
  Pallas kernels  24.9 us (19%)
  between operations  13.6 us (11%)
  local copies, waits for them, and re-layouts  6.24 us (5%)
  matrix products  2.34 us (2%)
  other arithmetic  1.75 us (1%)
    ppermute x6, starting transfers between devices, by_core(): return lax.ppermute(value, ('dp', 'blk'), pairs)  25.7 us
    ppermute x6, waiting for transfers between devices, by_core(): return lax.ppermute(value, ('dp', 'blk'), pairs)  15.5 us
    pallas_call x4, Pallas kernels, product(): pl.pallas_call(lambda *refs: product_kernel(moves, layout, *refs), out_sh...  15 us
    ppermute x11, starting transfers between devices, shift(): return lax.ppermute(value, ('dp', 'blk'), pairs)  14.7 us
    ppermute x11, waiting for transfers between devices, shift(): return lax.ppermute(value, ('dp', 'blk'), pairs)  13.8 us
    ppermute x3, waiting for transfers between devices, swap(): return lax.ppermute(value, ('dp', 'blk'), pairs)  7.96 us
    pallas_call x2, Pallas kernels, pieces(): pl.pallas_call(pieces_kernel, out_shape=jax.ShapeDtypeStruct(shape, activ...  5.63 us
    unnamed x10, local copies, waits for them, and re-layouts  4.36 us
  transfers between devices with their start and end apart: 22, of which 8 were waited for; matrix products, arithmetic and copies ran while one was open for 2% of the time, Pallas kernels for 16%

profile of v11, /device:TPU:1, one launch (start us, length us, event | category | flops | bytes accessed | tf_op | source)
XLA Modules:
  0.0 128.3 jit_solution(16257532819612713537)
XLA Ops:
  6.5 1.6 %copy-done = bf16[4096,256]{1,0:T(8,128)(2,1)S(1)} copy-done((bf16[4096,256]{1,0:T(8,128)(2,1)S(1)}, bf16[4096,256]{1,0:T(8,128)(2,1)}, u32[]{:S(2)}) %copy-start) | copy-done | bytes 2097176
  8.1 2.3 %convolution_convert_fusion = bf16[256,256]{1,0:T(8,128)(2,1)S(1)} fusion(bf16[4096,256]{1,0:T(8,128)(2,1)S(1)} %copy-done, bf16[256,4096]{1,0:T(8,128)(2,1)} %param.5), kind=kOutput, calls=%fused_computation | convolution fusion | flops 536936448 | bytes 4325376 | tf_op jit(solution)/shard_map/dot_general | solution.py:62
  10.5 0.7 collective-permute-start
  11.2 10.6 %collective-permute-start.2 = (bf16[896,512]{1,0:T(8,128)(2,1)}, bf16[896,512]{1,0:T(8,128)(2,1)S(1)}, u32[]{:S(2)}, u32[]{:S(2)}) collective-permute-start(bf16[896,512]{1,0:T(8,128)(2,1)} %refs_3_.1), channel_id=1, source_target_pairs={{0,32},{16,112},{1,33},{17,113},{2,34},{18,114},{3,35},{19,115},{4... | collective-permute-start | bytes 2752520 | tf_op jit(solution)/shard_map/ppermute | solution.py:47
  21.8 0.6 dynamic_slice.3.columns_ref
  22.4 2.6 %shard_map.46 = bf16[2,256,896]{2,1,0:T(8,128)(2,1)} custom-call(s32[2]{0:T(128)} %dynamic_slice.3.columns_ref, bf16[256,14336]{1,0:T(8,128)(2,1)} %source.3), custom_call_target="tpu_custom_call" | custom-call | bytes 4194304 | tf_op jit(solution)/shard_map/pallas_call | solution.py:92
  25.1 2.6 %collective-permute-start.9 = (bf16[2,256,896]{2,1,0:T(8,128)(2,1)}, bf16[2,256,896]{2,1,0:T(8,128)(2,1)}, u32[]{:S(2)}, u32[]{:S(2)}) collective-permute-start(bf16[2,256,896]{2,1,0:T(8,128)(2,1)} %shard_map.46), channel_id=1, source_target_pairs={{0,128},{16,152},{1,129},{17,153},{2,130},{18,154},{3,131},{19,155... | collective-permute-start | bytes 2752520 | tf_op jit(solution)/shard_map/ppermute | solution.py:47
  27.6 1.4 %collective-permute-start.1 = (bf16[256,256]{1,0:T(8,128)(2,1)S(1)}, bf16[256,256]{1,0:T(8,128)(2,1)S(1)}, u32[]{:S(2)}, u32[]{:S(2)}) collective-permute-start(bf16[256,256]{1,0:T(8,128)(2,1)S(1)} %collective-permute-done), channel_id=1, source_target_pairs={{0,8},{16,24},{1,9},{17,25},{2,10},{18,26},{3,11},{19,27},{4,12},{... | collective-permute-start | bytes 393224 | tf_op jit(solution)/shard_map/ppermute | solution.py:35
  29.1 4.0 %collective-permute-done.2.refs_4_.refs_5_ = bf16[896,512]{1,0:T(8,128)(2,1)S(1)} collective-permute-done((bf16[896,512]{1,0:T(8,128)(2,1)}, bf16[896,512]{1,0:T(8,128)(2,1)S(1)}, u32[]{:S(2)}, u32[]{:S(2)}) %collective-permute-start.2) | collective-permute-done | bytes 917536 | tf_op jit(solution)/shard_map/ppermute | solution.py:47
  33.1 1.3 %collective-permute-done.1 = bf16[256,256]{1,0:T(8,128)(2,1)S(1)} collective-permute-done((bf16[256,256]{1,0:T(8,128)(2,1)S(1)}, bf16[256,256]{1,0:T(8,128)(2,1)S(1)}, u32[]{:S(2)}, u32[]{:S(2)}) %collective-permute-start.1) | collective-permute-done | bytes 131104 | tf_op jit(solution)/shard_map/ppermute | solution.py:35
  34.4 6.3 %collective-permute-start.4 = (bf16[896,512]{1,0:T(8,128)(2,1)S(1)}, bf16[896,512]{1,0:T(8,128)(2,1)}, u32[]{:S(2)}, u32[]{:S(2)}) collective-permute-start(bf16[896,512]{1,0:T(8,128)(2,1)S(1)} %collective-permute-done.2.refs_4_.refs_5_), channel_id=1, source_target_pairs={{0,16},{16,0},{1,17},{17,1},{2,18},{18,2},{3,19},{19,3},{4,20},{20... | collective-permute-start | bytes 2752520 | tf_op jit(solution)/shard_map/ppermute | solution.py:35
  40.7 0.6 slice.11.columns_ref
  41.3 3.0 %shard_map.49 = bf16[4,256,896]{2,1,0:T(8,128)(2,1)} custom-call(s32[4]{0:T(128)} %slice.11.columns_ref, bf16[256,14336]{1,0:T(8,128)(2,1)} %source.3), custom_call_target="tpu_custom_call" | custom-call | bytes 4194304 | tf_op jit(solution)/shard_map/pallas_call | solution.py:92
  44.3 8.9 %collective-permute-start.7 = (bf16[896,512]{1,0:T(8,128)(2,1)S(1)}, bf16[896,512]{1,0:T(8,128)(2,1)}, u32[]{:S(2)}, u32[]{:S(2)}) collective-permute-start(bf16[896,512]{1,0:T(8,128)(2,1)S(1)} %collective-permute-done.2.refs_4_.refs_5_), channel_id=1, source_target_pairs={{0,32},{16,112},{1,33},{17,113},{2,34},{18,114},{3,35},{19,115},{4... | collective-permute-start | bytes 2752520 | tf_op jit(solution)/shard_map/ppermute | solution.py:47
  53.2 0.7 pad_maximum_fusion
  54.5 3.7 %collective-permute-start.11 = (bf16[2,256,896]{2,1,0:T(8,128)(2,1)}, bf16[2,256,896]{2,1,0:T(8,128)(2,1)}, u32[]{:S(2)}, u32[]{:S(2)}) collective-permute-start(bf16[2,256,896]{2,1,0:T(8,128)(2,1)} %collective-permute-done.9.refs_1_), channel_id=1, source_target_pairs={{0,1},{16,23},{1,2},{17,16},{2,3},{18,17},{3,4},{19,18},{4,5},{20,... | collective-permute-start | bytes 2752520 | tf_op jit(solution)/shard_map/ppermute | solution.py:47
  58.3 4.7 %shard_map.47.refs_6_ = f32[256,512]{1,0:T(8,128)} custom-call(s32[4]{0:T(128)} %get-tuple-element.29.refs_0_, bf16[256,14336]{1,0:T(8,128)(2,1)} %source.3, bf16[896,512]{1,0:T(8,128)(2,1)} %refs_3_.1, bf16[896,512]{1,0:T(8,128)(2,1)} %collective-permute-done.3.refs_3_.refs_4_, bf16[896,512]{1,0:T(8,128)(2,1)} %copy-done.1, ...), custom_call_target="tpu_custom_call" | custom-call | flops 939524096 | bytes 4194304 | tf_op jit(solution)/shard_map/pallas_call | solution.py:150
  62.9 11.5 %collective-permute-done.5.refs_2_ = bf16[896,512]{1,0:T(8,128)(2,1)} collective-permute-done((bf16[896,512]{1,0:T(8,128)(2,1)}, bf16[896,512]{1,0:T(8,128)(2,1)}, u32[]{:S(2)}, u32[]{:S(2)}) %collective-permute-start.5) | collective-permute-done | bytes 917536 | tf_op jit(solution)/shard_map/ppermute | solution.py:47
  74.9 1.2 copy-done.2
  76.1 3.2 %shard_map.50.refs_6_ = f32[256,512]{1,0:T(8,128)S(1)} custom-call(s32[1]{0:T(128)} %bitcast.19.refs_0_, bf16[2,256,896]{2,1,0:T(8,128)(2,1)} %collective-permute-done.9.refs_1_, bf16[2,256,896]{2,1,0:T(8,128)(2,1)} %collective-permute-done.11.refs_2_, bf16[896,512]{1,0:T(8,128)(2,1)} %refs_3_.1, bf16[896,512]{1,0:T(8,128)(2,1)} %collective-permute-done.3.refs_3_.refs_4_, ...), custom_call_target="tpu_custom_call" | custom-call | flops 939524096 | bytes 4194304 | tf_op jit(solution)/shard_map/pallas_call | solution.py:150
  79.4 3.3 %shard_map.51 = f32[256,512]{1,0:T(8,128)S(1)} custom-call(s32[1]{0:T(128)} %bitcast.19.refs_0_, bf16[4,256,896]{2,1,0:T(8,128)(2,1)} %collective-permute-done.10.refs_1_, bf16[896,512]{1,0:T(8,128)(2,1)} %collective-permute-done.5.refs_2_, bf16[896,512]{1,0:T(8,128)(2,1)S(1)} %collective-permute-done.6.refs_3_, ...), custom_call_target="tpu_custom_call" | custom-call | flops 6939524096 | bytes 4194304 | tf_op jit(solution)/shard_map/pallas_call | solution.py:150
  83.0 3.8 %shard_map.48 = f32[256,512]{1,0:T(8,128)S(1)} custom-call(s32[4]{0:T(128)S(1)} %get-tuple-element.30.refs_0_, bf16[256,14336]{1,0:T(8,128)(2,1)} %source.3, bf16[896,512]{1,0:T(8,128)(2,1)} %collective-permute-done.5.refs_2_, bf16[896,512]{1,0:T(8,128)(2,1)S(1)} %collective-permute-done.6.refs_3_, bf16[896,512]{1,0:T(8,128)(2,1)} %collective-permute-done.7.refs_4_, ...), custom_call_target="tpu_custom_call" | custom-call | flops 939524096 | bytes 4194304 | tf_op jit(solution)/shard_map/pallas_call | solution.py:150
  86.9 4.2 %collective-permute-done.12 = f16[256,512]{1,0:T(8,128)(2,1)S(1)} collective-permute-done((f16[256,512]{1,0:T(8,128)(2,1)S(1)}, f16[256,512]{1,0:T(8,128)(2,1)S(1)}, u32[]{:S(2)}, u32[]{:S(2)}) %collective-permute-start.12) | collective-permute-done | bytes 262176 | tf_op jit(solution)/shard_map/ppermute | solution.py:58
  91.9 2.1 %collective-permute-start.13 = (bf16[256,512]{1,0:T(8,128)(2,1)S(1)}, bf16[256,512]{1,0:T(8,128)(2,1)S(1)}, u32[]{:S(2)}, u32[]{:S(2)}) collective-permute-start(bf16[256,512]{1,0:T(8,128)(2,1)S(1)} %add_convert_fusion.refs_0_), channel_id=1, source_target_pairs={{0,32},{16,48},{1,33},{17,49},{2,34},{18,50},{3,35},{19,51},{4,36}... | collective-permute-start | bytes 786440 | tf_op jit(solution)/shard_map/ppermute | solution.py:35
  94.6 3.8 %collective-permute-done.15.refs_3_ = bf16[256,512]{1,0:T(8,128)(2,1)S(1)} collective-permute-done((bf16[256,512]{1,0:T(8,128)(2,1)S(1)}, bf16[256,512]{1,0:T(8,128)(2,1)S(1)}, u32[]{:S(2)}, u32[]{:S(2)}) %collective-permute-start.15) | collective-permute-done | bytes 262176 | tf_op jit(solution)/shard_map/ppermute | solution.py:58
  98.4 2.7 %collective-permute-start.18 = (bf16[256,512]{1,0:T(8,128)(2,1)S(1)}, bf16[256,512]{1,0:T(8,128)(2,1)}, u32[]{:S(2)}, u32[]{:S(2)}) collective-permute-start(bf16[256,512]{1,0:T(8,128)(2,1)S(1)} %collective-permute-done.15.refs_3_), channel_id=1, source_target_pairs={{0,96},{16,112},{1,97},{17,113},{2,98},{18,114},{3,99},{19,115},{4... | collective-permute-start | bytes 786440 | tf_op jit(solution)/shard_map/ppermute | solution.py:35
  101.6 5.2 %collective-permute-done.13.refs_1_ = bf16[256,512]{1,0:T(8,128)(2,1)S(1)} collective-permute-done((bf16[256,512]{1,0:T(8,128)(2,1)S(1)}, bf16[256,512]{1,0:T(8,128)(2,1)S(1)}, u32[]{:S(2)}, u32[]{:S(2)}) %collective-permute-start.13) | collective-permute-done | bytes 262176 | tf_op jit(solution)/shard_map/ppermute | solution.py:35
  106.8 5.7 %collective-permute-done.17.refs_5_ = bf16[256,512]{1,0:T(8,128)(2,1)} collective-permute-done((bf16[256,512]{1,0:T(8,128)(2,1)S(1)}, bf16[256,512]{1,0:T(8,128)(2,1)}, u32[]{:S(2)}, u32[]{:S(2)}) %collective-permute-start.17) | collective-permute-done | bytes 262176 | tf_op jit(solution)/shard_map/ppermute | solution.py:35
  112.5 1.6 %copy-done.4 = bf16[16,256,256]{2,1,0:T(8,128)(2,1)S(1)} copy-done((bf16[16,256,256]{2,1,0:T(8,128)(2,1)S(1)}, bf16[16,256,256]{2,1,0:T(8,128)(2,1)}, u32[]{:S(2)}) %copy-start.4) | copy-done | bytes 2097176
  114.1 4.3 %shard_map.52 = (f32[256,512]{1,0:T(8,128)S(1)}, f32[256,512]{1,0:T(8,128)S(1)}) custom-call(s32[18]{0:T(128)S(1)} %stack.81.where_ref, bf16[8,2,256,256]{3,2,1,0:T(8,128)(2,1)S(1)} %bitcast.22, bf16[256,512]{1,0:T(8,128)(2,1)S(1)} %add_convert_fusion.refs_0_, bf16[256,512]{1,0:T(8,128)(2,1)S(1)} %collective-permute-done.13.refs_1_, ...), custom_call_target="tpu_custom_call" | custom-call | flops 1073741824 | bytes 3145728 | tf_op jit(solution)/shard_map/pallas_call | solution.py:222
  119.0 1.5 %collective-permute-done.20 = f32[256,512]{1,0:T(8,128)S(1)} collective-permute-done((f32[256,512]{1,0:T(8,128)S(1)}, f32[256,512]{1,0:T(8,128)S(1)}, u32[]{:S(2)}, u32[]{:S(2)}) %collective-permute-start.20) | collective-permute-done | bytes 524320 | tf_op jit(solution)/shard_map/ppermute | solution.py:35
  120.5 0.9 add_multiply_fusion
  (41 shorter events, 4.0 us)
Async XLA Ops:
  6.5 1.6 %copy-start = (bf16[4096,256]{1,0:T(8,128)(2,1)S(1)}, bf16[4096,256]{1,0:T(8,128)(2,1)}, u32[]{:S(2)}) copy-start(bf16[4096,256]{1,0:T(8,128)(2,1)} %param.7) | copy-start | bytes 6291460
  6.5 106.0 %all-gather.3.cloned.1.call-start = ((), (), s32[]{:S(2)}) async-start(), calls=%async_computation | async-start | bytes 2359296 | tf_op jit(solution)/shard_map/all_gather | solution.py:279
  10.5 14.6 %collective-permute-start = (bf16[256,256]{1,0:T(8,128)(2,1)S(1)}, bf16[256,256]{1,0:T(8,128)(2,1)S(1)}, u32[]{:S(2)}, u32[]{:S(2)}) collective-permute-start(bf16[256,256]{1,0:T(8,128)(2,1)S(1)} %convolution_convert_fusion), channel_id=1, source_target_pairs={{0,0},{1,1},{2,32},{3,33},{4,64},{5,65},{6,96},{7,97},{8,128},{9,1... | collective-permute-start | bytes 393224 | tf_op jit(solution)/shard_map/ppermute | solution.py:249
  11.2 22.0 %collective-permute-start.2 = (bf16[896,512]{1,0:T(8,128)(2,1)}, bf16[896,512]{1,0:T(8,128)(2,1)S(1)}, u32[]{:S(2)}, u32[]{:S(2)}) collective-permute-start(bf16[896,512]{1,0:T(8,128)(2,1)} %refs_3_.1), channel_id=1, source_target_pairs={{0,32},{16,112},{1,33},{17,113},{2,34},{18,114},{3,35},{19,115},{4... | collective-permute-start | bytes 2752520 | tf_op jit(solution)/shard_map/ppermute | solution.py:47
  25.1 28.2 %collective-permute-start.9 = (bf16[2,256,896]{2,1,0:T(8,128)(2,1)}, bf16[2,256,896]{2,1,0:T(8,128)(2,1)}, u32[]{:S(2)}, u32[]{:S(2)}) collective-permute-start(bf16[2,256,896]{2,1,0:T(8,128)(2,1)} %shard_map.46), channel_id=1, source_target_pairs={{0,128},{16,152},{1,129},{17,153},{2,130},{18,154},{3,131},{19,155... | collective-permute-start | bytes 2752520 | tf_op jit(solution)/shard_map/ppermute | solution.py:47
  27.6 6.8 %collective-permute-start.1 = (bf16[256,256]{1,0:T(8,128)(2,1)S(1)}, bf16[256,256]{1,0:T(8,128)(2,1)S(1)}, u32[]{:S(2)}, u32[]{:S(2)}) collective-permute-start(bf16[256,256]{1,0:T(8,128)(2,1)S(1)} %collective-permute-done), channel_id=1, source_target_pairs={{0,8},{16,24},{1,9},{17,25},{2,10},{18,26},{3,11},{19,27},{4,12},{... | collective-permute-start | bytes 393224 | tf_op jit(solution)/shard_map/ppermute | solution.py:35
  29.1 25.5 %collective-permute-start.3 = (bf16[896,512]{1,0:T(8,128)(2,1)}, bf16[896,512]{1,0:T(8,128)(2,1)}, u32[]{:S(2)}, u32[]{:S(2)}) collective-permute-start(bf16[896,512]{1,0:T(8,128)(2,1)} %refs_3_.1), channel_id=1, source_target_pairs={{0,16},{16,0},{1,17},{17,1},{2,18},{18,2},{3,19},{19,3},{4,20},{20... | collective-permute-start | bytes 2752520 | tf_op jit(solution)/shard_map/ppermute | solution.py:35
  33.1 25.1 %copy-start.1 = (bf16[896,512]{1,0:T(8,128)(2,1)}, bf16[896,512]{1,0:T(8,128)(2,1)S(1)}, u32[]{:S(2)}) copy-start(bf16[896,512]{1,0:T(8,128)(2,1)S(1)} %collective-permute-done.2.refs_4_.refs_5_) | copy-start | bytes 2752516
  34.4 23.8 %collective-permute-start.4 = (bf16[896,512]{1,0:T(8,128)(2,1)S(1)}, bf16[896,512]{1,0:T(8,128)(2,1)}, u32[]{:S(2)}, u32[]{:S(2)}) collective-permute-start(bf16[896,512]{1,0:T(8,128)(2,1)S(1)} %collective-permute-done.2.refs_4_.refs_5_), channel_id=1, source_target_pairs={{0,16},{16,0},{1,17},{17,1},{2,18},{18,2},{3,19},{19,3},{4,20},{20... | collective-permute-start | bytes 2752520 | tf_op jit(solution)/shard_map/ppermute | solution.py:35
  44.3 30.1 %collective-permute-start.7 = (bf16[896,512]{1,0:T(8,128)(2,1)S(1)}, bf16[896,512]{1,0:T(8,128)(2,1)}, u32[]{:S(2)}, u32[]{:S(2)}) collective-permute-start(bf16[896,512]{1,0:T(8,128)(2,1)S(1)} %collective-permute-done.2.refs_4_.refs_5_), channel_id=1, source_target_pairs={{0,32},{16,112},{1,33},{17,113},{2,34},{18,114},{3,35},{19,115},{4... | collective-permute-start | bytes 2752520 | tf_op jit(solution)/shard_map/ppermute | solution.py:47
  53.2 21.2 %collective-permute-start.5 = (bf16[896,512]{1,0:T(8,128)(2,1)}, bf16[896,512]{1,0:T(8,128)(2,1)}, u32[]{:S(2)}, u32[]{:S(2)}) collective-permute-start(bf16[896,512]{1,0:T(8,128)(2,1)} %refs_3_.1), channel_id=1, source_target_pairs={{0,96},{16,48},{1,97},{17,49},{2,98},{18,50},{3,99},{19,51},{4,100... | collective-permute-start | bytes 2752520 | tf_op jit(solution)/shard_map/ppermute | solution.py:47
  53.2 26.1 %collective-permute-start.10 = (bf16[4,256,896]{2,1,0:T(8,128)(2,1)}, bf16[4,256,896]{2,1,0:T(8,128)(2,1)}, u32[]{:S(2)}, u32[]{:S(2)}) collective-permute-start(bf16[4,256,896]{2,1,0:T(8,128)(2,1)} %shard_map.49), channel_id=1, source_target_pairs={{0,128},{16,152},{1,129},{17,153},{2,130},{18,154},{3,131},{19,155... | collective-permute-start | bytes 5505032 | tf_op jit(solution)/shard_map/ppermute | solution.py:47
  54.5 20.4 %collective-permute-start.11 = (bf16[2,256,896]{2,1,0:T(8,128)(2,1)}, bf16[2,256,896]{2,1,0:T(8,128)(2,1)}, u32[]{:S(2)}, u32[]{:S(2)}) collective-permute-start(bf16[2,256,896]{2,1,0:T(8,128)(2,1)} %collective-permute-done.9.refs_1_), channel_id=1, source_target_pairs={{0,1},{16,23},{1,2},{17,16},{2,3},{18,17},{3,4},{19,18},{4,5},{20,... | collective-permute-start | bytes 2752520 | tf_op jit(solution)/shard_map/ppermute | solution.py:47
  74.4 4.9 %collective-permute-start.6 = (bf16[896,512]{1,0:T(8,128)(2,1)}, bf16[896,512]{1,0:T(8,128)(2,1)S(1)}, u32[]{:S(2)}, u32[]{:S(2)}) collective-permute-start(bf16[896,512]{1,0:T(8,128)(2,1)} %collective-permute-done.5.refs_2_), channel_id=1, source_target_pairs={{0,16},{16,0},{1,17},{17,1},{2,18},{18,2},{3,19},{19,3},{4,20},{20... | collective-permute-start | bytes 2752520 | tf_op jit(solution)/shard_map/ppermute | solution.py:35
  74.4 4.9 %collective-permute-start.8 = (bf16[896,512]{1,0:T(8,128)(2,1)}, bf16[896,512]{1,0:T(8,128)(2,1)S(1)}, u32[]{:S(2)}, u32[]{:S(2)}) collective-permute-start(bf16[896,512]{1,0:T(8,128)(2,1)} %collective-permute-done.7.refs_4_), channel_id=1, source_target_pairs={{0,16},{16,0},{1,17},{17,1},{2,18},{18,2},{3,19},{19,3},{4,20},{20... | collective-permute-start | bytes 2752520 | tf_op jit(solution)/shard_map/ppermute | solution.py:35
  74.9 1.2 copy-start.2
  79.3 3.7 %copy-start.3 = (f32[256,512]{1,0:T(8,128)S(1)}, f32[256,512]{1,0:T(8,128)}, u32[]{:S(2)}) copy-start(f32[256,512]{1,0:T(8,128)} %shard_map.47.refs_6_) | copy-start | bytes 1572868
  82.7 8.3 %collective-permute-start.12 = (f16[256,512]{1,0:T(8,128)(2,1)S(1)}, f16[256,512]{1,0:T(8,128)(2,1)S(1)}, u32[]{:S(2)}, u32[]{:S(2)}) collective-permute-start(f16[256,512]{1,0:T(8,128)(2,1)S(1)} %multiply_convert_fusion), channel_id=1, source_target_pairs={{0,128},{16,144},{1,129},{17,145},{2,130},{18,146},{3,131},{19,147... | collective-permute-start | bytes 786440 | tf_op jit(solution)/shard_map/ppermute | solution.py:58
  91.1 7.2 %collective-permute-start.15 = (bf16[256,512]{1,0:T(8,128)(2,1)S(1)}, bf16[256,512]{1,0:T(8,128)(2,1)S(1)}, u32[]{:S(2)}, u32[]{:S(2)}) collective-permute-start(bf16[256,512]{1,0:T(8,128)(2,1)S(1)} %add_convert_fusion.refs_0_), channel_id=1, source_target_pairs={{0,128},{16,144},{1,129},{17,145},{2,130},{18,146},{3,131},{19,147... | collective-permute-start | bytes 786440 | tf_op jit(solution)/shard_map/ppermute | solution.py:58
  91.4 9.6 %collective-permute-start.16 = (bf16[256,512]{1,0:T(8,128)(2,1)S(1)}, bf16[256,512]{1,0:T(8,128)(2,1)S(1)}, u32[]{:S(2)}, u32[]{:S(2)}) collective-permute-start(bf16[256,512]{1,0:T(8,128)(2,1)S(1)} %add_convert_fusion.refs_0_), channel_id=1, source_target_pairs={{0,64},{16,80},{1,65},{17,81},{2,66},{18,82},{3,67},{19,83},{4,68}... | collective-permute-start | bytes 786440 | tf_op jit(solution)/shard_map/ppermute | solution.py:35
  91.9 14.9 %collective-permute-start.13 = (bf16[256,512]{1,0:T(8,128)(2,1)S(1)}, bf16[256,512]{1,0:T(8,128)(2,1)S(1)}, u32[]{:S(2)}, u32[]{:S(2)}) collective-permute-start(bf16[256,512]{1,0:T(8,128)(2,1)S(1)} %add_convert_fusion.refs_0_), channel_id=1, source_target_pairs={{0,32},{16,48},{1,33},{17,49},{2,34},{18,50},{3,35},{19,51},{4,36}... | collective-permute-start | bytes 786440 | tf_op jit(solution)/shard_map/ppermute | solution.py:35
  94.0 12.7 %collective-permute-start.14 = (bf16[256,512]{1,0:T(8,128)(2,1)S(1)}, bf16[256,512]{1,0:T(8,128)(2,1)S(1)}, u32[]{:S(2)}, u32[]{:S(2)}) collective-permute-start(bf16[256,512]{1,0:T(8,128)(2,1)S(1)} %add_convert_fusion.refs_0_), channel_id=1, source_target_pairs={{0,96},{16,112},{1,97},{17,113},{2,98},{18,114},{3,99},{19,115},{4... | collective-permute-start | bytes 786440 | tf_op jit(solution)/shard_map/ppermute | solution.py:35
  98.4 14.1 %collective-permute-start.17 = (bf16[256,512]{1,0:T(8,128)(2,1)S(1)}, bf16[256,512]{1,0:T(8,128)(2,1)}, u32[]{:S(2)}, u32[]{:S(2)}) collective-permute-start(bf16[256,512]{1,0:T(8,128)(2,1)S(1)} %collective-permute-done.15.refs_3_), channel_id=1, source_target_pairs={{0,32},{16,48},{1,33},{17,49},{2,34},{18,50},{3,35},{19,51},{4,36}... | collective-permute-start | bytes 786440 | tf_op jit(solution)/shard_map/ppermute | solution.py:35
  98.4 14.1 %collective-permute-start.18 = (bf16[256,512]{1,0:T(8,128)(2,1)S(1)}, bf16[256,512]{1,0:T(8,128)(2,1)}, u32[]{:S(2)}, u32[]{:S(2)}) collective-permute-start(bf16[256,512]{1,0:T(8,128)(2,1)S(1)} %collective-permute-done.15.refs_3_), channel_id=1, source_target_pairs={{0,96},{16,112},{1,97},{17,113},{2,98},{18,114},{3,99},{19,115},{4... | collective-permute-start | bytes 786440 | tf_op jit(solution)/shard_map/ppermute | solution.py:35
  101.0 11.4 %collective-permute-start.19 = (bf16[256,512]{1,0:T(8,128)(2,1)S(1)}, bf16[256,512]{1,0:T(8,128)(2,1)}, u32[]{:S(2)}, u32[]{:S(2)}) collective-permute-start(bf16[256,512]{1,0:T(8,128)(2,1)S(1)} %collective-permute-done.16.refs_4_), channel_id=1, source_target_pairs={{0,128},{16,144},{1,129},{17,145},{2,130},{18,146},{3,131},{19,147... | collective-permute-start | bytes 786440 | tf_op jit(solution)/shard_map/ppermute | solution.py:58
  112.5 1.6 %copy-start.4 = (bf16[16,256,256]{2,1,0:T(8,128)(2,1)S(1)}, bf16[16,256,256]{2,1,0:T(8,128)(2,1)}, u32[]{:S(2)}) copy-start(bf16[16,256,256]{2,1,0:T(8,128)(2,1)} %all-gather.3.cloned.1.call-done) | copy-start | bytes 6291460
  118.4 2.1 %collective-permute-start.20 = (f32[256,512]{1,0:T(8,128)S(1)}, f32[256,512]{1,0:T(8,128)S(1)}, u32[]{:S(2)}, u32[]{:S(2)}) collective-permute-start(f32[256,512]{1,0:T(8,128)S(1)} %get-tuple-element.28), channel_id=1, source_target_pairs={{0,16},{16,0},{1,17},{17,1},{2,18},{18,2},{3,19},{19,3},{4,20},{20... | collective-permute-start | bytes 1572872 | tf_op jit(solution)/shard_map/ppermute | solution.py:35
Sparse Core Ops, SparseCore 0:
  54.1 40.2 all-gather.2

commit v12 on v11

--- a/solution.py
+++ b/solution.py
@@ -12,7 +12,7 @@
 SPLIT = 2
 FACTOR = 32.0
 VMEM = 60 * 1024 * 1024
-FOLLOWED = 6 * 10**9
+FOLLOWED = 10 * 10**9
 TAIL_VMEM = 16 * 1024 * 1024
 OWN_VMEM = 48 * 1024 * 1024
 BLOCKS = ((0, 0), (0, 1), (3, 0), (1, 1), (1, 0), (3, 1), (2, 0), (2, 1))
@@ -271,11 +271,11 @@
     near = by_core(near, dx=1)
     first, again = lax.optimization_barrier((first, basis_in))
     second, far = by_core(again, dy=NY - 1), by_core(first, dy=1)
-    near, rest = lax.optimization_barrier((near, rest))
+    near, rest, first = lax.optimization_barrier((near, rest, first))
+    first_other = shift(first, dc=1)
     rest, away = by_core(rest, dx=1), by_core(near, dz=1)
 
-    other, first = lax.optimization_barrier((shift(block, dx=NX), first))
-    first_other = shift(first, dc=1)
+    other = shift(block, dx=NX)
     out_rows = lax.all_gather(
         jnp.stack([block, other]),
         "blk",

time: 129 us -> 124 us (0.961)
  the two profiles are of different devices: /device:TPU:1 before, /device:TPU:99 now
where the time goes in v12:
time: 124 us; the launch traced here: 123 us
  starting transfers between devices  48.2 us (39%)
  waiting for transfers between devices  26.3 us (21%)
  Pallas kernels  24.9 us (20%)
  between operations  13.6 us (11%)
  local copies, waits for them, and re-layouts  6.33 us (5%)
  matrix products  2.34 us (2%)
  other arithmetic  1.75 us (1%)
    ppermute x11, starting transfers between devices, shift(): return lax.ppermute(value, ('dp', 'blk'), pairs)  33.6 us
    pallas_call x4, Pallas kernels, product(): pl.pallas_call(lambda *refs: product_kernel(moves, layout, *refs), out_sh...  14.9 us
    ppermute x6, waiting for transfers between devices, by_core(): return lax.ppermute(value, ('dp', 'blk'), pairs)  12 us
    ppermute x6, starting transfers between devices, by_core(): return lax.ppermute(value, ('dp', 'blk'), pairs)  10.9 us
    ppermute x11, waiting for transfers between devices, shift(): return lax.ppermute(value, ('dp', 'blk'), pairs)  8.22 us
    pallas_call x2, Pallas kernels, pieces(): pl.pallas_call(pieces_kernel, out_shape=jax.ShapeDtypeStruct(shape, activ...  5.64 us
    unnamed x10, local copies, waits for them, and re-layouts  4.39 us
    pallas_call x1, Pallas kernels, sums_of_squares(): pl.pallas_call(squares_kernel, out_shape=[jax.ShapeDtypeStruct((rows, wid...  4.3 us
  transfers between devices with their start and end apart: 22, of which 13 were waited for; matrix products, arithmetic and copies ran while one was open for 2% of the time, Pallas kernels for 17%

profile of v12, /device:TPU:99, one launch (start us, length us, event | category | flops | bytes accessed | tf_op | source)
XLA Modules:
  0.0 123.3 jit_solution(1806032543128688324)
XLA Ops:
  6.5 1.6 %copy-done = bf16[4096,256]{1,0:T(8,128)(2,1)S(1)} copy-done((bf16[4096,256]{1,0:T(8,128)(2,1)S(1)}, bf16[4096,256]{1,0:T(8,128)(2,1)}, u32[]{:S(2)}) %copy-start) | copy-done | bytes 2097176
  8.1 2.3 %convolution_convert_fusion = bf16[256,256]{1,0:T(8,128)(2,1)S(1)} fusion(bf16[4096,256]{1,0:T(8,128)(2,1)S(1)} %copy-done, bf16[256,4096]{1,0:T(8,128)(2,1)} %param.5), kind=kOutput, calls=%fused_computation | convolution fusion | flops 536936448 | bytes 4325376 | tf_op jit(solution)/shard_map/dot_general | solution.py:62
  10.5 3.2 %collective-permute-start = (bf16[256,256]{1,0:T(8,128)(2,1)S(1)}, bf16[256,256]{1,0:T(8,128)(2,1)S(1)}, u32[]{:S(2)}, u32[]{:S(2)}) collective-permute-start(bf16[256,256]{1,0:T(8,128)(2,1)S(1)} %convolution_convert_fusion), channel_id=1, source_target_pairs={{0,0},{1,1},{2,32},{3,33},{4,64},{5,65},{6,96},{7,97},{8,128},{9,1... | collective-permute-start | bytes 393224 | tf_op jit(solution)/shard_map/ppermute | solution.py:249
  13.7 7.3 %collective-permute-start.4 = (bf16[896,512]{1,0:T(8,128)(2,1)}, bf16[896,512]{1,0:T(8,128)(2,1)S(1)}, u32[]{:S(2)}, u32[]{:S(2)}) collective-permute-start(bf16[896,512]{1,0:T(8,128)(2,1)} %refs_3_.1), channel_id=1, source_target_pairs={{0,32},{16,112},{1,33},{17,113},{2,34},{18,114},{3,35},{19,115},{4... | collective-permute-start | bytes 2752520 | tf_op jit(solution)/shard_map/ppermute | solution.py:47
  21.7 2.6 %shard_map.46 = bf16[2,256,896]{2,1,0:T(8,128)(2,1)} custom-call(s32[2]{0:T(128)} %dynamic_slice.3.columns_ref, bf16[256,14336]{1,0:T(8,128)(2,1)} %refs_1_.3), custom_call_target="tpu_custom_call" | custom-call | bytes 4194304 | tf_op jit(solution)/shard_map/pallas_call | solution.py:92
  24.3 3.0 %collective-permute-done = bf16[256,256]{1,0:T(8,128)(2,1)S(1)} collective-permute-done((bf16[256,256]{1,0:T(8,128)(2,1)S(1)}, bf16[256,256]{1,0:T(8,128)(2,1)S(1)}, u32[]{:S(2)}, u32[]{:S(2)}) %collective-permute-start) | collective-permute-done | bytes 131104 | tf_op jit(solution)/shard_map/ppermute | solution.py:249
  27.3 2.5 %collective-permute-start.1 = (bf16[256,256]{1,0:T(8,128)(2,1)S(1)}, bf16[256,256]{1,0:T(8,128)(2,1)S(1)}, u32[]{:S(2)}, u32[]{:S(2)}) collective-permute-start(bf16[256,256]{1,0:T(8,128)(2,1)S(1)} %collective-permute-done), channel_id=1, source_target_pairs={{0,8},{16,24},{1,9},{17,25},{2,10},{18,26},{3,11},{19,27},{4,12},{... | collective-permute-start | bytes 393224 | tf_op jit(solution)/shard_map/ppermute | solution.py:35
  30.6 3.0 %shard_map.47 = bf16[4,256,896]{2,1,0:T(8,128)(2,1)} custom-call(s32[4]{0:T(128)} %slice.11.columns_ref, bf16[256,14336]{1,0:T(8,128)(2,1)} %refs_1_.3), custom_call_target="tpu_custom_call" | custom-call | bytes 4194304 | tf_op jit(solution)/shard_map/pallas_call | solution.py:92
  34.5 3.6 %collective-permute-start.8 = (bf16[896,512]{1,0:T(8,128)(2,1)S(1)}, bf16[896,512]{1,0:T(8,128)(2,1)}, u32[]{:S(2)}, u32[]{:S(2)}) collective-permute-start(bf16[896,512]{1,0:T(8,128)(2,1)S(1)} %collective-permute-done.4.refs_4_.refs_5_), channel_id=1, source_target_pairs={{0,32},{16,112},{1,33},{17,113},{2,34},{18,114},{3,35},{19,115},{4... | collective-permute-start | bytes 2752520 | tf_op jit(solution)/shard_map/ppermute | solution.py:47
  38.1 3.5 %collective-permute-done.3.refs_1_ = bf16[2,256,896]{2,1,0:T(8,128)(2,1)} collective-permute-done((bf16[2,256,896]{2,1,0:T(8,128)(2,1)}, bf16[2,256,896]{2,1,0:T(8,128)(2,1)}, u32[]{:S(2)}, u32[]{:S(2)}) %collective-permute-start.3) | collective-permute-done | bytes 917536 | tf_op jit(solution)/shard_map/ppermute | solution.py:47
  41.6 2.5 %collective-permute-start.5 = (bf16[896,512]{1,0:T(8,128)(2,1)S(1)}, bf16[896,512]{1,0:T(8,128)(2,1)}, u32[]{:S(2)}, u32[]{:S(2)}) collective-permute-start(bf16[896,512]{1,0:T(8,128)(2,1)S(1)} %collective-permute-done.4.refs_4_.refs_5_), channel_id=1, source_target_pairs={{0,16},{16,0},{1,17},{17,1},{2,18},{18,2},{3,19},{19,3},{4,20},{20... | collective-permute-start | bytes 2752520 | tf_op jit(solution)/shard_map/ppermute | solution.py:35
  45.4 3.0 %collective-permute-done.8.refs_4_ = bf16[896,512]{1,0:T(8,128)(2,1)} collective-permute-done((bf16[896,512]{1,0:T(8,128)(2,1)S(1)}, bf16[896,512]{1,0:T(8,128)(2,1)}, u32[]{:S(2)}, u32[]{:S(2)}) %collective-permute-start.8) | collective-permute-done | bytes 917536 | tf_op jit(solution)/shard_map/ppermute | solution.py:47
  48.4 5.1 %collective-permute-start.9 = (bf16[896,512]{1,0:T(8,128)(2,1)}, bf16[896,512]{1,0:T(8,128)(2,1)}, u32[]{:S(2)}, u32[]{:S(2)}) collective-permute-start(bf16[896,512]{1,0:T(8,128)(2,1)} %collective-permute-done.8.refs_4_), channel_id=1, source_target_pairs={{0,16},{16,0},{1,17},{17,1},{2,18},{18,2},{3,19},{19,3},{4,20},{20... | collective-permute-start | bytes 2752520 | tf_op jit(solution)/shard_map/ppermute | solution.py:35
  53.5 4.7 %shard_map.48.refs_6_ = f32[256,512]{1,0:T(8,128)} custom-call(s32[4]{0:T(128)} %get-tuple-element.27.refs_0_, bf16[256,14336]{1,0:T(8,128)(2,1)} %refs_1_.3, bf16[896,512]{1,0:T(8,128)(2,1)} %refs_3_.1, bf16[896,512]{1,0:T(8,128)(2,1)} %collective-permute-done.2.refs_3_.refs_4_, bf16[896,512]{1,0:T(8,128)(2,1)} %copy-done.1, ...), custom_call_target="tpu_custom_call" | custom-call | flops 939524096 | bytes 4194304 | tf_op jit(solution)/shard_map/pallas_call | solution.py:150
  59.2 1.2 copy-done.2
  60.4 3.2 %shard_map.50.refs_6_ = f32[256,512]{1,0:T(8,128)S(1)} custom-call(s32[1]{0:T(128)} %bitcast.19.refs_0_, bf16[2,256,896]{2,1,0:T(8,128)(2,1)} %collective-permute-done.3.refs_1_, bf16[2,256,896]{2,1,0:T(8,128)(2,1)} %collective-permute-done.11.refs_2_, bf16[896,512]{1,0:T(8,128)(2,1)} %refs_3_.1, bf16[896,512]{1,0:T(8,128)(2,1)} %collective-permute-done.2.refs_3_.refs_4_, ...), custom_call_target="tpu_custom_call" | custom-call | flops 939524096 | bytes 4194304 | tf_op jit(solution)/shard_map/pallas_call | solution.py:150
  63.6 3.8 %collective-permute-done.10.refs_1_ = bf16[4,256,896]{2,1,0:T(8,128)(2,1)} collective-permute-done((bf16[4,256,896]{2,1,0:T(8,128)(2,1)}, bf16[4,256,896]{2,1,0:T(8,128)(2,1)}, u32[]{:S(2)}, u32[]{:S(2)}) %collective-permute-start.10) | collective-permute-done | bytes 1835040 | tf_op jit(solution)/shard_map/ppermute | solution.py:47
  67.4 3.2 %shard_map.51 = f32[256,512]{1,0:T(8,128)S(1)} custom-call(s32[1]{0:T(128)} %bitcast.19.refs_0_, bf16[4,256,896]{2,1,0:T(8,128)(2,1)} %collective-permute-done.10.refs_1_, bf16[896,512]{1,0:T(8,128)(2,1)} %collective-permute-done.6.refs_2_, bf16[896,512]{1,0:T(8,128)(2,1)S(1)} %collective-permute-done.7.refs_3_, ...), custom_call_target="tpu_custom_call" | custom-call | flops 10939524096 | bytes 4194304 | tf_op jit(solution)/shard_map/pallas_call | solution.py:150
  71.0 3.8 %shard_map.49 = f32[256,512]{1,0:T(8,128)S(1)} custom-call(s32[4]{0:T(128)S(1)} %get-tuple-element.28.refs_0_, bf16[256,14336]{1,0:T(8,128)(2,1)} %refs_1_.3, bf16[896,512]{1,0:T(8,128)(2,1)} %collective-permute-done.6.refs_2_, bf16[896,512]{1,0:T(8,128)(2,1)S(1)} %collective-permute-done.7.refs_3_, bf16[896,512]{1,0:T(8,128)(2,1)} %collective-permute-done.8.refs_4_, ...), custom_call_target="tpu_custom_call" | custom-call | flops 939524096 | bytes 4194304 | tf_op jit(solution)/shard_map/pallas_call | solution.py:150
  74.8 1.8 %collective-permute-done.12 = f16[256,512]{1,0:T(8,128)(2,1)S(1)} collective-permute-done((f16[256,512]{1,0:T(8,128)(2,1)S(1)}, f16[256,512]{1,0:T(8,128)(2,1)S(1)}, u32[]{:S(2)}, u32[]{:S(2)}) %collective-permute-start.12) | collective-permute-done | bytes 262176 | tf_op jit(solution)/shard_map/ppermute | solution.py:58
  76.8 7.5 %collective-permute-start.16 = (bf16[256,512]{1,0:T(8,128)(2,1)S(1)}, bf16[256,512]{1,0:T(8,128)(2,1)S(1)}, u32[]{:S(2)}, u32[]{:S(2)}) collective-permute-start(bf16[256,512]{1,0:T(8,128)(2,1)S(1)} %add_convert_fusion.refs_0_), channel_id=1, source_target_pairs={{0,64},{16,80},{1,65},{17,81},{2,66},{18,82},{3,67},{19,83},{4,68}... | collective-permute-start | bytes 786440 | tf_op jit(solution)/shard_map/ppermute | solution.py:35
  84.3 2.7 %collective-permute-start.14 = (bf16[256,512]{1,0:T(8,128)(2,1)S(1)}, bf16[256,512]{1,0:T(8,128)(2,1)S(1)}, u32[]{:S(2)}, u32[]{:S(2)}) collective-permute-start(bf16[256,512]{1,0:T(8,128)(2,1)S(1)} %add_convert_fusion.refs_0_), channel_id=1, source_target_pairs={{0,96},{16,112},{1,97},{17,113},{2,98},{18,114},{3,99},{19,115},{4... | collective-permute-start | bytes 786440 | tf_op jit(solution)/shard_map/ppermute | solution.py:35
  86.9 2.7 %collective-permute-start.18 = (bf16[256,512]{1,0:T(8,128)(2,1)S(1)}, bf16[256,512]{1,0:T(8,128)(2,1)}, u32[]{:S(2)}, u32[]{:S(2)}) collective-permute-start(bf16[256,512]{1,0:T(8,128)(2,1)S(1)} %collective-permute-done.15.refs_3_), channel_id=1, source_target_pairs={{0,96},{16,112},{1,97},{17,113},{2,98},{18,114},{3,99},{19,115},{4... | collective-permute-start | bytes 786440 | tf_op jit(solution)/shard_map/ppermute | solution.py:35
  89.8 1.0 collective-permute-done.13.refs_1_
  90.8 1.6 %collective-permute-done.14.refs_2_ = bf16[256,512]{1,0:T(8,128)(2,1)S(1)} collective-permute-done((bf16[256,512]{1,0:T(8,128)(2,1)S(1)}, bf16[256,512]{1,0:T(8,128)(2,1)S(1)}, u32[]{:S(2)}, u32[]{:S(2)}) %collective-permute-start.14) | collective-permute-done | bytes 262176 | tf_op jit(solution)/shard_map/ppermute | solution.py:35
  92.4 4.0 %collective-permute-done.17.refs_5_ = bf16[256,512]{1,0:T(8,128)(2,1)} collective-permute-done((bf16[256,512]{1,0:T(8,128)(2,1)S(1)}, bf16[256,512]{1,0:T(8,128)(2,1)}, u32[]{:S(2)}, u32[]{:S(2)}) %collective-permute-start.17) | collective-permute-done | bytes 262176 | tf_op jit(solution)/shard_map/ppermute | solution.py:35
  96.5 1.4 %collective-permute-done.19.refs_7_ = bf16[256,512]{1,0:T(8,128)(2,1)} collective-permute-done((bf16[256,512]{1,0:T(8,128)(2,1)S(1)}, bf16[256,512]{1,0:T(8,128)(2,1)}, u32[]{:S(2)}, u32[]{:S(2)}) %collective-permute-start.19) | collective-permute-done | bytes 262176 | tf_op jit(solution)/shard_map/ppermute | solution.py:58
  97.9 1.6 %copy-done.4 = bf16[16,256,256]{2,1,0:T(8,128)(2,1)S(1)} copy-done((bf16[16,256,256]{2,1,0:T(8,128)(2,1)S(1)}, bf16[16,256,256]{2,1,0:T(8,128)(2,1)}, u32[]{:S(2)}) %copy-start.4) | copy-done | bytes 2097176
  99.5 4.3 %shard_map.52 = (f32[256,512]{1,0:T(8,128)S(1)}, f32[256,512]{1,0:T(8,128)S(1)}) custom-call(s32[18]{0:T(128)S(1)} %stack.81.where_ref, bf16[8,2,256,256]{3,2,1,0:T(8,128)(2,1)S(1)} %bitcast.22, bf16[256,512]{1,0:T(8,128)(2,1)S(1)} %add_convert_fusion.refs_0_, bf16[256,512]{1,0:T(8,128)(2,1)S(1)} %collective-permute-done.13.refs_1_, ...), custom_call_target="tpu_custom_call" | custom-call | flops 1073741824 | bytes 3145728 | tf_op jit(solution)/shard_map/pallas_call | solution.py:222
  103.8 10.3 %collective-permute-start.20 = (f32[256,512]{1,0:T(8,128)S(1)}, f32[256,512]{1,0:T(8,128)S(1)}, u32[]{:S(2)}, u32[]{:S(2)}) collective-permute-start(f32[256,512]{1,0:T(8,128)S(1)} %get-tuple-element.26), channel_id=1, source_target_pairs={{0,16},{16,0},{1,17},{17,1},{2,18},{18,2},{3,19},{19,3},{4,20},{20... | collective-permute-start | bytes 1572872 | tf_op jit(solution)/shard_map/ppermute | solution.py:35
  114.0 1.5 %collective-permute-done.20 = f32[256,512]{1,0:T(8,128)S(1)} collective-permute-done((f32[256,512]{1,0:T(8,128)S(1)}, f32[256,512]{1,0:T(8,128)S(1)}, u32[]{:S(2)}, u32[]{:S(2)}) %collective-permute-start.20) | collective-permute-done | bytes 524320 | tf_op jit(solution)/shard_map/ppermute | solution.py:35
  115.6 0.9 add_multiply_fusion
  (41 shorter events, 5.5 us)
Async XLA Ops:
  6.5 1.6 %copy-start = (bf16[4096,256]{1,0:T(8,128)(2,1)S(1)}, bf16[4096,256]{1,0:T(8,128)(2,1)}, u32[]{:S(2)}) copy-start(bf16[4096,256]{1,0:T(8,128)(2,1)} %param.7) | copy-start | bytes 6291460
  6.5 91.3 %all-gather.3.cloned.1.call-start = ((), (), s32[]{:S(2)}) async-start(), calls=%async_computation | async-start | bytes 2359296 | tf_op jit(solution)/shard_map/all_gather | solution.py:279
  10.5 16.8 %collective-permute-start = (bf16[256,256]{1,0:T(8,128)(2,1)S(1)}, bf16[256,256]{1,0:T(8,128)(2,1)S(1)}, u32[]{:S(2)}, u32[]{:S(2)}) collective-permute-start(bf16[256,256]{1,0:T(8,128)(2,1)S(1)} %convolution_convert_fusion), channel_id=1, source_target_pairs={{0,0},{1,1},{2,32},{3,33},{4,64},{5,65},{6,96},{7,97},{8,128},{9,1... | collective-permute-start | bytes 393224 | tf_op jit(solution)/shard_map/ppermute | solution.py:249
  13.7 20.8 %collective-permute-start.4 = (bf16[896,512]{1,0:T(8,128)(2,1)}, bf16[896,512]{1,0:T(8,128)(2,1)S(1)}, u32[]{:S(2)}, u32[]{:S(2)}) collective-permute-start(bf16[896,512]{1,0:T(8,128)(2,1)} %refs_3_.1), channel_id=1, source_target_pairs={{0,32},{16,112},{1,33},{17,113},{2,34},{18,114},{3,35},{19,115},{4... | collective-permute-start | bytes 2752520 | tf_op jit(solution)/shard_map/ppermute | solution.py:47
  27.3 14.3 %collective-permute-start.3 = (bf16[2,256,896]{2,1,0:T(8,128)(2,1)}, bf16[2,256,896]{2,1,0:T(8,128)(2,1)}, u32[]{:S(2)}, u32[]{:S(2)}) collective-permute-start(bf16[2,256,896]{2,1,0:T(8,128)(2,1)} %shard_map.46), channel_id=1, source_target_pairs={{0,128},{16,152},{1,129},{17,153},{2,130},{18,154},{3,131},{19,155... | collective-permute-start | bytes 2752520 | tf_op jit(solution)/shard_map/ppermute | solution.py:47
  27.3 16.7 %collective-permute-start.1 = (bf16[256,256]{1,0:T(8,128)(2,1)S(1)}, bf16[256,256]{1,0:T(8,128)(2,1)S(1)}, u32[]{:S(2)}, u32[]{:S(2)}) collective-permute-start(bf16[256,256]{1,0:T(8,128)(2,1)S(1)} %collective-permute-done), channel_id=1, source_target_pairs={{0,8},{16,24},{1,9},{17,25},{2,10},{18,26},{3,11},{19,27},{4,12},{... | collective-permute-start | bytes 393224 | tf_op jit(solution)/shard_map/ppermute | solution.py:35
  29.8 15.5 %collective-permute-start.2 = (bf16[896,512]{1,0:T(8,128)(2,1)}, bf16[896,512]{1,0:T(8,128)(2,1)}, u32[]{:S(2)}, u32[]{:S(2)}) collective-permute-start(bf16[896,512]{1,0:T(8,128)(2,1)} %refs_3_.1), channel_id=1, source_target_pairs={{0,16},{16,0},{1,17},{17,1},{2,18},{18,2},{3,19},{19,3},{4,20},{20... | collective-permute-start | bytes 2752520 | tf_op jit(solution)/shard_map/ppermute | solution.py:35
  34.5 19.0 %copy-start.1 = (bf16[896,512]{1,0:T(8,128)(2,1)}, bf16[896,512]{1,0:T(8,128)(2,1)S(1)}, u32[]{:S(2)}) copy-start(bf16[896,512]{1,0:T(8,128)(2,1)S(1)} %collective-permute-done.4.refs_4_.refs_5_) | copy-start | bytes 2752516
  34.5 13.9 %collective-permute-start.8 = (bf16[896,512]{1,0:T(8,128)(2,1)S(1)}, bf16[896,512]{1,0:T(8,128)(2,1)}, u32[]{:S(2)}, u32[]{:S(2)}) collective-permute-start(bf16[896,512]{1,0:T(8,128)(2,1)S(1)} %collective-permute-done.4.refs_4_.refs_5_), channel_id=1, source_target_pairs={{0,32},{16,112},{1,33},{17,113},{2,34},{18,114},{3,35},{19,115},{4... | collective-permute-start | bytes 2752520 | tf_op jit(solution)/shard_map/ppermute | solution.py:47
  41.6 11.9 %collective-permute-start.5 = (bf16[896,512]{1,0:T(8,128)(2,1)S(1)}, bf16[896,512]{1,0:T(8,128)(2,1)}, u32[]{:S(2)}, u32[]{:S(2)}) collective-permute-start(bf16[896,512]{1,0:T(8,128)(2,1)S(1)} %collective-permute-done.4.refs_4_.refs_5_), channel_id=1, source_target_pairs={{0,16},{16,0},{1,17},{17,1},{2,18},{18,2},{3,19},{19,3},{4,20},{20... | collective-permute-start | bytes 2752520 | tf_op jit(solution)/shard_map/ppermute | solution.py:35
  44.0 14.9 %collective-permute-start.6 = (bf16[896,512]{1,0:T(8,128)(2,1)}, bf16[896,512]{1,0:T(8,128)(2,1)}, u32[]{:S(2)}, u32[]{:S(2)}) collective-permute-start(bf16[896,512]{1,0:T(8,128)(2,1)} %refs_3_.1), channel_id=1, source_target_pairs={{0,96},{16,48},{1,97},{17,49},{2,98},{18,50},{3,99},{19,51},{4,100... | collective-permute-start | bytes 2752520 | tf_op jit(solution)/shard_map/ppermute | solution.py:47
  44.0 23.4 %collective-permute-start.10 = (bf16[4,256,896]{2,1,0:T(8,128)(2,1)}, bf16[4,256,896]{2,1,0:T(8,128)(2,1)}, u32[]{:S(2)}, u32[]{:S(2)}) collective-permute-start(bf16[4,256,896]{2,1,0:T(8,128)(2,1)} %shard_map.47), channel_id=1, source_target_pairs={{0,128},{16,152},{1,129},{17,153},{2,130},{18,154},{3,131},{19,155... | collective-permute-start | bytes 5505032 | tf_op jit(solution)/shard_map/ppermute | solution.py:47
  45.4 13.8 %collective-permute-start.11 = (bf16[2,256,896]{2,1,0:T(8,128)(2,1)}, bf16[2,256,896]{2,1,0:T(8,128)(2,1)}, u32[]{:S(2)}, u32[]{:S(2)}) collective-permute-start(bf16[2,256,896]{2,1,0:T(8,128)(2,1)} %collective-permute-done.3.refs_1_), channel_id=1, source_target_pairs={{0,1},{16,23},{1,2},{17,16},{2,3},{18,17},{3,4},{19,18},{4,5},{20,... | collective-permute-start | bytes 2752520 | tf_op jit(solution)/shard_map/ppermute | solution.py:47
  48.4 15.2 %collective-permute-start.9 = (bf16[896,512]{1,0:T(8,128)(2,1)}, bf16[896,512]{1,0:T(8,128)(2,1)}, u32[]{:S(2)}, u32[]{:S(2)}) collective-permute-start(bf16[896,512]{1,0:T(8,128)(2,1)} %collective-permute-done.8.refs_4_), channel_id=1, source_target_pairs={{0,16},{16,0},{1,17},{17,1},{2,18},{18,2},{3,19},{19,3},{4,20},{20... | collective-permute-start | bytes 2752520 | tf_op jit(solution)/shard_map/ppermute | solution.py:35
  59.0 4.7 %collective-permute-start.7 = (bf16[896,512]{1,0:T(8,128)(2,1)}, bf16[896,512]{1,0:T(8,128)(2,1)S(1)}, u32[]{:S(2)}, u32[]{:S(2)}) collective-permute-start(bf16[896,512]{1,0:T(8,128)(2,1)} %collective-permute-done.6.refs_2_), channel_id=1, source_target_pairs={{0,16},{16,0},{1,17},{17,1},{2,18},{18,2},{3,19},{19,3},{4,20},{20... | collective-permute-start | bytes 2752520 | tf_op jit(solution)/shard_map/ppermute | solution.py:35
  59.2 1.2 copy-start.2
  63.6 7.4 %copy-start.3 = (f32[256,512]{1,0:T(8,128)S(1)}, f32[256,512]{1,0:T(8,128)}, u32[]{:S(2)}) copy-start(f32[256,512]{1,0:T(8,128)} %shard_map.48.refs_6_) | copy-start | bytes 1572868
  70.7 5.9 %collective-permute-start.12 = (f16[256,512]{1,0:T(8,128)(2,1)S(1)}, f16[256,512]{1,0:T(8,128)(2,1)S(1)}, u32[]{:S(2)}, u32[]{:S(2)}) collective-permute-start(f16[256,512]{1,0:T(8,128)(2,1)S(1)} %multiply_convert_fusion), channel_id=1, source_target_pairs={{0,128},{16,144},{1,129},{17,145},{2,130},{18,146},{3,131},{19,147... | collective-permute-start | bytes 786440 | tf_op jit(solution)/shard_map/ppermute | solution.py:58
  76.7 10.2 %collective-permute-start.15 = (bf16[256,512]{1,0:T(8,128)(2,1)S(1)}, bf16[256,512]{1,0:T(8,128)(2,1)S(1)}, u32[]{:S(2)}, u32[]{:S(2)}) collective-permute-start(bf16[256,512]{1,0:T(8,128)(2,1)S(1)} %add_convert_fusion.refs_0_), channel_id=1, source_target_pairs={{0,128},{16,144},{1,129},{17,145},{2,130},{18,146},{3,131},{19,147... | collective-permute-start | bytes 786440 | tf_op jit(solution)/shard_map/ppermute | solution.py:58
  76.8 12.8 %collective-permute-start.16 = (bf16[256,512]{1,0:T(8,128)(2,1)S(1)}, bf16[256,512]{1,0:T(8,128)(2,1)S(1)}, u32[]{:S(2)}, u32[]{:S(2)}) collective-permute-start(bf16[256,512]{1,0:T(8,128)(2,1)S(1)} %add_convert_fusion.refs_0_), channel_id=1, source_target_pairs={{0,64},{16,80},{1,65},{17,81},{2,66},{18,82},{3,67},{19,83},{4,68}... | collective-permute-start | bytes 786440 | tf_op jit(solution)/shard_map/ppermute | solution.py:35
  84.3 6.6 %collective-permute-start.13 = (bf16[256,512]{1,0:T(8,128)(2,1)S(1)}, bf16[256,512]{1,0:T(8,128)(2,1)S(1)}, u32[]{:S(2)}, u32[]{:S(2)}) collective-permute-start(bf16[256,512]{1,0:T(8,128)(2,1)S(1)} %add_convert_fusion.refs_0_), channel_id=1, source_target_pairs={{0,32},{16,48},{1,33},{17,49},{2,34},{18,50},{3,35},{19,51},{4,36}... | collective-permute-start | bytes 786440 | tf_op jit(solution)/shard_map/ppermute | solution.py:35
  84.3 8.2 %collective-permute-start.14 = (bf16[256,512]{1,0:T(8,128)(2,1)S(1)}, bf16[256,512]{1,0:T(8,128)(2,1)S(1)}, u32[]{:S(2)}, u32[]{:S(2)}) collective-permute-start(bf16[256,512]{1,0:T(8,128)(2,1)S(1)} %add_convert_fusion.refs_0_), channel_id=1, source_target_pairs={{0,96},{16,112},{1,97},{17,113},{2,98},{18,114},{3,99},{19,115},{4... | collective-permute-start | bytes 786440 | tf_op jit(solution)/shard_map/ppermute | solution.py:35
  86.9 9.4 %collective-permute-start.17 = (bf16[256,512]{1,0:T(8,128)(2,1)S(1)}, bf16[256,512]{1,0:T(8,128)(2,1)}, u32[]{:S(2)}, u32[]{:S(2)}) collective-permute-start(bf16[256,512]{1,0:T(8,128)(2,1)S(1)} %collective-permute-done.15.refs_3_), channel_id=1, source_target_pairs={{0,32},{16,48},{1,33},{17,49},{2,34},{18,50},{3,35},{19,51},{4,36}... | collective-permute-start | bytes 786440 | tf_op jit(solution)/shard_map/ppermute | solution.py:35
  86.9 9.5 %collective-permute-start.18 = (bf16[256,512]{1,0:T(8,128)(2,1)S(1)}, bf16[256,512]{1,0:T(8,128)(2,1)}, u32[]{:S(2)}, u32[]{:S(2)}) collective-permute-start(bf16[256,512]{1,0:T(8,128)(2,1)S(1)} %collective-permute-done.15.refs_3_), channel_id=1, source_target_pairs={{0,96},{16,112},{1,97},{17,113},{2,98},{18,114},{3,99},{19,115},{4... | collective-permute-start | bytes 786440 | tf_op jit(solution)/shard_map/ppermute | solution.py:35
  89.6 8.2 %collective-permute-start.19 = (bf16[256,512]{1,0:T(8,128)(2,1)S(1)}, bf16[256,512]{1,0:T(8,128)(2,1)}, u32[]{:S(2)}, u32[]{:S(2)}) collective-permute-start(bf16[256,512]{1,0:T(8,128)(2,1)S(1)} %collective-permute-done.16.refs_4_), channel_id=1, source_target_pairs={{0,128},{16,144},{1,129},{17,145},{2,130},{18,146},{3,131},{19,147... | collective-permute-start | bytes 786440 | tf_op jit(solution)/shard_map/ppermute | solution.py:58
  97.9 1.6 %copy-start.4 = (bf16[16,256,256]{2,1,0:T(8,128)(2,1)S(1)}, bf16[16,256,256]{2,1,0:T(8,128)(2,1)}, u32[]{:S(2)}) copy-start(bf16[16,256,256]{2,1,0:T(8,128)(2,1)} %all-gather.3.cloned.1.call-done) | copy-start | bytes 6291460
  103.8 11.8 %collective-permute-start.20 = (f32[256,512]{1,0:T(8,128)S(1)}, f32[256,512]{1,0:T(8,128)S(1)}, u32[]{:S(2)}, u32[]{:S(2)}) collective-permute-start(f32[256,512]{1,0:T(8,128)S(1)} %get-tuple-element.26), channel_id=1, source_target_pairs={{0,16},{16,0},{1,17},{17,1},{2,18},{18,2},{3,19},{19,3},{4,20},{20... | collective-permute-start | bytes 1572872 | tf_op jit(solution)/shard_map/ppermute | solution.py:35
Sparse Core Ops, SparseCore 0:
  44.9 42.5 all-gather.2
